TPU v7x, 32 devices: a whole 2x2x4 slice. The times are simulated.
32 devices in a mesh: row: 8 (over y, x, core), col: 4 (over z).
Axes of the slice: x: 2, y: 2, z: 4, core: 2. Of those that a mesh axis runs over, the one named last changes fastest.
Arguments:
- inputs: bfloat16 [12288, 768], P(('row', 'col')), may hold values from -6 to 6
- attn_gain: bfloat16 [768], replicated, may hold values from 0.5 to 1.5
- qkv_weight: bfloat16 [768, 2304], P('row', 'col'), may hold values from -0.21875 to 0.21875
- out_weight: bfloat16 [768, 768], P('col', 'row'), may hold values from -1.5 to 1.5
- ffn_gain: bfloat16 [768], replicated, may hold values from 0.5 to 1.5
- router_weight: bfloat16 [768, 12], replicated, may hold values from -0.15625 to 0.15625
- carry_weight: bfloat16 [12, 12], replicated, may hold values from -1.75 to 1.75
- const_weight: bfloat16 [2, 768, 2], replicated, may hold values from -0.21875 to 0.21875
- const_vector: bfloat16 [2, 768], replicated, may hold values from -6 to 6
- gate_weight: bfloat16 [8, 768, 2048], P(None, 'row', 'col'), may hold values from -0.21875 to 0.21875
- up_weight: bfloat16 [8, 768, 2048], P(None, 'row', 'col'), may hold values from -0.21875 to 0.21875
- down_weight: bfloat16 [8, 2048, 768], P(None, 'col', 'row'), may hold values from -0.125 to 0.125
- prev_logits: bfloat16 [12, 12288], P(None, ('row', 'col')), may hold values from -4 to 4
- seq_lengths: int32 [8, 4], P('row'), may hold values from 1 to 1533, as said below
- expert_routes: int32 [12288, 2], P('row'), may hold values from 0 to 11, all different within a row; in each aligned block of 1536 rows (0 to 1535, 1536 to 3071, ...) at most 384 rows name the same one
- cotangent: bfloat16 [12288, 768], P(('row', 'col')), may hold values from -6 to 6
Outputs:
- layer_out: bfloat16 [12288, 768], P(('row', 'col'))
- input_grad: float32 [12288, 768], P(('row', 'col'))
- attn_gain_grad: float32 [768], replicated
- qkv_grad: float32 [768, 2304], P('row', 'col')
- out_grad: float32 [768, 768], P('col', 'row')
- ffn_gain_grad: float32 [768], replicated
- router_grad: float32 [768, 12], replicated
- carry_grad: float32 [12, 12], replicated
- const_grad: float32 [2, 768, 2], replicated
- vector_grad: float32 [2, 768], replicated
- gate_grad: float32 [8, 768, 2048], P(None, 'row', 'col')
- up_grad: float32 [8, 768, 2048], P(None, 'row', 'col')
- down_grad: float32 [8, 2048, 768], P(None, 'col', 'row')
- prev_grad: float32 [12, 12288], P(None, ('row', 'col'))
Inputs may be any that keep to these rules, and one draw needn't show every extreme that they name: `seq_lengths`: in each row group the lengths sum to at most 1536; the remaining tokens at the end of the group are padding. One sequence of each group starts within the group's first 384 tokens and ends within its last 384. `expert_routes`: each token names two different routes: 0 to 7 are feed-forward experts, 8 is the zero expert, 9 the copy expert, 10 and 11 the constant experts. Among the tokens of one row group no route is named more than 384 times.
All inputs are finite; a program needn't handle non-finite values.
Results may differ from a plain program's by a relative error of at most 0.02.
Values may be sent and summed in bfloat16 or wider, within the bound.
A program may use at most 256 MiB of HBM per device.

v0:
```python
import math

import jax
import jax.numpy as jnp
from jax import lax
from jax.sharding import PartitionSpec as P

D = 768
HEADS = 12
HEAD_DIM = 64
EXPERTS = 8
ROUTES = 12


EPS = 1e-06
BASE = 10000.0
NEG = -1e30
HIGH = lax.Precision.HIGHEST
CONTRACT_FIRST = (((0,), (0,)), ((), ()))
CONTRACT_LAST = (((1,), (1,)), ((), ()))


def rotate(block_value, positions, first_col, direction):
    row_count, col_count = block_value.shape
    column = first_col + jnp.arange(0, col_count, 2, dtype=jnp.int32)
    inner_col = column % D
    section = column // D
    head_pair = inner_col % HEAD_DIM // 2
    exponent = (2 * head_pair).astype(jnp.float32) / HEAD_DIM
    frequency = jnp.exp(-exponent * math.log(BASE))
    turned_on = (section < 2).astype(jnp.float32)
    angles = positions.astype(jnp.float32)[:, None] * (frequency * turned_on)[None, :]
    cosine = jnp.cos(angles)
    sines = direction * jnp.sin(angles)
    paired = block_value.reshape(row_count, col_count // 2, 2)
    first_part = paired[:, :, 0]
    second_part = paired[:, :, 1]
    rotated = jnp.stack(
        [first_part * cosine - second_part * sines, second_part * cosine + first_part * sines],
        axis=2,
    )
    return rotated.reshape(row_count, col_count)


def sequence_info(lengths_row, row_total):
    seq_count = lengths_row.shape[0]
    ends = jnp.cumsum(lengths_row)
    starts = ends - lengths_row
    token_place = jnp.arange(row_total, dtype=jnp.int32)
    seq_index = jnp.sum((token_place[:, None] >= ends[None, :]).astype(jnp.int32), axis=1)
    member = seq_index[:, None] == jnp.arange(seq_count, dtype=jnp.int32)[None, :]
    begin = jnp.sum(jnp.where(member, starts[None, :], 0), axis=1)
    return (seq_index, token_place - begin, seq_index < seq_count)


def partial_sums(term_value):
    return lax.psum_scatter(
        term_value.astype(jnp.bfloat16), "col", scatter_dimension=0, tiled=True
    ).astype(jnp.float32)


def whole_columns(part_value):
    return lax.all_gather(part_value, "col", axis=0, tiled=True)


def to_heads(block_value):
    return lax.all_to_all(block_value, "col", split_axis=0, concat_axis=1, tiled=True)


def to_features(block_value):
    return lax.all_to_all(block_value, "col", split_axis=1, concat_axis=0, tiled=True)


def key_scores(query_heads, key_block, query_seq, query_place, key_seq, key_place, score_scale):
    raw_scores = (
        jnp.einsum("qhd,khd->hqk", query_heads, key_block, preferred_element_type=jnp.float32)
        * score_scale
    )
    allowed = (query_seq[:, None] == key_seq[None, :]) & (
        key_place[None, :] <= query_place[:, None]
    )
    return (jnp.where(allowed[None], raw_scores, NEG), allowed)


def split_keys(key_values, seq_index, token_place, block_rows):
    count_blocks = key_values.shape[0] // block_rows
    blocks_kv = key_values.reshape(count_blocks, block_rows, 2, HEADS, HEAD_DIM)
    return (
        blocks_kv,
        seq_index.reshape(count_blocks, block_rows),
        token_place.reshape(count_blocks, block_rows),
    )


def attend_forward(
    queries, key_values, query_seq, query_place, seq_index, token_place, block_rows, score_scale
):
    local_rows = queries.shape[0]
    query_heads = queries.reshape(local_rows, HEADS, HEAD_DIM)
    key_items = split_keys(key_values, seq_index, token_place, block_rows)

    def max_step(running, block_items):
        running_max, running_sum = running
        kv_block, key_seq, key_place = block_items
        scores, allowed = key_scores(
            query_heads, kv_block[:, 0], query_seq, query_place, key_seq, key_place, score_scale
        )
        new_max = jnp.maximum(running_max, jnp.max(scores, axis=2))
        shifted = jnp.where(allowed[None], jnp.exp(scores - new_max[:, :, None]), 0.0)
        new_sum = running_sum * jnp.exp(running_max - new_max) + jnp.sum(shifted, axis=2)
        return ((new_max, new_sum), None)

    start_state = (
        jnp.full((HEADS, local_rows), NEG, jnp.float32),
        jnp.zeros((HEADS, local_rows), jnp.float32),
    )
    (final_max, final_sum), unused = lax.scan(max_step, start_state, key_items)
    log_total = final_max + jnp.log(final_sum)

    def out_step(running, block_items):
        kv_block, key_seq, key_place = block_items
        scores, allowed = key_scores(
            query_heads, kv_block[:, 0], query_seq, query_place, key_seq, key_place, score_scale
        )
        probs_low = jnp.exp(scores - log_total[:, :, None]).astype(jnp.bfloat16)
        return (
            running
            + jnp.einsum(
                "hqk,khd->qhd", probs_low, kv_block[:, 1], preferred_element_type=jnp.float32
            ),
            None,
        )

    attended, unused = lax.scan(
        out_step, jnp.zeros((local_rows, HEADS, HEAD_DIM), jnp.float32), key_items
    )
    return (attended.reshape(local_rows, D), log_total)


def attend_backward(
    queries,
    key_values,
    log_total,
    row_delta,
    grad_heads_in,
    query_seq,
    query_place,
    seq_index,
    token_place,
    block_rows,
    score_scale,
):
    local_rows = queries.shape[0]
    query_heads = queries.reshape(local_rows, HEADS, HEAD_DIM)
    grad_heads = grad_heads_in.reshape(local_rows, HEADS, HEAD_DIM)
    key_items = split_keys(key_values, seq_index, token_place, block_rows)

    def grad_step(running, block_items):
        kv_block, key_seq, key_place = block_items
        scores, allowed = key_scores(
            query_heads, kv_block[:, 0], query_seq, query_place, key_seq, key_place, score_scale
        )
        probs_full = jnp.exp(scores - log_total[:, :, None])
        probs_low = probs_full.astype(jnp.bfloat16)
        grad_probs = jnp.einsum(
            "qhd,khd->hqk", grad_heads, kv_block[:, 1], preferred_element_type=jnp.float32
        )
        grad_scores = (probs_full * (grad_probs - row_delta[:, :, None])).astype(jnp.bfloat16)
        new_running = (
            running
            + jnp.einsum(
                "hqk,khd->qhd", grad_scores, kv_block[:, 0], preferred_element_type=jnp.float32
            )
            * score_scale
        )
        grad_keys = (
            jnp.einsum("hqk,qhd->khd", grad_scores, query_heads, preferred_element_type=jnp.float32)
            * score_scale
        )
        grad_values = jnp.einsum(
            "hqk,qhd->khd", probs_low, grad_heads, preferred_element_type=jnp.float32
        )
        return (new_running, jnp.stack([grad_keys, grad_values], axis=1))

    grad_queries, grad_kv = lax.scan(
        grad_step, jnp.zeros((local_rows, HEADS, HEAD_DIM), jnp.float32), key_items
    )
    return (grad_queries.reshape(local_rows, D), grad_kv.reshape(key_values.shape[0], 2 * D))


def on_device(
    inputs,
    attn_gain,
    qkv_weight,
    out_weight,
    ffn_gain,
    router_weight,
    carry_weight,
    const_weight,
    const_vector,
    gate_weight,
    up_weight,
    down_weight,
    prev_logits,
    seq_lengths,
    expert_routes,
    cotangent,
):
    col_index = lax.axis_index("col")
    row_total = expert_routes.shape[0]
    local_rows = inputs.shape[0]
    capacity = row_total // 4
    block_rows = min(row_total, 512)
    score_scale = 1.0 / math.sqrt(HEAD_DIM)
    full_weights = (
        lax.all_gather(qkv_weight, "row", axis=0, tiled=True),
        lax.all_gather(out_weight, "row", axis=1, tiled=True),
        lax.all_gather(gate_weight, "row", axis=1, tiled=True),
        lax.all_gather(up_weight, "row", axis=1, tiled=True),
        lax.all_gather(down_weight, "row", axis=2, tiled=True),
    )
    qkv_full, out_full, gate_full, up_full, down_full = full_weights
    whole_in, whole_cot, whole_prev = (
        lax.all_gather(inputs, "col", axis=0, tiled=True),
        lax.all_gather(cotangent, "col", axis=0, tiled=True),
        lax.all_gather(prev_logits, "col", axis=1, tiled=True),
    )
    seq_index, positions, valid_all = sequence_info(seq_lengths[0], row_total)
    token_place = jnp.arange(row_total, dtype=jnp.int32)
    first_row = col_index * local_rows

    def own_rows(whole_value):
        return lax.dynamic_slice_in_dim(whole_value, first_row, local_rows, 0)

    query_seq = own_rows(seq_index)
    query_place = own_rows(token_place)
    query_pos = own_rows(positions)
    query_valid = own_rows(valid_all).astype(jnp.float32)[:, None]
    input_rows = whole_in.astype(jnp.float32)
    attn_gain_full = attn_gain.astype(jnp.float32)
    scale_attn = lax.rsqrt(jnp.mean(input_rows * input_rows, axis=1, keepdims=True) + EPS)
    normed1 = (input_rows * scale_attn * attn_gain_full).astype(jnp.bfloat16)
    projected = jnp.dot(normed1, qkv_full, preferred_element_type=jnp.float32)
    turned = rotate(projected, positions, col_index * projected.shape[1], 1.0).astype(jnp.bfloat16)
    token_qkv = to_heads(turned)
    queries = token_qkv[:, :D]
    key_values = lax.all_gather(token_qkv[:, D:], "col", axis=0, tiled=True)
    attended, log_total = attend_forward(
        queries, key_values, query_seq, query_place, seq_index, token_place, block_rows, score_scale
    )
    attn_tok = (attended * query_valid).astype(jnp.bfloat16)
    attn_feat = to_features(attn_tok)
    attn_out = partial_sums(jnp.dot(attn_feat, out_full, preferred_element_type=jnp.float32))
    input_local = inputs.astype(jnp.float32)
    middle = input_local + attn_out
    scale_ffn = lax.rsqrt(jnp.mean(middle * middle, axis=1, keepdims=True) + EPS)
    ffn_gain_full = ffn_gain.astype(jnp.float32)
    normed2_local = (middle * scale_ffn * ffn_gain_full).astype(jnp.bfloat16)
    normed2 = whole_columns(normed2_local)
    carry_full = carry_weight.astype(jnp.float32)
    prev_rows = whole_prev.astype(jnp.float32).T
    route_hot = (
        expert_routes[:, :, None] == jnp.arange(ROUTES, dtype=jnp.int32)[None, None, :]
    ).astype(jnp.float32)
    logits = jnp.dot(normed2, router_weight, preferred_element_type=jnp.float32) + jnp.dot(
        prev_rows, carry_full, precision=HIGH
    )
    picked = jnp.sum(route_hot * logits[:, None, :], axis=2)
    gate_values = jax.nn.softmax(picked, axis=1)
    flat_route = expert_routes.reshape(-1)
    route_hits = (flat_route[:, None] == jnp.arange(EXPERTS, dtype=jnp.int32)[None, :]).astype(
        jnp.int32
    )
    slot_index = jnp.sum((jnp.cumsum(route_hits, axis=0) - 1) * route_hits, axis=1)
    dump_slot = EXPERTS * capacity
    target = jnp.where(flat_route < EXPERTS, flat_route * capacity + slot_index, dump_slot)
    slot_owner = (
        jnp.full((dump_slot + 1,), row_total, jnp.int32)
        .at[target]
        .set(jnp.arange(2 * row_total, dtype=jnp.int32) // 2)[:dump_slot]
    )
    slot_gate = (
        jnp.zeros((dump_slot + 1,), jnp.float32)
        .at[target]
        .set(gate_values.reshape(-1))[:dump_slot]
        .reshape(EXPERTS, capacity, 1)
    )
    zero_row = jnp.zeros((1, D), jnp.bfloat16)
    expert_in = jnp.concatenate([normed2, zero_row], axis=0)[slot_owner].reshape(
        EXPERTS, capacity, D
    )
    gate_pre = jnp.einsum("ecd,edf->ecf", expert_in, gate_full, preferred_element_type=jnp.float32)
    up_pre = jnp.einsum("ecd,edf->ecf", expert_in, up_full, preferred_element_type=jnp.float32)
    sigmoid_gate = jax.nn.sigmoid(gate_pre)
    activated = gate_pre * sigmoid_gate
    hidden = (activated * up_pre).astype(jnp.bfloat16)
    expert_out = jnp.einsum("ecf,efd->ecd", hidden, down_full, preferred_element_type=jnp.float32)
    out_rows = jnp.concatenate(
        [expert_out.reshape(dump_slot, D), jnp.zeros((1, D), jnp.float32)], axis=0
    )
    chosen_out = out_rows[target].reshape(row_total, 2, D)
    cot_rows = whole_cot.astype(jnp.float32)
    ffn_mix = jnp.sum(gate_values[:, :, None] * chosen_out, axis=1)
    ffn_dots = jnp.sum(cot_rows[:, None, :] * chosen_out, axis=2)
    mix_local = partial_sums(ffn_mix)
    normed_local = normed2_local.astype(jnp.float32)
    vector_full = const_vector.astype(jnp.float32)
    routes_local = own_rows(expert_routes)
    gates_local = own_rows(gate_values)
    hot_local = own_rows(route_hot)
    copy_hit = (routes_local == EXPERTS + 1).astype(jnp.float32)
    const_hit = (
        routes_local[:, :, None] == (EXPERTS + 2 + jnp.arange(2, dtype=jnp.int32))[None, None, :]
    ).astype(jnp.float32)
    copy_share = jnp.sum(gates_local * copy_hit, axis=1)
    const_share = jnp.sum(gates_local[:, :, None] * const_hit, axis=1)
    const_alpha = jax.nn.softmax(
        jnp.einsum("td,jdk->tjk", normed2_local, const_weight, preferred_element_type=jnp.float32),
        axis=2,
    )
    keep_share = copy_share + jnp.sum(const_share * const_alpha[:, :, 0], axis=1)
    local_mix = keep_share[:, None] * normed_local + jnp.dot(
        const_share * const_alpha[:, :, 1], vector_full, precision=HIGH
    )
    layer_out = (middle + mix_local + local_mix).astype(jnp.bfloat16)
    qkv_full, out_full, gate_full, up_full, down_full = full_weights
    ffn_total = lax.psum(ffn_dots, "col")
    ffn_local = own_rows(ffn_total)
    cot_local = cotangent.astype(jnp.float32)
    dot_keep = jnp.sum(cot_local * normed_local, axis=1)
    dot_vector = jnp.dot(cot_local, vector_full.T, precision=HIGH)
    const_dots = const_alpha[:, :, 0] * dot_keep[:, None] + const_alpha[:, :, 1] * dot_vector
    grad_gates = (
        ffn_local
        + copy_hit * dot_keep[:, None]
        + jnp.sum(const_hit * const_dots[:, None, :], axis=2)
    )
    grad_picked = gates_local * (
        grad_gates - jnp.sum(gates_local * grad_gates, axis=1, keepdims=True)
    )
    grad_logits = jnp.sum(hot_local * grad_picked[:, :, None], axis=1)
    prev_local = prev_logits.astype(jnp.float32).T
    router_grad = lax.dot_general(normed_local, grad_logits, CONTRACT_FIRST, precision=HIGH)
    carry_grad = lax.dot_general(prev_local, grad_logits, CONTRACT_FIRST, precision=HIGH)
    prev_grad = lax.dot_general(carry_full, grad_logits, CONTRACT_LAST, precision=HIGH)
    grad_alpha_keep = const_share * dot_keep[:, None]
    grad_alpha_vector = const_share * dot_vector
    alpha_mean = const_alpha[:, :, 0] * grad_alpha_keep + const_alpha[:, :, 1] * grad_alpha_vector
    grad_alpha_logits = jnp.stack(
        [
            const_alpha[:, :, 0] * (grad_alpha_keep - alpha_mean),
            const_alpha[:, :, 1] * (grad_alpha_vector - alpha_mean),
        ],
        axis=2,
    )
    const_grad = jnp.einsum("td,tjk->jdk", normed_local, grad_alpha_logits, precision=HIGH)
    vector_grad = lax.dot_general(
        const_share * const_alpha[:, :, 1], cot_local, CONTRACT_FIRST, precision=HIGH
    )
    router_full = router_weight.astype(jnp.float32)
    const_full = const_weight.astype(jnp.float32)
    grad_normed_local = (
        keep_share[:, None] * cot_local
        + lax.dot_general(grad_logits, router_full, CONTRACT_LAST, precision=HIGH)
        + jnp.einsum("tjk,jdk->td", grad_alpha_logits, const_full, precision=HIGH)
    )
    cot_in = jnp.concatenate([whole_cot, zero_row], axis=0)[slot_owner].reshape(
        EXPERTS, capacity, D
    )
    grad_expert = (slot_gate * cot_in.astype(jnp.float32)).astype(jnp.bfloat16)
    down_grad = jnp.einsum("ecf,ecd->efd", hidden, grad_expert, preferred_element_type=jnp.float32)
    grad_hidden = jnp.einsum(
        "ecd,efd->ecf", grad_expert, down_full, preferred_element_type=jnp.float32
    )
    grad_gate_pre = (
        grad_hidden * up_pre * sigmoid_gate * (1.0 + gate_pre * (1.0 - sigmoid_gate))
    ).astype(jnp.bfloat16)
    grad_up_pre = (grad_hidden * activated).astype(jnp.bfloat16)
    gate_grad = jnp.einsum(
        "ecd,ecf->edf", expert_in, grad_gate_pre, preferred_element_type=jnp.float32
    )
    up_grad = jnp.einsum("ecd,ecf->edf", expert_in, grad_up_pre, preferred_element_type=jnp.float32)
    grad_expert_in = jnp.einsum(
        "ecf,edf->ecd", grad_gate_pre, gate_full, preferred_element_type=jnp.float32
    ) + jnp.einsum("ecf,edf->ecd", grad_up_pre, up_full, preferred_element_type=jnp.float32)
    grad_slots = jnp.concatenate(
        [grad_expert_in.reshape(dump_slot, D), jnp.zeros((1, D), jnp.float32)], axis=0
    )
    grad_tokens = jnp.sum(grad_slots[target].reshape(row_total, 2, D), axis=1)
    grad_normed = partial_sums(grad_tokens) + grad_normed_local
    gained_ffn = grad_normed * ffn_gain_full
    ffn_dots_rows = jnp.sum(gained_ffn * middle, axis=1, keepdims=True)
    grad_middle = scale_ffn * gained_ffn - middle * scale_ffn**3 * (ffn_dots_rows / D)
    ffn_gain_grad = jnp.sum(grad_normed * middle * scale_ffn, axis=0)
    grad_resid = cot_local + grad_middle
    branch_cot = whole_columns(grad_resid.astype(jnp.bfloat16))
    out_grad = lax.dot_general(
        attn_feat, branch_cot, CONTRACT_FIRST, preferred_element_type=jnp.float32
    )
    grad_mixed = lax.dot_general(
        branch_cot, out_full, CONTRACT_LAST, preferred_element_type=jnp.float32
    )
    grad_tok = to_heads(grad_mixed.astype(jnp.bfloat16))
    grad_heads_in = (grad_tok.astype(jnp.float32) * query_valid).astype(jnp.bfloat16)
    row_delta = jnp.sum(
        grad_heads_in.astype(jnp.float32).reshape(local_rows, HEADS, HEAD_DIM)
        * attended.reshape(local_rows, HEADS, HEAD_DIM),
        axis=2,
    ).T
    grad_queries, grad_kv = attend_backward(
        queries,
        key_values,
        log_total,
        row_delta,
        grad_heads_in,
        query_seq,
        query_place,
        seq_index,
        token_place,
        block_rows,
        score_scale,
    )
    grad_kv_local = lax.psum_scatter(
        grad_kv.astype(jnp.bfloat16), "col", scatter_dimension=0, tiled=True
    ).astype(jnp.float32)
    grad_turned = jnp.concatenate([grad_queries, grad_kv_local], axis=1)
    grad_proj_tok = rotate(grad_turned, query_pos, 0, -1.0).astype(jnp.bfloat16)
    grad_projected = to_features(grad_proj_tok)
    qkv_grad = lax.dot_general(
        normed1, grad_projected, CONTRACT_FIRST, preferred_element_type=jnp.float32
    )
    grad_normed1 = partial_sums(
        lax.dot_general(grad_projected, qkv_full, CONTRACT_LAST, preferred_element_type=jnp.float32)
    )
    scale_attn_local = own_rows(scale_attn)
    gained_attn = grad_normed1 * attn_gain_full
    attn_dots_rows = jnp.sum(gained_attn * input_local, axis=1, keepdims=True)
    input_grad = (
        grad_resid
        + scale_attn_local * gained_attn
        - input_local * scale_attn_local**3 * (attn_dots_rows / D)
    )
    attn_gain_grad = jnp.sum(grad_normed1 * input_local * scale_attn_local, axis=0)
    qkv_grad, out_grad, gate_grad, up_grad, down_grad = (
        lax.psum_scatter(
            qkv_grad.astype(jnp.bfloat16), "row", scatter_dimension=0, tiled=True
        ).astype(jnp.float32),
        lax.psum_scatter(
            out_grad.astype(jnp.bfloat16), "row", scatter_dimension=1, tiled=True
        ).astype(jnp.float32),
        lax.psum_scatter(
            gate_grad.astype(jnp.bfloat16), "row", scatter_dimension=1, tiled=True
        ).astype(jnp.float32),
        lax.psum_scatter(
            up_grad.astype(jnp.bfloat16), "row", scatter_dimension=1, tiled=True
        ).astype(jnp.float32),
        lax.psum_scatter(
            down_grad.astype(jnp.bfloat16), "row", scatter_dimension=2, tiled=True
        ).astype(jnp.float32),
    )
    attn_gain_grad, ffn_gain_grad, router_grad, carry_grad, const_grad, vector_grad = lax.psum(
        (attn_gain_grad, ffn_gain_grad, router_grad, carry_grad, const_grad, vector_grad),
        ("row", "col"),
    )
    return (
        layer_out,
        input_grad,
        attn_gain_grad,
        qkv_grad,
        out_grad,
        ffn_gain_grad,
        router_grad,
        carry_grad,
        const_grad,
        vector_grad,
        gate_grad,
        up_grad,
        down_grad,
        prev_grad,
    )


def solution(mesh):
    placed = (
        P(("row", "col"), None),
        P(),
        P("row", "col"),
        P("col", "row"),
        P(),
        P(),
        P(),
        P(),
        P(),
        P(None, "row", "col"),
        P(None, "row", "col"),
        P(None, "col", "row"),
        P(None, ("row", "col")),
        P("row", None),
        P("row", None),
        P(("row", "col"), None),
    )
    return jax.shard_map(
        on_device,
        mesh=mesh,
        in_specs=placed,
        out_specs=(
            P(("row", "col"), None),
            P(("row", "col"), None),
            P(),
            P("row", "col"),
            P("col", "row"),
            P(),
            P(),
            P(),
            P(),
            P(),
            P(None, "row", "col"),
            P(None, "row", "col"),
            P(None, "col", "row"),
            P(None, ("row", "col")),
        ),
        check_vma=False,
    )
```

profile of v0, /device:TPU:0, one launch (start us, length us, event | category | flops | bytes accessed | tf_op | source)
XLA Modules:
  0.0 1503.8 jit_solution(2507498035337334190)
XLA Ops:
  23.7 39.2 %all-gather.9.cloned.1.call-done = bf16[1536,768]{1,0:T(8,128)(2,1)} async-done(((bf16[384,768]{1,0:T(8,128)(2,1)}), bf16[1536,768]{1,0:T(8,128)(2,1)}) %all-gather.9.cloned.1.call-update) | async-done | bytes 2359312 | tf_op jit(solution)/shard_map/all_gather | solution.py:224
  93.4 44.1 %all_to_all.61 = bf16[4,384,576]{1,2,0:T(8,128)(2,1)S(1)} all-to-all(bf16[4,384,576]{1,2,0:T(8,128)(2,1)S(1)} %copy.250), channel_id=1, replica_groups=mesh['row'=8,'col'=4] {'col'}, dimensions={0} | all-to-all | bytes 3538944 | tf_op jit(solution)/shard_map/all_to_all | solution.py:67
  138.9 88.3 %all-gather.11.cloned.1.call-done = bf16[1536,1536]{0,1:T(8,128)(2,1)} async-done(((bf16[384,1536]{0,1:T(8,128)(2,1)}), bf16[1536,1536]{0,1:T(8,128)(2,1)}) %all-gather.11.cloned.1.call-update) | async-done | bytes 4718608 | tf_op jit(solution)/shard_map/all_gather | solution.py:247
  245.4 39.1 %while.37 = (s32[]{:T(128)}, f32[12,384]{1,0:T(8,128)S(1)}, f32[12,384]{1,0:T(8,128)S(1)}, s32[384]{0:T(512)S(1)}, s32[3,512]{1,0:T(4,128)S(1)}, /*index=5*/s32[...) while((s32[]{:T(128)}, f32[12,384]{1,0:T(8,128)S(1)}, ...), condition=%wide.region_7.8_spmd.clone, body=%wide.region_4.7_spmd.clone.sunk | while | flops 321477120 | bytes 24241288 | solution.py:117
  284.5 20.2 %while.38 = (s32[]{:T(128)}, f32[384,12,64]{0,2,1:T(8,128)}, bf16[3,512,2,12,64]{1,4,3,2,0:T(8,128)(2,1)}, s32[384]{0:T(512)S(1)}, s32[3,512]{1,0:T(4,128)S(1)},...) while((s32[]{:T(128)}, f32[384,12,64]{0,2,1:T(8,128)}, ...), condition=%wide.region_9.10_spmd.clone, body=%wide.region_8.9_spmd.clone.sunk | while | flops 614596608 | bytes 8094855 | solution.py:134
  331.1 46.2 %reduce-scatter.15.cloned.1.call-done = bf16[384,768]{1,0:T(8,128)(2,1)} async-done(((bf16[1536,768]{1,0:T(8,128)(2,1)}), bf16[384,768]{1,0:T(8,128)(2,1)}) %reduce-scatter.15.cloned.1.call-update) | async-done | bytes 589840 | tf_op jit(solution)/shard_map/reduce_scatter | solution.py:57
  414.7 14.7 all-gather.21.cloned.1.call-done
  431.2 13.6 gather_fusion.2
  452.2 28.4 %all-gather.13.cloned.1.call-done = bf16[1536,768]{1,0:T(8,128)(2,1)} async-done(((bf16[384,768]{1,0:T(8,128)(2,1)}), bf16[1536,768]{1,0:T(8,128)(2,1)}) %all-gather.13.cloned.1.call-update) | async-done | bytes 2359312 | tf_op jit(solution)/shard_map/all_gather | solution.py:63
  482.5 13.6 gather_fusion
  511.4 15.4 %all-gather.15.cloned.1.call-done = bf16[8,768,512]{2,1,0:T(8,128)(2,1)} async-done(((bf16[8,96,512]{2,1,0:T(8,128)(2,1)}), bf16[8,768,512]{2,1,0:T(8,128)(2,1)}) %all-gather.15.cloned.1.call-update) | async-done | bytes 6291472 | tf_op jit(solution)/shard_map/all_gather | solution.py:218
  536.3 38.0 %all-gather.17.cloned.1.call-done = bf16[8,768,512]{2,1,0:T(8,128)(2,1)} async-done(((bf16[8,96,512]{2,1,0:T(8,128)(2,1)}), bf16[8,768,512]{2,1,0:T(8,128)(2,1)}) %all-gather.17.cloned.1.call-update) | async-done | bytes 6291472 | tf_op jit(solution)/shard_map/all_gather | solution.py:219
  583.7 38.0 %all-gather.19.cloned.1.call-done = bf16[8,512,768]{1,2,0:T(8,128)(2,1)} async-done(((bf16[8,512,96]{1,2,0:T(8,128)(2,1)}), bf16[8,512,768]{1,2,0:T(8,128)(2,1)}) %all-gather.19.cloned.1.call-update) | async-done | bytes 6291472 | tf_op jit(solution)/shard_map/all_gather | solution.py:220
  621.7 14.4 multiply_convert_fusion.1
  660.7 19.2 %gather_fusion.3 = f32[3072,768]{1,0:T(8,128)} fusion(f32[3073,768]{1,0:T(8,128)} %concatenate.18, s32[3072]{0:T(1024)S(1)} %broadcast_clamp_fusion), kind=kCustom, calls=%fused_computation.3 | custom fusion | bytes 18886656 | tf_op jit(solution)/shard_map/gather | solution.py:389
  691.9 27.5 %reduce_sum.231 = bf16[1536,768]{1,0:T(8,128)(2,1)} reduce(f32[1536,2,768]{2,1,0:T(2,128)} %reshape.800, f32[]{:T(128)} %constant.178.clone.1), dimensions={1}, to_apply=%region_27.28 | reduce | flops 1179648 | bytes 11796484 | tf_op jit(solution)/shard_map/reduce_sum | solution.py:389
  735.6 19.2 %gather_fusion.1 = f32[3072,768]{1,0:T(8,128)} fusion(f32[3073,768]{1,0:T(8,128)} %concatenate.16, s32[3072]{0:T(1024)S(1)} %broadcast_clamp_fusion), kind=kCustom, calls=%fused_computation.1 | custom fusion | bytes 18886656 | tf_op jit(solution)/shard_map/gather | solution.py:301
  766.9 24.3 %multiply_reduce_fusion = (f32[1536,2]{1,0:T(8,128)}, bf16[1536,768]{1,0:T(8,128)(2,1)}) fusion(f32[1536,2,768]{2,1,0:T(2,128)} %reshape.798, f32[1536,768]{1,0:T(8,128)} %convert_element_type.237, f32[1536,2]{1,0:T(8,128)S(1)} %copy.255), kind=kLoop, calls=%fused_computation.60 | loop fusion | flops 8254464 | bytes 16539648 | tf_op jit(solution)/shard_map/reduce_sum | solution.py:304
  792.7 19.2 %psum.49 = f32[1536,2]{0,1:T(2,128)S(1)} all-reduce(f32[1536,2]{0,1:T(2,128)S(1)} %copy.264), channel_id=1, replica_groups=mesh['row'=8,'col'=4] {'col'}, use_global_device_ids=true, to_apply=%region_30.31 | all-reduce | flops 3072 | bytes 24576 | tf_op jit(solution)/shard_map/psum | solution.py:327
  818.7 47.9 %all-gather.23.cloned.1.call-done = bf16[1536,768]{1,0:T(8,128)(2,1)} async-done(((bf16[384,768]{1,0:T(8,128)(2,1)}), bf16[1536,768]{1,0:T(8,128)(2,1)}) %all-gather.23.cloned.1.call-update) | async-done | bytes 2359312 | tf_op jit(solution)/shard_map/all_gather | solution.py:63
  874.4 16.1 %all-to-all-done.2 = bf16[4,384,192]{1,2,0:T(8,128)(2,1)} async-done(((bf16[4,384,192]{1,2,0:T(8,128)(2,1)}), bf16[4,384,192]{1,2,0:T(8,128)(2,1)}, u32[]{:S(2)}, u32[]{:S(2)}) %all-to-all-start.2) | async-done | bytes 589856 | tf_op jit(solution)/shard_map/all_to_all | solution.py:67
  892.7 64.9 %while.39 = (s32[]{:T(128)}, f32[384,12,64]{0,2,1:T(8,128)S(1)}, bf16[3,512,2,12,64]{1,4,3,2,0:T(8,128)(2,1)}, bf16[3,512,2,12,64]{1,4,3,2,0:T(8,128)(2,1)}, s32...) while((s32[]{:T(128)}, f32[384,12,64]{0,2,1:T(8,128)S(1)}, ...), condition=%wide.region_38.39_spmd.clone, body=%wide.region_37.38_spmd.clone.sunk | while | flops 1538949120 | bytes 116278632 | solution.py:185
  957.7 18.2 %copy.288 = bf16[3,512,2,12,64]{4,3,2,1,0:T(8,128)(2,1)} copy(bf16[3,512,2,12,64]{1,4,3,2,0:T(8,128)(2,1)} %get-tuple-element.176) | data formatting | bytes 9437184
  975.9 16.3 %reshape.857 = bf16[1536,1536]{1,0:T(8,128)(2,1)} reshape(bf16[3,512,2,12,64]{4,3,2,1,0:T(8,128)(2,1)} %copy.288) | data formatting | bytes 9437184
  1029.0 47.7 %reduce-scatter.31.cloned.1.call-done = bf16[384,1536]{1,0:T(8,128)(2,1)} async-done(((bf16[1536,1536]{1,0:T(8,128)(2,1)}), bf16[384,1536]{1,0:T(8,128)(2,1)}) %reduce-scatter.31.cloned.1.call-update) | async-done | bytes 1179664
  1119.7 45.2 %all_to_all.62 = bf16[384,4,576]{0,2,1:T(8,128)(2,1)S(1)} all-to-all(bf16[384,4,576]{0,2,1:T(8,128)(2,1)S(1)} %convert_element_type.250), channel_id=1, replica_groups=mesh['row'=8,'col'=4] {'col'}, dimensions={1} | all-to-all | bytes 3538944 | tf_op jit(solution)/shard_map/all_to_all | solution.py:71
  1181.3 48.1 %reduce-scatter.25.cloned.1.call-done = bf16[8,96,512]{2,1,0:T(8,128)(2,1)} async-done(((bf16[8,768,512]{2,1,0:T(8,128)(2,1)}), bf16[8,96,512]{2,1,0:T(8,128)(2,1)}) %reduce-scatter.25.cloned.1.call-update) | async-done | bytes 786448 | tf_op jit(solution)/shard_map/reduce_scatter | solution.py:451
  1231.9 62.9 %reduce-scatter.27.cloned.1.call-done = bf16[8,96,512]{2,1,0:T(8,128)(2,1)} async-done(((bf16[8,768,512]{2,1,0:T(8,128)(2,1)}), bf16[8,96,512]{2,1,0:T(8,128)(2,1)}) %reduce-scatter.27.cloned.1.call-update) | async-done | bytes 786448 | tf_op jit(solution)/shard_map/reduce_scatter | solution.py:454
  1297.3 62.5 %reduce-scatter.29.cloned.1.call-done = bf16[8,512,96]{1,2,0:T(8,128)(2,1)} async-done(((bf16[8,512,768]{1,2,0:T(8,128)(2,1)}), bf16[8,512,96]{1,2,0:T(8,128)(2,1)}) %reduce-scatter.29.cloned.1.call-update) | async-done | bytes 786448 | tf_op jit(solution)/shard_map/reduce_scatter | solution.py:457
  1362.3 37.3 %reduce-scatter.23.cloned.1.call-done = bf16[96,576]{1,0:T(8,128)(2,1)} async-done(((bf16[768,576]{1,0:T(8,128)(2,1)}), bf16[96,576]{1,0:T(8,128)(2,1)}) %reduce-scatter.23.cloned.1.call-update) | async-done | bytes 110608 | tf_op jit(solution)/shard_map/reduce_scatter | solution.py:445
  1401.2 48.6 %reduce-scatter.21.cloned.1.call-done = bf16[384,768]{1,0:T(8,128)(2,1)} async-done(((bf16[1536,768]{1,0:T(8,128)(2,1)}), bf16[384,768]{1,0:T(8,128)(2,1)}) %reduce-scatter.21.cloned.1.call-update) | async-done | bytes 589840 | tf_op jit(solution)/shard_map/reduce_scatter | solution.py:57
  1451.4 41.6 %all-reduce.4 = (f32[768]{0:T(1024)}, f32[768]{0:T(1024)}, f32[768,12]{0,1:T(8,128)}, f32[12,12]{0,1:T(8,128)S(1)}, f32[2,768,2]{1,2,0:T(2,128)}, /*index=5*/f32[2,768]{1,0:T(2,128)}) all-reduce(f32[768]{0:T(1024)S(1)} %get-tuple-element.611, f32[768]{0:T(1024)S(1)} %copy-done.71, ...), channel_id=1, replica_groups=mesh['row'=8,'col'=4] {'row','col'}, use_global_device_ids=true, to_apply=%region_43.44 | all-reduce | flops 15504 | bytes 124032 | tf_op jit(solution)/shard_map/psum | solution.py:461
  (442 shorter events, 491.4 us)
Async XLA Ops:
  7.2 488.9 %copy-start = (bf16[768,12]{0,1:T(8,128)(2,1)S(1)}, bf16[768,12]{0,1:T(8,128)(2,1)}, u32[]{:S(2)}) copy-start(bf16[768,12]{0,1:T(8,128)(2,1)} %param.27) | copy-start | bytes 55300
  7.2 55.6 %all-gather.9.cloned.1.call-start = ((), (), s32[]{:S(2)}) async-start(), calls=%async_computation.14 | async-start | bytes 2949120 | tf_op jit(solution)/shard_map/all_gather | solution.py:224
  7.9 219.3 %all-gather.11.cloned.1.call-start = ((), (), s32[]{:S(2)}) async-start(), calls=%async_computation.15 | async-start | bytes 5898240 | tf_op jit(solution)/shard_map/all_gather | solution.py:247
  8.7 60.1 %copy-start.52 = (f32[768]{0:T(1024)}, f32[768]{0:T(1024)S(1)}, u32[]{:S(2)}) copy-start(f32[768]{0:T(1024)S(1)} %convert_element_type.210) | copy-start | bytes 9220
  138.8 166.0 %copy-start.67 = (f32[384]{0:T(512)}, f32[384]{0:T(512)S(1)}, u32[]{:S(2)}) copy-start(f32[384]{0:T(512)S(1)} %get-tuple-element.688) | copy-start | bytes 4612
  307.2 19.7 %all-to-all-start.1 = ((bf16[384,4,192]{0,2,1:T(8,128)(2,1)}), bf16[384,4,192]{0,2,1:T(8,128)(2,1)S(1)}, u32[]{:S(2)}, u32[]{:S(2)}) async-start(bf16[384,4,192]{0,2,1:T(8,128)(2,1)} %fusion.70), calls=%async_computation.1 | async-start | bytes 1179648 | tf_op jit(solution)/shard_map/all_to_all | solution.py:71
  310.7 66.6 %reduce-scatter.15.cloned.1.call-start = ((), (), s32[]{:S(2)}) async-start(), calls=%async_computation.16 | async-start | bytes 2949120 | tf_op jit(solution)/shard_map/reduce_scatter | solution.py:57
  330.0 99.3 %all-gather.21.cloned.1.call-start = ((), (), s32[]{:S(2)}) async-start(), calls=%async_computation.22 | async-start | bytes 2949120 | tf_op jit(solution)/shard_map/all_gather | solution.py:225
  330.6 150.1 %all-gather.13.cloned.1.call-start = ((), (), s32[]{:S(2)}) async-start(), calls=%async_computation.17 | async-start | bytes 2949120 | tf_op jit(solution)/shard_map/all_gather | solution.py:63
  381.5 145.3 %all-gather.15.cloned.1.call-start = ((), (), s32[]{:S(2)}) async-start(), calls=%async_computation.18 | async-start | bytes 7077888 | tf_op jit(solution)/shard_map/all_gather | solution.py:218
  382.1 192.2 %all-gather.17.cloned.1.call-start = ((), (), s32[]{:S(2)}) async-start(), calls=%async_computation.19 | async-start | bytes 7077888 | tf_op jit(solution)/shard_map/all_gather | solution.py:219
  382.8 238.9 %all-gather.19.cloned.1.call-start = ((), (), s32[]{:S(2)}) async-start(), calls=%async_computation.20 | async-start | bytes 7077888 | tf_op jit(solution)/shard_map/all_gather | solution.py:220
  383.6 430.4 %reduce-scatter.19.cloned.1.call-start = ((), (), s32[]{:S(2)}) async-start(), calls=%async_computation.23 | async-start | bytes 2949120 | tf_op jit(solution)/shard_map/reduce_scatter | solution.py:57
  511.4 110.4 %copy-start.45 = (f32[8,384]{1,0:T(8,128)}, f32[8,384]{1,0:T(8,128)S(1)}, u32[]{:S(2)}) copy-start(f32[8,384]{1,0:T(8,128)S(1)} %mul.552) | copy-start | bytes 36868
  719.4 147.2 %all-gather.23.cloned.1.call-start = ((), (), s32[]{:S(2)}) async-start(), calls=%async_computation.24 | async-start | bytes 2949120 | tf_op jit(solution)/shard_map/all_gather | solution.py:63
  724.2 87.8 %copy-start.40 = (f32[384,2,1]{0,2,1:T(1,128)}, f32[384,2,1]{0,2,1:T(1,128)S(1)}, u32[]{:S(2)}) copy-start(f32[384,2,1]{0,2,1:T(1,128)S(1)} %get-tuple-element.714) | copy-start | bytes 9220
  817.4 51.9 %copy-start.13 = (f32[384,768]{1,0:T(8,128)}, f32[384,768]{1,0:T(8,128)S(1)}, u32[]{:S(2)}) copy-start(f32[384,768]{1,0:T(8,128)S(1)} %get-tuple-element.725) | copy-start | bytes 3538948
  870.1 20.4 %all-to-all-start.2 = ((bf16[4,384,192]{1,2,0:T(8,128)(2,1)}), bf16[4,384,192]{1,2,0:T(8,128)(2,1)}, u32[]{:S(2)}, u32[]{:S(2)}) async-start(bf16[4,384,192]{1,2,0:T(8,128)(2,1)} %bitcast.248), calls=%async_computation.5 | async-start | bytes 1179648 | tf_op jit(solution)/shard_map/all_to_all | solution.py:67
  874.3 202.4 %reduce-scatter.31.cloned.1.call-start = ((), (), s32[]{:S(2)}) async-start(), calls=%async_computation.30 | async-start | bytes 5898240
  992.2 184.4 %reduce-scatter.17.cloned.1.call-start = ((), (), s32[]{:S(2)}) async-start(), calls=%async_computation.21 | async-start | bytes 2949120 | tf_op jit(solution)/shard_map/reduce_scatter | solution.py:57
  992.8 186.9 %reduce-scatter.33.cloned.1.call-start = ((), (), s32[]{:S(2)}) async-start(), calls=%async_computation.31 | async-start | bytes 442368
  996.5 232.9 %reduce-scatter.25.cloned.1.call-start = ((), (), s32[]{:S(2)}) async-start(), calls=%async_computation.27 | async-start | bytes 7077888 | tf_op jit(solution)/shard_map/reduce_scatter | solution.py:451
  1006.9 287.9 %reduce-scatter.27.cloned.1.call-start = ((), (), s32[]{:S(2)}) async-start(), calls=%async_computation.28 | async-start | bytes 7077888 | tf_op jit(solution)/shard_map/reduce_scatter | solution.py:454
  1016.4 343.4 %reduce-scatter.29.cloned.1.call-start = ((), (), s32[]{:S(2)}) async-start(), calls=%async_computation.29 | async-start | bytes 7077888 | tf_op jit(solution)/shard_map/reduce_scatter | solution.py:457
  1027.9 371.7 %reduce-scatter.23.cloned.1.call-start = ((), (), s32[]{:S(2)}) async-start(), calls=%async_computation.26 | async-start | bytes 1105920 | tf_op jit(solution)/shard_map/reduce_scatter | solution.py:445
  1170.0 279.8 %reduce-scatter.21.cloned.1.call-start = ((), (), s32[]{:S(2)}) async-start(), calls=%async_computation.25 | async-start | bytes 2949120 | tf_op jit(solution)/shard_map/reduce_scatter | solution.py:57
  1297.3 154.1 %copy-start.71 = (f32[768]{0:T(1024)S(1)}, f32[768]{0:T(1024)}, u32[]{:S(2)}) copy-start(f32[768]{0:T(1024)} %get-tuple-element.609) | copy-start | bytes 9220
  1297.3 196.4 %copy-start.14 = (f32[384,768]{1,0:T(8,128)S(1)}, f32[384,768]{1,0:T(8,128)}, u32[]{:S(2)}) copy-start(f32[384,768]{1,0:T(8,128)} %copy-done.13) | copy-start | bytes 3538948
  1297.3 196.4 %copy-start.39 = (f32[768]{0:T(1024)S(1)}, f32[768]{0:T(1024)}, u32[]{:S(2)}) copy-start(f32[768]{0:T(1024)} %copy-done.37) | copy-start | bytes 9220
  1297.3 196.4 %copy-start.44 = (f32[384]{0:T(512)S(1)}, f32[384]{0:T(512)}, u32[]{:S(2)}) copy-start(f32[384]{0:T(512)} %copy-done.42) | copy-start | bytes 4612
  1297.3 196.4 %copy-start.64 = (f32[384]{0:T(512)S(1)}, f32[384]{0:T(512)}, u32[]{:S(2)}) copy-start(f32[384]{0:T(512)} %get-tuple-element.716) | copy-start | bytes 4612
  1297.3 196.4 %copy-start.66 = (f32[384]{0:T(512)S(1)}, f32[384]{0:T(512)}, u32[]{:S(2)}) copy-start(f32[384]{0:T(512)} %copy-done.65) | copy-start | bytes 4612
  (81 other events, 873.9 us)
Sparse Core Ops, SparseCore 0:
  9.6 53.1 all-gather.8
  138.8 88.3 all-gather.10
  330.1 47.0 reduce-scatter.14
  378.7 50.6 all-gather.20
  431.4 49.2 all-gather.12
  482.4 44.3 all-gather.14
  528.7 45.5 all-gather.16
  576.2 45.5 all-gather.18
  719.6 48.0 reduce-scatter.18
  818.8 47.7 all-gather.22
  992.3 84.2 reduce-scatter.30
  1078.8 48.5 reduce-scatter.16
  1131.1 33.3 reduce-scatter.32
  1167.6 61.7 reduce-scatter.24
  1233.0 61.7 reduce-scatter.26
  1298.0 61.7 reduce-scatter.28
  1363.7 35.7 reduce-scatter.22
  1401.7 48.0 reduce-scatter.20
where the time goes:
time: 1520 us; the launch traced here: 1500 us
  waiting for transfers between devices  690 us (45%)
  local copies, waits for them, and re-layouts  269 us (18%)
  matrix products  201 us (13%)
  blocking collectives  186 us (12%)
  other arithmetic  132 us (9%)
  between operations  15.9 us (1%)
    reduce_scatter x4, waiting for transfers between devices, partial_sums(): lax.psum_scatter(term_value.astype(jnp.bfloat16), 'col', scatter_dimensio...  94.8 us
    all_gather x1, waiting for transfers between devices, on_device(): key_values = lax.all_gather(token_qkv[:, D:], 'col', axis=0, tiled=True)  88.3 us
    all_gather x2, waiting for transfers between devices, whole_columns(): return lax.all_gather(part_value, 'col', axis=0, tiled=True)  76.4 us
    reduce_scatter x1, waiting for transfers between devices, on_device(): lax.psum_scatter(up_grad.astype(jnp.bfloat16), 'row', scatter_dimension=1...  62.9 us
    reduce_scatter x1, waiting for transfers between devices, on_device(): lax.psum_scatter(down_grad.astype(jnp.bfloat16), 'row', scatter_dimension...  62.5 us
    unnamed x155, local copies, waits for them, and re-layouts  58.6 us
    unnamed x20, waiting for transfers between devices  51.5 us
    reduce_scatter x1, waiting for transfers between devices, on_device(): lax.psum_scatter(gate_grad.astype(jnp.bfloat16), 'row', scatter_dimension...  48.1 us
  transfers between devices with their start and end apart: 20, of which 17 were waited for; matrix products, arithmetic and copies ran while one was open for 18% of the time, Pallas kernels for 0%

commit v1 on v0

--- a/solution.py
+++ b/solution.py
@@ -1,8 +1,11 @@
+import functools
 import math
 
 import jax
 import jax.numpy as jnp
 from jax import lax
+from jax.experimental import pallas as pl
+from jax.experimental.pallas import tpu as pltpu
 from jax.sharding import PartitionSpec as P
 
 D = 768
@@ -480,7 +483,722 @@
     )
 
 
+BF = jnp.bfloat16
+F32 = jnp.float32
+LANES = 128
+NN = (((1,), (0,)), ((), ()))
+NT = (((1,), (1,)), ((), ()))
+TN = (((0,), (0,)), ((), ()))
+ROW_CONST = 12
+ROW_VEC = 16
+ROW_GAIN = 18
+SMALL_ROWS = 24
+Q_ROWS = 256
+MIB = 1 << 20
+
+
+def mm(a, b, dims=NN):
+    return lax.dot_general(a, b, dims, preferred_element_type=F32)
+
+
+def lane_iota(shape):
+    return lax.broadcasted_iota(jnp.int32, shape, len(shape) - 1)
+
+
+def whole(shape):
+    return pl.BlockSpec(shape, lambda *_: (0,) * len(shape), pipeline_mode=pl.Buffered(1))
+
+
+def swap_pairs(v):
+    even = lane_iota(v.shape) % 2 == 0
+    return jnp.where(even, pltpu.roll(v, LANES - 1, 1), pltpu.roll(v, 1, 1))
+
+
+def norm_rows(x):
+    return lax.rsqrt(jnp.mean(x * x, axis=1, keepdims=True) + EPS)
+
+
+def qkv_kernel(heads, x_ref, gain_ref, w_ref, cos_ref, sin_ref, out_ref):
+    x = x_ref[...].astype(F32)
+    normed = (x * norm_rows(x) * gain_ref[...]).astype(BF)
+    proj = mm(normed, w_ref[...])
+    cosine, sines = cos_ref[...], sin_ref[...]
+    width = heads * HEAD_DIM
+    for part in range(2 * width // LANES):
+        v = proj[:, part * LANES : (part + 1) * LANES]
+        t = v * cosine + swap_pairs(v) * sines
+        for half in range(2):
+            head = 2 * part + half
+            piece = t[:, half * HEAD_DIM : (half + 1) * HEAD_DIM].astype(BF)
+            if head < heads:
+                piece = piece * jnp.asarray(1.0 / math.sqrt(HEAD_DIM), BF)
+            out_ref[head] = piece
+    for head in range(2 * heads, 3 * heads):
+        out_ref[head] = proj[:, head * HEAD_DIM : (head + 1) * HEAD_DIM].astype(BF)
+
+
+def project_heads(heads, whole_in, gain, weight, cosine, sines):
+    rows = whole_in.shape[0]
+    blk = 256
+    return pl.pallas_call(
+        functools.partial(qkv_kernel, heads),
+        grid=(rows // blk,),
+        out_shape=jax.ShapeDtypeStruct((3 * heads, rows, HEAD_DIM), BF),
+        in_specs=[
+            pl.BlockSpec((blk, D), lambda i: (i, 0)),
+            whole((1, D)),
+            whole((D, 3 * heads * HEAD_DIM)),
+            pl.BlockSpec((blk, LANES), lambda i: (i, 0)),
+            pl.BlockSpec((blk, LANES), lambda i: (i, 0)),
+        ],
+        out_specs=pl.BlockSpec((3 * heads, blk, HEAD_DIM), lambda i: (0, i, 0)),
+        compiler_params=pltpu.CompilerParams(vmem_limit_bytes=32 * MIB),
+        cost_estimate=pl.CostEstimate(
+            flops=2 * rows * D * 3 * heads * HEAD_DIM, bytes_accessed=8 * MIB, transcendentals=0
+        ),
+        name="project_heads",
+    )(whole_in, gain, weight, cosine, sines)
+
+
+def seen(begin, first, rows, length):
+    u = lax.broadcasted_iota(jnp.int32, (rows, length), 1)
+    t = lax.broadcasted_iota(jnp.int32, (rows, length), 0) + first
+    return (u >= begin) & (u <= t)
+
+
+def attend_kernel(q_ref, k_ref, v_ref, begin_ref, valid_ref, o_ref, lse_ref):
+    rows = q_ref.shape[1]
+    for i in range(rows // Q_ROWS):
+        at = slice(i * Q_ROWS, (i + 1) * Q_ROWS)
+        length = (i + 1) * Q_ROWS
+        s = mm(q_ref[0, at], k_ref[0, :length], NT)
+        s = jnp.where(seen(begin_ref[at], i * Q_ROWS, Q_ROWS, length), s, NEG)
+        top = jnp.max(s, axis=1, keepdims=True)
+        p = jnp.exp(s - top)
+        total = jnp.sum(p, axis=1, keepdims=True)
+        o = mm(p.astype(BF), v_ref[0, :length]) * (valid_ref[at] / total)
+        o_ref[0, at] = o.astype(BF)
+        lse_ref[0, at] = top + jnp.log(total)
+
+
+def attend(heads, qkv, begin, valid):
+    rows = qkv.shape[1]
+    head_block = (1, rows, HEAD_DIM)
+    return pl.pallas_call(
+        attend_kernel,
+        grid=(heads,),
+        out_shape=(
+            jax.ShapeDtypeStruct((heads, rows, HEAD_DIM), BF),
+            jax.ShapeDtypeStruct((heads, rows, 1), F32),
+        ),
+        in_specs=[
+            pl.BlockSpec(head_block, lambda h: (h, 0, 0)),
+            pl.BlockSpec(head_block, lambda h: (h + heads, 0, 0)),
+            pl.BlockSpec(head_block, lambda h: (h + 2 * heads, 0, 0)),
+            whole((rows, 1)),
+            whole((rows, 1)),
+        ],
+        out_specs=(
+            pl.BlockSpec(head_block, lambda h: (h, 0, 0)),
+            pl.BlockSpec((1, rows, 1), lambda h: (h, 0, 0)),
+        ),
+        compiler_params=pltpu.CompilerParams(vmem_limit_bytes=48 * MIB),
+        cost_estimate=pl.CostEstimate(
+            flops=8 * heads * rows * rows * HEAD_DIM, bytes_accessed=8 * MIB, transcendentals=heads * rows * rows
+        ),
+        name="attend",
+    )(qkv, qkv, qkv, begin, valid)
+
+
+def attend_back_kernel(
+    q_ref, k_ref, v_ref, begin_ref, o_ref, lse_ref, do_ref, dq_ref, dk_ref, dv_ref
+):
+    rows = q_ref.shape[1]
+    score_scale = 1.0 / math.sqrt(HEAD_DIM)
+    count = rows // Q_ROWS
+    for i in reversed(range(count)):
+        at = slice(i * Q_ROWS, (i + 1) * Q_ROWS)
+        length = (i + 1) * Q_ROWS
+        q, do = q_ref[0, at], do_ref[0, at]
+        k, v = k_ref[0, :length], v_ref[0, :length]
+        delta = jnp.sum(do.astype(F32) * o_ref[0, at].astype(F32), axis=1, keepdims=True)
+        s = mm(q, k, NT)
+        ok = seen(begin_ref[at], i * Q_ROWS, Q_ROWS, length)
+        p = jnp.where(ok, jnp.exp(s - lse_ref[0, at]), 0.0)
+        dp = mm(do, v, NT)
+        ds = (p * (dp - delta)).astype(BF)
+        dq_ref[0, at] = mm(ds, k) * score_scale
+        dk, dv = mm(ds, q, TN), mm(p.astype(BF), do, TN)
+        if i == count - 1:
+            dk_ref[0], dv_ref[0] = dk, dv
+        else:
+            dk_ref[0, :length] += dk
+            dv_ref[0, :length] += dv
+
+
+def attend_back(heads, qkv, begin, mixed, lse, grad_mixed):
+    rows = qkv.shape[1]
+    head_block = (1, rows, HEAD_DIM)
+    per_head = pl.BlockSpec(head_block, lambda h: (h, 0, 0))
+    grad = jax.ShapeDtypeStruct((heads, rows, HEAD_DIM), F32)
+    return pl.pallas_call(
+        attend_back_kernel,
+        grid=(heads,),
+        out_shape=(grad, grad, grad),
+        in_specs=[
+            per_head,
+            pl.BlockSpec(head_block, lambda h: (h + heads, 0, 0)),
+            pl.BlockSpec(head_block, lambda h: (h + 2 * heads, 0, 0)),
+            whole((rows, 1)),
+            per_head,
+            pl.BlockSpec((1, rows, 1), lambda h: (h, 0, 0)),
+            per_head,
+        ],
+        out_specs=(per_head, per_head, per_head),
+        compiler_params=pltpu.CompilerParams(vmem_limit_bytes=56 * MIB),
+        cost_estimate=pl.CostEstimate(
+            flops=20 * heads * rows * rows * HEAD_DIM, bytes_accessed=12 * MIB, transcendentals=heads * rows * rows
+        ),
+        name="attend_back",
+    )(qkv, qkv, qkv, begin, mixed, lse, grad_mixed)
+
+
+def branch_kernel(a_ref, w_ref, x_ref, gain_ref, mixed_ref, middle_ref, normed_ref):
+    mixed = jnp.concatenate([a_ref[i] for i in range(a_ref.shape[0])], axis=1)
+    mixed_ref[...] = mixed
+    middle = x_ref[...].astype(F32) + mm(mixed, w_ref[...], NT)
+    middle_ref[...] = middle
+    normed_ref[...] = (middle * norm_rows(middle) * gain_ref[...]).astype(BF)
+
+
+def branch(attn_parts, out_t, inputs, gain):
+    rows = inputs.shape[0]
+    return pl.pallas_call(
+        branch_kernel,
+        out_shape=(
+            jax.ShapeDtypeStruct((rows, D), BF),
+            jax.ShapeDtypeStruct((rows, D), F32),
+            jax.ShapeDtypeStruct((rows, D), BF),
+        ),
+        compiler_params=pltpu.CompilerParams(vmem_limit_bytes=32 * MIB),
+        cost_estimate=pl.CostEstimate(flops=2 * rows * D * D, bytes_accessed=6 * MIB, transcendentals=0),
+        name="branch",
+    )(attn_parts, out_t, inputs, gain)
+
+
+def gate_lanes(logits, routes):
+    lane = lane_iota(logits.shape)
+    hit = (lane == routes[:, 0:1]) | (lane == routes[:, 1:2])
+    held = jnp.where(hit, logits, NEG)
+    e = jnp.where(hit, jnp.exp(held - jnp.max(held, axis=1, keepdims=True)), 0.0)
+    return e / jnp.sum(e, axis=1, keepdims=True)
+
+
+def moe_kernel(ranks, capacity, *refs):
+    (n2_ref, cotx_ref, rw_ref, carry_ref, routes_ref, tsr_ref, tsc_ref), refs = refs[:7], refs[7:]
+    w_parts, refs = refs[:ranks], refs[ranks:]
+    (mix_ref, gtx_ref), refs = refs[:2], refs[2:]
+    g_parts, refs = refs[:ranks], refs[ranks:]
+    wbuf, wsem, gbuf, gsem, gates, mix_acc, gt_acc = refs
+    e = pl.program_id(0)
+    me = lax.axis_index("row")
+    experts = pl.num_programs(0)
+    rows = n2_ref.shape[0]
+    depth = w_parts[0].shape[2]
+    slot = lax.rem(e, 2)
+
+    def at(m):
+        return pl.ds(pl.multiple_of((me ^ m) * depth, 16), depth)
+
+    def w_copies(expert, place):
+        return [
+            pltpu.make_async_copy(
+                w_parts[m].at[t, expert], wbuf.at[place, t, at(m)], wsem.at[place, t * ranks + m]
+            )
+            for t in range(3)
+            for m in range(ranks)
+        ]
+
+    def g_copies(expert, place):
+        return [
+            pltpu.make_async_copy(
+                gbuf.at[place, t, at(m)], g_parts[m].at[t, expert], gsem.at[place, t * ranks + m]
+            )
+            for t in range(3)
+            for m in range(ranks)
+        ]
+
+    @pl.when(e == 0)
+    def _():
+        for c in w_copies(0, 0):
+            c.start()
+        logits = mm(n2_ref[...], rw_ref[...], NT) + mm(cotx_ref[:, D:], carry_ref[...])
+        g = gate_lanes(logits, routes_ref[...])
+        high = g.astype(BF)
+        gates[:, :LANES] = high
+        gates[:, LANES:] = (g - high.astype(F32)).astype(BF)
+        mix_acc[...] = jnp.zeros_like(mix_acc)
+        gt_acc[...] = jnp.zeros_like(gt_acc)
+
+    @pl.when(e + 1 < experts)
+    def _():
+        for c in w_copies(e + 1, 1 - slot):
+            c.start()
+
+    one = jnp.where(lax.broadcasted_iota(jnp.int32, (capacity, rows), 0) == tsr_ref[0], 1.0, 0.0).astype(BF)
+    x = mm(one, n2_ref[...]).astype(BF)
+    c = mm(one, cotx_ref[:, :D]).astype(BF)
+    sg = mm(one, gates[...])
+    sg = jnp.sum(jnp.where(lane_iota(sg.shape) % LANES == e, sg, 0.0), axis=1, keepdims=True)
+
+    for cp in w_copies(e, slot):
+        cp.wait()
+    wg, wu, wd = wbuf.at[slot, 0], wbuf.at[slot, 1], wbuf.at[slot, 2]
+    g = mm(x, wg[...])
+    u = mm(x, wu[...])
+    v = mm(c, wd[...])
+    sig = jax.nn.sigmoid(g)
+    act = g * sig
+    h = act * u
+    dot = jnp.sum(h * v, axis=1, keepdims=True)
+    gh = (h * sg).astype(BF)
+    gv = v * sg
+    dg = (gv * u * (sig * (1.0 + g * (1.0 - sig)))).astype(BF)
+    du = (gv * act).astype(BF)
+    y = mm(gh, wd[...], NT).astype(BF)
+    dx = (mm(dg, wg[...], NT) + mm(du, wu[...], NT)).astype(BF)
+    dot_high = dot.astype(BF).astype(F32)
+    lane = lane_iota((capacity, LANES))
+    dots = jnp.where(lane == e, dot_high, 0.0) + jnp.where(lane == e + EXPERTS, dot - dot_high, 0.0)
+    dxx = jnp.concatenate([dx, dots.astype(BF)], axis=1)
+
+    tsc = jnp.sum(jnp.where(lane_iota(tsc_ref.shape) == e, tsc_ref[...], 0), axis=1, keepdims=True)
+    step = 256
+    for b in range(rows // step):
+        rs = slice(b * step, (b + 1) * step)
+        one_t = jnp.where(lane_iota((step, capacity)) == tsc[rs], 1.0, 0.0).astype(BF)
+        mix_acc[rs] += mm(one_t, y)
+        gt_acc[rs] += mm(one_t, dxx)
+
+    @pl.when(e >= 2)
+    def _():
+        for cp in g_copies(e - 2, slot):
+            cp.wait()
+
+    gbuf[slot, 0] = mm(x, dg, TN).astype(BF)
+    gbuf[slot, 1] = mm(x, du, TN).astype(BF)
+    gbuf[slot, 2] = mm(c, gh, TN).astype(BF)
+    for cp in g_copies(e, slot):
+        cp.start()
+
+    @pl.when(e == experts - 1)
+    def _():
+        mix_ref[...] = mix_acc[...].astype(BF)
+        gtx_ref[...] = gt_acc[...].astype(BF)
+        for cp in g_copies(e - 1, 1 - slot) + g_copies(e, slot):
+            cp.wait()
+
+
+def experts_both_ways(n2, cotx, rw, carry, routes, slots, w_parts):
+    rows = n2.shape[0]
+    capacity = rows // 4
+    ranks = len(w_parts)
+    three, experts, depth, ff = w_parts[0].shape
+    anyspec = pl.BlockSpec(memory_space=pl.ANY)
+    outs = pl.pallas_call(
+        functools.partial(moe_kernel, ranks, capacity),
+        grid=(experts,),
+        out_shape=[
+            jax.ShapeDtypeStruct((rows, D), BF),
+            jax.ShapeDtypeStruct((rows, D + LANES), BF),
+        ]
+        + [jax.ShapeDtypeStruct((three, experts, depth, ff), BF)] * ranks,
+        in_specs=[
+            whole((rows, D)),
+            whole((rows, D + LANES)),
+            whole((LANES, D)),
+            whole((LANES, LANES)),
+            whole((rows, 2)),
+            pl.BlockSpec((1, 1, rows), lambda e: (e, 0, 0)),
+            whole((rows, experts)),
+        ]
+        + [anyspec] * ranks,
+        out_specs=[whole((rows, D)), whole((rows, D + LANES))] + [anyspec] * ranks,
+        scratch_shapes=[
+            pltpu.VMEM((2, 3, depth * ranks, ff), BF),
+            pltpu.SemaphoreType.DMA((2, 3 * ranks)),
+            pltpu.VMEM((2, 3, depth * ranks, ff), BF),
+            pltpu.SemaphoreType.DMA((2, 3 * ranks)),
+            pltpu.VMEM((rows, 2 * LANES), BF),
+            pltpu.VMEM((rows, D), F32),
+            pltpu.VMEM((rows, D + LANES), F32),
+        ],
+        compiler_params=pltpu.CompilerParams(vmem_limit_bytes=60 * MIB),
+        cost_estimate=pl.CostEstimate(
+            flops=experts * capacity * 2 * D * (9 * ff + 5 * rows),
+            bytes_accessed=48 * MIB,
+            transcendentals=experts * capacity * ff,
+        ),
+        name="experts_both_ways",
+    )(n2, cotx, rw, carry, routes, slots.T[:, None, :], slots, *w_parts)
+    return outs[0], outs[1], outs[2:]
+
+
+def resid_kernel(
+    gtx_ref,
+    n2_ref,
+    middle_ref,
+    cot_ref,
+    routes_ref,
+    prev_ref,
+    rw_ref,
+    carry_ref,
+    gain_ref,
+    out_t_ref,
+    mixed_ref,
+    valid_ref,
+    midmix_ref,
+    resid_ref,
+    gm_ref,
+    og_ref,
+    small_ref,
+    pg_ref,
+):
+    n2, cot = n2_ref[...], cot_ref[...]
+    n2f, cotf = n2.astype(F32), cot.astype(F32)
+    middle = middle_ref[...]
+    rw = rw_ref[...]
+    lin = mm(n2, rw, NT)
+    prev = prev_ref[...]
+    gates = gate_lanes(lin + mm(prev, carry_ref[...]), routes_ref[...])
+    rows = n2.shape[0]
+    lane = lane_iota((rows, LANES))
+    cot_lin = mm(cot, rw, NT)
+    dot_keep = jnp.sum(cotf * n2f, axis=1, keepdims=True)
+    copy_share = gates[:, EXPERTS + 1 : EXPERTS + 2]
+    d = gtx_ref[:, D:].astype(F32)
+    g_gates = jnp.where(lane < EXPERTS, d + pltpu.roll(d, LANES - EXPERTS, 1), 0.0)
+    g_gates = jnp.where(lane == EXPERTS + 1, dot_keep, g_gates)
+    keep = copy_share
+    mixes, packs = [], jnp.zeros((rows, LANES), F32)
+    for j in range(2):
+        l0 = lin[:, ROW_CONST + 2 * j : ROW_CONST + 2 * j + 1]
+        l1 = lin[:, ROW_CONST + 2 * j + 1 : ROW_CONST + 2 * j + 2]
+        top = jnp.maximum(l0, l1)
+        e0, e1 = jnp.exp(l0 - top), jnp.exp(l1 - top)
+        a0, a1 = e0 / (e0 + e1), e1 / (e0 + e1)
+        share = gates[:, EXPERTS + 2 + j : EXPERTS + 3 + j]
+        dot_vec = cot_lin[:, ROW_VEC + j : ROW_VEC + j + 1]
+        keep = keep + share * a0
+        mixes.append(share * a1)
+        g_gates = jnp.where(lane == EXPERTS + 2 + j, a0 * dot_keep + a1 * dot_vec, g_gates)
+        gk, gv = share * dot_keep, share * dot_vec
+        mean = a0 * gk + a1 * gv
+        packs = packs + jnp.where(lane == ROW_CONST + 2 * j, a0 * (gk - mean), 0.0)
+        packs = packs + jnp.where(lane == ROW_CONST + 2 * j + 1, a1 * (gv - mean), 0.0)
+        packs = packs + jnp.where(lane == ROW_VEC + j, share * a1, 0.0)
+    packs = packs + gates * (g_gates - jnp.sum(gates * g_gates, axis=1, keepdims=True))
+    vec = rw[ROW_VEC : ROW_VEC + 2].astype(F32)
+    midmix_ref[...] = middle + keep * n2f + mixes[0] * vec[0:1] + mixes[1] * vec[1:2]
+
+    high = packs.astype(BF)
+    low = (packs - high.astype(F32)).astype(BF)
+    back = lane < ROW_VEC
+    high_b, low_b = jnp.where(back, high, 0), jnp.where(back, low, 0)
+    grad_normed = (
+        gtx_ref[:, :D].astype(F32) + keep * cotf + mm(high_b, rw) + mm(low_b, rw)
+    )
+    by_n2 = mm(high, n2, TN) + mm(low, n2, TN)
+    by_cot = mm(high, cot, TN) + mm(low, cot, TN)
+    by_prev = mm(high, prev, TN) + mm(low, prev, TN)
+    pg = mm(carry_ref[...], high_b, NT) + mm(carry_ref[...], low_b, NT)
+    pg_ref[...] = pg[:ROUTES]
+
+    scale = norm_rows(middle)
+    gained = grad_normed * gain_ref[...]
+    mid_dot = jnp.sum(gained * middle, axis=1, keepdims=True)
+    resid = cotf + scale * gained - middle * (scale * scale * scale * (mid_dot * (1.0 / D)))
+    resid_ref[...] = resid
+    gain_grad = jnp.sum(grad_normed * middle * scale, axis=0, keepdims=True)
+    sub = lax.broadcasted_iota(jnp.int32, (SMALL_ROWS, D), 0)
+    small = jnp.where(sub < ROW_VEC, by_n2[:SMALL_ROWS], by_cot[:SMALL_ROWS])
+    small = jnp.where(sub >= ROW_GAIN, jnp.where(sub == ROW_GAIN, gain_grad, 0.0), small)
+    small_ref[:, :D] = small
+    small_ref[:, D:] = by_prev[:SMALL_ROWS]
+
+    cut = resid.astype(BF)
+    gm = (mm(cut, out_t_ref[...]) * valid_ref[...]).astype(BF)
+    parts, _, width = gm_ref.shape
+    for i in range(parts):
+        gm_ref[i] = gm[:, i * width : (i + 1) * width]
+    og_ref[...] = mm(cut, mixed_ref[...], TN).astype(BF)
+
+
+def resid_step(parts, gtx, n2, middle, cot, routes, prev, rw, carry, gain, out_t, mixed, valid):
+    rows = n2.shape[0]
+    return pl.pallas_call(
+        resid_kernel,
+        out_shape=(
+            jax.ShapeDtypeStruct((rows, D), F32),
+            jax.ShapeDtypeStruct((rows, D), F32),
+            jax.ShapeDtypeStruct((parts, rows, D // parts), BF),
+            jax.ShapeDtypeStruct((D, D), BF),
+            jax.ShapeDtypeStruct((SMALL_ROWS, D + LANES), F32),
+            jax.ShapeDtypeStruct((ROUTES, rows), F32),
+        ),
+        compiler_params=pltpu.CompilerParams(vmem_limit_bytes=48 * MIB),
+        cost_estimate=pl.CostEstimate(flops=6 * rows * D * D, bytes_accessed=12 * MIB, transcendentals=0),
+        name="resid_step",
+    )(gtx, n2, middle, cot, routes, prev, rw, carry, gain, out_t, mixed, valid)
+
+
+def project_back_kernel(
+    heads, dq_ref, dk_ref, dv_ref, x_ref, gain_ref, w_ref, cos_ref, sin_ref, gn_ref, wg_ref, gg_ref, acc
+):
+    step = pl.program_id(0)
+    cosine, sines = cos_ref[...], sin_ref[...]
+    turned = [dq_ref[h] for h in range(heads)] + [dk_ref[h] for h in range(heads)]
+    cols = []
+    for part in range(heads):
+        v = jnp.concatenate(turned[2 * part : 2 * part + 2], axis=1)
+        cols.append((v * cosine - swap_pairs(v) * sines).astype(BF))
+    cols += [dv_ref[h].astype(BF) for h in range(heads)]
+    gp = jnp.concatenate(cols, axis=1)
+    x = x_ref[...].astype(F32)
+    xs = x * norm_rows(x)
+    normed = (xs * gain_ref[...]).astype(BF)
+    gn = mm(gp, w_ref[...], NT)
+    gn_ref[...] = gn.astype(BF)
+    part_grad = mm(normed, gp, TN)
+    gain_part = jnp.sum(gn * xs, axis=0, keepdims=True)
+
+    @pl.when(step == 0)
+    def _():
+        acc[...] = part_grad
+        gg_ref[...] = gain_part
+
+    @pl.when(step > 0)
+    def _():
+        acc[...] += part_grad
+        gg_ref[...] += gain_part
+
+    @pl.when(step == pl.num_programs(0) - 1)
+    def _():
+        wg_ref[...] = acc[...].astype(BF)
+
+
+def project_back(heads, dq, dk, dv, whole_in, gain, weight, cosine, sines):
+    rows = whole_in.shape[0]
+    blk = 256
+    width = 3 * heads * HEAD_DIM
+    head_spec = pl.BlockSpec((heads, blk, HEAD_DIM), lambda i: (0, i, 0))
+    return pl.pallas_call(
+        functools.partial(project_back_kernel, heads),
+        grid=(rows // blk,),
+        out_shape=(
+            jax.ShapeDtypeStruct((rows, D), BF),
+            jax.ShapeDtypeStruct((D, width), BF),
+            jax.ShapeDtypeStruct((1, D), F32),
+        ),
+        in_specs=[
+            head_spec,
+            head_spec,
+            head_spec,
+            pl.BlockSpec((blk, D), lambda i: (i, 0)),
+            whole((1, D)),
+            whole((D, width)),
+            pl.BlockSpec((blk, LANES), lambda i: (i, 0)),
+            pl.BlockSpec((blk, LANES), lambda i: (i, 0)),
+        ],
+        out_specs=(pl.BlockSpec((blk, D), lambda i: (i, 0)), whole((D, width)), whole((1, D))),
+        scratch_shapes=[pltpu.VMEM((D, width), F32)],
+        compiler_params=pltpu.CompilerParams(vmem_limit_bytes=48 * MIB),
+        cost_estimate=pl.CostEstimate(flops=4 * rows * D * width, bytes_accessed=16 * MIB, transcendentals=0),
+        name="project_back",
+    )(dq, dk, dv, whole_in, gain, weight, cosine, sines)
+
+
+def swap_rows(value, ranks, mask):
+    return lax.ppermute(value, "row", [(i, i ^ mask) for i in range(ranks)])
+
+
+def gather_rows(value, ranks):
+    parts = {0: value}
+    for m in range(2, ranks, 2):
+        parts[m] = swap_rows(value, ranks, m)
+    for m in range(0, ranks, 2):
+        parts[m + 1] = swap_rows(parts[m], ranks, 1)
+    return [parts[m] for m in range(ranks)]
+
+
+def scatter_rows(parts, ranks):
+    held = {}
+    for m in range(0, ranks, 2):
+        arrived = swap_rows(parts[m + 1], ranks, 1)
+        held[m] = parts[m].astype(F32) + arrived.astype(F32)
+    total = held[0]
+    for m in range(2, ranks, 2):
+        total = total + swap_rows(held[m].astype(BF), ranks, m).astype(F32)
+    return total
+
+
+def on_device_heads(
+    sizes,
+    inputs,
+    attn_gain,
+    qkv_weight,
+    out_weight,
+    ffn_gain,
+    router_weight,
+    carry_weight,
+    const_weight,
+    const_vector,
+    gate_weight,
+    up_weight,
+    down_weight,
+    prev_logits,
+    seq_lengths,
+    expert_routes,
+    cotangent,
+):
+    ranks, cols = sizes
+    heads = HEADS // cols
+    width = heads * HEAD_DIM
+    col_index = lax.axis_index("col")
+    row_total = expert_routes.shape[0]
+    local_rows = inputs.shape[0]
+    first_row = col_index * local_rows
+
+    def own_rows(value):
+        return lax.dynamic_slice_in_dim(value, first_row, local_rows, 0)
+
+    w_stack = jnp.stack([gate_weight, up_weight, down_weight.transpose(0, 2, 1)])
+    w_parts = gather_rows(w_stack, ranks)
+
+    w_cat = jnp.concatenate([out_weight.T, qkv_weight], axis=1)
+    w_all = lax.all_gather(w_cat, "col", axis=0, tiled=False)
+    depth = qkv_weight.shape[0]
+    blocks = w_all[:, :, width:].reshape(cols, depth, 3, width).transpose(0, 2, 1, 3)
+    blocks = blocks.reshape(3, cols, depth, width)
+    own = lax.dynamic_index_in_dim(blocks, col_index, 1, keepdims=False)
+    w_own = jnp.concatenate([own[0], own[1], own[2]], axis=1)
+    out_rows = w_all[:, :, :width].transpose(1, 0, 2).reshape(depth, D)
+    w_full = lax.all_gather(jnp.concatenate([out_rows, w_own], axis=1), "row", axis=0, tiled=True)
+    out_t, qkv_own = w_full[:, :D], w_full[:, D:]
+
+    whole_in = lax.all_gather(inputs, "col", axis=0, tiled=True)
+    prev_t = jnp.pad(prev_logits.T, ((0, 0), (0, LANES - ROUTES)))
+    cotx = lax.all_gather(jnp.concatenate([cotangent, prev_t], axis=1), "col", axis=0, tiled=True)
+
+    lengths = seq_lengths[0]
+    ends = jnp.cumsum(lengths)
+    starts = ends - lengths
+    place = jnp.arange(row_total, dtype=jnp.int32)
+    seq_index = jnp.sum((place[:, None] >= ends[None, :]).astype(jnp.int32), axis=1)
+    member = seq_index[:, None] == jnp.arange(lengths.shape[0], dtype=jnp.int32)[None, :]
+    begin = jnp.sum(jnp.where(member, starts[None, :], 0), axis=1)
+    is_valid = seq_index < lengths.shape[0]
+    positions = place - begin
+    valid = is_valid.astype(F32)[:, None]
+    seq_begin = jnp.where(is_valid, begin, ends[-1])[:, None]
+    pair = jnp.arange(HEAD_DIM // 2, dtype=jnp.int32)
+    frequency = jnp.exp(-((2 * pair).astype(F32) / HEAD_DIM) * math.log(BASE))
+    angles = positions.astype(F32)[:, None] * frequency[None, :]
+    cosine, sines = jnp.cos(angles), jnp.sin(angles)
+    cosine = jnp.tile(jnp.repeat(cosine, 2, axis=1), (1, LANES // HEAD_DIM))
+    sines = jnp.tile(
+        jnp.stack([-sines, sines], axis=2).reshape(row_total, HEAD_DIM), (1, LANES // HEAD_DIM)
+    )
+
+    hit = jnp.any(
+        expert_routes[:, :, None] == jnp.arange(EXPERTS, dtype=jnp.int32)[None, None, :], axis=1
+    ).astype(jnp.int32)
+    slots = jnp.where(hit > 0, jnp.cumsum(hit, axis=0) - 1, -1)
+
+    rw = jnp.concatenate(
+        [
+            router_weight.T,
+            const_weight.transpose(0, 2, 1).reshape(4, D),
+            const_vector,
+            jnp.zeros((LANES - ROW_GAIN, D), BF),
+        ],
+        axis=0,
+    )
+    carry = jnp.pad(carry_weight, ((0, LANES - ROUTES), (0, LANES - ROUTES)))
+    attn_gain_row = attn_gain.astype(F32)[None, :]
+    ffn_gain_row = ffn_gain.astype(F32)[None, :]
+
+    qkv = project_heads(heads, whole_in, attn_gain_row, qkv_own, cosine, sines)
+    mixed_heads, lse = attend(heads, qkv, seq_begin, valid)
+    to_send = mixed_heads.transpose(1, 0, 2).reshape(cols, local_rows, width)
+    attn_parts = lax.all_to_all(to_send, "col", split_axis=0, concat_axis=0, tiled=True)
+    mixed, middle, n2 = branch(attn_parts, out_t, inputs, ffn_gain_row)
+    n2_whole = lax.all_gather(n2, "col", axis=0, tiled=True)
+    mix, gtx, g_parts = experts_both_ways(n2_whole, cotx, rw, carry, expert_routes, slots, w_parts)
+    gtx_own = lax.psum_scatter(gtx, "col", scatter_dimension=0, tiled=True)
+    mix_own = lax.psum_scatter(mix, "col", scatter_dimension=0, tiled=True)
+    midmix, resid, gm, og, small, prev_grad = resid_step(
+        cols,
+        gtx_own,
+        n2,
+        middle,
+        cotangent,
+        own_rows(expert_routes),
+        prev_t,
+        rw,
+        carry,
+        ffn_gain_row,
+        out_t,
+        mixed,
+        own_rows(valid),
+    )
+    layer_out = (midmix + mix_own.astype(F32)).astype(BF)
+    gm_heads = lax.all_to_all(gm, "col", split_axis=0, concat_axis=0, tiled=True)
+    gm_heads = gm_heads.reshape(row_total, heads, HEAD_DIM).transpose(1, 0, 2)
+    dq, dk, dv = attend_back(heads, qkv, seq_begin, mixed_heads, lse, gm_heads)
+    gn, qg, gain_part = project_back(
+        heads, dq, dk, dv, whole_in, attn_gain_row, qkv_own, cosine, sines
+    )
+    gn_own = lax.psum_scatter(gn, "col", scatter_dimension=0, tiled=True).astype(F32)
+
+    grads = scatter_rows(g_parts, ranks)
+    og_rows = lax.psum_scatter(og, "row", scatter_dimension=0, tiled=True)
+    og_own = lax.psum_scatter(og_rows, "col", scatter_dimension=1, tiled=True)
+    qg_rows = lax.psum_scatter(qg, "row", scatter_dimension=0, tiled=True)
+    qg_all = lax.all_gather(qg_rows.reshape(depth, 3, width).transpose(1, 0, 2), "col", axis=1)
+    qg_all = qg_all.reshape(3 * cols, depth, width)
+    qg_own = lax.dynamic_slice_in_dim(qg_all, 3 * col_index, 3, 0)
+    qkv_grad = qg_own.transpose(1, 0, 2).reshape(depth, 3 * width).astype(F32)
+    small_all, gain_all = lax.psum((small, gain_part), ("row", "col"))
+
+    x = inputs.astype(F32)
+    scale = lax.rsqrt(jnp.mean(x * x, axis=1, keepdims=True) + EPS)
+    gained = gn_own * attn_gain_row
+    dots = jnp.sum(gained * x, axis=1, keepdims=True)
+    input_grad = resid + scale * gained - x * scale**3 * (dots / D)
+    return (
+        layer_out,
+        input_grad,
+        gain_all[0],
+        qkv_grad,
+        og_own.T.astype(F32),
+        small_all[ROW_GAIN, :D],
+        small_all[:ROUTES, :D].T,
+        small_all[:ROUTES, D : D + ROUTES].T,
+        small_all[ROW_CONST:ROW_VEC, :D].reshape(2, 2, D).transpose(0, 2, 1),
+        small_all[ROW_VEC:ROW_GAIN, :D],
+        grads[0],
+        grads[1],
+        grads[2].transpose(0, 2, 1),
+        prev_grad,
+    )
+
+
 def solution(mesh):
+    sizes = (mesh.shape["row"], mesh.shape["col"])
+    ranks, cols = sizes
+    per_heads = HEADS % cols == 0 and ranks == 8 and (HEADS // cols) * HEAD_DIM * 2 % LANES == 0
+    body = functools.partial(on_device_heads, sizes) if per_heads else on_device
     placed = (
         P(("row", "col"), None),
         P(),
@@ -500,7 +1218,7 @@
         P(("row", "col"), None),
     )
     return jax.shard_map(
-        on_device,
+        body,
         mesh=mesh,
         in_specs=placed,
         out_specs=(

time: 1520 us -> 805 us (0.53)
  waiting for transfers between devices: 690 us -> 432 us
  local copies, waits for them, and re-layouts: 269 us -> 60.7 us
  matrix products: 201 us -> 0 us
  Pallas kernels: 0 us -> 142 us
  blocking collectives: 186 us -> 87.6 us
  other arithmetic: 132 us -> 39.8 us
    dot_general x47 -> x0, matrix products: 201 us -> none  [the longest x6 20.1 us: key_scores(): jnp.einsum('qhd,khd->hqk', query_heads, key_block, preferred_element_type...]
    all_gather x8 -> x4, waiting for transfers between devices: 310 us -> 110 us  [the longest x1 50.8 us: on_device_heads(): whole_in = lax.all_gather(inputs, 'col', axis=0, tiled=True)]
    reduce_scatter x8 -> x5, waiting for transfers between devices: 306 us -> 107 us  [the longest x1 50.3 us: on_device_heads(): gtx_own = lax.psum_scatter(gtx, 'col', scatter_dimension=0, tiled=True)]
    pallas_call x0 -> x7, Pallas kernels: none -> 142 us  [the longest x1 85 us: experts_both_ways(): pl.pallas_call(functools.partial(moe_kernel, ranks, capacity), grid=(expe...]
    ppermute x0 -> x14, waiting for transfers between devices: none -> 99 us  [swap_rows(): return lax.ppermute(value, 'row', [(i, i ^ mask) for i in range(ranks)])]
    all_to_all x2 -> x0, blocking collectives: 89.3 us -> none  [the longest x1 45.2 us: to_features(): lax.all_to_all(block_value, 'col', split_axis=1, concat_axis=0, tiled=True)]
    reduce_sum x17 -> x3, other arithmetic: 78.7 us -> 1.59 us  [the longest x1 1.41 us: on_device_heads(): scale = lax.rsqrt(jnp.mean(x * x, axis=1, keepdims=True) + EPS)]
    psum x0 -> x1, waiting for transfers between devices: none -> 68.5 us  [on_device_heads(): small_all, gain_all = lax.psum((small, gain_part), ('row', 'col'))]
  transfers between devices with their start and end apart: 20 -> 27, of which waited for: 17 -> 13; matrix products, arithmetic and copies ran while one was open for 18% -> 9% of each run, Pallas kernels for 0% -> 6%
where the time goes in v1:
time: 805 us; the launch traced here: 795 us
  waiting for transfers between devices  432 us (54%)
  Pallas kernels  142 us (18%)
  blocking collectives  87.6 us (11%)
  local copies, waits for them, and re-layouts  60.7 us (8%)
  other arithmetic  39.8 us (5%)
  starting transfers between devices  17.8 us (2%)
  between operations  14.8 us (2%)
    ppermute x14, waiting for transfers between devices, swap_rows(): return lax.ppermute(value, 'row', [(i, i ^ mask) for i in range(ranks)])  99 us
    pallas_call x1, Pallas kernels, experts_both_ways(): pl.pallas_call(functools.partial(moe_kernel, ranks, capacity), grid=(expe...  85 us
    psum x1, waiting for transfers between devices, on_device_heads(): small_all, gain_all = lax.psum((small, gain_part), ('row', 'col'))  68.5 us
    all_gather x1, waiting for transfers between devices, on_device_heads(): whole_in = lax.all_gather(inputs, 'col', axis=0, tiled=True)  50.8 us
    reduce_scatter x1, waiting for transfers between devices, on_device_heads(): gtx_own = lax.psum_scatter(gtx, 'col', scatter_dimension=0, tiled=True)  50.3 us
    psum x1, blocking collectives, on_device_heads(): small_all, gain_all = lax.psum((small, gain_part), ('row', 'col'))  42.2 us
    all_gather x1, waiting for transfers between devices, on_device_heads(): n2_whole = lax.all_gather(n2, 'col', axis=0, tiled=True)  36.3 us
    all_to_all x1, waiting for transfers between devices, on_device_heads(): lax.all_to_all(to_send, 'col', split_axis=0, concat_axis=0, tiled=True)  31 us
  transfers between devices with their start and end apart: 27, of which 13 were waited for; matrix products, arithmetic and copies ran while one was open for 9% of the time, Pallas kernels for 6%

profile of v1, /device:TPU:0, one launch (start us, length us, event | category | flops | bytes accessed | tf_op | source)
XLA Modules:
  0.0 794.5 jit_solution(7827934649818903858)
XLA Ops:
  9.1 18.2 %all-gather = bf16[384,768]{1,0:T(8,128)(2,1)S(1)} all-gather(bf16[96,768]{1,0:T(8,128)(2,1)S(1)} %pad_maximum_fusion.3), channel_id=2, replica_groups=mesh['row'=8,'col'=4] {'col'}, dimensions={0}, use_global_device_ids=true | all-gather | bytes 737280 | tf_op jit(solution)/shard_map/all_gather | solution.py:1079
  32.0 2.9 pad_maximum_fusion.refs_7_
  45.6 22.5 %all-gather.9.cloned.1.call-done = bf16[768,1344]{1,0:T(8,128)(2,1)} async-done(((bf16[96,1344]{1,0:T(8,128)(2,1)}), bf16[768,1344]{1,0:T(8,128)(2,1)}) %all-gather.9.cloned.1.call-update) | async-done | bytes 2064400 | tf_op jit(solution)/shard_map/all_gather | solution.py:1086
  69.3 50.8 %all-gather.7.cloned.1.call-done.x_ref = bf16[1536,768]{1,0:T(8,128)(2,1)} async-done(((bf16[384,768]{1,0:T(8,128)(2,1)}), bf16[1536,768]{1,0:T(8,128)(2,1)}) %all-gather.7.cloned.1.call-update) | async-done | bytes 2359312 | tf_op jit(solution)/shard_map/all_gather | solution.py:1089
  121.8 5.0 project_heads.1.q_ref.k_ref.v_ref
  128.6 12.3 %attend.1 = (bf16[3,1536,64]{2,1,0:T(8,128)(2,1)S(1)}, f32[3,1536,1]{2,1,0:T(8,128)S(1)}) custom-call(bf16[9,1536,64]{2,1,0:T(8,128)(2,1)} %copy-done.5, bf16[9,1536,64]{2,1,0:T(8,128)(2,1)} %copy-done.5, bf16[9,1536,64]{2,1,0:T(8,128)(2,1)} %copy-done.5, s32[1536,1]{1,0:T(8,128)S(1)} %copy-done.20, f32[1536,1]{1,0:T(8,128)S(1)} %copy-done.21), custom_call_target="tpu_custom_call" | custom-call | flops 3623878656 | bytes 8388608 | tf_op jit(solution)/shard_map/attend/pallas_call | solution.py:587
  145.9 4.3 all-to-all-start
  151.7 31.0 %all-to-all-done = bf16[4,384,192]{1,2,0:T(8,128)(2,1)} async-done(((bf16[4,384,192]{1,2,0:T(8,128)(2,1)}), bf16[4,384,192]{1,2,0:T(8,128)(2,1)}, u32[]{:S(2)}, u32[]{:S(2)}) %all-to-all-start) | async-done | bytes 589856 | tf_op jit(solution)/shard_map/all_to_all | solution.py:1134
  194.2 2.3 reduce-window.11
  197.3 2.3 bitcast_select_fusion.1
  204.9 36.3 %all-gather.11.cloned.1.call-done.refs_0_ = bf16[1536,768]{1,0:T(8,128)(2,1)} async-done(((bf16[384,768]{1,0:T(8,128)(2,1)}), bf16[1536,768]{1,0:T(8,128)(2,1)}) %all-gather.11.cloned.1.call-update) | async-done | bytes 2359312 | tf_op jit(solution)/shard_map/all_gather | solution.py:1136
  241.1 85.0 %experts_both_ways.1 = (bf16[1536,768]{1,0:T(8,128)(2,1)}, bf16[1536,896]{1,0:T(8,128)(2,1)}, bf16[3,8,96,512]{3,2,1,0:T(8,128)(2,1)}, bf16[3,8,96,512]{3,2,1,0:...) custom-call(bf16[1536,768]{1,0:T(8,128)(2,1)} %all-gather.11.cloned., ...), custom_call_target="tpu_custom_call" | custom-call | flops 57982058496 | bytes 50331648 | tf_op jit(solution)/shard_map/experts_both_ways/pallas_call | solution.py:808
  329.1 50.3 %reduce-scatter.9.cloned.1.call-done.gtx_ref = bf16[384,896]{1,0:T(8,128)(2,1)} async-done(((bf16[1536,896]{1,0:T(8,128)(2,1)}), bf16[384,896]{1,0:T(8,128)(2,1)}) %reduce-scatter.9.cloned.1.call-update) | async-done | bytes 688144 | tf_op jit(solution)/shard_map/reduce_scatter | solution.py:1138
  386.0 10.5 %resid_step.1 = (f32[384,768]{1,0:T(8,128)S(1)}, f32[384,768]{1,0:T(8,128)}, bf16[4,384,192]{2,1,0:T(8,128)(2,1)S(1)}, bf16[768,768]{1,0:T(8,128)(2,1)}, f32[24,896]{1,0:T(8,128)}, /*index=5*/f32[12,384]{1,0:T(8,128)}) custom-call(bf16[384,896]{1,0:T(8,128)(2,1)S(1)} %copy-done.24, bf16[384,768]{1,0:T(8,128)(2,1)S(1)} %copy-done.8, f32[384,768]{1,0:T(8,128)} %copy-done.14, ...), custom_call_target="tpu_custom_call" | custom-call | flops 1358954496 | bytes 12582912 | tf_op jit(solution)/shard_map/resid_step/pallas_call | solution.py:939
  400.7 3.5 all-to-all-start.1
  405.0 15.7 %all-to-all-done.1 = bf16[4,384,192]{1,2,0:T(8,128)(2,1)S(1)} async-done(((bf16[4,384,192]{1,2,0:T(8,128)(2,1)}), bf16[4,384,192]{1,2,0:T(8,128)(2,1)S(1)}, u32[]{:S(2)}, u32[]{:S(2)}) %all-to-all-start.1) | async-done | bytes 589856 | tf_op jit(solution)/shard_map/all_to_all | solution.py:1156
  422.8 17.3 %reduce-scatter.17.cloned.1.call-done = bf16[96,768]{1,0:T(8,128)(2,1)} async-done(((bf16[768,768]{1,0:T(8,128)(2,1)}), bf16[96,768]{1,0:T(8,128)(2,1)}) %reduce-scatter.17.cloned.1.call-update) | async-done | bytes 147472 | tf_op jit(solution)/shard_map/reduce_scatter | solution.py:1165
  442.0 17.1 %attend_back.1 = (f32[3,1536,64]{2,1,0:T(8,128)}, f32[3,1536,64]{2,1,0:T(8,128)}, f32[3,1536,64]{2,1,0:T(8,128)}) custom-call(bf16[9,1536,64]{2,1,0:T(8,128)(2,1)} %copy-done.5, bf16[9,1536,64]{2,1,0:T(8,128)(2,1)} %copy-done.5, bf16[9,1536,64]{2,1,0:T(8,128)(2,1)} %copy-done.5, s32[1536,1]{1,0:T(8,128)} %select_n.43.begin_ref, ...), custom_call_target="tpu_custom_call" | custom-call | flops 9059696640 | bytes 12582912 | tf_op jit(solution)/shard_map/attend_back/pallas_call | solution.py:644
  459.2 11.0 %project_back.1 = (bf16[1536,768]{1,0:T(8,128)(2,1)}, bf16[768,576]{1,0:T(8,128)(2,1)}, f32[1,768]{1,0:T(1,128)S(1)}) custom-call(f32[3,1536,64]{2,1,0:T(8,128)} %get-tuple-element.51.dq_ref, f32[3,1536,64]{2,1,0:T(8,128)} %get-tuple-element.52.dk_ref, f32[3,1536,64]{2,1,0:T(8,128)} %get-tuple-element.53.dv_ref, ...), custom_call_target="tpu_custom_call" | custom-call | flops 2717908992 | bytes 16777216 | tf_op jit(solution)/shard_map/project_back/pallas_call | solution.py:995
  470.3 4.9 add_convert_fusion.2
  476.6 4.1 add_convert_fusion.1
  481.3 4.0 add_convert_fusion
  486.8 43.0 %collective-permute-done.9 = bf16[3,8,96,512]{3,2,1,0:T(8,128)(2,1)} collective-permute-done((bf16[3,8,96,512]{3,2,1,0:T(8,128)(2,1)}, bf16[3,8,96,512]{3,2,1,0:T(8,128)(2,1)}, u32[]{:S(2)}, u32[]{:S(2)}) %collective-permute-start.9) | collective-permute-done | bytes 2359328 | tf_op jit(solution)/shard_map/ppermute | solution.py:1022
  529.8 55.5 %collective-permute-done.11 = bf16[3,8,96,512]{3,2,1,0:T(8,128)(2,1)} collective-permute-done((bf16[3,8,96,512]{3,2,1,0:T(8,128)(2,1)}, bf16[3,8,96,512]{3,2,1,0:T(8,128)(2,1)}, u32[]{:S(2)}, u32[]{:S(2)}) %collective-permute-start.11) | collective-permute-done | bytes 2359328 | tf_op jit(solution)/shard_map/ppermute | solution.py:1022
  585.3 6.4 convert_add_fusion
  591.8 2.3 slice_bitcast_fusion
  596.1 68.5 %all-reduce.4.cloned.1.call-done = f32[24,896]{1,0:T(8,128)} async-done(((f32[24,896]{1,0:T(8,128)}), f32[24,896]{1,0:T(8,128)}) %all-reduce.4.cloned.1.call-update) | async-done | bytes 86032 | tf_op jit(solution)/shard_map/psum | solution.py:1172
  671.5 42.2 %psum.14 = f32[768]{0:T(1024)} all-reduce(f32[768]{0:T(1024)S(1)} %reduce.1), channel_id=1, replica_groups=mesh['row'=8,'col'=4] {'row','col'}, use_global_device_ids=true, to_apply=%region_11.12 | all-reduce | flops 768 | bytes 6144 | tf_op jit(solution)/shard_map/psum | solution.py:1172
  715.3 11.4 %reduce-scatter.15.cloned.1.call-done = bf16[96,576]{1,0:T(8,128)(2,1)} async-done(((bf16[768,576]{1,0:T(8,128)(2,1)}), bf16[96,576]{1,0:T(8,128)(2,1)}) %reduce-scatter.15.cloned.1.call-update) | async-done | bytes 110608 | tf_op jit(solution)/shard_map/reduce_scatter | solution.py:1167
  727.9 27.3 %all-gather.1 = bf16[3,384,192]{2,0,1:T(4,128)(2,1)S(1)} all-gather(bf16[3,96,192]{2,0,1:T(4,128)(2,1)S(1)} %copy.193), channel_id=3, replica_groups=mesh['row'=8,'col'=4] {'col'}, dimensions={1}, use_global_device_ids=true | all-gather | bytes 552960 | tf_op jit(solution)/shard_map/all_gather | solution.py:1168
  756.3 27.6 %reduce-scatter.13.cloned.1.call-done = bf16[384,768]{1,0:T(8,128)(2,1)} async-done(((bf16[1536,768]{1,0:T(8,128)(2,1)}), bf16[384,768]{1,0:T(8,128)(2,1)}) %reduce-scatter.13.cloned.1.call-update) | async-done | bytes 589840 | tf_op jit(solution)/shard_map/reduce_scatter | solution.py:1162
  785.4 2.4 fusion.2
  (229 shorter events, 82.0 us)
Async XLA Ops:
  7.2 60.9 %all-gather.9.cloned.1.call-start = ((), (), s32[]{:S(2)}) async-start(), calls=%async_computation.9 | async-start | bytes 2433024 | tf_op jit(solution)/shard_map/all_gather | solution.py:1086
  29.4 90.7 %all-gather.7.cloned.1.call-start = ((), (), s32[]{:S(2)}) async-start(), calls=%async_computation.8 | async-start | bytes 2949120 | tf_op jit(solution)/shard_map/all_gather | solution.py:1089
  30.2 174.3 %all-gather.13.cloned.1.call-start = ((), (), s32[]{:S(2)}) async-start(), calls=%async_computation.11 | async-start | bytes 3440640 | tf_op jit(solution)/shard_map/all_gather | solution.py:1091
  34.9 155.0 %collective-permute-start.1 = (bf16[3,8,96,512]{3,2,1,0:T(8,128)(2,1)}, bf16[3,8,96,512]{3,2,1,0:T(8,128)(2,1)}, u32[]{:S(2)}, u32[]{:S(2)}) collective-permute-start(bf16[3,8,96,512]{3,2,1,0:T(8,128)(2,1)} %pad_maximum_fusion.refs_7_), channel_id=1, source_target_pairs={{0,8},{4,12},{8,0},{12,4},{16,24},{20,28},{24,16},{28,20},{1,9},{5... | collective-permute-start | bytes 7077896 | tf_op jit(solution)/shard_map/ppermute | solution.py:1022
  36.4 154.0 %collective-permute-start.3 = (bf16[3,8,96,512]{3,2,1,0:T(8,128)(2,1)}, bf16[3,8,96,512]{3,2,1,0:T(8,128)(2,1)}, u32[]{:S(2)}, u32[]{:S(2)}) collective-permute-start(bf16[3,8,96,512]{3,2,1,0:T(8,128)(2,1)} %pad_maximum_fusion.refs_7_), channel_id=1, source_target_pairs={{0,16},{4,20},{8,24},{12,28},{16,0},{20,4},{24,8},{28,12},{1,17},{... | collective-permute-start | bytes 7077896 | tf_op jit(solution)/shard_map/ppermute | solution.py:1022
  37.9 152.6 %collective-permute-start.5 = (bf16[3,8,96,512]{3,2,1,0:T(8,128)(2,1)}, bf16[3,8,96,512]{3,2,1,0:T(8,128)(2,1)}, u32[]{:S(2)}, u32[]{:S(2)}) collective-permute-start(bf16[3,8,96,512]{3,2,1,0:T(8,128)(2,1)} %pad_maximum_fusion.refs_7_), channel_id=1, source_target_pairs={{0,24},{4,28},{8,16},{12,20},{16,8},{20,12},{24,0},{28,4},{1,25},{... | collective-permute-start | bytes 7077896 | tf_op jit(solution)/shard_map/ppermute | solution.py:1022
  43.2 83.6 %copy-start.3 = (f32[1536,128]{1,0:T(8,128)}, f32[1536,128]{1,0:T(8,128)S(1)}, u32[]{:S(2)}) copy-start(f32[1536,128]{1,0:T(8,128)S(1)} %copy.170.cos_ref) | copy-start | bytes 2359300
  145.9 36.7 %all-to-all-start = ((bf16[4,384,192]{1,2,0:T(8,128)(2,1)}), bf16[4,384,192]{1,2,0:T(8,128)(2,1)}, u32[]{:S(2)}, u32[]{:S(2)}) async-start(bf16[4,384,192]{1,2,0:T(8,128)(2,1)} %copy.175), calls=%async_computation | async-start | bytes 1179648 | tf_op jit(solution)/shard_map/all_to_all | solution.py:1134
  150.2 90.9 %all-gather.11.cloned.1.call-start = ((), (), s32[]{:S(2)}) async-start(), calls=%async_computation.10 | async-start | bytes 2949120 | tf_op jit(solution)/shard_map/all_gather | solution.py:1136
  151.6 41.1 %copy-start = (bf16[768,768]{1,0:T(8,128)(2,1)}, bf16[768,768]{1,0:T(8,128)(2,1)S(1)}, u32[]{:S(2)}) copy-start(bf16[768,768]{1,0:T(8,128)(2,1)S(1)} %slice.79.w_ref.out_t_ref) | copy-start | bytes 3538948
  189.5 189.9 %reduce-scatter.9.cloned.1.call-start = ((), (), s32[]{:S(2)}) async-start(), calls=%async_computation.12 | async-start | bytes 3440640 | tf_op jit(solution)/shard_map/reduce_scatter | solution.py:1138
  189.8 14.6 %collective-permute-start = (bf16[3,8,96,512]{3,2,1,0:T(8,128)(2,1)}, bf16[3,8,96,512]{3,2,1,0:T(8,128)(2,1)}, u32[]{:S(2)}, u32[]{:S(2)}) collective-permute-start(bf16[3,8,96,512]{3,2,1,0:T(8,128)(2,1)} %pad_maximum_fusion.refs_7_), channel_id=1, source_target_pairs={{0,4},{4,0},{8,12},{12,8},{16,20},{20,16},{24,28},{28,24},{1,5},{5... | collective-permute-start | bytes 7077896 | tf_op jit(solution)/shard_map/ppermute | solution.py:1022
  189.9 14.5 %collective-permute-start.2 = (bf16[3,8,96,512]{3,2,1,0:T(8,128)(2,1)}, bf16[3,8,96,512]{3,2,1,0:T(8,128)(2,1)}, u32[]{:S(2)}, u32[]{:S(2)}) collective-permute-start(bf16[3,8,96,512]{3,2,1,0:T(8,128)(2,1)} %collective-permute-done.1.refs_9_), channel_id=1, source_target_pairs={{0,4},{4,0},{8,12},{12,8},{16,20},{20,16},{24,28},{28,24},{1,5},{5... | collective-permute-start | bytes 7077896 | tf_op jit(solution)/shard_map/ppermute | solution.py:1022
  190.4 14.0 %collective-permute-start.4 = (bf16[3,8,96,512]{3,2,1,0:T(8,128)(2,1)}, bf16[3,8,96,512]{3,2,1,0:T(8,128)(2,1)}, u32[]{:S(2)}, u32[]{:S(2)}) collective-permute-start(bf16[3,8,96,512]{3,2,1,0:T(8,128)(2,1)} %collective-permute-done.3.refs_11_), channel_id=1, source_target_pairs={{0,4},{4,0},{8,12},{12,8},{16,20},{20,16},{24,28},{28,24},{1,5},{5... | collective-permute-start | bytes 7077896 | tf_op jit(solution)/shard_map/ppermute | solution.py:1022
  190.5 14.4 %collective-permute-start.6 = (bf16[3,8,96,512]{3,2,1,0:T(8,128)(2,1)}, bf16[3,8,96,512]{3,2,1,0:T(8,128)(2,1)}, u32[]{:S(2)}, u32[]{:S(2)}) collective-permute-start(bf16[3,8,96,512]{3,2,1,0:T(8,128)(2,1)} %collective-permute-done.5.refs_13_), channel_id=1, source_target_pairs={{0,4},{4,0},{8,12},{12,8},{16,20},{20,16},{24,28},{28,24},{1,5},{5... | collective-permute-start | bytes 7077896 | tf_op jit(solution)/shard_map/ppermute | solution.py:1022
  326.1 53.3 %copy-start.8 = (bf16[384,768]{1,0:T(8,128)(2,1)S(1)}, bf16[384,768]{1,0:T(8,128)(2,1)}, u32[]{:S(2)}) copy-start(bf16[384,768]{1,0:T(8,128)(2,1)} %copy-done.7) | copy-start | bytes 1769476
  326.1 53.3 %copy-start.10 = (bf16[384,768]{1,0:T(8,128)(2,1)S(1)}, bf16[384,768]{1,0:T(8,128)(2,1)}, u32[]{:S(2)}) copy-start(bf16[384,768]{1,0:T(8,128)(2,1)} %cot_ref.1) | copy-start | bytes 1769476
  326.2 113.9 %reduce-scatter.17.cloned.1.call-start = ((), (), s32[]{:S(2)}) async-start(), calls=%async_computation.16 | async-start | bytes 1327104 | tf_op jit(solution)/shard_map/reduce_scatter | solution.py:1165
  398.5 195.6 %reduce-scatter.11.cloned.1.call-start = ((), (), s32[]{:S(2)}) async-start(), calls=%async_computation.13 | async-start | bytes 2949120 | tf_op jit(solution)/shard_map/reduce_scatter | solution.py:1139
  399.3 71.0 %collective-permute-start.8 = (bf16[3,8,96,512]{3,2,1,0:T(8,128)(2,1)}, bf16[3,8,96,512]{3,2,1,0:T(8,128)(2,1)}, u32[]{:S(2)}, u32[]{:S(2)}) collective-permute-start(bf16[3,8,96,512]{3,2,1,0:T(8,128)(2,1)} %get-tuple-element.62), channel_id=1, source_target_pairs={{0,4},{4,0},{8,12},{12,8},{16,20},{20,16},{24,28},{28,24},{1,5},{5... | collective-permute-start | bytes 7077896 | tf_op jit(solution)/shard_map/ppermute | solution.py:1022
  400.7 20.0 %all-to-all-start.1 = ((bf16[4,384,192]{1,2,0:T(8,128)(2,1)}), bf16[4,384,192]{1,2,0:T(8,128)(2,1)S(1)}, u32[]{:S(2)}, u32[]{:S(2)}) async-start(bf16[4,384,192]{1,2,0:T(8,128)(2,1)} %copy.186), calls=%async_computation.3 | async-start | bytes 1179648 | tf_op jit(solution)/shard_map/all_to_all | solution.py:1156
  404.2 260.4 %all-reduce.4.cloned.1.call-start = ((), (), s32[]{:S(2)}) async-start(), calls=%async_computation.17 | async-start | bytes 172032 | tf_op jit(solution)/shard_map/psum | solution.py:1172
  404.2 72.4 %collective-permute-start.10 = (bf16[3,8,96,512]{3,2,1,0:T(8,128)(2,1)}, bf16[3,8,96,512]{3,2,1,0:T(8,128)(2,1)}, u32[]{:S(2)}, u32[]{:S(2)}) collective-permute-start(bf16[3,8,96,512]{3,2,1,0:T(8,128)(2,1)} %get-tuple-element.64), channel_id=1, source_target_pairs={{0,4},{4,0},{8,12},{12,8},{16,20},{20,16},{24,28},{28,24},{1,5},{5... | collective-permute-start | bytes 7077896 | tf_op jit(solution)/shard_map/ppermute | solution.py:1022
  404.5 76.7 %collective-permute-start.12 = (bf16[3,8,96,512]{3,2,1,0:T(8,128)(2,1)}, bf16[3,8,96,512]{3,2,1,0:T(8,128)(2,1)}, u32[]{:S(2)}, u32[]{:S(2)}) collective-permute-start(bf16[3,8,96,512]{3,2,1,0:T(8,128)(2,1)} %get-tuple-element.66), channel_id=1, source_target_pairs={{0,4},{4,0},{8,12},{12,8},{16,20},{20,16},{24,28},{28,24},{1,5},{5... | collective-permute-start | bytes 7077896 | tf_op jit(solution)/shard_map/ppermute | solution.py:1022
  404.9 308.7 %reduce-scatter.19.cloned.1.call-start = ((), (), s32[]{:S(2)}) async-start(), calls=%async_computation.18 | async-start | bytes 245760
  441.8 284.9 %reduce-scatter.15.cloned.1.call-start = ((), (), s32[]{:S(2)}) async-start(), calls=%async_computation.15 | async-start | bytes 1105920 | tf_op jit(solution)/shard_map/reduce_scatter | solution.py:1167
  470.2 313.7 %reduce-scatter.13.cloned.1.call-start = ((), (), s32[]{:S(2)}) async-start(), calls=%async_computation.14 | async-start | bytes 2949120 | tf_op jit(solution)/shard_map/reduce_scatter | solution.py:1162
  470.2 16.6 %collective-permute-start.7 = (bf16[3,8,96,512]{3,2,1,0:T(8,128)(2,1)}, bf16[3,8,96,512]{3,2,1,0:T(8,128)(2,1)}, u32[]{:S(2)}, u32[]{:S(2)}) collective-permute-start(bf16[3,8,96,512]{3,2,1,0:T(8,128)(2,1)} %get-tuple-element.60), channel_id=1, source_target_pairs={{0,4},{4,0},{8,12},{12,8},{16,20},{20,16},{24,28},{28,24},{1,5},{5... | collective-permute-start | bytes 7077896 | tf_op jit(solution)/shard_map/ppermute | solution.py:1022
  475.2 54.6 %collective-permute-start.9 = (bf16[3,8,96,512]{3,2,1,0:T(8,128)(2,1)}, bf16[3,8,96,512]{3,2,1,0:T(8,128)(2,1)}, u32[]{:S(2)}, u32[]{:S(2)}) collective-permute-start(bf16[3,8,96,512]{3,2,1,0:T(8,128)(2,1)} %add_convert_fusion.2), channel_id=1, source_target_pairs={{0,8},{4,12},{8,0},{12,4},{16,24},{20,28},{24,16},{28,20},{1,9},{5... | collective-permute-start | bytes 7077896 | tf_op jit(solution)/shard_map/ppermute | solution.py:1022
  480.7 104.7 %collective-permute-start.11 = (bf16[3,8,96,512]{3,2,1,0:T(8,128)(2,1)}, bf16[3,8,96,512]{3,2,1,0:T(8,128)(2,1)}, u32[]{:S(2)}, u32[]{:S(2)}) collective-permute-start(bf16[3,8,96,512]{3,2,1,0:T(8,128)(2,1)} %add_convert_fusion.1), channel_id=1, source_target_pairs={{0,16},{4,20},{8,24},{12,28},{16,0},{20,4},{24,8},{28,12},{1,17},{... | collective-permute-start | bytes 7077896 | tf_op jit(solution)/shard_map/ppermute | solution.py:1022
  485.2 100.1 %collective-permute-start.13 = (bf16[3,8,96,512]{3,2,1,0:T(8,128)(2,1)}, bf16[3,8,96,512]{3,2,1,0:T(8,128)(2,1)}, u32[]{:S(2)}, u32[]{:S(2)}) collective-permute-start(bf16[3,8,96,512]{3,2,1,0:T(8,128)(2,1)} %add_convert_fusion), channel_id=1, source_target_pairs={{0,24},{4,28},{8,16},{12,20},{16,8},{20,12},{24,0},{28,4},{1,25},{... | collective-permute-start | bytes 7077896 | tf_op jit(solution)/shard_map/ppermute | solution.py:1022
  727.9 57.4 %copy-start.32 = (f32[384,768]{1,0:T(8,128)S(1)}, f32[384,768]{1,0:T(8,128)}, u32[]{:S(2)}) copy-start(f32[384,768]{1,0:T(8,128)} %get-tuple-element.48) | copy-start | bytes 3538948
  (39 other events, 168.3 us)
Sparse Core Ops, SparseCore 0:
  29.5 38.4 all-gather.8
  69.6 50.4 all-gather.6
  121.7 68.1 all-gather.12
  191.9 49.1 all-gather.10
  326.3 53.0 reduce-scatter.8
  398.6 41.3 reduce-scatter.16
  442.5 47.9 reduce-scatter.10
  497.6 166.9 all-reduce.3
  667.5 21.2 reduce-scatter.18
  692.5 34.1 reduce-scatter.14
  729.1 54.7 reduce-scatter.12

commit v2 on v1

--- a/solution.py
+++ b/solution.py
@@ -610,59 +610,6 @@
     )(qkv, qkv, qkv, begin, valid)
 
 
-def attend_back_kernel(
-    q_ref, k_ref, v_ref, begin_ref, o_ref, lse_ref, do_ref, dq_ref, dk_ref, dv_ref
-):
-    rows = q_ref.shape[1]
-    score_scale = 1.0 / math.sqrt(HEAD_DIM)
-    count = rows // Q_ROWS
-    for i in reversed(range(count)):
-        at = slice(i * Q_ROWS, (i + 1) * Q_ROWS)
-        length = (i + 1) * Q_ROWS
-        q, do = q_ref[0, at], do_ref[0, at]
-        k, v = k_ref[0, :length], v_ref[0, :length]
-        delta = jnp.sum(do.astype(F32) * o_ref[0, at].astype(F32), axis=1, keepdims=True)
-        s = mm(q, k, NT)
-        ok = seen(begin_ref[at], i * Q_ROWS, Q_ROWS, length)
-        p = jnp.where(ok, jnp.exp(s - lse_ref[0, at]), 0.0)
-        dp = mm(do, v, NT)
-        ds = (p * (dp - delta)).astype(BF)
-        dq_ref[0, at] = mm(ds, k) * score_scale
-        dk, dv = mm(ds, q, TN), mm(p.astype(BF), do, TN)
-        if i == count - 1:
-            dk_ref[0], dv_ref[0] = dk, dv
-        else:
-            dk_ref[0, :length] += dk
-            dv_ref[0, :length] += dv
-
-
-def attend_back(heads, qkv, begin, mixed, lse, grad_mixed):
-    rows = qkv.shape[1]
-    head_block = (1, rows, HEAD_DIM)
-    per_head = pl.BlockSpec(head_block, lambda h: (h, 0, 0))
-    grad = jax.ShapeDtypeStruct((heads, rows, HEAD_DIM), F32)
-    return pl.pallas_call(
-        attend_back_kernel,
-        grid=(heads,),
-        out_shape=(grad, grad, grad),
-        in_specs=[
-            per_head,
-            pl.BlockSpec(head_block, lambda h: (h + heads, 0, 0)),
-            pl.BlockSpec(head_block, lambda h: (h + 2 * heads, 0, 0)),
-            whole((rows, 1)),
-            per_head,
-            pl.BlockSpec((1, rows, 1), lambda h: (h, 0, 0)),
-            per_head,
-        ],
-        out_specs=(per_head, per_head, per_head),
-        compiler_params=pltpu.CompilerParams(vmem_limit_bytes=56 * MIB),
-        cost_estimate=pl.CostEstimate(
-            flops=20 * heads * rows * rows * HEAD_DIM, bytes_accessed=12 * MIB, transcendentals=heads * rows * rows
-        ),
-        name="attend_back",
-    )(qkv, qkv, qkv, begin, mixed, lse, grad_mixed)
-
-
 def branch_kernel(a_ref, w_ref, x_ref, gain_ref, mixed_ref, middle_ref, normed_ref):
     mixed = jnp.concatenate([a_ref[i] for i in range(a_ref.shape[0])], axis=1)
     mixed_ref[...] = mixed
@@ -694,158 +641,592 @@
     return e / jnp.sum(e, axis=1, keepdims=True)
 
 
-def moe_kernel(ranks, capacity, *refs):
-    (n2_ref, cotx_ref, rw_ref, carry_ref, routes_ref, tsr_ref, tsc_ref), refs = refs[:7], refs[7:]
-    w_parts, refs = refs[:ranks], refs[ranks:]
-    (mix_ref, gtx_ref), refs = refs[:2], refs[2:]
-    g_parts, refs = refs[:ranks], refs[ranks:]
-    wbuf, wsem, gbuf, gsem, gates, mix_acc, gt_acc = refs
+MESH = pl.DeviceIdType.MESH
+ANY = pl.BlockSpec(memory_space=pl.ANY)
+PACK = 3 * HEAD_DIM // 2
+
+
+def place():
+    return lax.axis_index("row"), lax.axis_index("col")
+
+
+def flip(index, mask):
+    for bit in (1, 2, 4):
+        if mask & bit:
+            index = index + bit - 2 * bit * (index // bit % 2)
+    return index
+
+
+def greet(devices):
+    barrier = pltpu.get_barrier_semaphore()
+    for device in devices:
+        pl.semaphore_signal(barrier, inc=1, device_id=device, device_id_type=MESH)
+    pl.semaphore_wait(barrier, len(devices))
+
+
+def send_to(src, dst, send, recv, device):
+    return pltpu.make_async_remote_copy(
+        src_ref=src, dst_ref=dst, send_sem=send, recv_sem=recv, device_id=device, device_id_type=MESH
+    )
+
+
+def col_peers(n):
+    r, c = place()
+    return [(r, (c + k) % n) for k in range(1, n)]
+
+
+def gather_chain(own, dst, send, recv, n):
+    r, c = place()
+
+    def right(k):
+        i = jnp.maximum(c - k, 0)
+        src = own if k == 0 else dst.at[i]
+        return send_to(src, dst.at[i], send.at[0, k], recv.at[0, k], (r, jnp.minimum(c + 1, n - 1)))
+
+    def left(k):
+        i = jnp.minimum(c + k, n - 1)
+        src = own if k == 0 else dst.at[i]
+        return send_to(src, dst.at[i], send.at[1, k], recv.at[1, k], (r, jnp.maximum(c - 1, 0)))
+
+    def step(k):
+        if k > 0:
+
+            @pl.when(c >= k)
+            def _():
+                right(k - 1).wait_recv()
+
+            @pl.when(c + k < n)
+            def _():
+                left(k - 1).wait_recv()
+
+        if k < n - 1:
+
+            @pl.when((c >= k) & (c + 1 < n))
+            def _():
+                right(k).start()
+
+            @pl.when((c + k < n) & (c >= 1))
+            def _():
+                left(k).start()
+
+    def drain():
+        for k in range(n - 1):
+
+            @pl.when((c >= k) & (c + 1 < n))
+            def _():
+                right(k).wait_send()
+
+            @pl.when((c + k < n) & (c >= 1))
+            def _():
+                left(k).wait_send()
+
+    return step, drain
+
+
+def reduce_chain(own, out, arrived, send, recv, n):
+    r, c = place()
+
+    def right(k):
+        return send_to(out.at[0, k], arrived.at[0, k], send.at[0, k], recv.at[0, k], (r, jnp.minimum(c + 1, n - 1)))
+
+    def left(k):
+        return send_to(out.at[1, k], arrived.at[1, k], send.at[1, k], recv.at[1, k], (r, jnp.maximum(c - 1, 0)))
+
+    def slot(s):
+        if s == n - 1:
+
+            @pl.when(c >= 1)
+            def _():
+                right(n - 1 - c).wait_recv()
+
+            @pl.when(c <= n - 2)
+            def _():
+                left(c).wait_recv()
+
+            return
+
+        @pl.when(c <= s)
+        def _():
+            k = jnp.maximum(s - c, 0)
+
+            @pl.when(c >= 1)
+            def _():
+                right(k).wait_recv()
+                out[0, k] = (own(n - 1 - k).astype(F32) + arrived[0, k].astype(F32)).astype(BF)
+
+            @pl.when(c == 0)
+            def _():
+                out[0, k] = own(n - 1 - k).astype(BF)
+
+            right(k).start()
+
+        @pl.when(n - 1 - c <= s)
+        def _():
+            k = jnp.maximum(s - (n - 1 - c), 0)
+
+            @pl.when(c <= n - 2)
+            def _():
+                left(k).wait_recv()
+                out[1, k] = (own(k).astype(F32) + arrived[1, k].astype(F32)).astype(BF)
+
+            @pl.when(c == n - 1)
+            def _():
+                out[1, k] = own(k).astype(BF)
+
+            left(k).start()
+
+    def total(dst):
+        dst[...] = own(c).astype(F32)
+
+        @pl.when(c >= 1)
+        def _():
+            dst[...] += arrived[0, n - 1 - c].astype(F32)
+
+        @pl.when(c <= n - 2)
+        def _():
+            dst[...] += arrived[1, c].astype(F32)
+
+    def drain():
+        for k in range(n - 1):
+
+            @pl.when(c < n - 1 - k)
+            def _():
+                right(k).wait_send()
+
+            @pl.when(c > k)
+            def _():
+                left(k).wait_send()
+
+    return slot, total, drain
+
+
+def chain_scratch(n, rows):
+    return [
+        pltpu.VMEM((2, n - 1, rows, D), BF),
+        pltpu.VMEM((2, n - 1, rows, D), BF),
+        pltpu.SemaphoreType.DMA((2, n - 1)),
+        pltpu.SemaphoreType.DMA((2, n - 1)),
+    ]
+
+
+def slot_rows(tsr_ref, capacity):
+    rows = tsr_ref.shape[2]
+    return jnp.where(lax.broadcasted_iota(jnp.int32, (capacity, rows), 0) == tsr_ref[0], 1.0, 0.0).astype(BF)
+
+
+def slot_column(tsc_ref, e):
+    return jnp.sum(jnp.where(lane_iota(tsc_ref.shape) == e, tsc_ref[...], 0), axis=1, keepdims=True)
+
+
+def full_weight(w_ref, t):
+    ranks, _, _, depth, ff = w_ref.shape
+    return w_ref[:, t, 0].reshape(ranks * depth, ff)
+
+
+COMBINE = 256
+
+
+def experts_forward_kernel(
+    cols,
+    capacity,
+    n2_ref,
+    prev_ref,
+    cot_ref,
+    rw_ref,
+    carry_ref,
+    routes_ref,
+    tsr_ref,
+    tsc_ref,
+    w_ref,
+    x_ref,
+    gu_ref,
+    mix_ref,
+    gates_ref,
+    cotw_ref,
+    mix_acc,
+    send,
+    recv,
+    local_sem,
+):
     e = pl.program_id(0)
-    me = lax.axis_index("row")
     experts = pl.num_programs(0)
+    r, c = place()
     rows = n2_ref.shape[0]
-    depth = w_parts[0].shape[2]
-    slot = lax.rem(e, 2)
-
-    def at(m):
-        return pl.ds(pl.multiple_of((me ^ m) * depth, 16), depth)
-
-    def w_copies(expert, place):
-        return [
-            pltpu.make_async_copy(
-                w_parts[m].at[t, expert], wbuf.at[place, t, at(m)], wsem.at[place, t * ranks + m]
-            )
-            for t in range(3)
-            for m in range(ranks)
-        ]
-
-    def g_copies(expert, place):
-        return [
-            pltpu.make_async_copy(
-                gbuf.at[place, t, at(m)], g_parts[m].at[t, expert], gsem.at[place, t * ranks + m]
-            )
-            for t in range(3)
-            for m in range(ranks)
-        ]
+    local = rows // cols
+    step, drain = gather_chain(cot_ref, cotw_ref, send, recv, cols)
+    own_copy = pltpu.make_async_copy(cot_ref, cotw_ref.at[c], local_sem.at[0])
 
     @pl.when(e == 0)
     def _():
-        for c in w_copies(0, 0):
-            c.start()
-        logits = mm(n2_ref[...], rw_ref[...], NT) + mm(cotx_ref[:, D:], carry_ref[...])
-        g = gate_lanes(logits, routes_ref[...])
+        greet(col_peers(cols))
+        own_copy.start()
+        step(0)
+        prev = jnp.concatenate([mm(prev_ref[i], carry_ref[...], TN) for i in range(cols)], axis=0)
+        g = gate_lanes(mm(n2_ref[...], rw_ref[...], NT) + prev, routes_ref[...])
         high = g.astype(BF)
-        gates[:, :LANES] = high
-        gates[:, LANES:] = (g - high.astype(F32)).astype(BF)
+        gates_ref[:, :LANES] = high
+        gates_ref[:, LANES:] = (g - high.astype(F32)).astype(BF)
         mix_acc[...] = jnp.zeros_like(mix_acc)
+
+    @pl.when(e == 3)
+    def _():
+        step(1)
+
+    one = slot_rows(tsr_ref, capacity)
+    x = mm(one, n2_ref[...]).astype(BF)
+    x_ref[0] = x
+    sg = mm(one, gates_ref[...])
+    sg = jnp.sum(jnp.where(lane_iota(sg.shape) % LANES == e, sg, 0.0), axis=1, keepdims=True)
+    g = mm(x, full_weight(w_ref, 0))
+    u = mm(x, full_weight(w_ref, 1))
+    gu_ref[0, 0] = g.astype(BF)
+    gu_ref[0, 1] = u.astype(BF)
+    gh = (g * jax.nn.sigmoid(g) * u * sg).astype(BF)
+    y = mm(gh, full_weight(w_ref, 2), NT).astype(BF)
+    tsc = slot_column(tsc_ref, e)
+    for b in range(rows // COMBINE):
+        rs = slice(b * COMBINE, (b + 1) * COMBINE)
+        one_t = jnp.where(lane_iota((COMBINE, capacity)) == tsc[rs], 1.0, 0.0).astype(BF)
+        mix_acc[rs] += mm(one_t, y)
+
+    @pl.when(e == experts - 1)
+    def _():
+        for k in range(2, cols):
+            step(k)
+        for d in range(cols):
+            mix_ref[d] = mix_acc[d * local : (d + 1) * local].astype(BF)
+        drain()
+        own_copy.wait()
+
+
+def experts_forward(cols, n2, prev, cot, rw, carry, routes, slots, slots_t, w_all):
+    rows = n2.shape[0]
+    capacity = rows // 4
+    ranks, three, experts, depth, ff = w_all.shape
+    local = rows // cols
+    return pl.pallas_call(
+        functools.partial(experts_forward_kernel, cols, capacity),
+        grid=(experts,),
+        out_shape=(
+            jax.ShapeDtypeStruct((experts, capacity, D), BF),
+            jax.ShapeDtypeStruct((experts, 2, capacity, ff), BF),
+            jax.ShapeDtypeStruct((cols, local, D), BF),
+            jax.ShapeDtypeStruct((rows, 2 * LANES), BF),
+            jax.ShapeDtypeStruct((cols, local, D), BF),
+        ),
+        in_specs=[
+            whole((rows, D)),
+            whole((cols, 16, local)),
+            whole((local, D)),
+            whole((LANES, D)),
+            whole((16, LANES)),
+            whole((rows, 2)),
+            pl.BlockSpec((1, 1, rows), lambda e: (e, 0, 0)),
+            whole((rows, experts)),
+            pl.BlockSpec((ranks, three, 1, depth, ff), lambda e: (0, 0, e, 0, 0)),
+        ],
+        out_specs=(
+            pl.BlockSpec((1, capacity, D), lambda e: (e, 0, 0)),
+            pl.BlockSpec((1, 2, capacity, ff), lambda e: (e, 0, 0, 0)),
+            whole((cols, local, D)),
+            whole((rows, 2 * LANES)),
+            ANY,
+        ),
+        scratch_shapes=[
+            pltpu.VMEM((rows, D), F32),
+            pltpu.SemaphoreType.DMA((2, cols - 1)),
+            pltpu.SemaphoreType.DMA((2, cols - 1)),
+            pltpu.SemaphoreType.DMA((1,)),
+        ],
+        compiler_params=pltpu.CompilerParams(
+            vmem_limit_bytes=60 * MIB, collective_id=1, has_side_effects=True
+        ),
+        cost_estimate=pl.CostEstimate(
+            flops=experts * capacity * 4 * D * (2 * ff + rows),
+            bytes_accessed=40 * MIB,
+            transcendentals=experts * capacity * ff,
+        ),
+        name="experts_forward",
+    )(n2, prev, cot, rw, carry, routes, slots_t, slots, w_all)
+
+
+def experts_backward_kernel(
+    cols,
+    capacity,
+    cot_ref,
+    mix_ref,
+    gates_ref,
+    tsr_ref,
+    tsc_ref,
+    w_ref,
+    x_ref,
+    gu_ref,
+    gt_ref,
+    dots_ref,
+    mixsum_ref,
+    gown_ref,
+    sib_ref,
+    gt_acc,
+    gbuf,
+    out,
+    arrived,
+    send,
+    recv,
+    own_sem,
+    sib_send,
+    sib_recv,
+):
+    e = pl.program_id(0)
+    experts = pl.num_programs(0)
+    r, c = place()
+    core = r % 2
+    rows = cot_ref.shape[0]
+    local = rows // cols
+    place_now = lax.rem(e, 2)
+    slot, total, drain = reduce_chain(lambda d: mix_ref[d], out, arrived, send, recv, cols)
+
+    def own_copy(expert, at):
+        return pltpu.make_async_copy(gbuf.at[at, :, :, core], gown_ref.at[expert], own_sem.at[at])
+
+    def sib_copy(expert, at):
+        return send_to(
+            gbuf.at[at, :, :, 1 - core],
+            sib_ref.at[expert],
+            sib_send.at[at],
+            sib_recv.at[expert],
+            (flip(r, 1), c),
+        )
+
+    @pl.when(e == 0)
+    def _():
+        greet(col_peers(cols) + [(flip(r, 1), c)])
+        slot(0)
         gt_acc[...] = jnp.zeros_like(gt_acc)
 
-    @pl.when(e + 1 < experts)
+    @pl.when(e == 2)
     def _():
-        for c in w_copies(e + 1, 1 - slot):
-            c.start()
-
-    one = jnp.where(lax.broadcasted_iota(jnp.int32, (capacity, rows), 0) == tsr_ref[0], 1.0, 0.0).astype(BF)
-    x = mm(one, n2_ref[...]).astype(BF)
-    c = mm(one, cotx_ref[:, :D]).astype(BF)
-    sg = mm(one, gates[...])
+        slot(1)
+
+    @pl.when(e == 5)
+    def _():
+        slot(2)
+
+    one = slot_rows(tsr_ref, capacity)
+    ct = mm(one, cot_ref[...]).astype(BF)
+    sg = mm(one, gates_ref[...])
     sg = jnp.sum(jnp.where(lane_iota(sg.shape) % LANES == e, sg, 0.0), axis=1, keepdims=True)
-
-    for cp in w_copies(e, slot):
-        cp.wait()
-    wg, wu, wd = wbuf.at[slot, 0], wbuf.at[slot, 1], wbuf.at[slot, 2]
-    g = mm(x, wg[...])
-    u = mm(x, wu[...])
-    v = mm(c, wd[...])
+    x = x_ref[0]
+    g, u = gu_ref[0, 0].astype(F32), gu_ref[0, 1].astype(F32)
+    wg, wu = full_weight(w_ref, 0), full_weight(w_ref, 1)
+    v = mm(ct, full_weight(w_ref, 2))
     sig = jax.nn.sigmoid(g)
     act = g * sig
     h = act * u
     dot = jnp.sum(h * v, axis=1, keepdims=True)
+    dots_ref[pl.ds(e, 1)] = jnp.sum(one.astype(F32) * dot, axis=0, keepdims=True)
     gh = (h * sg).astype(BF)
     gv = v * sg
     dg = (gv * u * (sig * (1.0 + g * (1.0 - sig)))).astype(BF)
     du = (gv * act).astype(BF)
-    y = mm(gh, wd[...], NT).astype(BF)
-    dx = (mm(dg, wg[...], NT) + mm(du, wu[...], NT)).astype(BF)
-    dot_high = dot.astype(BF).astype(F32)
-    lane = lane_iota((capacity, LANES))
-    dots = jnp.where(lane == e, dot_high, 0.0) + jnp.where(lane == e + EXPERTS, dot - dot_high, 0.0)
-    dxx = jnp.concatenate([dx, dots.astype(BF)], axis=1)
-
-    tsc = jnp.sum(jnp.where(lane_iota(tsc_ref.shape) == e, tsc_ref[...], 0), axis=1, keepdims=True)
-    step = 256
-    for b in range(rows // step):
-        rs = slice(b * step, (b + 1) * step)
-        one_t = jnp.where(lane_iota((step, capacity)) == tsc[rs], 1.0, 0.0).astype(BF)
-        mix_acc[rs] += mm(one_t, y)
-        gt_acc[rs] += mm(one_t, dxx)
+    dx = (mm(dg, wg, NT) + mm(du, wu, NT)).astype(BF)
+    tsc = slot_column(tsc_ref, e)
+    for b in range(rows // COMBINE):
+        rs = slice(b * COMBINE, (b + 1) * COMBINE)
+        one_t = jnp.where(lane_iota((COMBINE, capacity)) == tsc[rs], 1.0, 0.0).astype(BF)
+        gt_acc[rs] += mm(one_t, dx)
 
     @pl.when(e >= 2)
     def _():
-        for cp in g_copies(e - 2, slot):
-            cp.wait()
-
-    gbuf[slot, 0] = mm(x, dg, TN).astype(BF)
-    gbuf[slot, 1] = mm(x, du, TN).astype(BF)
-    gbuf[slot, 2] = mm(c, gh, TN).astype(BF)
-    for cp in g_copies(e, slot):
-        cp.start()
+        own_copy(e - 2, place_now).wait()
+        sib_copy(e - 2, place_now).wait_send()
+
+    shape = gbuf.shape[2:]
+    gbuf[place_now, 0] = mm(x, dg, TN).astype(BF).reshape(shape)
+    gbuf[place_now, 1] = mm(x, du, TN).astype(BF).reshape(shape)
+    gbuf[place_now, 2] = mm(ct, gh, TN).astype(BF).reshape(shape)
+    own_copy(e, place_now).start()
+    sib_copy(e, place_now).start()
 
     @pl.when(e == experts - 1)
     def _():
-        mix_ref[...] = mix_acc[...].astype(BF)
-        gtx_ref[...] = gt_acc[...].astype(BF)
-        for cp in g_copies(e - 1, 1 - slot) + g_copies(e, slot):
-            cp.wait()
-
-
-def experts_both_ways(n2, cotx, rw, carry, routes, slots, w_parts):
-    rows = n2.shape[0]
+        for d in range(cols):
+            gt_ref[d] = gt_acc[d * local : (d + 1) * local].astype(BF)
+        for s in range(3, cols):
+            slot(s)
+        total(mixsum_ref)
+        drain()
+        for back in (1, 0):
+            own_copy(e - back, lax.rem(e - back, 2)).wait()
+            sib_copy(e - back, lax.rem(e - back, 2)).wait_send()
+        for i in range(8):
+            sib_copy(i, i % 2).wait_recv()
+
+
+def experts_backward(cols, cot, mix, gates, slots, slots_t, w_all, x, gu):
+    rows = cot.shape[0]
     capacity = rows // 4
-    ranks = len(w_parts)
-    three, experts, depth, ff = w_parts[0].shape
-    anyspec = pl.BlockSpec(memory_space=pl.ANY)
-    outs = pl.pallas_call(
-        functools.partial(moe_kernel, ranks, capacity),
+    ranks, three, experts, depth, ff = w_all.shape
+    local = rows // cols
+    chips = ranks // 2
+    half = jax.ShapeDtypeStruct((experts, three, chips, depth, ff), BF)
+    return pl.pallas_call(
+        functools.partial(experts_backward_kernel, cols, capacity),
         grid=(experts,),
-        out_shape=[
-            jax.ShapeDtypeStruct((rows, D), BF),
-            jax.ShapeDtypeStruct((rows, D + LANES), BF),
-        ]
-        + [jax.ShapeDtypeStruct((three, experts, depth, ff), BF)] * ranks,
+        out_shape=(
+            jax.ShapeDtypeStruct((cols, local, D), BF),
+            jax.ShapeDtypeStruct((experts, rows), F32),
+            jax.ShapeDtypeStruct((local, D), F32),
+            half,
+            half,
+        ),
         in_specs=[
             whole((rows, D)),
-            whole((rows, D + LANES)),
-            whole((LANES, D)),
-            whole((LANES, LANES)),
-            whole((rows, 2)),
+            whole((cols, local, D)),
+            whole((rows, 2 * LANES)),
             pl.BlockSpec((1, 1, rows), lambda e: (e, 0, 0)),
             whole((rows, experts)),
+            pl.BlockSpec((ranks, three, 1, depth, ff), lambda e: (0, 0, e, 0, 0)),
+            pl.BlockSpec((1, capacity, D), lambda e: (e, 0, 0)),
+            pl.BlockSpec((1, 2, capacity, ff), lambda e: (e, 0, 0, 0)),
+        ],
+        out_specs=(
+            whole((cols, local, D)),
+            whole((experts, rows)),
+            whole((local, D)),
+            ANY,
+            ANY,
+        ),
+        scratch_shapes=[
+            pltpu.VMEM((rows, D), F32),
+            pltpu.VMEM((2, three, chips, 2, depth, ff), BF),
+            *chain_scratch(cols, local),
+            pltpu.SemaphoreType.DMA((2,)),
+            pltpu.SemaphoreType.DMA((2,)),
+            pltpu.SemaphoreType.DMA((experts,)),
+        ],
+        compiler_params=pltpu.CompilerParams(
+            vmem_limit_bytes=60 * MIB, collective_id=2, has_side_effects=True
+        ),
+        cost_estimate=pl.CostEstimate(
+            flops=experts * capacity * 4 * D * (3 * ff + rows),
+            bytes_accessed=60 * MIB,
+            transcendentals=experts * capacity * ff,
+        ),
+        name="experts_backward",
+    )(cot, mix, gates, slots_t, slots, w_all, x, gu)
+
+
+def pack_heads(dst, value):
+    rows = value.shape[0]
+    half = rows // 2
+    dst[:rows] = value[:, :LANES]
+    dst[rows:] = jnp.concatenate([value[:half, LANES:], value[half:, LANES:]], axis=1)
+
+
+def unpack_heads(packed, rows):
+    top, rest = packed[:rows], packed[rows:]
+    return (
+        top[:, :HEAD_DIM],
+        top[:, HEAD_DIM:],
+        jnp.concatenate([rest[:, :HEAD_DIM], rest[:, HEAD_DIM:]], axis=0),
+    )
+
+
+def to_rows(src_of, dst, send, recv, ranks):
+    r, c = place()
+    copies = []
+    for m in range(1, ranks):
+        there = flip(r, m)
+        copies.append(send_to(src_of(there), dst.at[r], send.at[m - 1], recv.at[m - 1], (there, c)))
+    return copies
+
+
+def to_cols(src_of, dst, send, recv, n):
+    r, c = place()
+    copies = []
+    for k in range(1, n):
+        there = (c + k) % n
+        copies.append(send_to(src_of(there), dst.at[c], send.at[k - 1], recv.at[k - 1], (r, there)))
+    return copies
+
+
+def all_sum(ref, count):
+    total = ref[0].astype(F32)
+    for i in range(1, count):
+        total = total + ref[i].astype(F32)
+    return total
+
+
+def send_weight_grads(first, count, gown, sib, hin, lbuf, hbuf, load_sem, send, recv):
+    r, c = place()
+    chip = r // 2
+
+    def loads(i):
+        at = lax.rem(i, 2)
+        return [
+            pltpu.make_async_copy(ref.at[first + i], lbuf.at[at, j], load_sem.at[at, j])
+            for j, ref in enumerate((gown, sib))
         ]
-        + [anyspec] * ranks,
-        out_specs=[whole((rows, D)), whole((rows, D + LANES))] + [anyspec] * ranks,
-        scratch_shapes=[
-            pltpu.VMEM((2, 3, depth * ranks, ff), BF),
-            pltpu.SemaphoreType.DMA((2, 3 * ranks)),
-            pltpu.VMEM((2, 3, depth * ranks, ff), BF),
-            pltpu.SemaphoreType.DMA((2, 3 * ranks)),
-            pltpu.VMEM((rows, 2 * LANES), BF),
-            pltpu.VMEM((rows, D), F32),
-            pltpu.VMEM((rows, D + LANES), F32),
-        ],
-        compiler_params=pltpu.CompilerParams(vmem_limit_bytes=60 * MIB),
-        cost_estimate=pl.CostEstimate(
-            flops=experts * capacity * 2 * D * (9 * ff + 5 * rows),
-            bytes_accessed=48 * MIB,
-            transcendentals=experts * capacity * ff,
-        ),
-        name="experts_both_ways",
-    )(n2, cotx, rw, carry, routes, slots.T[:, None, :], slots, *w_parts)
-    return outs[0], outs[1], outs[2:]
+
+    def sends(i):
+        return [
+            send_to(
+                hbuf.at[i, :, flip(chip, k)],
+                hin.at[i, k - 1],
+                send.at[i, k - 1],
+                recv.at[i, k - 1],
+                (flip(r, 2 * k), c),
+            )
+            for k in range(1, 4)
+        ]
+
+    for copy in loads(0):
+        copy.start()
+
+    def body(i, carry):
+        @pl.when(i + 1 < count)
+        def _():
+            for copy in loads(i + 1):
+                copy.start()
+
+        for copy in loads(i):
+            copy.wait()
+        at = lax.rem(i, 2)
+        hbuf[i] = (lbuf[at, 0].astype(F32) + lbuf[at, 1].astype(F32)).astype(BF)
+        for copy in sends(i):
+            copy.start()
+        return carry
+
+    lax.fori_loop(0, count, body, 0)
+
+    def finish():
+        def wait(i, carry):
+            for copy in sends(i):
+                copy.wait()
+            return carry
+
+        lax.fori_loop(0, count, wait, 0)
+
+    return finish
+
+
+def weight_scratch(count, block):
+    three, chips, depth, ff = block
+    return [
+        pltpu.VMEM((2, 2, three, chips, depth, ff), BF),
+        pltpu.VMEM((count, three, chips, depth, ff), BF),
+        pltpu.SemaphoreType.DMA((2, 2)),
+        pltpu.SemaphoreType.DMA((count, 3)),
+        pltpu.SemaphoreType.DMA((count, 3)),
+    ]
 
 
 def resid_kernel(
-    gtx_ref,
+    cols,
+    count,
+    gt_ref,
+    dots_ref,
+    mixsum_ref,
     n2_ref,
     middle_ref,
     cot_ref,
@@ -857,30 +1238,61 @@
     out_t_ref,
     mixed_ref,
     valid_ref,
-    midmix_ref,
+    gown_ref,
+    sib_ref,
+    layer_ref,
     resid_ref,
     gm_ref,
     og_ref,
     small_ref,
     pg_ref,
+    hin_ref,
+    out,
+    arrived,
+    send,
+    recv,
+    dots_in,
+    dsend,
+    drecv,
+    grad,
+    gm_out,
+    gsend,
+    grecv,
+    gm_sem,
+    *weight_refs,
 ):
+    r, c = place()
+    local = n2_ref.shape[0]
+    greet(col_peers(cols) + [(flip(r, 2 * k), c) for k in range(1, 4)])
+    slot, total, drain = reduce_chain(lambda d: gt_ref[d], out, arrived, send, recv, cols)
+
+    def dots_of(d):
+        return dots_ref.at[:, pl.ds(pl.multiple_of(d * local, LANES), local)]
+
+    dot_copies = to_cols(dots_of, dots_in, dsend, drecv, cols)
+    for copy in dot_copies:
+        copy.start()
+    dots_in[c] = dots_of(c)[...]
+    slot(0)
+    finish = send_weight_grads(0, count, gown_ref, sib_ref, hin_ref, *weight_refs)
+    slot(1)
+
     n2, cot = n2_ref[...], cot_ref[...]
     n2f, cotf = n2.astype(F32), cot.astype(F32)
     middle = middle_ref[...]
     rw = rw_ref[...]
     lin = mm(n2, rw, NT)
     prev = prev_ref[...]
-    gates = gate_lanes(lin + mm(prev, carry_ref[...]), routes_ref[...])
-    rows = n2.shape[0]
-    lane = lane_iota((rows, LANES))
+    gates = gate_lanes(lin + mm(prev, carry_ref[...], TN), routes_ref[...])
+    lane = lane_iota((local, LANES))
     cot_lin = mm(cot, rw, NT)
     dot_keep = jnp.sum(cotf * n2f, axis=1, keepdims=True)
-    copy_share = gates[:, EXPERTS + 1 : EXPERTS + 2]
-    d = gtx_ref[:, D:].astype(F32)
-    g_gates = jnp.where(lane < EXPERTS, d + pltpu.roll(d, LANES - EXPERTS, 1), 0.0)
-    g_gates = jnp.where(lane == EXPERTS + 1, dot_keep, g_gates)
-    keep = copy_share
-    mixes, packs = [], jnp.zeros((rows, LANES), F32)
+    for copy in dot_copies:
+        copy.wait()
+    d = jnp.concatenate([all_sum(dots_in, cols), jnp.zeros((LANES - EXPERTS, local), F32)], axis=0).T
+    g_gates = jnp.where(lane == EXPERTS + 1, dot_keep, d)
+    keep = gates[:, EXPERTS + 1 : EXPERTS + 2]
+    mixes, packs = [], jnp.zeros((local, LANES), F32)
     for j in range(2):
         l0 = lin[:, ROW_CONST + 2 * j : ROW_CONST + 2 * j + 1]
         l1 = lin[:, ROW_CONST + 2 * j + 1 : ROW_CONST + 2 * j + 2]
@@ -899,147 +1311,344 @@
         packs = packs + jnp.where(lane == ROW_VEC + j, share * a1, 0.0)
     packs = packs + gates * (g_gates - jnp.sum(gates * g_gates, axis=1, keepdims=True))
     vec = rw[ROW_VEC : ROW_VEC + 2].astype(F32)
-    midmix_ref[...] = middle + keep * n2f + mixes[0] * vec[0:1] + mixes[1] * vec[1:2]
+    layer = middle + mixsum_ref[...] + keep * n2f + mixes[0] * vec[0:1] + mixes[1] * vec[1:2]
+    layer_ref[...] = layer.astype(BF)
 
     high = packs.astype(BF)
     low = (packs - high.astype(F32)).astype(BF)
     back = lane < ROW_VEC
-    high_b, low_b = jnp.where(back, high, 0), jnp.where(back, low, 0)
-    grad_normed = (
-        gtx_ref[:, :D].astype(F32) + keep * cotf + mm(high_b, rw) + mm(low_b, rw)
-    )
+    high_b = jnp.where(back, packs, 0.0).astype(BF)
+    low_b = jnp.where(back, packs - high.astype(F32), 0.0).astype(BF)
+    grad_local = keep * cotf + mm(high_b, rw) + mm(low_b, rw)
     by_n2 = mm(high, n2, TN) + mm(low, n2, TN)
     by_cot = mm(high, cot, TN) + mm(low, cot, TN)
-    by_prev = mm(high, prev, TN) + mm(low, prev, TN)
+    by_prev = mm(prev, high) + mm(prev, low)
     pg = mm(carry_ref[...], high_b, NT) + mm(carry_ref[...], low_b, NT)
     pg_ref[...] = pg[:ROUTES]
-
+    sub = lax.broadcasted_iota(jnp.int32, (SMALL_ROWS, D), 0)
+    small_ref[:, :D] = jnp.where(sub < ROW_VEC, by_n2[:SMALL_ROWS], by_cot[:SMALL_ROWS])
+    small_ref[:16, D:] = by_prev
+    small_ref[16:, D:] = jnp.zeros((SMALL_ROWS - 16, LANES), F32)
+
+    for s in range(2, cols):
+        slot(s)
+    total(grad)
+    grad_normed = grad[...] + grad_local
     scale = norm_rows(middle)
     gained = grad_normed * gain_ref[...]
     mid_dot = jnp.sum(gained * middle, axis=1, keepdims=True)
     resid = cotf + scale * gained - middle * (scale * scale * scale * (mid_dot * (1.0 / D)))
     resid_ref[...] = resid
-    gain_grad = jnp.sum(grad_normed * middle * scale, axis=0, keepdims=True)
-    sub = lax.broadcasted_iota(jnp.int32, (SMALL_ROWS, D), 0)
-    small = jnp.where(sub < ROW_VEC, by_n2[:SMALL_ROWS], by_cot[:SMALL_ROWS])
-    small = jnp.where(sub >= ROW_GAIN, jnp.where(sub == ROW_GAIN, gain_grad, 0.0), small)
-    small_ref[:, :D] = small
-    small_ref[:, D:] = by_prev[:SMALL_ROWS]
-
     cut = resid.astype(BF)
     gm = (mm(cut, out_t_ref[...]) * valid_ref[...]).astype(BF)
-    parts, _, width = gm_ref.shape
-    for i in range(parts):
-        gm_ref[i] = gm[:, i * width : (i + 1) * width]
+    width = D // cols
+    for i in range(cols):
+        pack_heads(gm_out.at[i], gm[:, i * width : (i + 1) * width])
+    gm_copies = to_cols(lambda i: gm_out.at[i], gm_ref, gsend, grecv, cols)
+    for copy in gm_copies:
+        copy.start()
+    keep_own = pltpu.make_async_copy(gm_out.at[c], gm_ref.at[c], gm_sem.at[0])
+    keep_own.start()
+    small_ref[ROW_GAIN : ROW_GAIN + 1, :D] = jnp.sum(grad_normed * middle * scale, axis=0, keepdims=True)
     og_ref[...] = mm(cut, mixed_ref[...], TN).astype(BF)
-
-
-def resid_step(parts, gtx, n2, middle, cot, routes, prev, rw, carry, gain, out_t, mixed, valid):
-    rows = n2.shape[0]
+    keep_own.wait()
+    for copy in gm_copies:
+        copy.wait()
+    drain()
+    finish()
+
+
+def resid_step(cols, count, gt, dots, mixsum, n2, middle, cot, routes, prev, rw, carry, gain, out_t, mixed, valid, gown, sib):
+    local = n2.shape[0]
+    experts, three, chips, depth, ff = gown.shape
+    vm = pl.BlockSpec(memory_space=pltpu.VMEM)
     return pl.pallas_call(
-        resid_kernel,
+        functools.partial(resid_kernel, cols, count),
         out_shape=(
-            jax.ShapeDtypeStruct((rows, D), F32),
-            jax.ShapeDtypeStruct((rows, D), F32),
-            jax.ShapeDtypeStruct((parts, rows, D // parts), BF),
+            jax.ShapeDtypeStruct((local, D), BF),
+            jax.ShapeDtypeStruct((local, D), F32),
+            jax.ShapeDtypeStruct((cols, local * 3 // 2, LANES), BF),
             jax.ShapeDtypeStruct((D, D), BF),
             jax.ShapeDtypeStruct((SMALL_ROWS, D + LANES), F32),
-            jax.ShapeDtypeStruct((ROUTES, rows), F32),
-        ),
-        compiler_params=pltpu.CompilerParams(vmem_limit_bytes=48 * MIB),
-        cost_estimate=pl.CostEstimate(flops=6 * rows * D * D, bytes_accessed=12 * MIB, transcendentals=0),
+            jax.ShapeDtypeStruct((ROUTES, local), F32),
+            jax.ShapeDtypeStruct((count, 3, three, depth, ff), BF),
+        ),
+        in_specs=[vm] * 14 + [ANY, ANY],
+        out_specs=(vm, vm, ANY, vm, vm, vm, ANY),
+        scratch_shapes=[
+            *chain_scratch(cols, local),
+            pltpu.VMEM((cols, EXPERTS, local), F32),
+            pltpu.SemaphoreType.DMA((cols - 1,)),
+            pltpu.SemaphoreType.DMA((cols - 1,)),
+            pltpu.VMEM((local, D), F32),
+            pltpu.VMEM((cols, local * 3 // 2, LANES), BF),
+            pltpu.SemaphoreType.DMA((cols - 1,)),
+            pltpu.SemaphoreType.DMA((cols - 1,)),
+            pltpu.SemaphoreType.DMA((1,)),
+            *weight_scratch(count, (three, chips, depth, ff)),
+        ],
+        compiler_params=pltpu.CompilerParams(
+            vmem_limit_bytes=60 * MIB, collective_id=3, has_side_effects=True
+        ),
+        cost_estimate=pl.CostEstimate(flops=6 * local * D * D, bytes_accessed=40 * MIB, transcendentals=0),
         name="resid_step",
-    )(gtx, n2, middle, cot, routes, prev, rw, carry, gain, out_t, mixed, valid)
-
-
-def project_back_kernel(
-    heads, dq_ref, dk_ref, dv_ref, x_ref, gain_ref, w_ref, cos_ref, sin_ref, gn_ref, wg_ref, gg_ref, acc
+    )(gt, dots, mixsum, n2, middle, cot, routes, prev, rw, carry, gain, out_t, mixed, valid, gown, sib)
+
+
+def finish_kernel(
+    cols,
+    ranks,
+    first,
+    count,
+    gm_ref,
+    qkv_ref,
+    begin_ref,
+    o_ref,
+    lse_ref,
+    x_ref,
+    gain_ref,
+    w_ref,
+    cos_ref,
+    sin_ref,
+    small_ref,
+    og_ref,
+    resid_ref,
+    xown_ref,
+    gown_ref,
+    sib_ref,
+    ig_ref,
+    small_out,
+    gain_out,
+    qg_out,
+    og_out,
+    hin_ref,
+    do_s,
+    dq_s,
+    dk_s,
+    dv_s,
+    gn_s,
+    qg_acc,
+    qg_cut,
+    out,
+    arrived,
+    send,
+    recv,
+    small_rows,
+    small_cols,
+    og_rows,
+    og_parts,
+    og_cols,
+    gain_rows,
+    gain_cols,
+    qg_rows,
+    q_parts,
+    q_land,
+    total_s,
+    row_send,
+    row_recv,
+    col_send,
+    col_recv,
+    *weight_refs,
 ):
-    step = pl.program_id(0)
-    cosine, sines = cos_ref[...], sin_ref[...]
-    turned = [dq_ref[h] for h in range(heads)] + [dk_ref[h] for h in range(heads)]
-    cols = []
-    for part in range(heads):
-        v = jnp.concatenate(turned[2 * part : 2 * part + 2], axis=1)
-        cols.append((v * cosine - swap_pairs(v) * sines).astype(BF))
-    cols += [dv_ref[h].astype(BF) for h in range(heads)]
-    gp = jnp.concatenate(cols, axis=1)
-    x = x_ref[...].astype(F32)
-    xs = x * norm_rows(x)
-    normed = (xs * gain_ref[...]).astype(BF)
-    gn = mm(gp, w_ref[...], NT)
-    gn_ref[...] = gn.astype(BF)
-    part_grad = mm(normed, gp, TN)
-    gain_part = jnp.sum(gn * xs, axis=0, keepdims=True)
-
-    @pl.when(step == 0)
-    def _():
-        acc[...] = part_grad
-        gg_ref[...] = gain_part
-
-    @pl.when(step > 0)
-    def _():
-        acc[...] += part_grad
-        gg_ref[...] += gain_part
-
-    @pl.when(step == pl.num_programs(0) - 1)
-    def _():
-        wg_ref[...] = acc[...].astype(BF)
-
-
-def project_back(heads, dq, dk, dv, whole_in, gain, weight, cosine, sines):
-    rows = whole_in.shape[0]
-    blk = 256
-    width = 3 * heads * HEAD_DIM
-    head_spec = pl.BlockSpec((heads, blk, HEAD_DIM), lambda i: (0, i, 0))
+    r, c = place()
+    heads = 3
+    rows = x_ref.shape[0]
+    local = rows // cols
+    depth = D // ranks
+    width = heads * HEAD_DIM
+    score_scale = 1.0 / math.sqrt(HEAD_DIM)
+    greet(col_peers(cols) + [(flip(r, m), c) for m in range(1, ranks)])
+
+    def rows_of(ref, d):
+        return ref.at[pl.ds(pl.multiple_of(d * depth, 16), depth)]
+
+    small_to_rows = to_rows(lambda d: small_ref, small_rows, row_send.at[0], row_recv.at[0], ranks)
+    og_to_rows = to_rows(lambda d: rows_of(og_ref, d), og_rows, row_send.at[1], row_recv.at[1], ranks)
+    for copy in small_to_rows + og_to_rows:
+        copy.start()
+    small_rows[r] = small_ref[...]
+    og_rows[r] = rows_of(og_ref, r)[...]
+    finish = send_weight_grads(first, count, gown_ref, sib_ref, hin_ref, *weight_refs)
+
+    for d in range(cols):
+        at = slice(d * local, (d + 1) * local)
+        for h, value in enumerate(unpack_heads(gm_ref[d], local)):
+            do_s[h, at] = value
+
+    blocks = rows // Q_ROWS
+
+    def one_head(h, carry):
+        for i in reversed(range(blocks)):
+            at = slice(i * Q_ROWS, (i + 1) * Q_ROWS)
+            length = (i + 1) * Q_ROWS
+            q, do = qkv_ref[h, at], do_s[h, at]
+            k, v = qkv_ref[heads + h, :length], qkv_ref[2 * heads + h, :length]
+            delta = jnp.sum(do.astype(F32) * o_ref[h, at].astype(F32), axis=1, keepdims=True)
+            s = mm(q, k, NT)
+            ok = seen(begin_ref[at], i * Q_ROWS, Q_ROWS, length)
+            p = jnp.where(ok, jnp.exp(s - lse_ref[h, at]), 0.0)
+            ds = (p * (mm(do, v, NT) - delta)).astype(BF)
+            dq_s[h, at] = mm(ds, k) * score_scale
+            dk, dv = mm(ds, q, TN), mm(p.astype(BF), do, TN)
+            if i == blocks - 1:
+                dk_s[h], dv_s[h] = dk, dv
+            else:
+                dk_s[h, :length] += dk
+                dv_s[h, :length] += dv
+        return carry
+
+    lax.fori_loop(0, 2, one_head, 0)
+    for copy in small_to_rows + og_to_rows:
+        copy.wait()
+    small_cols[c] = all_sum(small_rows, ranks)
+    og_sum = all_sum(og_rows, ranks)
+    for i in range(cols):
+        og_parts[i] = og_sum[:, i * width : (i + 1) * width]
+    small_to_cols = to_cols(lambda d: small_cols.at[c], small_cols, col_send.at[0], col_recv.at[0], cols)
+    og_to_cols = to_cols(lambda d: og_parts.at[d], og_cols, col_send.at[1], col_recv.at[1], cols)
+    for copy in small_to_cols + og_to_cols:
+        copy.start()
+    og_cols[c] = og_parts[c]
+    lax.fori_loop(2, 3, one_head, 0)
+
+    slot, total, drain = reduce_chain(lambda d: gn_s[d], out, arrived, send, recv, cols)
+    gain_total = jnp.zeros((1, D), F32)
+    weight = w_ref[...]
+    for n, d in enumerate((3, 0, 2, 1)):
+        at = slice(d * local, (d + 1) * local)
+        cosine, sines = cos_ref[at], sin_ref[at]
+        turned = [dq_s[h, at] for h in range(heads)] + [dk_s[h, at] for h in range(heads)]
+        parts = []
+        for part in range(heads):
+            v = jnp.concatenate(turned[2 * part : 2 * part + 2], axis=1)
+            parts.append((v * cosine - swap_pairs(v) * sines).astype(BF))
+        parts += [dv_s[h, at].astype(BF) for h in range(heads)]
+        gp = jnp.concatenate(parts, axis=1)
+        x = x_ref[at].astype(F32)
+        xs = x * norm_rows(x)
+        gn = mm(gp, weight, NT)
+        gn_s[d] = gn.astype(BF)
+        gain_total = gain_total + jnp.sum(gn * xs, axis=0, keepdims=True)
+        grad = mm((xs * gain_ref[...]).astype(BF), gp, TN)
+        if n == 0:
+            qg_acc[...] = grad
+        else:
+            qg_acc[...] += grad
+        if n == 1:
+            slot(0)
+        if n == 3:
+            slot(1)
+    qg_cut[...] = qg_acc[...].astype(BF)
+    gain_rows[r] = jnp.broadcast_to(gain_total, (8, D))
+    qg_to_rows = to_rows(lambda d: rows_of(qg_cut, d), qg_rows, row_send.at[2], row_recv.at[2], ranks)
+    gain_to_rows = to_rows(lambda d: gain_rows.at[r], gain_rows, row_send.at[3], row_recv.at[3], ranks)
+    for copy in gain_to_rows + qg_to_rows:
+        copy.start()
+    qg_rows[r] = rows_of(qg_cut, r)[...]
+    for s in range(2, cols - 1):
+        slot(s)
+    for copy in gain_to_rows + qg_to_rows:
+        copy.wait()
+    gain_cols[c] = all_sum(gain_rows, ranks)
+    q_sum = all_sum(qg_rows, ranks)
+    for i in range(3):
+        q_parts[i] = q_sum[:, i * width : (i + 1) * width]
+    gain_to_cols = to_cols(lambda d: gain_cols.at[c], gain_cols, col_send.at[2], col_recv.at[2], cols)
+    odd, high = c % 2, c // 2
+    q_copies = [
+        send_to(
+            q_parts.at[1 - odd + high],
+            q_land.at[1],
+            col_send.at[3, 0],
+            col_recv.at[3, 0],
+            (r, flip(c, 1)),
+        ),
+        send_to(
+            q_parts.at[2 - 2 * high],
+            q_land.at[2 - 2 * odd],
+            col_send.at[3, 1],
+            col_recv.at[3, 1],
+            (r, flip(c, 2)),
+        ),
+    ]
+    for copy in gain_to_cols + q_copies:
+        copy.start()
+    q_land[2 * odd] = q_parts[(c + 1) // 2]
+    slot(cols - 1)
+    total(total_s)
+    gn = total_s[...]
+    x = xown_ref[...].astype(F32)
+    scale = norm_rows(x)
+    gained = gn * gain_ref[...]
+    x_dot = jnp.sum(gained * x, axis=1, keepdims=True)
+    ig_ref[...] = resid_ref[...] + scale * gained - x * (scale * scale * scale * (x_dot * (1.0 / D)))
+    for copy in small_to_cols + og_to_cols + gain_to_cols + q_copies:
+        copy.wait()
+    small_out[...] = all_sum(small_cols, cols)
+    og_out[...] = all_sum(og_cols, cols)
+    gain_out[...] = all_sum(gain_cols, cols)
+    qg_out[...] = q_land[...]
+    drain()
+    finish()
+
+
+def finish_step(cols, ranks, first, gm, qkv, begin, o, lse, x, gain, w, cosine, sines, small, og, resid, xown, gown, sib):
+    rows = x.shape[0]
+    local = rows // cols
+    experts, three, chips, depth, ff = gown.shape
+    count = experts - first
+    heads, width = 3, 3 * HEAD_DIM
+    vm = pl.BlockSpec(memory_space=pltpu.VMEM)
+    wide = D + LANES
     return pl.pallas_call(
-        functools.partial(project_back_kernel, heads),
-        grid=(rows // blk,),
+        functools.partial(finish_kernel, cols, ranks, first, count),
         out_shape=(
-            jax.ShapeDtypeStruct((rows, D), BF),
-            jax.ShapeDtypeStruct((D, width), BF),
-            jax.ShapeDtypeStruct((1, D), F32),
-        ),
-        in_specs=[
-            head_spec,
-            head_spec,
-            head_spec,
-            pl.BlockSpec((blk, D), lambda i: (i, 0)),
-            whole((1, D)),
-            whole((D, width)),
-            pl.BlockSpec((blk, LANES), lambda i: (i, 0)),
-            pl.BlockSpec((blk, LANES), lambda i: (i, 0)),
+            jax.ShapeDtypeStruct((local, D), F32),
+            jax.ShapeDtypeStruct((SMALL_ROWS, wide), F32),
+            jax.ShapeDtypeStruct((8, D), F32),
+            jax.ShapeDtypeStruct((3, depth, width), F32),
+            jax.ShapeDtypeStruct((depth, width), F32),
+            jax.ShapeDtypeStruct((count, 3, three, depth, ff), BF),
+        ),
+        in_specs=[vm] * 14 + [ANY, ANY],
+        out_specs=(vm, vm, vm, vm, vm, ANY),
+        scratch_shapes=[
+            pltpu.VMEM((heads, rows, HEAD_DIM), BF),
+            pltpu.VMEM((heads, rows, HEAD_DIM), F32),
+            pltpu.VMEM((heads, rows, HEAD_DIM), F32),
+            pltpu.VMEM((heads, rows, HEAD_DIM), F32),
+            pltpu.VMEM((cols, local, D), BF),
+            pltpu.VMEM((D, 3 * width), F32),
+            pltpu.VMEM((D, 3 * width), BF),
+            *chain_scratch(cols, local),
+            pltpu.VMEM((ranks, SMALL_ROWS, wide), F32),
+            pltpu.VMEM((cols, SMALL_ROWS, wide), F32),
+            pltpu.VMEM((ranks, depth, D), BF),
+            pltpu.VMEM((cols, depth, width), F32),
+            pltpu.VMEM((cols, depth, width), F32),
+            pltpu.VMEM((ranks, 8, D), F32),
+            pltpu.VMEM((cols, 8, D), F32),
+            pltpu.VMEM((ranks, depth, 3 * width), BF),
+            pltpu.VMEM((3, depth, width), F32),
+            pltpu.VMEM((3, depth, width), F32),
+            pltpu.VMEM((local, D), F32),
+            pltpu.SemaphoreType.DMA((4, ranks - 1)),
+            pltpu.SemaphoreType.DMA((4, ranks - 1)),
+            pltpu.SemaphoreType.DMA((4, cols - 1)),
+            pltpu.SemaphoreType.DMA((4, cols - 1)),
+            *weight_scratch(count, (three, chips, depth, ff)),
         ],
-        out_specs=(pl.BlockSpec((blk, D), lambda i: (i, 0)), whole((D, width)), whole((1, D))),
-        scratch_shapes=[pltpu.VMEM((D, width), F32)],
-        compiler_params=pltpu.CompilerParams(vmem_limit_bytes=48 * MIB),
-        cost_estimate=pl.CostEstimate(flops=4 * rows * D * width, bytes_accessed=16 * MIB, transcendentals=0),
-        name="project_back",
-    )(dq, dk, dv, whole_in, gain, weight, cosine, sines)
-
-
-def swap_rows(value, ranks, mask):
-    return lax.ppermute(value, "row", [(i, i ^ mask) for i in range(ranks)])
-
-
-def gather_rows(value, ranks):
-    parts = {0: value}
-    for m in range(2, ranks, 2):
-        parts[m] = swap_rows(value, ranks, m)
-    for m in range(0, ranks, 2):
-        parts[m + 1] = swap_rows(parts[m], ranks, 1)
-    return [parts[m] for m in range(ranks)]
-
-
-def scatter_rows(parts, ranks):
-    held = {}
-    for m in range(0, ranks, 2):
-        arrived = swap_rows(parts[m + 1], ranks, 1)
-        held[m] = parts[m].astype(F32) + arrived.astype(F32)
-    total = held[0]
-    for m in range(2, ranks, 2):
-        total = total + swap_rows(held[m].astype(BF), ranks, m).astype(F32)
-    return total
+        compiler_params=pltpu.CompilerParams(
+            vmem_limit_bytes=62 * MIB, collective_id=4, has_side_effects=True
+        ),
+        cost_estimate=pl.CostEstimate(
+            flops=20 * heads * rows * rows * HEAD_DIM, bytes_accessed=40 * MIB, transcendentals=heads * rows * rows
+        ),
+        name="finish_step",
+    )(gm, qkv, begin, o, lse, x, gain, w, cosine, sines, small, og, resid, xown, gown, sib)
+
+
+SENT_FIRST = 5
 
 
 def on_device_heads(
@@ -1064,7 +1673,7 @@
     ranks, cols = sizes
     heads = HEADS // cols
     width = heads * HEAD_DIM
-    col_index = lax.axis_index("col")
+    row_index, col_index = lax.axis_index("row"), lax.axis_index("col")
     row_total = expert_routes.shape[0]
     local_rows = inputs.shape[0]
     first_row = col_index * local_rows
@@ -1073,32 +1682,17 @@
         return lax.dynamic_slice_in_dim(value, first_row, local_rows, 0)
 
     w_stack = jnp.stack([gate_weight, up_weight, down_weight.transpose(0, 2, 1)])
-    w_parts = gather_rows(w_stack, ranks)
-
-    w_cat = jnp.concatenate([out_weight.T, qkv_weight], axis=1)
-    w_all = lax.all_gather(w_cat, "col", axis=0, tiled=False)
-    depth = qkv_weight.shape[0]
-    blocks = w_all[:, :, width:].reshape(cols, depth, 3, width).transpose(0, 2, 1, 3)
-    blocks = blocks.reshape(3, cols, depth, width)
-    own = lax.dynamic_index_in_dim(blocks, col_index, 1, keepdims=False)
-    w_own = jnp.concatenate([own[0], own[1], own[2]], axis=1)
-    out_rows = w_all[:, :, :width].transpose(1, 0, 2).reshape(depth, D)
-    w_full = lax.all_gather(jnp.concatenate([out_rows, w_own], axis=1), "row", axis=0, tiled=True)
-    out_t, qkv_own = w_full[:, :D], w_full[:, D:]
-
-    whole_in = lax.all_gather(inputs, "col", axis=0, tiled=True)
-    prev_t = jnp.pad(prev_logits.T, ((0, 0), (0, LANES - ROUTES)))
-    cotx = lax.all_gather(jnp.concatenate([cotangent, prev_t], axis=1), "col", axis=0, tiled=True)
+    w_all = lax.all_gather(w_stack, "row", axis=0)
 
     lengths = seq_lengths[0]
     ends = jnp.cumsum(lengths)
     starts = ends - lengths
-    place = jnp.arange(row_total, dtype=jnp.int32)
-    seq_index = jnp.sum((place[:, None] >= ends[None, :]).astype(jnp.int32), axis=1)
+    spot = jnp.arange(row_total, dtype=jnp.int32)
+    seq_index = jnp.sum((spot[:, None] >= ends[None, :]).astype(jnp.int32), axis=1)
     member = seq_index[:, None] == jnp.arange(lengths.shape[0], dtype=jnp.int32)[None, :]
     begin = jnp.sum(jnp.where(member, starts[None, :], 0), axis=1)
     is_valid = seq_index < lengths.shape[0]
-    positions = place - begin
+    positions = spot - begin
     valid = is_valid.astype(F32)[:, None]
     seq_begin = jnp.where(is_valid, begin, ends[-1])[:, None]
     pair = jnp.arange(HEAD_DIM // 2, dtype=jnp.int32)
@@ -1114,6 +1708,7 @@
         expert_routes[:, :, None] == jnp.arange(EXPERTS, dtype=jnp.int32)[None, None, :], axis=1
     ).astype(jnp.int32)
     slots = jnp.where(hit > 0, jnp.cumsum(hit, axis=0) - 1, -1)
+    slots_t = slots.T[:, None, :]
 
     rw = jnp.concatenate(
         [
@@ -1124,81 +1719,103 @@
         ],
         axis=0,
     )
-    carry = jnp.pad(carry_weight, ((0, LANES - ROUTES), (0, LANES - ROUTES)))
+    carry = jnp.pad(carry_weight, ((0, 16 - ROUTES), (0, LANES - ROUTES)))
+    prev = jnp.pad(prev_logits, ((0, 16 - ROUTES), (0, 0)))
     attn_gain_row = attn_gain.astype(F32)[None, :]
     ffn_gain_row = ffn_gain.astype(F32)[None, :]
 
+    w_cat = jnp.concatenate([out_weight.T, qkv_weight], axis=1)
+    w_cols = lax.all_gather(w_cat, "col", axis=0, tiled=False)
+    depth = qkv_weight.shape[0]
+    blocks = w_cols[:, :, width:].reshape(cols, depth, 3, width).transpose(0, 2, 1, 3)
+    blocks = blocks.reshape(3, cols, depth, width)
+    own = lax.dynamic_index_in_dim(blocks, col_index, 1, keepdims=False)
+    w_own = jnp.concatenate([own[0], own[1], own[2]], axis=1)
+    out_rows = w_cols[:, :, :width].transpose(1, 0, 2).reshape(depth, D)
+    w_full = lax.all_gather(jnp.concatenate([out_rows, w_own], axis=1), "row", axis=0, tiled=True)
+    out_t, qkv_own = w_full[:, :D], w_full[:, D:]
+    whole_in = lax.all_gather(inputs, "col", axis=0, tiled=True)
+    prev_whole = lax.all_gather(prev, "col", axis=0)
     qkv = project_heads(heads, whole_in, attn_gain_row, qkv_own, cosine, sines)
     mixed_heads, lse = attend(heads, qkv, seq_begin, valid)
     to_send = mixed_heads.transpose(1, 0, 2).reshape(cols, local_rows, width)
     attn_parts = lax.all_to_all(to_send, "col", split_axis=0, concat_axis=0, tiled=True)
     mixed, middle, n2 = branch(attn_parts, out_t, inputs, ffn_gain_row)
     n2_whole = lax.all_gather(n2, "col", axis=0, tiled=True)
-    mix, gtx, g_parts = experts_both_ways(n2_whole, cotx, rw, carry, expert_routes, slots, w_parts)
-    gtx_own = lax.psum_scatter(gtx, "col", scatter_dimension=0, tiled=True)
-    mix_own = lax.psum_scatter(mix, "col", scatter_dimension=0, tiled=True)
-    midmix, resid, gm, og, small, prev_grad = resid_step(
+    x, gu, mix, gates, cot_whole = experts_forward(
+        cols, n2_whole, prev_whole, cotangent, rw, carry, expert_routes, slots, slots_t, w_all
+    )
+    gt, dots, mixsum, gown, sib = experts_backward(
+        cols, cot_whole.reshape(row_total, D), mix, gates, slots, slots_t, w_all, x, gu
+    )
+    layer_out, resid, gm, og, small, prev_grad, hin0 = resid_step(
         cols,
-        gtx_own,
+        SENT_FIRST,
+        gt,
+        dots,
+        mixsum,
         n2,
         middle,
         cotangent,
         own_rows(expert_routes),
-        prev_t,
+        prev,
         rw,
         carry,
         ffn_gain_row,
         out_t,
         mixed,
         own_rows(valid),
-    )
-    layer_out = (midmix + mix_own.astype(F32)).astype(BF)
-    gm_heads = lax.all_to_all(gm, "col", split_axis=0, concat_axis=0, tiled=True)
-    gm_heads = gm_heads.reshape(row_total, heads, HEAD_DIM).transpose(1, 0, 2)
-    dq, dk, dv = attend_back(heads, qkv, seq_begin, mixed_heads, lse, gm_heads)
-    gn, qg, gain_part = project_back(
-        heads, dq, dk, dv, whole_in, attn_gain_row, qkv_own, cosine, sines
-    )
-    gn_own = lax.psum_scatter(gn, "col", scatter_dimension=0, tiled=True).astype(F32)
-
-    grads = scatter_rows(g_parts, ranks)
-    og_rows = lax.psum_scatter(og, "row", scatter_dimension=0, tiled=True)
-    og_own = lax.psum_scatter(og_rows, "col", scatter_dimension=1, tiled=True)
-    qg_rows = lax.psum_scatter(qg, "row", scatter_dimension=0, tiled=True)
-    qg_all = lax.all_gather(qg_rows.reshape(depth, 3, width).transpose(1, 0, 2), "col", axis=1)
-    qg_all = qg_all.reshape(3 * cols, depth, width)
-    qg_own = lax.dynamic_slice_in_dim(qg_all, 3 * col_index, 3, 0)
-    qkv_grad = qg_own.transpose(1, 0, 2).reshape(depth, 3 * width).astype(F32)
-    small_all, gain_all = lax.psum((small, gain_part), ("row", "col"))
-
-    x = inputs.astype(F32)
-    scale = lax.rsqrt(jnp.mean(x * x, axis=1, keepdims=True) + EPS)
-    gained = gn_own * attn_gain_row
-    dots = jnp.sum(gained * x, axis=1, keepdims=True)
-    input_grad = resid + scale * gained - x * scale**3 * (dots / D)
+        gown,
+        sib,
+    )
+    input_grad, small_all, gain_all, qg, og_own, hin1 = finish_step(
+        cols,
+        ranks,
+        SENT_FIRST,
+        gm,
+        qkv,
+        seq_begin,
+        mixed_heads,
+        lse,
+        whole_in,
+        attn_gain_row,
+        qkv_own,
+        cosine,
+        sines,
+        small,
+        og,
+        resid,
+        inputs,
+        gown,
+        sib,
+    )
+    chip = row_index // 2
+    grads = lax.dynamic_index_in_dim(gown, chip, 2, keepdims=False).astype(F32)
+    grads = grads + lax.dynamic_index_in_dim(sib, chip, 2, keepdims=False).astype(F32)
+    hin = jnp.concatenate([hin0, hin1], axis=0)
+    grads = grads + jnp.sum(hin.astype(F32), axis=1)
+    depth = qkv_weight.shape[0]
     return (
         layer_out,
         input_grad,
         gain_all[0],
-        qkv_grad,
-        og_own.T.astype(F32),
+        qg.transpose(1, 0, 2).reshape(depth, 3 * width),
+        og_own.T,
         small_all[ROW_GAIN, :D],
         small_all[:ROUTES, :D].T,
-        small_all[:ROUTES, D : D + ROUTES].T,
+        small_all[:ROUTES, D : D + ROUTES],
         small_all[ROW_CONST:ROW_VEC, :D].reshape(2, 2, D).transpose(0, 2, 1),
         small_all[ROW_VEC:ROW_GAIN, :D],
-        grads[0],
-        grads[1],
-        grads[2].transpose(0, 2, 1),
+        grads[:, 0],
+        grads[:, 1],
+        grads[:, 2].transpose(0, 2, 1),
         prev_grad,
     )
 
 
 def solution(mesh):
     sizes = (mesh.shape["row"], mesh.shape["col"])
-    ranks, cols = sizes
-    per_heads = HEADS % cols == 0 and ranks == 8 and (HEADS // cols) * HEAD_DIM * 2 % LANES == 0
-    body = functools.partial(on_device_heads, sizes) if per_heads else on_device
+    body = functools.partial(on_device_heads, sizes) if sizes == (8, 4) else on_device
     placed = (
         P(("row", "col"), None),
         P(),

time: 805 us -> 635 us (0.79)
  waiting for transfers between devices: 432 us -> 210 us
  Pallas kernels: 142 us -> 302 us
  blocking collectives: 87.6 us -> 32.3 us
  other arithmetic: 39.8 us -> 19.9 us
  local copies, waits for them, and re-layouts: 60.7 us -> 41.3 us
  starting transfers between devices: 17.8 us -> 3.98 us
    pallas_call x4, Pallas kernels: 124 us -> 283 us  [the longest x1 91.8 us: finish_step(): pl.pallas_call(functools.partial(finish_kernel, cols, ranks, first, count...]
    reduce_scatter x5 -> x0, waiting for transfers between devices: 107 us -> none  [the longest x1 50.3 us: on_device_heads(): gtx_own = lax.psum_scatter(gtx, 'col', scatter_dimension=0, tiled=True)]
    all_gather x1, waiting for transfers between devices: 0.01 us -> 99.3 us  [on_device_heads(): w_all = lax.all_gather(w_stack, 'row', axis=0)]
    ppermute x14 -> x0, waiting for transfers between devices: 99 us -> none  [swap_rows(): return lax.ppermute(value, 'row', [(i, i ^ mask) for i in range(ranks)])]
    psum x1 -> x0, waiting for transfers between devices: 68.5 us -> none  [on_device_heads(): small_all, gain_all = lax.psum((small, gain_part), ('row', 'col'))]
    psum x1 -> x0, blocking collectives: 42.2 us -> none  [on_device_heads(): small_all, gain_all = lax.psum((small, gain_part), ('row', 'col'))]
    all_to_all x1, waiting for transfers between devices: 31 us -> 14.6 us  [on_device_heads(): lax.all_to_all(to_send, 'col', split_axis=0, concat_axis=0, tiled=True)]
    all_to_all x1 -> x0, waiting for transfers between devices: 15.7 us -> none  [on_device_heads(): lax.all_to_all(gm, 'col', split_axis=0, concat_axis=0, tiled=True)]
  transfers between devices with their start and end apart: 27 -> 5, of which waited for: 13 -> 5; matrix products, arithmetic and copies ran while one was open for 9% -> 4% of each run, Pallas kernels for 6% -> 0%
where the time goes in v2:
time: 635 us; the launch traced here: 624 us
  Pallas kernels  302 us (48%)
  waiting for transfers between devices  210 us (33%)
  local copies, waits for them, and re-layouts  41.3 us (7%)
  blocking collectives  32.3 us (5%)
  other arithmetic  19.9 us (3%)
  between operations  14.8 us (2%)
    all_gather x1, waiting for transfers between devices, on_device_heads(): w_all = lax.all_gather(w_stack, 'row', axis=0)  99.3 us
    pallas_call x1, Pallas kernels, finish_step(): pl.pallas_call(functools.partial(finish_kernel, cols, ranks, first, count...  91.8 us
    pallas_call x1, Pallas kernels, resid_step(): pl.pallas_call(functools.partial(resid_kernel, cols, count), out_shape=(j...  77.8 us
    pallas_call x1, Pallas kernels, experts_forward(): pl.pallas_call(functools.partial(experts_forward_kernel, cols, capacity),...  56.8 us
    pallas_call x1, Pallas kernels, experts_backward(): pl.pallas_call(functools.partial(experts_backward_kernel, cols, capacity)...  56.3 us
    all_gather x1, waiting for transfers between devices, on_device_heads(): whole_in = lax.all_gather(inputs, 'col', axis=0, tiled=True)  50.8 us
    all_gather x1, waiting for transfers between devices, on_device_heads(): n2_whole = lax.all_gather(n2, 'col', axis=0, tiled=True)  22.6 us
    all_gather x1, waiting for transfers between devices, on_device_heads(): lax.all_gather(jnp.concatenate([out_rows, w_own], axis=1), 'row', axis=0,...  21.8 us
  transfers between devices with their start and end apart: 5, of which 5 were waited for; matrix products, arithmetic and copies ran while one was open for 4% of the time, Pallas kernels for 0%

profile of v2, /device:TPU:0, one launch (start us, length us, event | category | flops | bytes accessed | tf_op | source)
XLA Modules:
  0.0 623.8 jit_solution(4908580229031062509)
XLA Ops:
  9.1 18.2 %all-gather = bf16[384,768]{1,0:T(8,128)(2,1)S(1)} all-gather(bf16[96,768]{1,0:T(8,128)(2,1)S(1)} %pad_maximum_fusion.2), channel_id=2, replica_groups=mesh['row'=8,'col'=4] {'col'}, dimensions={0}, use_global_device_ids=true | all-gather | bytes 737280 | tf_op jit(solution)/shard_map/all_gather | solution.py:1728
  36.1 1.1 reshape.248.valid_ref
  37.3 21.8 %all-gather.10.cloned.1.call-done = bf16[768,1344]{1,0:T(8,128)(2,1)} async-done(((bf16[96,1344]{1,0:T(8,128)(2,1)}), bf16[768,1344]{1,0:T(8,128)(2,1)}) %all-gather.10.cloned.1.call-update) | async-done | bytes 2064400 | tf_op jit(solution)/shard_map/all_gather | solution.py:1735
  59.1 1.3 slice.82.w_ref
  60.4 50.8 %all-gather.8.cloned.1.call-done.x_ref = bf16[1536,768]{1,0:T(8,128)(2,1)} async-done(((bf16[384,768]{1,0:T(8,128)(2,1)}), bf16[1536,768]{1,0:T(8,128)(2,1)}) %all-gather.8.cloned.1.call-update) | async-done | bytes 2359312 | tf_op jit(solution)/shard_map/all_gather | solution.py:1737
  111.2 1.7 copy-done.2
  112.9 5.0 project_heads.1.q_ref.k_ref.v_ref.qkv_ref
  117.9 1.7 copy-done
  119.7 12.2 %attend.1 = (bf16[3,1536,64]{2,1,0:T(8,128)(2,1)S(1)}, f32[3,1536,1]{2,1,0:T(8,128)S(1)}) custom-call(bf16[9,1536,64]{2,1,0:T(8,128)(2,1)} %copy-done, bf16[9,1536,64]{2,1,0:T(8,128)(2,1)} %copy-done, bf16[9,1536,64]{2,1,0:T(8,128)(2,1)} %copy-done, s32[1536,1]{1,0:T(8,128)S(1)} %copy-done.8, f32[1536,1]{1,0:T(8,128)S(1)} %copy-done.11), custom_call_target="tpu_custom_call" | custom-call | flops 3623878656 | bytes 8388608 | tf_op jit(solution)/shard_map/attend/pallas_call | solution.py:587
  132.9 1.4 copy-done.9
  134.3 1.6 copy.149
  136.9 3.6 all-to-all-start
  140.6 1.3 slice.83.w_ref.out_t_ref
  142.0 14.6 %all-to-all-done = bf16[4,384,192]{1,2,0:T(8,128)(2,1)S(1)} async-done(((bf16[4,384,192]{1,2,0:T(8,128)(2,1)}), bf16[4,384,192]{1,2,0:T(8,128)(2,1)S(1)}, u32[]{:S(2)}, u32[]{:S(2)}) %all-to-all-start) | async-done | bytes 589856 | tf_op jit(solution)/shard_map/all_to_all | solution.py:1742
  156.9 1.7 branch.1
  160.7 3.3 pad_maximum_fusion
  167.5 2.3 reduce-window.11
  171.6 14.1 %all-gather.1 = bf16[64,384]{1,0:T(8,128)(2,1)} all-gather(bf16[16,384]{1,0:T(8,128)(2,1)S(1)} %pad.8.prev_ref), channel_id=3, replica_groups=mesh['row'=8,'col'=4] {'col'}, dimensions={0}, use_global_device_ids=true | all-gather | bytes 61440 | tf_op jit(solution)/shard_map/all_gather | solution.py:1738
  188.2 22.6 %all-gather.12.cloned.1.call-done.n2_ref = bf16[1536,768]{1,0:T(8,128)(2,1)} async-done(((bf16[384,768]{1,0:T(8,128)(2,1)}), bf16[1536,768]{1,0:T(8,128)(2,1)}) %all-gather.12.cloned.1.call-update) | async-done | bytes 2359312 | tf_op jit(solution)/shard_map/all_gather | solution.py:1744
  210.8 99.3 %all-gather.14.cloned.1.call-done = bf16[24,8,96,512]{3,2,1,0:T(8,128)(2,1)} async-done(((bf16[3,8,96,512]{3,2,1,0:T(8,128)(2,1)}), bf16[24,8,96,512]{3,2,1,0:T(8,128)(2,1)}) %all-gather.14.cloned.1.call-update) | async-done | bytes 18874384 | tf_op jit(solution)/shard_map/all_gather | solution.py:1685
  310.0 56.8 %experts_forward.1 = (bf16[8,384,768]{2,1,0:T(8,128)(2,1)}, bf16[8,2,384,512]{3,2,1,0:T(8,128)(2,1)}, bf16[4,384,768]{2,1,0:T(8,128)(2,1)}, bf16[1536,256]{1,0:T(8,128)(2,1)}, bf16[4,384,768]{2,1,0:T(8,128)(2,1)}) custom-call(bf16[1536,768]{1,0:T(8,128)(2,1)} %all-gather.12.cloned.1.call-done.n2_ref, bf16[4,16,384]{2,1,0:T(8,128)(2,1)} %bitcast.87, ...), custom_call_target="tpu_custom_call" | custom-call | flops 24159191040 | bytes 41943040 | tf_op jit(solution)/shard_map/experts_forward/pallas_call | solution.py:907
  366.8 56.3 %experts_backward.1 = (bf16[4,384,768]{2,1,0:T(8,128)(2,1)}, f32[8,1536]{1,0:T(8,128)}, f32[384,768]{1,0:T(8,128)}, bf16[8,3,4,96,512]{4,3,2,1,0:T(8,128)(2,1)}, bf16[8,3,4,96,512]{4,3,2,1,0:T(8,128)(2,1)}) custom-call(bf16[1536,768]{1,0:T(8,128)(2,1)} %bitcast.96, bf16[4,384,768]{2,1,0:T(8,128)(2,1)} %get-tuple-element.45.mix_ref, ...), custom_call_target="tpu_custom_call" | custom-call | flops 28991029248 | bytes 62914560 | tf_op jit(solution)/shard_map/experts_backward/pallas_call | solution.py:1072
  423.2 77.8 %resid_step.1 = (bf16[384,768]{1,0:T(8,128)(2,1)}, f32[384,768]{1,0:T(8,128)}, bf16[4,576,128]{2,1,0:T(8,128)(2,1)}, bf16[768,768]{1,0:T(8,128)(2,1)}, f32[24,89...) custom-call(bf16[4,384,768]{2,1,0:T(8,128)(2,1)} %get-tuple-element.49.gt_ref, ...), custom_call_target="tpu_custom_call" | custom-call | flops 1358954496 | bytes 41943040 | tf_op jit(solution)/shard_map/resid_step/pallas_call | solution.py:1365
  501.0 91.8 %finish_step.1 = (f32[384,768]{1,0:T(8,128)}, f32[24,896]{1,0:T(8,128)}, f32[8,768]{1,0:T(8,128)}, f32[3,96,192]{2,1,0:T(8,128)}, f32[96,192]{1,0:T(8,128)}, /*index=5*/bf16[3,3,3,96,512]{4,3,2,1,0:T(8,128)(2,1)}) custom-call(bf16[4,576,128]{2,1,0:T(8,128)(2,1)} %get-tuple-element.57.gm_ref, bf16[9,1536,64]{2,1,0:T(8,128)(2,1)} %copy-done, ...), custom_call_target="tpu_custom_call" | custom-call | flops 9059696640 | bytes 41943040 | tf_op jit(solution)/shard_map/finish_step/pallas_call | solution.py:1603
  592.9 1.3 slice.76
  594.2 1.3 slice.74
  596.2 1.4 slice_bitcast_fusion.4
  597.6 1.4 slice_reduce_fusion.1
  599.6 1.6 copy.166
  603.2 5.2 convert_reduce_fusion
  608.4 3.6 bitcast_add_fusion
  612.0 2.4 slice_bitcast_fusion
  (127 shorter events, 28.5 us)
Async XLA Ops:
  7.2 51.9 %all-gather.10.cloned.1.call-start = ((), (), s32[]{:S(2)}) async-start(), calls=%async_computation.2 | async-start | bytes 2433024 | tf_op jit(solution)/shard_map/all_gather | solution.py:1735
  27.6 2.6 copy-start.28
  27.6 3.3 copy-start.26
  29.4 81.8 %all-gather.8.cloned.1.call-start = ((), (), s32[]{:S(2)}) async-start(), calls=%async_computation.1 | async-start | bytes 2949120 | tf_op jit(solution)/shard_map/all_gather | solution.py:1737
  30.9 80.3 %copy-start.13 = (f32[1,768]{1,0:T(1,128)}, f32[1,768]{1,0:T(1,128)S(1)}, u32[]{:S(2)}) copy-start(f32[1,768]{1,0:T(1,128)S(1)} %reshape.242.gain_ref) | copy-start | bytes 9220
  34.6 76.6 %copy-start.4 = (f32[1536,128]{1,0:T(8,128)}, f32[1536,128]{1,0:T(8,128)S(1)}, u32[]{:S(2)}) copy-start(f32[1536,128]{1,0:T(8,128)S(1)} %copy.146.sin_ref) | copy-start | bytes 2359300
  35.0 82.9 %copy-start.5 = (f32[1536,128]{1,0:T(8,128)}, f32[1536,128]{1,0:T(8,128)S(1)}, u32[]{:S(2)}) copy-start(f32[1536,128]{1,0:T(8,128)S(1)} %copy.145.cos_ref) | copy-start | bytes 2359300
  60.4 57.5 %copy-start.3 = (bf16[768,576]{1,0:T(8,128)(2,1)}, bf16[768,576]{1,0:T(8,128)(2,1)S(1)}, u32[]{:S(2)}) copy-start(bf16[768,576]{1,0:T(8,128)(2,1)S(1)} %slice.82.w_ref) | copy-start | bytes 2654212
  111.2 1.7 copy-start.2
  112.9 6.8 %copy-start.8 = (s32[1536,1]{1,0:T(8,128)S(1)}, s32[1536,1]{1,0:T(8,128)}, u32[]{:S(2)}) copy-start(s32[1536,1]{1,0:T(8,128)} %select_n.51.begin_ref) | copy-start | bytes 18436
  112.9 6.8 %copy-start.11 = (f32[1536,1]{1,0:T(8,128)S(1)}, f32[1536,1]{1,0:T(8,128)}, u32[]{:S(2)}) copy-start(f32[1536,1]{1,0:T(8,128)} %reshape.248.valid_ref) | copy-start | bytes 18436
  117.9 1.7 copy-start
  131.9 1.0 copy-start.7
  132.9 1.4 copy-start.9
  134.3 6.3 %copy-start.27 = (bf16[768]{0:T(1024)(128)(2,1)S(1)}, bf16[768]{0:T(1024)(128)(2,1)}, u32[]{:S(2)}) copy-start(bf16[768]{0:T(1024)(128)(2,1)} %param.20) | copy-start | bytes 4612
  136.9 20.0 %copy-start.6 = (bf16[384,768]{1,0:T(8,128)(2,1)S(1)}, bf16[384,768]{1,0:T(8,128)(2,1)}, u32[]{:S(2)}) copy-start(bf16[384,768]{1,0:T(8,128)(2,1)} %xown_ref.1) | copy-start | bytes 1769476
  136.9 19.7 %all-to-all-start = ((bf16[4,384,192]{1,2,0:T(8,128)(2,1)}), bf16[4,384,192]{1,2,0:T(8,128)(2,1)S(1)}, u32[]{:S(2)}, u32[]{:S(2)}) async-start(bf16[4,384,192]{1,2,0:T(8,128)(2,1)} %copy.150), calls=%async_computation | async-start | bytes 1179648 | tf_op jit(solution)/shard_map/all_to_all | solution.py:1742
  140.5 70.3 %all-gather.12.cloned.1.call-start = ((), (), s32[]{:S(2)}) async-start(), calls=%async_computation.3 | async-start | bytes 2949120 | tf_op jit(solution)/shard_map/all_gather | solution.py:1744
  140.6 18.0 %copy-start.14 = (f32[1,768]{1,0:T(1,128)}, f32[1,768]{1,0:T(1,128)S(1)}, u32[]{:S(2)}) copy-start(f32[1,768]{1,0:T(1,128)S(1)} %reshape.244.gain_ref) | copy-start | bytes 9220
  141.9 22.0 %copy-start.1 = (bf16[768,768]{1,0:T(8,128)(2,1)}, bf16[768,768]{1,0:T(8,128)(2,1)S(1)}, u32[]{:S(2)}) copy-start(bf16[768,768]{1,0:T(8,128)(2,1)S(1)} %slice.83.w_ref.out_t_ref) | copy-start | bytes 3538948
  158.6 1.0 copy-start.10
  159.6 0.8 copy-start.12
  160.4 149.6 %all-gather.14.cloned.1.call-start = ((), (), s32[]{:S(2)}) async-start(), calls=%async_computation.4 | async-start | bytes 21233664 | tf_op jit(solution)/shard_map/all_gather | solution.py:1685
  164.0 1.4 copy-start.22
  164.0 1.4 copy-start.19
  165.4 6.3 %copy-start.18 = (bf16[16,384]{1,0:T(8,128)(2,1)}, bf16[16,384]{1,0:T(8,128)(2,1)S(1)}, u32[]{:S(2)}) copy-start(bf16[16,384]{1,0:T(8,128)(2,1)S(1)} %pad.8.prev_ref) | copy-start | bytes 36868
  165.7 20.0 %copy-start.15 = (s32[1536,2]{1,0:T(8,128)}, s32[1536,2]{1,0:T(8,128)S(1)}, u32[]{:S(2)}) copy-start(s32[1536,2]{1,0:T(8,128)S(1)} %copy.156.routes_ref) | copy-start | bytes 36868
  169.7 16.6 %copy-start.20 = (bf16[768,12]{0,1:T(8,128)(2,1)S(1)}, bf16[768,12]{0,1:T(8,128)(2,1)}, u32[]{:S(2)}) copy-start(bf16[768,12]{0,1:T(8,128)(2,1)} %param.21) | copy-start | bytes 55300
  169.7 16.6 %copy-start.25 = (bf16[2,768]{1,0:T(2,128)(2,1)S(1)}, bf16[2,768]{1,0:T(2,128)(2,1)}, u32[]{:S(2)}) copy-start(bf16[2,768]{1,0:T(2,128)(2,1)} %param.24) | copy-start | bytes 9220
  612.0 2.4 copy-start.17
  612.0 3.2 copy-start.16
  614.4 1.8 copy-start.21
  (2 other events, 1.5 us)
Sparse Core Ops, SparseCore 0:
  29.5 29.5 all-gather.9
  60.7 50.4 all-gather.7
  160.5 50.1 all-gather.11
  212.5 97.4 all-gather.13

commit v3 on v2

--- a/solution.py
+++ b/solution.py
@@ -3,6 +3,7 @@
 
 import jax
 import jax.numpy as jnp
+import numpy as np
 from jax import lax
 from jax.experimental import pallas as pl
 from jax.experimental.pallas import tpu as pltpu
@@ -518,124 +519,15 @@
     return lax.rsqrt(jnp.mean(x * x, axis=1, keepdims=True) + EPS)
 
 
-def qkv_kernel(heads, x_ref, gain_ref, w_ref, cos_ref, sin_ref, out_ref):
-    x = x_ref[...].astype(F32)
-    normed = (x * norm_rows(x) * gain_ref[...]).astype(BF)
-    proj = mm(normed, w_ref[...])
-    cosine, sines = cos_ref[...], sin_ref[...]
-    width = heads * HEAD_DIM
-    for part in range(2 * width // LANES):
-        v = proj[:, part * LANES : (part + 1) * LANES]
-        t = v * cosine + swap_pairs(v) * sines
-        for half in range(2):
-            head = 2 * part + half
-            piece = t[:, half * HEAD_DIM : (half + 1) * HEAD_DIM].astype(BF)
-            if head < heads:
-                piece = piece * jnp.asarray(1.0 / math.sqrt(HEAD_DIM), BF)
-            out_ref[head] = piece
-    for head in range(2 * heads, 3 * heads):
-        out_ref[head] = proj[:, head * HEAD_DIM : (head + 1) * HEAD_DIM].astype(BF)
-
-
-def project_heads(heads, whole_in, gain, weight, cosine, sines):
-    rows = whole_in.shape[0]
-    blk = 256
-    return pl.pallas_call(
-        functools.partial(qkv_kernel, heads),
-        grid=(rows // blk,),
-        out_shape=jax.ShapeDtypeStruct((3 * heads, rows, HEAD_DIM), BF),
-        in_specs=[
-            pl.BlockSpec((blk, D), lambda i: (i, 0)),
-            whole((1, D)),
-            whole((D, 3 * heads * HEAD_DIM)),
-            pl.BlockSpec((blk, LANES), lambda i: (i, 0)),
-            pl.BlockSpec((blk, LANES), lambda i: (i, 0)),
-        ],
-        out_specs=pl.BlockSpec((3 * heads, blk, HEAD_DIM), lambda i: (0, i, 0)),
-        compiler_params=pltpu.CompilerParams(vmem_limit_bytes=32 * MIB),
-        cost_estimate=pl.CostEstimate(
-            flops=2 * rows * D * 3 * heads * HEAD_DIM, bytes_accessed=8 * MIB, transcendentals=0
-        ),
-        name="project_heads",
-    )(whole_in, gain, weight, cosine, sines)
-
-
 def seen(begin, first, rows, length):
     u = lax.broadcasted_iota(jnp.int32, (rows, length), 1)
     t = lax.broadcasted_iota(jnp.int32, (rows, length), 0) + first
     return (u >= begin) & (u <= t)
 
 
-def attend_kernel(q_ref, k_ref, v_ref, begin_ref, valid_ref, o_ref, lse_ref):
-    rows = q_ref.shape[1]
-    for i in range(rows // Q_ROWS):
-        at = slice(i * Q_ROWS, (i + 1) * Q_ROWS)
-        length = (i + 1) * Q_ROWS
-        s = mm(q_ref[0, at], k_ref[0, :length], NT)
-        s = jnp.where(seen(begin_ref[at], i * Q_ROWS, Q_ROWS, length), s, NEG)
-        top = jnp.max(s, axis=1, keepdims=True)
-        p = jnp.exp(s - top)
-        total = jnp.sum(p, axis=1, keepdims=True)
-        o = mm(p.astype(BF), v_ref[0, :length]) * (valid_ref[at] / total)
-        o_ref[0, at] = o.astype(BF)
-        lse_ref[0, at] = top + jnp.log(total)
-
-
-def attend(heads, qkv, begin, valid):
-    rows = qkv.shape[1]
-    head_block = (1, rows, HEAD_DIM)
-    return pl.pallas_call(
-        attend_kernel,
-        grid=(heads,),
-        out_shape=(
-            jax.ShapeDtypeStruct((heads, rows, HEAD_DIM), BF),
-            jax.ShapeDtypeStruct((heads, rows, 1), F32),
-        ),
-        in_specs=[
-            pl.BlockSpec(head_block, lambda h: (h, 0, 0)),
-            pl.BlockSpec(head_block, lambda h: (h + heads, 0, 0)),
-            pl.BlockSpec(head_block, lambda h: (h + 2 * heads, 0, 0)),
-            whole((rows, 1)),
-            whole((rows, 1)),
-        ],
-        out_specs=(
-            pl.BlockSpec(head_block, lambda h: (h, 0, 0)),
-            pl.BlockSpec((1, rows, 1), lambda h: (h, 0, 0)),
-        ),
-        compiler_params=pltpu.CompilerParams(vmem_limit_bytes=48 * MIB),
-        cost_estimate=pl.CostEstimate(
-            flops=8 * heads * rows * rows * HEAD_DIM, bytes_accessed=8 * MIB, transcendentals=heads * rows * rows
-        ),
-        name="attend",
-    )(qkv, qkv, qkv, begin, valid)
-
-
-def branch_kernel(a_ref, w_ref, x_ref, gain_ref, mixed_ref, middle_ref, normed_ref):
-    mixed = jnp.concatenate([a_ref[i] for i in range(a_ref.shape[0])], axis=1)
-    mixed_ref[...] = mixed
-    middle = x_ref[...].astype(F32) + mm(mixed, w_ref[...], NT)
-    middle_ref[...] = middle
-    normed_ref[...] = (middle * norm_rows(middle) * gain_ref[...]).astype(BF)
-
-
-def branch(attn_parts, out_t, inputs, gain):
-    rows = inputs.shape[0]
-    return pl.pallas_call(
-        branch_kernel,
-        out_shape=(
-            jax.ShapeDtypeStruct((rows, D), BF),
-            jax.ShapeDtypeStruct((rows, D), F32),
-            jax.ShapeDtypeStruct((rows, D), BF),
-        ),
-        compiler_params=pltpu.CompilerParams(vmem_limit_bytes=32 * MIB),
-        cost_estimate=pl.CostEstimate(flops=2 * rows * D * D, bytes_accessed=6 * MIB, transcendentals=0),
-        name="branch",
-    )(attn_parts, out_t, inputs, gain)
-
-
-def gate_lanes(logits, routes):
+def gate_lanes(logits, meta):
     lane = lane_iota(logits.shape)
-    hit = (lane == routes[:, 0:1]) | (lane == routes[:, 1:2])
+    hit = (pltpu.roll(meta, LANES - META_HIT, 1) > 0.0) & (lane < ROUTES)
     held = jnp.where(hit, logits, NEG)
     e = jnp.where(hit, jnp.exp(held - jnp.max(held, axis=1, keepdims=True)), 0.0)
     return e / jnp.sum(e, axis=1, keepdims=True)
@@ -809,13 +701,15 @@
     ]
 
 
-def slot_rows(tsr_ref, capacity):
-    rows = tsr_ref.shape[2]
-    return jnp.where(lax.broadcasted_iota(jnp.int32, (capacity, rows), 0) == tsr_ref[0], 1.0, 0.0).astype(BF)
-
-
-def slot_column(tsc_ref, e):
-    return jnp.sum(jnp.where(lane_iota(tsc_ref.shape) == e, tsc_ref[...], 0), axis=1, keepdims=True)
+def slot_rows(tsr_ref, e, capacity):
+    rows = tsr_ref.shape[1]
+    spots = lax.broadcasted_iota(jnp.int32, (capacity, rows), 0)
+    return jnp.where(spots == tsr_ref[pl.ds(e, 1)], 1.0, 0.0).astype(BF)
+
+
+def slot_column(meta_ref, e):
+    picked = jnp.where(lane_iota(meta_ref.shape) == e, meta_ref[...], 0.0)
+    return jnp.sum(picked, axis=1, keepdims=True).astype(jnp.int32)
 
 
 def full_weight(w_ref, t):
@@ -834,9 +728,8 @@
     cot_ref,
     rw_ref,
     carry_ref,
-    routes_ref,
     tsr_ref,
-    tsc_ref,
+    meta_ref,
     w_ref,
     x_ref,
     gu_ref,
@@ -862,7 +755,7 @@
         own_copy.start()
         step(0)
         prev = jnp.concatenate([mm(prev_ref[i], carry_ref[...], TN) for i in range(cols)], axis=0)
-        g = gate_lanes(mm(n2_ref[...], rw_ref[...], NT) + prev, routes_ref[...])
+        g = gate_lanes(mm(n2_ref[...], rw_ref[...], NT) + prev, meta_ref[...])
         high = g.astype(BF)
         gates_ref[:, :LANES] = high
         gates_ref[:, LANES:] = (g - high.astype(F32)).astype(BF)
@@ -872,7 +765,7 @@
     def _():
         step(1)
 
-    one = slot_rows(tsr_ref, capacity)
+    one = slot_rows(tsr_ref, e, capacity)
     x = mm(one, n2_ref[...]).astype(BF)
     x_ref[0] = x
     sg = mm(one, gates_ref[...])
@@ -883,7 +776,7 @@
     gu_ref[0, 1] = u.astype(BF)
     gh = (g * jax.nn.sigmoid(g) * u * sg).astype(BF)
     y = mm(gh, full_weight(w_ref, 2), NT).astype(BF)
-    tsc = slot_column(tsc_ref, e)
+    tsc = slot_column(meta_ref, e)
     for b in range(rows // COMBINE):
         rs = slice(b * COMBINE, (b + 1) * COMBINE)
         one_t = jnp.where(lane_iota((COMBINE, capacity)) == tsc[rs], 1.0, 0.0).astype(BF)
@@ -899,7 +792,7 @@
         own_copy.wait()
 
 
-def experts_forward(cols, n2, prev, cot, rw, carry, routes, slots, slots_t, w_all):
+def experts_forward(cols, n2, prev, cot, rw, carry, meta, slots, w_all):
     rows = n2.shape[0]
     capacity = rows // 4
     ranks, three, experts, depth, ff = w_all.shape
@@ -920,9 +813,8 @@
             whole((local, D)),
             whole((LANES, D)),
             whole((16, LANES)),
-            whole((rows, 2)),
-            pl.BlockSpec((1, 1, rows), lambda e: (e, 0, 0)),
-            whole((rows, experts)),
+            whole((experts, rows)),
+            whole((rows, LANES)),
             pl.BlockSpec((ranks, three, 1, depth, ff), lambda e: (0, 0, e, 0, 0)),
         ],
         out_specs=(
@@ -947,7 +839,7 @@
             transcendentals=experts * capacity * ff,
         ),
         name="experts_forward",
-    )(n2, prev, cot, rw, carry, routes, slots_t, slots, w_all)
+    )(n2, prev, cot, rw, carry, slots, meta, w_all)
 
 
 def experts_backward_kernel(
@@ -957,7 +849,7 @@
     mix_ref,
     gates_ref,
     tsr_ref,
-    tsc_ref,
+    meta_ref,
     w_ref,
     x_ref,
     gu_ref,
@@ -1011,7 +903,7 @@
     def _():
         slot(2)
 
-    one = slot_rows(tsr_ref, capacity)
+    one = slot_rows(tsr_ref, e, capacity)
     ct = mm(one, cot_ref[...]).astype(BF)
     sg = mm(one, gates_ref[...])
     sg = jnp.sum(jnp.where(lane_iota(sg.shape) % LANES == e, sg, 0.0), axis=1, keepdims=True)
@@ -1029,7 +921,7 @@
     dg = (gv * u * (sig * (1.0 + g * (1.0 - sig)))).astype(BF)
     du = (gv * act).astype(BF)
     dx = (mm(dg, wg, NT) + mm(du, wu, NT)).astype(BF)
-    tsc = slot_column(tsc_ref, e)
+    tsc = slot_column(meta_ref, e)
     for b in range(rows // COMBINE):
         rs = slice(b * COMBINE, (b + 1) * COMBINE)
         one_t = jnp.where(lane_iota((COMBINE, capacity)) == tsc[rs], 1.0, 0.0).astype(BF)
@@ -1062,7 +954,7 @@
             sib_copy(i, i % 2).wait_recv()
 
 
-def experts_backward(cols, cot, mix, gates, slots, slots_t, w_all, x, gu):
+def experts_backward(cols, cot, mix, gates, meta, slots, w_all, x, gu):
     rows = cot.shape[0]
     capacity = rows // 4
     ranks, three, experts, depth, ff = w_all.shape
@@ -1083,8 +975,8 @@
             whole((rows, D)),
             whole((cols, local, D)),
             whole((rows, 2 * LANES)),
-            pl.BlockSpec((1, 1, rows), lambda e: (e, 0, 0)),
-            whole((rows, experts)),
+            whole((experts, rows)),
+            whole((rows, LANES)),
             pl.BlockSpec((ranks, three, 1, depth, ff), lambda e: (0, 0, e, 0, 0)),
             pl.BlockSpec((1, capacity, D), lambda e: (e, 0, 0)),
             pl.BlockSpec((1, 2, capacity, ff), lambda e: (e, 0, 0, 0)),
@@ -1113,7 +1005,7 @@
             transcendentals=experts * capacity * ff,
         ),
         name="experts_backward",
-    )(cot, mix, gates, slots_t, slots, w_all, x, gu)
+    )(cot, mix, gates, slots, meta, w_all, x, gu)
 
 
 def pack_heads(dst, value):
@@ -1230,14 +1122,13 @@
     n2_ref,
     middle_ref,
     cot_ref,
-    routes_ref,
+    meta_ref,
     prev_ref,
     rw_ref,
     carry_ref,
     gain_ref,
     out_t_ref,
     mixed_ref,
-    valid_ref,
     gown_ref,
     sib_ref,
     layer_ref,
@@ -1277,13 +1168,14 @@
     finish = send_weight_grads(0, count, gown_ref, sib_ref, hin_ref, *weight_refs)
     slot(1)
 
+    meta = meta_ref[pl.ds(pl.multiple_of(c * local, LANES), local)]
     n2, cot = n2_ref[...], cot_ref[...]
     n2f, cotf = n2.astype(F32), cot.astype(F32)
     middle = middle_ref[...]
     rw = rw_ref[...]
     lin = mm(n2, rw, NT)
     prev = prev_ref[...]
-    gates = gate_lanes(lin + mm(prev, carry_ref[...], TN), routes_ref[...])
+    gates = gate_lanes(lin + mm(prev, carry_ref[...], TN), meta)
     lane = lane_iota((local, LANES))
     cot_lin = mm(cot, rw, NT)
     dot_keep = jnp.sum(cotf * n2f, axis=1, keepdims=True)
@@ -1340,7 +1232,7 @@
     resid = cotf + scale * gained - middle * (scale * scale * scale * (mid_dot * (1.0 / D)))
     resid_ref[...] = resid
     cut = resid.astype(BF)
-    gm = (mm(cut, out_t_ref[...]) * valid_ref[...]).astype(BF)
+    gm = (mm(cut, out_t_ref[...]) * meta[:, META_VALID : META_VALID + 1]).astype(BF)
     width = D // cols
     for i in range(cols):
         pack_heads(gm_out.at[i], gm[:, i * width : (i + 1) * width])
@@ -1358,7 +1250,7 @@
     finish()
 
 
-def resid_step(cols, count, gt, dots, mixsum, n2, middle, cot, routes, prev, rw, carry, gain, out_t, mixed, valid, gown, sib):
+def resid_step(cols, count, gt, dots, mixsum, n2, middle, cot, meta, prev, rw, carry, gain, out_t, mixed, gown, sib):
     local = n2.shape[0]
     experts, three, chips, depth, ff = gown.shape
     vm = pl.BlockSpec(memory_space=pltpu.VMEM)
@@ -1373,7 +1265,7 @@
             jax.ShapeDtypeStruct((ROUTES, local), F32),
             jax.ShapeDtypeStruct((count, 3, three, depth, ff), BF),
         ),
-        in_specs=[vm] * 14 + [ANY, ANY],
+        in_specs=[vm] * 13 + [ANY, ANY],
         out_specs=(vm, vm, ANY, vm, vm, vm, ANY),
         scratch_shapes=[
             *chain_scratch(cols, local),
@@ -1392,7 +1284,7 @@
         ),
         cost_estimate=pl.CostEstimate(flops=6 * local * D * D, bytes_accessed=40 * MIB, transcendentals=0),
         name="resid_step",
-    )(gt, dots, mixsum, n2, middle, cot, routes, prev, rw, carry, gain, out_t, mixed, valid, gown, sib)
+    )(gt, dots, mixsum, n2, middle, cot, meta, prev, rw, carry, gain, out_t, mixed, gown, sib)
 
 
 def finish_kernel(
@@ -1402,7 +1294,7 @@
     count,
     gm_ref,
     qkv_ref,
-    begin_ref,
+    meta_ref,
     o_ref,
     lse_ref,
     x_ref,
@@ -1485,7 +1377,7 @@
             k, v = qkv_ref[heads + h, :length], qkv_ref[2 * heads + h, :length]
             delta = jnp.sum(do.astype(F32) * o_ref[h, at].astype(F32), axis=1, keepdims=True)
             s = mm(q, k, NT)
-            ok = seen(begin_ref[at], i * Q_ROWS, Q_ROWS, length)
+            ok = seen(column(meta_ref, at, META_BEGIN).astype(jnp.int32), i * Q_ROWS, Q_ROWS, length)
             p = jnp.where(ok, jnp.exp(s - lse_ref[h, at]), 0.0)
             ds = (p * (mm(do, v, NT) - delta)).astype(BF)
             dq_s[h, at] = mm(ds, k) * score_scale
@@ -1592,7 +1484,7 @@
     finish()
 
 
-def finish_step(cols, ranks, first, gm, qkv, begin, o, lse, x, gain, w, cosine, sines, small, og, resid, xown, gown, sib):
+def finish_step(cols, ranks, first, gm, qkv, meta, o, lse, x, gain, w, cosine, sines, small, og, resid, xown, gown, sib):
     rows = x.shape[0]
     local = rows // cols
     experts, three, chips, depth, ff = gown.shape
@@ -1645,7 +1537,382 @@
             flops=20 * heads * rows * rows * HEAD_DIM, bytes_accessed=40 * MIB, transcendentals=heads * rows * rows
         ),
         name="finish_step",
-    )(gm, qkv, begin, o, lse, x, gain, w, cosine, sines, small, og, resid, xown, gown, sib)
+    )(gm, qkv, meta, o, lse, x, gain, w, cosine, sines, small, og, resid, xown, gown, sib)
+
+
+META_HIT, META_BEGIN, META_VALID = 8, 20, 21
+
+
+def column(ref, at, lane):
+    return ref[at, lane : lane + 1]
+
+
+def tokens_meta(routes_ref, lengths_ref, rows, experts):
+    kinds = lax.broadcasted_iota(jnp.int32, (16, rows), 0)
+    hits = jnp.where((kinds == routes_ref[0:1]) | (kinds == routes_ref[1:2]), 1.0, 0.0)
+    step = 256
+    earlier = lax.broadcasted_iota(jnp.int32, (step, step), 0) < lax.broadcasted_iota(
+        jnp.int32, (step, step), 1
+    )
+    earlier = jnp.where(earlier, 1.0, 0.0).astype(BF)
+    counts, running = [], jnp.zeros((16, 1), F32)
+    for b in range(rows // step):
+        block = hits[:, b * step : (b + 1) * step]
+        counts.append(mm(block.astype(BF), earlier) + running)
+        running = running + jnp.sum(block, axis=1, keepdims=True)
+    slots = jnp.where(hits > 0.0, jnp.concatenate(counts, axis=1), -1.0)[:experts]
+    spot = lax.broadcasted_iota(jnp.int32, (8, rows), 1)
+    begin, end = jnp.zeros((8, rows), F32), 0
+    for i in range(lengths_ref.shape[1]):
+        end = end + lengths_ref[0, i]
+        begin = jnp.where(spot >= end, end.astype(F32), begin)
+    valid = jnp.where(spot < end, 1.0, 0.0)
+    tail = jnp.where(lax.broadcasted_iota(jnp.int32, (8, rows), 0) == 0, begin, valid)
+    spare = jnp.zeros((LANES - experts - 12 - 8, rows), F32)
+    meta = jnp.concatenate([slots, hits[:12], tail, spare], axis=0).T
+    return slots.astype(jnp.int32), meta
+
+
+def first_kernel(
+    cols,
+    ranks,
+    x_ref,
+    again_ref,
+    fgain_ref,
+    wq_ref,
+    wo_ref,
+    prev_ref,
+    routes_ref,
+    lengths_ref,
+    cos_ref,
+    sin_ref,
+    freq_ref,
+    gate_ref,
+    up_ref,
+    down_ref,
+    wall_ref,
+    qkv_ref,
+    o_ref,
+    lse_ref,
+    xw_ref,
+    wq_out,
+    wo_out,
+    cos_out,
+    sin_out,
+    meta_ref,
+    slots_ref,
+    mixed_ref,
+    middle_ref,
+    n2_ref,
+    n2w_ref,
+    prevw_ref,
+    xw,
+    q_parts,
+    q_land,
+    o_parts,
+    o_land,
+    wq,
+    wo,
+    a_out,
+    a_in,
+    prevw,
+    local_sem,
+    x_send,
+    x_recv,
+    n_send,
+    n_recv,
+    q_send,
+    q_recv,
+    c_send,
+    c_recv,
+    r_send,
+    r_recv,
+    e_send,
+    e_recv,
+    s_send,
+    s_recv,
+):
+    r, c = place()
+    heads = 3
+    local = x_ref.shape[0]
+    rows = local * cols
+    width = heads * HEAD_DIM
+    depth = D // ranks
+    odd, high = c % 2, c // 2
+    greet(col_peers(cols) + [(flip(r, m), c) for m in range(1, ranks)])
+
+    for s in range(3):
+        q_parts[s] = wq_ref[:, s * width : (s + 1) * width]
+    q_copies = [
+        send_to(q_parts.at[1], q_land.at[(c + 1) // 2], q_send.at[0], q_recv.at[0], (r, flip(c, 1))),
+        send_to(q_parts.at[2 - 2 * odd], q_land.at[2 * high], q_send.at[1], q_recv.at[1], (r, flip(c, 2))),
+    ]
+    for copy in q_copies:
+        copy.start()
+    o_parts[...] = wo_ref[...]
+    o_copies = to_cols(lambda d: o_parts, o_land, c_send.at[0], c_recv.at[0], cols)
+    prev_copies = to_cols(lambda d: prev_ref, prevw, c_send.at[1], c_recv.at[1], cols)
+    x_step, x_drain = gather_chain(x_ref, xw, x_send, x_recv, cols)
+    x_step(0)
+    for copy in o_copies + prev_copies:
+        copy.start()
+    q_land[(c + 1) // 2] = q_parts[2 * odd]
+    o_land[c] = wo_ref[...]
+    prevw[c] = prev_ref[...]
+    xw[c] = x_ref[...]
+
+    def rows_of(ref, d):
+        return ref.at[pl.ds(pl.multiple_of(d * depth, 16), depth)]
+
+    def push_rows(ref, at):
+        copies = []
+        for m in range(1, ranks):
+            there = flip(r, m)
+            copies.append(
+                send_to(rows_of(ref, r), rows_of(ref, r), r_send.at[at, m - 1], r_recv.at[at, m - 1], (there, c))
+            )
+        return copies
+
+    for copy in q_copies:
+        copy.wait()
+    rows_of(wq, r)[...] = jnp.concatenate([q_land[i] for i in range(3)], axis=1)
+    wq_copies = push_rows(wq, 0)
+    for copy in wq_copies:
+        copy.start()
+    for copy in o_copies:
+        copy.wait()
+    rows_of(wo, r)[...] = jnp.concatenate([o_land[i] for i in range(cols)], axis=1)
+    wo_copies = push_rows(wo, 1)
+    for copy in wo_copies:
+        copy.start()
+
+    weights = (gate_ref, up_ref, down_ref)
+    kept = [pltpu.make_async_copy(ref, wall_ref.at[r, t], local_sem.at[t]) for t, ref in enumerate(weights)]
+    chip_copies = [
+        [
+            send_to(ref, wall_ref.at[r, t], e_send.at[t, k - 1], e_recv.at[t, k - 1], (flip(r, 2 * k), c))
+            for k in range(1, 4)
+        ]
+        for t, ref in enumerate(weights)
+    ]
+    for copies in chip_copies:
+        for copy in copies:
+            copy.start()
+    for copy in kept:
+        copy.start()
+
+    def pass_on(t):
+        copies = []
+        for k in range(4):
+            there = flip(r, 2 * k)
+            src = weights[t] if k == 0 else wall_ref.at[there, t]
+            copies.append(send_to(src, wall_ref.at[there, t], s_send.at[t, k], s_recv.at[t, k], (flip(r, 1), c)))
+        return copies
+
+    def forward(t):
+        for k, copy in enumerate(pass_on(t)):
+            if k:
+                chip_copies[t][k - 1].wait_recv()
+            copy.start()
+
+    slots, meta = tokens_meta(routes_ref, lengths_ref, rows, EXPERTS)
+    slots_ref[...] = slots
+    meta_ref[...] = meta
+    sub = lax.broadcasted_iota(jnp.int32, (8, LANES), 0)
+    firsts, end, ends = jnp.zeros((8, LANES), F32), 0, []
+    for i in range(lengths_ref.shape[1]):
+        firsts = jnp.where(sub == i, jnp.asarray(end, jnp.int32).astype(F32), firsts)
+        end = end + lengths_ref[0, i]
+        ends.append(end)
+    angle = firsts * freq_ref[...]
+    cos_first, sin_first = jnp.cos(angle), jnp.sin(angle)
+    spot = lax.broadcasted_iota(jnp.int32, (rows, LANES), 0)
+    cb, sb = jnp.ones((rows, LANES), F32), jnp.zeros((rows, LANES), F32)
+    for i in range(1, len(ends)):
+        cb = jnp.where(spot >= ends[i - 1], cos_first[i : i + 1], cb)
+        sb = jnp.where(spot >= ends[i - 1], sin_first[i : i + 1], sb)
+    cb, sb = jnp.where(spot >= end, 1.0, cb), jnp.where(spot >= end, 0.0, sb)
+    sign = jnp.where(lane_iota((rows, LANES)) % 2 == 0, -1.0, 1.0)
+    cos_out[...] = cos_ref[...] * cb + sin_ref[...] * sb
+    sin_out[...] = (sin_ref[...] * cb - cos_ref[...] * sb) * sign
+
+    def project(d):
+        at = pl.ds(pl.multiple_of(d * local, LANES), local)
+        x = xw[d].astype(F32)
+        normed = (x * norm_rows(x) * again_ref[...]).astype(BF)
+        proj = mm(normed, wq[...])
+        cosine, sines = cos_out[at], sin_out[at]
+        for part in range(2 * width // LANES):
+            v = proj[:, part * LANES : (part + 1) * LANES]
+            t = v * cosine + swap_pairs(v) * sines
+            for half in range(2):
+                head = 2 * part + half
+                piece = t[:, half * HEAD_DIM : (half + 1) * HEAD_DIM].astype(BF)
+                if head < heads:
+                    piece = piece * jnp.asarray(1.0 / math.sqrt(HEAD_DIM), BF)
+                qkv_ref[head, at] = piece
+        for head in range(2 * heads, 3 * heads):
+            qkv_ref[head, at] = proj[:, head * HEAD_DIM : (head + 1) * HEAD_DIM].astype(BF)
+
+    x_step(1)
+    for copy in wq_copies:
+        copy.wait()
+    for k in range(cols):
+        if k > 1:
+            x_step(k)
+
+        def side(way, carry, k=k):
+            d = c + k * (2 * way - 1)
+
+            @pl.when((d >= 0) & (d < cols))
+            def _():
+                project(jnp.clip(d, 0, cols - 1))
+
+            return carry
+
+        lax.fori_loop(0, 2 if k else 1, side, 0)
+
+    blocks = rows // Q_ROWS
+
+    def one_head(h, carry):
+        for i in range(blocks):
+            at = slice(i * Q_ROWS, (i + 1) * Q_ROWS)
+            length = (i + 1) * Q_ROWS
+            s = mm(qkv_ref[h, at], qkv_ref[heads + h, :length], NT)
+            begin = column(meta_ref, at, META_BEGIN).astype(jnp.int32)
+            s = jnp.where(seen(begin, i * Q_ROWS, Q_ROWS, length), s, NEG)
+            top = jnp.max(s, axis=1, keepdims=True)
+            p = jnp.exp(s - top)
+            total = jnp.sum(p, axis=1, keepdims=True)
+            o = mm(p.astype(BF), qkv_ref[2 * heads + h, :length]) * (column(meta_ref, at, META_VALID) / total)
+            o_ref[h, at] = o.astype(BF)
+            lse_ref[h, at] = top + jnp.log(total)
+        return carry
+
+    lax.fori_loop(0, heads, one_head, 0)
+    for d in range(cols):
+        at = slice(d * local, (d + 1) * local)
+        pack_heads(a_out.at[d], jnp.concatenate([o_ref[h, at] for h in range(heads)], axis=1))
+    a_copies = to_cols(lambda d: a_out.at[d], a_in, c_send.at[2], c_recv.at[2], cols)
+    for copy in a_copies:
+        copy.start()
+    a_in[c] = a_out[c]
+    kept_out = [
+        pltpu.make_async_copy(xw, xw_ref, local_sem.at[3]),
+        pltpu.make_async_copy(wq, wq_out, local_sem.at[4]),
+    ]
+    for copy in kept_out:
+        copy.start()
+    for copy in wo_copies:
+        copy.wait()
+    forward(0)
+    for copy in a_copies:
+        copy.wait()
+    parts = []
+    for i in range(cols):
+        parts.extend(unpack_heads(a_in[i], local))
+    mixed = jnp.concatenate(parts, axis=1)
+    mixed_ref[...] = mixed
+    middle = x_ref[...].astype(F32) + mm(mixed, wo[...], NT)
+    middle_ref[...] = middle
+    n2_ref[...] = (middle * norm_rows(middle) * fgain_ref[...]).astype(BF)
+    n_step, n_drain = gather_chain(n2_ref, n2w_ref, n_send, n_recv, cols)
+    n_step(0)
+    kept_late = [
+        pltpu.make_async_copy(n2_ref, n2w_ref.at[c], local_sem.at[5]),
+        pltpu.make_async_copy(wo, wo_out, local_sem.at[6]),
+    ]
+    for copy in kept_late:
+        copy.start()
+    for copy in prev_copies:
+        copy.wait()
+    prevw_ref[...] = prevw[...]
+    n_step(1)
+    forward(1)
+    for k in range(2, cols):
+        n_step(k)
+    forward(2)
+    x_drain()
+    n_drain()
+    for copies in chip_copies:
+        for copy in copies:
+            copy.wait_send()
+    for t in range(3):
+        for copy in pass_on(t):
+            copy.wait()
+    for copy in kept + kept_out + kept_late:
+        copy.wait()
+
+
+def first_step(cols, ranks, x, again, fgain, wq, wo, prev, routes, lengths, gate, up, down):
+    local = x.shape[0]
+    rows = local * cols
+    heads, width = 3, 3 * HEAD_DIM
+    experts, depth, ff = gate.shape
+    spots = np.arange(rows, dtype=np.float64)[:, None]
+    pair = np.arange(LANES) % HEAD_DIM // 2
+    freq = np.exp(-(2.0 * pair / HEAD_DIM) * math.log(BASE))[None, :]
+    tables = [np.cos(spots * freq), np.sin(spots * freq), freq]
+    tables = [jnp.asarray(value.astype(np.float32)) for value in tables]
+    vm = pl.BlockSpec(memory_space=pltpu.VMEM)
+    dma = pltpu.SemaphoreType.DMA
+    return pl.pallas_call(
+        functools.partial(first_kernel, cols, ranks),
+        out_shape=(
+            jax.ShapeDtypeStruct((ranks, 3, experts, depth, ff), BF),
+            jax.ShapeDtypeStruct((3 * heads, rows, HEAD_DIM), BF),
+            jax.ShapeDtypeStruct((heads, rows, HEAD_DIM), BF),
+            jax.ShapeDtypeStruct((heads, rows, 1), F32),
+            jax.ShapeDtypeStruct((cols, local, D), BF),
+            jax.ShapeDtypeStruct((D, 3 * width), BF),
+            jax.ShapeDtypeStruct((D, D), BF),
+            jax.ShapeDtypeStruct((rows, LANES), F32),
+            jax.ShapeDtypeStruct((rows, LANES), F32),
+            jax.ShapeDtypeStruct((rows, LANES), F32),
+            jax.ShapeDtypeStruct((experts, rows), jnp.int32),
+            jax.ShapeDtypeStruct((local, D), BF),
+            jax.ShapeDtypeStruct((local, D), F32),
+            jax.ShapeDtypeStruct((local, D), BF),
+            jax.ShapeDtypeStruct((cols, local, D), BF),
+            jax.ShapeDtypeStruct((cols, 16, local), BF),
+        ),
+        in_specs=[vm] * 7 + [pl.BlockSpec(memory_space=pltpu.SMEM)] + [vm] * 3 + [ANY] * 3,
+        out_specs=(ANY, vm, vm, vm, ANY, ANY, ANY, vm, vm, vm, vm, vm, vm, vm, ANY, vm),
+        scratch_shapes=[
+            pltpu.VMEM((cols, local, D), BF),
+            pltpu.VMEM((3, depth, width), BF),
+            pltpu.VMEM((3, depth, width), BF),
+            pltpu.VMEM((depth, width), BF),
+            pltpu.VMEM((cols, depth, width), BF),
+            pltpu.VMEM((D, 3 * width), BF),
+            pltpu.VMEM((D, D), BF),
+            pltpu.VMEM((cols, local * 3 // 2, LANES), BF),
+            pltpu.VMEM((cols, local * 3 // 2, LANES), BF),
+            pltpu.VMEM((cols, 16, local), BF),
+            dma((7,)),
+            dma((2, cols - 1)),
+            dma((2, cols - 1)),
+            dma((2, cols - 1)),
+            dma((2, cols - 1)),
+            dma((2,)),
+            dma((2,)),
+            dma((3, cols - 1)),
+            dma((3, cols - 1)),
+            dma((2, ranks - 1)),
+            dma((2, ranks - 1)),
+            dma((3, 3)),
+            dma((3, 3)),
+            dma((3, 4)),
+            dma((3, 4)),
+        ],
+        compiler_params=pltpu.CompilerParams(
+            vmem_limit_bytes=60 * MIB, collective_id=5, has_side_effects=True
+        ),
+        cost_estimate=pl.CostEstimate(
+            flops=8 * heads * rows * rows * HEAD_DIM, bytes_accessed=40 * MIB, transcendentals=heads * rows * rows
+        ),
+        name="first_step",
+    )(x, again, fgain, wq, wo, prev, routes, lengths, *tables, gate, up, down)
 
 
 SENT_FIRST = 5
@@ -1673,43 +1940,8 @@
     ranks, cols = sizes
     heads = HEADS // cols
     width = heads * HEAD_DIM
-    row_index, col_index = lax.axis_index("row"), lax.axis_index("col")
+    row_index = lax.axis_index("row")
     row_total = expert_routes.shape[0]
-    local_rows = inputs.shape[0]
-    first_row = col_index * local_rows
-
-    def own_rows(value):
-        return lax.dynamic_slice_in_dim(value, first_row, local_rows, 0)
-
-    w_stack = jnp.stack([gate_weight, up_weight, down_weight.transpose(0, 2, 1)])
-    w_all = lax.all_gather(w_stack, "row", axis=0)
-
-    lengths = seq_lengths[0]
-    ends = jnp.cumsum(lengths)
-    starts = ends - lengths
-    spot = jnp.arange(row_total, dtype=jnp.int32)
-    seq_index = jnp.sum((spot[:, None] >= ends[None, :]).astype(jnp.int32), axis=1)
-    member = seq_index[:, None] == jnp.arange(lengths.shape[0], dtype=jnp.int32)[None, :]
-    begin = jnp.sum(jnp.where(member, starts[None, :], 0), axis=1)
-    is_valid = seq_index < lengths.shape[0]
-    positions = spot - begin
-    valid = is_valid.astype(F32)[:, None]
-    seq_begin = jnp.where(is_valid, begin, ends[-1])[:, None]
-    pair = jnp.arange(HEAD_DIM // 2, dtype=jnp.int32)
-    frequency = jnp.exp(-((2 * pair).astype(F32) / HEAD_DIM) * math.log(BASE))
-    angles = positions.astype(F32)[:, None] * frequency[None, :]
-    cosine, sines = jnp.cos(angles), jnp.sin(angles)
-    cosine = jnp.tile(jnp.repeat(cosine, 2, axis=1), (1, LANES // HEAD_DIM))
-    sines = jnp.tile(
-        jnp.stack([-sines, sines], axis=2).reshape(row_total, HEAD_DIM), (1, LANES // HEAD_DIM)
-    )
-
-    hit = jnp.any(
-        expert_routes[:, :, None] == jnp.arange(EXPERTS, dtype=jnp.int32)[None, None, :], axis=1
-    ).astype(jnp.int32)
-    slots = jnp.where(hit > 0, jnp.cumsum(hit, axis=0) - 1, -1)
-    slots_t = slots.T[:, None, :]
-
     rw = jnp.concatenate(
         [
             router_weight.T,
@@ -1724,29 +1956,43 @@
     attn_gain_row = attn_gain.astype(F32)[None, :]
     ffn_gain_row = ffn_gain.astype(F32)[None, :]
 
-    w_cat = jnp.concatenate([out_weight.T, qkv_weight], axis=1)
-    w_cols = lax.all_gather(w_cat, "col", axis=0, tiled=False)
-    depth = qkv_weight.shape[0]
-    blocks = w_cols[:, :, width:].reshape(cols, depth, 3, width).transpose(0, 2, 1, 3)
-    blocks = blocks.reshape(3, cols, depth, width)
-    own = lax.dynamic_index_in_dim(blocks, col_index, 1, keepdims=False)
-    w_own = jnp.concatenate([own[0], own[1], own[2]], axis=1)
-    out_rows = w_cols[:, :, :width].transpose(1, 0, 2).reshape(depth, D)
-    w_full = lax.all_gather(jnp.concatenate([out_rows, w_own], axis=1), "row", axis=0, tiled=True)
-    out_t, qkv_own = w_full[:, :D], w_full[:, D:]
-    whole_in = lax.all_gather(inputs, "col", axis=0, tiled=True)
-    prev_whole = lax.all_gather(prev, "col", axis=0)
-    qkv = project_heads(heads, whole_in, attn_gain_row, qkv_own, cosine, sines)
-    mixed_heads, lse = attend(heads, qkv, seq_begin, valid)
-    to_send = mixed_heads.transpose(1, 0, 2).reshape(cols, local_rows, width)
-    attn_parts = lax.all_to_all(to_send, "col", split_axis=0, concat_axis=0, tiled=True)
-    mixed, middle, n2 = branch(attn_parts, out_t, inputs, ffn_gain_row)
-    n2_whole = lax.all_gather(n2, "col", axis=0, tiled=True)
+    (
+        w_all,
+        qkv,
+        mixed_heads,
+        lse,
+        whole_in,
+        qkv_own,
+        out_t,
+        cosine,
+        sines,
+        meta,
+        slots,
+        mixed,
+        middle,
+        n2,
+        n2_whole,
+        prev_whole,
+    ) = first_step(
+        cols,
+        ranks,
+        inputs,
+        attn_gain_row,
+        ffn_gain_row,
+        qkv_weight,
+        out_weight.T,
+        prev,
+        expert_routes.T,
+        seq_lengths,
+        gate_weight,
+        up_weight,
+        down_weight.transpose(0, 2, 1),
+    )
     x, gu, mix, gates, cot_whole = experts_forward(
-        cols, n2_whole, prev_whole, cotangent, rw, carry, expert_routes, slots, slots_t, w_all
+        cols, n2_whole.reshape(row_total, D), prev_whole, cotangent, rw, carry, meta, slots, w_all
     )
     gt, dots, mixsum, gown, sib = experts_backward(
-        cols, cot_whole.reshape(row_total, D), mix, gates, slots, slots_t, w_all, x, gu
+        cols, cot_whole.reshape(row_total, D), mix, gates, meta, slots, w_all, x, gu
     )
     layer_out, resid, gm, og, small, prev_grad, hin0 = resid_step(
         cols,
@@ -1757,14 +2003,13 @@
         n2,
         middle,
         cotangent,
-        own_rows(expert_routes),
+        meta,
         prev,
         rw,
         carry,
         ffn_gain_row,
         out_t,
         mixed,
-        own_rows(valid),
         gown,
         sib,
     )
@@ -1774,10 +2019,10 @@
         SENT_FIRST,
         gm,
         qkv,
-        seq_begin,
+        meta,
         mixed_heads,
         lse,
-        whole_in,
+        whole_in.reshape(row_total, D),
         attn_gain_row,
         qkv_own,
         cosine,

time: 635 us -> 472 us (0.74)
  waiting for transfers between devices: 210 us -> 0 us
  Pallas kernels: 302 us -> 433 us
  blocking collectives: 32.3 us -> 0 us
  local copies, waits for them, and re-layouts: 41.3 us -> 16.5 us
  between operations: 14.8 us -> 1.2 us
  other arithmetic: 19.9 us -> 12.7 us
    all_gather x4 -> x0, waiting for transfers between devices: 194 us -> none  [the longest x1 99.3 us: on_device_heads(): w_all = lax.all_gather(w_stack, 'row', axis=0)]
    pallas_call x3 -> x1, Pallas kernels: 18.9 us -> 150 us  [first_step(): pl.pallas_call(functools.partial(first_kernel, cols, ranks), out_shape=(j...]
    all_gather x2 -> x0, blocking collectives: 32.3 us -> none  [the longest x1 18.2 us: on_device_heads(): w_cols = lax.all_gather(w_cat, 'col', axis=0, tiled=False)]
    all_to_all x1 -> x0, waiting for transfers between devices: 14.6 us -> none  [on_device_heads(): lax.all_to_all(to_send, 'col', split_axis=0, concat_axis=0, tiled=True)]
    unnamed x65 -> x26, local copies, waits for them, and re-layouts: 14.5 us -> 5.59 us
  transfers between devices with their start and end apart: 5 -> 0, of which waited for: 5 -> 0; matrix products, arithmetic and copies ran while one was open for 4% -> 0% of each run, Pallas kernels for 0% -> 0%
where the time goes in v3:
time: 472 us; the launch traced here: 464 us
  Pallas kernels  433 us (92%)
  local copies, waits for them, and re-layouts  16.5 us (3%)
  other arithmetic  12.7 us (3%)
    pallas_call x1, Pallas kernels, first_step(): pl.pallas_call(functools.partial(first_kernel, cols, ranks), out_shape=(j...  150 us
    pallas_call x1, Pallas kernels, finish_step(): pl.pallas_call(functools.partial(finish_kernel, cols, ranks, first, count...  92.3 us
    pallas_call x1, Pallas kernels, resid_step(): pl.pallas_call(functools.partial(resid_kernel, cols, count), out_shape=(j...  78 us
    pallas_call x1, Pallas kernels, experts_forward(): pl.pallas_call(functools.partial(experts_forward_kernel, cols, capacity),...  57 us
    pallas_call x1, Pallas kernels, experts_backward(): pl.pallas_call(functools.partial(experts_backward_kernel, cols, capacity)...  56 us

profile of v3, /device:TPU:0, one launch (start us, length us, event | category | flops | bytes accessed | tf_op | source)
XLA Modules:
  0.0 463.5 jit_solution(2635537704261764021)
XLA Ops:
  0.6 1.3 pad.8.prev_ref
  2.0 1.3 reshape.55.again_ref.gain_ref
  3.2 1.3 reshape.56.fgain_ref.gain_ref
  4.5 1.5 copy.35
  6.0 149.7 %first_step.1 = (bf16[8,3,8,96,512]{4,3,2,1,0:T(8,128)(2,1)}, bf16[9,1536,64]{2,1,0:T(8,128)(2,1)}, bf16[3,1536,64]{2,1,0:T(8,128)(2,1)}, f32[3,1536,1]{2,1,0:T(...) custom-call(bf16[384,768]{1,0:T(8,128)(2,1)} %xown_ref.1, ...), custom_call_target="tpu_custom_call" | custom-call | flops 3623878656 | bytes 41943040 | tf_op jit(solution)/shard_map/first_step/pallas_call | solution.py:1859
  155.7 0.0 copy-done.7
  155.8 0.1 pad.15.clone
  155.9 0.0 copy-done.5
  155.9 0.0 copy-done.9
  155.9 0.8 maximum_maximum_fusion.rw_ref
  156.6 0.0 copy-done.8
  156.6 0.6 pad.9.carry_ref
  157.2 57.0 %experts_forward.1 = (bf16[8,384,768]{2,1,0:T(8,128)(2,1)}, bf16[8,2,384,512]{3,2,1,0:T(8,128)(2,1)}, bf16[4,384,768]{2,1,0:T(8,128)(2,1)}, bf16[1536,256]{1,0:T(8,128)(2,1)}, bf16[4,384,768]{2,1,0:T(8,128)(2,1)}) custom-call(bf16[1536,768]{1,0:T(8,128)(2,1)} %bitcast.34, bf16[4,16,384]{2,1,0:T(8,128)(2,1)} %get-tuple-element.54.prev_ref, ...), custom_call_target="tpu_custom_call" | custom-call | flops 24159191040 | bytes 41943040 | tf_op jit(solution)/shard_map/experts_forward/pallas_call | solution.py:800
  214.3 56.0 %experts_backward.1 = (bf16[4,384,768]{2,1,0:T(8,128)(2,1)}, f32[8,1536]{1,0:T(8,128)}, f32[384,768]{1,0:T(8,128)}, bf16[8,3,4,96,512]{4,3,2,1,0:T(8,128)(2,1)}, bf16[8,3,4,96,512]{4,3,2,1,0:T(8,128)(2,1)}) custom-call(bf16[1536,768]{1,0:T(8,128)(2,1)} %bitcast.35, bf16[4,384,768]{2,1,0:T(8,128)(2,1)} %get-tuple-element.59.mix_ref, ...), custom_call_target="tpu_custom_call" | custom-call | flops 28991029248 | bytes 62914560 | tf_op jit(solution)/shard_map/experts_backward/pallas_call | solution.py:964
  270.3 78.0 %resid_step.1 = (bf16[384,768]{1,0:T(8,128)(2,1)}, f32[384,768]{1,0:T(8,128)}, bf16[4,576,128]{2,1,0:T(8,128)(2,1)}, bf16[768,768]{1,0:T(8,128)(2,1)}, f32[24,89...) custom-call(bf16[4,384,768]{2,1,0:T(8,128)(2,1)} %get-tuple-element.63.gt_ref, ...), custom_call_target="tpu_custom_call" | custom-call | flops 1358954496 | bytes 41943040 | tf_op jit(solution)/shard_map/resid_step/pallas_call | solution.py:1257
  348.3 92.3 %finish_step.1 = (f32[384,768]{1,0:T(8,128)}, f32[24,896]{1,0:T(8,128)}, f32[8,768]{1,0:T(8,128)}, f32[3,96,192]{2,1,0:T(8,128)}, f32[96,192]{1,0:T(8,128)}, /*index=5*/bf16[3,3,3,96,512]{4,3,2,1,0:T(8,128)(2,1)}) custom-call(bf16[4,576,128]{2,1,0:T(8,128)(2,1)} %get-tuple-element.73.gm_ref, bf16[9,1536,64]{2,1,0:T(8,128)(2,1)} %get-tuple-element.74.qkv_ref, ...), custom_call_target="tpu_custom_call" | custom-call | flops 9059696640 | bytes 41943040 | tf_op jit(solution)/shard_map/finish_step/pallas_call | solution.py:1495
  440.6 7.1 %convert_reduce_fusion = f32[8,3,96,512]{3,2,1,0:T(8,128)} fusion(bf16[3,3,3,96,512]{4,3,2,1,0:T(8,128)(2,1)} %get-tuple-element.90, bf16[5,3,3,96,512]{4,3,2,1,0:T(8,128)(2,1)} %get-tuple-element.89), kind=kLoop, calls=%fused_computation | loop fusion | flops 9437184 | bytes 11796480 | tf_op jit(solution)/shard_map/reduce_sum | solution.py:2041
  447.8 4.8 %bitcast_add_fusion = f32[8,3,96,512]{3,2,1,0:T(8,128)S(1)} fusion(f32[8,3,96,512]{3,2,1,0:T(8,128)} %convert_reduce_fusion, bf16[8,3,4,96,512]{4,3,2,1,0:T(8,128)(2,1)} %get-tuple-element.71.sib_ref, s32[]{:T(128)S(6)} %select_n.11, bf16[8,3,4,96,512]{4,3,2,1,0:T(8,128)(2,1)} %get-tuple-element.70.gown_ref), kind=kLoop, calls=%fused_computation.1 | loop fusion | flops 4718592 | bytes 14155780 | tf_op jit(solution)/shard_map/add | solution.py:2041
  452.6 0.0 copy-start.4
  452.6 2.4 slice_bitcast_fusion
  455.0 1.4 slice_reduce_fusion
  456.5 0.1 copy.36
  456.6 0.9 copy.37
  457.5 0.0 copy-done.3
  457.5 0.7 copy.38
  458.2 0.6 slice_bitcast_fusion.3
  458.8 0.6 reshape.54
  459.5 0.6 slice.30
  460.1 0.6 slice.32
  460.7 0.8 copy.42
  461.5 1.0 copy.43
  462.5 0.6 copy.44
  (17 shorter events, 0.0 us)
Async XLA Ops:
  6.0 149.8 %copy-start.7 = (bf16[2,768,2]{1,2,0:T(2,128)(2,1)S(1)}, bf16[2,768,2]{1,2,0:T(2,128)(2,1)}, u32[]{:S(2)}) copy-start(bf16[2,768,2]{1,2,0:T(2,128)(2,1)} %param.26) | copy-start | bytes 18436
  6.0 149.9 %copy-start.5 = (bf16[768,12]{0,1:T(8,128)(2,1)S(1)}, bf16[768,12]{0,1:T(8,128)(2,1)}, u32[]{:S(2)}) copy-start(bf16[768,12]{0,1:T(8,128)(2,1)} %param.24) | copy-start | bytes 55300
  6.0 149.9 %copy-start.9 = (bf16[2,768]{1,0:T(2,128)(2,1)S(1)}, bf16[2,768]{1,0:T(2,128)(2,1)}, u32[]{:S(2)}) copy-start(bf16[2,768]{1,0:T(2,128)(2,1)} %param.27) | copy-start | bytes 9220
  6.0 150.6 %copy-start.8 = (bf16[12,12]{1,0:T(8,128)(2,1)S(1)}, bf16[12,12]{1,0:T(8,128)(2,1)}, u32[]{:S(2)}) copy-start(bf16[12,12]{1,0:T(8,128)(2,1)} %param.25) | copy-start | bytes 868
  452.6 2.4 copy-start.4
  452.6 3.8 copy-start.2
  452.6 4.8 %copy-start.3 = (f32[96,192]{1,0:T(8,128)S(1)}, f32[96,192]{1,0:T(8,128)}, u32[]{:S(2)}) copy-start(f32[96,192]{1,0:T(8,128)} %get-tuple-element.87) | copy-start | bytes 221188
  452.6 8.0 %copy-start.1 = (bf16[384,768]{1,0:T(8,128)(2,1)S(1)}, bf16[384,768]{1,0:T(8,128)(2,1)}, u32[]{:S(2)}) copy-start(bf16[384,768]{1,0:T(8,128)(2,1)} %get-tuple-element.139) | copy-start | bytes 1769476
  455.0 6.5 %copy-start = (f32[384,768]{1,0:T(8,128)S(1)}, f32[384,768]{1,0:T(8,128)}, u32[]{:S(2)}) copy-start(f32[384,768]{1,0:T(8,128)} %get-tuple-element.140) | copy-start | bytes 3538948
  455.0 7.5 %copy-start.6 = (f32[12,384]{1,0:T(8,128)S(1)}, f32[12,384]{1,0:T(8,128)}, u32[]{:S(2)}) copy-start(f32[12,384]{1,0:T(8,128)} %get-tuple-element.152) | copy-start | bytes 55300

commit v4 on v0

--- a/solution.py
+++ b/solution.py
@@ -1,8 +1,12 @@
+import functools
 import math
 
 import jax
 import jax.numpy as jnp
+import numpy as np
 from jax import lax
+from jax.experimental import pallas as pl
+from jax.experimental.pallas import tpu as pltpu
 from jax.sharding import PartitionSpec as P
 
 D = 768
@@ -480,7 +484,1921 @@
     )
 
 
+BF = jnp.bfloat16
+F32 = jnp.float32
+LANES = 128
+NN = (((1,), (0,)), ((), ()))
+NT = (((1,), (1,)), ((), ()))
+TN = (((0,), (0,)), ((), ()))
+ROW_CONST = 12
+ROW_VEC = 16
+ROW_GAIN = 18
+SMALL_ROWS = 24
+Q_ROWS = 256
+MIB = 1 << 20
+
+
+def mm(a, b, dims=NN):
+    return lax.dot_general(a, b, dims, preferred_element_type=F32)
+
+
+def lane_iota(shape):
+    return lax.broadcasted_iota(jnp.int32, shape, len(shape) - 1)
+
+
+def whole(shape):
+    return pl.BlockSpec(tuple(shape), lambda *_: (0,) * len(shape), pipeline_mode=pl.Buffered(1))
+
+
+def swap_pairs(v):
+    even = lane_iota(v.shape) % 2 == 0
+    return jnp.where(even, pltpu.roll(v, LANES - 1, 1), pltpu.roll(v, 1, 1))
+
+
+def norm_rows(x):
+    return lax.rsqrt(jnp.mean(x * x, axis=1, keepdims=True) + EPS)
+
+
+def seen(begin, first, rows, length):
+    u = lax.broadcasted_iota(jnp.int32, (rows, length), 1)
+    t = lax.broadcasted_iota(jnp.int32, (rows, length), 0) + first
+    return (u >= begin) & (u <= t)
+
+
+def gate_lanes(logits, meta):
+    lane = lane_iota(logits.shape)
+    hit = (pltpu.roll(meta, LANES - META_HIT, 1) > 0.0) & (lane < ROUTES)
+    held = jnp.where(hit, logits, NEG)
+    e = jnp.where(hit, jnp.exp(held - jnp.max(held, axis=1, keepdims=True)), 0.0)
+    return e / jnp.sum(e, axis=1, keepdims=True)
+
+
+MESH = pl.DeviceIdType.MESH
+ANY = pl.BlockSpec(memory_space=pl.ANY)
+
+
+def place():
+    return lax.axis_index("row"), lax.axis_index("col")
+
+
+def flip(index, mask):
+    for bit in (1, 2, 4):
+        if mask & bit:
+            index = index + bit - 2 * bit * (index // bit % 2)
+    return index
+
+
+def greet(devices):
+    barrier = pltpu.get_barrier_semaphore()
+    for device in devices:
+        pl.semaphore_signal(barrier, inc=1, device_id=device, device_id_type=MESH)
+    pl.semaphore_wait(barrier, len(devices))
+
+
+def send_to(src, dst, send, recv, device):
+    return pltpu.make_async_remote_copy(
+        src_ref=src, dst_ref=dst, send_sem=send, recv_sem=recv, device_id=device, device_id_type=MESH
+    )
+
+
+def col_peers(n):
+    r, c = place()
+    return [(r, (c + k) % n) for k in range(1, n)]
+
+
+def gather_chain(own, dst, send, recv, n):
+    r, c = place()
+
+    def right(k):
+        i = jnp.maximum(c - k, 0)
+        src = own if k == 0 else dst.at[i]
+        return send_to(src, dst.at[i], send.at[0, k], recv.at[0, k], (r, jnp.minimum(c + 1, n - 1)))
+
+    def left(k):
+        i = jnp.minimum(c + k, n - 1)
+        src = own if k == 0 else dst.at[i]
+        return send_to(src, dst.at[i], send.at[1, k], recv.at[1, k], (r, jnp.maximum(c - 1, 0)))
+
+    def step(k):
+        if k > 0:
+
+            @pl.when(c >= k)
+            def _():
+                right(k - 1).wait_recv()
+
+            @pl.when(c + k < n)
+            def _():
+                left(k - 1).wait_recv()
+
+        if k < n - 1:
+
+            @pl.when((c >= k) & (c + 1 < n))
+            def _():
+                right(k).start()
+
+            @pl.when((c + k < n) & (c >= 1))
+            def _():
+                left(k).start()
+
+    def drain():
+        for k in range(n - 1):
+
+            @pl.when((c >= k) & (c + 1 < n))
+            def _():
+                right(k).wait_send()
+
+            @pl.when((c + k < n) & (c >= 1))
+            def _():
+                left(k).wait_send()
+
+    return step, drain
+
+
+def reduce_chain(own, out, arrived, send, recv, n):
+    r, c = place()
+
+    def right(k):
+        return send_to(out.at[0, k], arrived.at[0, k], send.at[0, k], recv.at[0, k], (r, jnp.minimum(c + 1, n - 1)))
+
+    def left(k):
+        return send_to(out.at[1, k], arrived.at[1, k], send.at[1, k], recv.at[1, k], (r, jnp.maximum(c - 1, 0)))
+
+    def slot(s):
+        if s == n - 1:
+
+            @pl.when(c >= 1)
+            def _():
+                right(n - 1 - c).wait_recv()
+
+            @pl.when(c <= n - 2)
+            def _():
+                left(c).wait_recv()
+
+            return
+
+        @pl.when(c <= s)
+        def _():
+            k = jnp.maximum(s - c, 0)
+
+            @pl.when(c >= 1)
+            def _():
+                right(k).wait_recv()
+                out[0, k] = (own(n - 1 - k).astype(F32) + arrived[0, k].astype(F32)).astype(BF)
+
+            @pl.when(c == 0)
+            def _():
+                out[0, k] = own(n - 1 - k).astype(BF)
+
+            right(k).start()
+
+        @pl.when(n - 1 - c <= s)
+        def _():
+            k = jnp.maximum(s - (n - 1 - c), 0)
+
+            @pl.when(c <= n - 2)
+            def _():
+                left(k).wait_recv()
+                out[1, k] = (own(k).astype(F32) + arrived[1, k].astype(F32)).astype(BF)
+
+            @pl.when(c == n - 1)
+            def _():
+                out[1, k] = own(k).astype(BF)
+
+            left(k).start()
+
+    def total(dst):
+        dst[...] = own(c).astype(F32)
+
+        @pl.when(c >= 1)
+        def _():
+            dst[...] += arrived[0, n - 1 - c].astype(F32)
+
+        @pl.when(c <= n - 2)
+        def _():
+            dst[...] += arrived[1, c].astype(F32)
+
+    def drain():
+        for k in range(n - 1):
+
+            @pl.when(c < n - 1 - k)
+            def _():
+                right(k).wait_send()
+
+            @pl.when(c > k)
+            def _():
+                left(k).wait_send()
+
+    return slot, total, drain
+
+
+def chain_scratch(n, rows):
+    return [
+        pltpu.VMEM((2, n - 1, rows, D), BF),
+        pltpu.VMEM((2, n - 1, rows, D), BF),
+        pltpu.SemaphoreType.DMA((2, n - 1)),
+        pltpu.SemaphoreType.DMA((2, n - 1)),
+    ]
+
+
+def slot_rows(slots_ref, e, capacity):
+    rows = slots_ref.shape[1]
+    spots = lax.broadcasted_iota(jnp.int32, (capacity, rows), 0)
+    return jnp.where(spots == slots_ref[pl.ds(e, 1)], 1.0, 0.0).astype(BF)
+
+
+def slot_gates(one, gates_ref, e):
+    sg = mm(one, gates_ref[...])
+    return jnp.sum(jnp.where(lane_iota(sg.shape) % LANES == e, sg, 0.0), axis=1, keepdims=True)
+
+
+def combine(meta_ref, y_ref, d, local):
+    experts, capacity, width = y_ref.shape
+    at = slice(d * local, (d + 1) * local)
+    lane = lane_iota((local, capacity)).astype(F32)
+    ones = [jnp.where(lane == column(meta_ref, at, e), 1.0, 0.0).astype(BF) for e in range(experts)]
+    return mm(jnp.concatenate(ones, axis=1), y_ref[...].reshape(experts * capacity, width)).astype(BF)
+
+
+META_HIT, META_BEGIN, META_VALID = 8, 20, 21
+EARLY = 3
+SENT_SOON, SENT_NEXT = 2, 3
+
+
+def column(ref, at, lane):
+    return ref[at, lane : lane + 1]
+
+
+def start_all(copies):
+    for copy in copies:
+        copy.start()
+
+
+def wait_all(copies):
+    for copy in copies:
+        copy.wait()
+
+
+def moves(pairs, sem):
+    return [pltpu.make_async_copy(src, dst, sem.at[i]) for i, (src, dst) in enumerate(pairs)]
+
+
+def pack_head(value):
+    half = value.shape[0] // 2
+    return jnp.concatenate([value[:half], value[half:]], axis=1)
+
+
+def unpack_head(packed):
+    return jnp.concatenate([packed[:, :HEAD_DIM], packed[:, HEAD_DIM:]], axis=0)
+
+
+def to_rows(src_of, dst, send, recv, ranks):
+    r, c = place()
+    copies = []
+    for m in range(1, ranks):
+        there = flip(r, m)
+        copies.append(send_to(src_of(there), dst.at[r], send.at[m - 1], recv.at[m - 1], (there, c)))
+    return copies
+
+
+def to_cols(src_of, dst, send, recv, n):
+    r, c = place()
+    copies = []
+    for k in range(1, n):
+        there = (c + k) % n
+        copies.append(send_to(src_of(there), dst.at[c], send.at[k - 1], recv.at[k - 1], (r, there)))
+    return copies
+
+
+def to_chips(src_of, dst, send, recv):
+    r, c = place()
+    return [
+        send_to(src_of(flip(r // 2, k)), dst.at[k - 1], send.at[k - 1], recv.at[k - 1], (flip(r, 2 * k), c))
+        for k in range(1, 4)
+    ]
+
+
+def all_sum(ref, count):
+    total = ref[0].astype(F32)
+    for i in range(1, count):
+        total = total + ref[i].astype(F32)
+    return total
+
+
+def tokens_meta(routes_ref, lengths_ref, rows, experts):
+    kinds = lax.broadcasted_iota(jnp.int32, (16, rows), 0)
+    hits = jnp.where((kinds == routes_ref[0:1]) | (kinds == routes_ref[1:2]), 1.0, 0.0)
+    step = 256
+    earlier = lax.broadcasted_iota(jnp.int32, (step, step), 0) < lax.broadcasted_iota(
+        jnp.int32, (step, step), 1
+    )
+    earlier = jnp.where(earlier, 1.0, 0.0).astype(BF)
+    counts, running = [], jnp.zeros((16, 1), F32)
+    for b in range(rows // step):
+        block = hits[:, b * step : (b + 1) * step]
+        counts.append(mm(block.astype(BF), earlier) + running)
+        running = running + jnp.sum(block, axis=1, keepdims=True)
+    slots = jnp.where(hits > 0.0, jnp.concatenate(counts, axis=1), -1.0)[:experts]
+    spot = lax.broadcasted_iota(jnp.int32, (8, rows), 1)
+    begin, end = jnp.zeros((8, rows), F32), 0
+    for i in range(lengths_ref.shape[1]):
+        end = end + lengths_ref[0, i]
+        begin = jnp.where(spot >= end, end.astype(F32), begin)
+    valid = jnp.where(spot < end, 1.0, 0.0)
+    tail = jnp.where(lax.broadcasted_iota(jnp.int32, (8, rows), 0) == 0, begin, valid)
+    spare = jnp.zeros((LANES - experts - 12 - 8, rows), F32)
+    meta = jnp.concatenate([slots, hits[:12], tail, spare], axis=0).T
+    return slots.astype(jnp.int32), meta
+
+
+def first_kernel(
+    cols,
+    ranks,
+    x_ref,
+    cot_ref,
+    router_ref,
+    const_ref,
+    vector_ref,
+    again_ref,
+    fgain_ref,
+    carry_ref,
+    wq_ref,
+    wo_ref,
+    prev_ref,
+    routes_ref,
+    lengths_ref,
+    cos_ref,
+    sin_ref,
+    freq_ref,
+    gate_ref,
+    up_ref,
+    down_ref,
+    wall_ref,
+    qkv_out,
+    o_out,
+    lse_out,
+    xw_out,
+    wq_out,
+    wo_out,
+    cos_out,
+    sin_out,
+    meta_out,
+    slots_ref,
+    mixed_out,
+    middle_out,
+    n2w_ref,
+    prevw_out,
+    cota_ref,
+    rw_out,
+    carry_out,
+    xw,
+    q_parts,
+    q_land,
+    o_parts,
+    o_land,
+    wq,
+    wo,
+    a_send,
+    a_land,
+    prev_s,
+    prevw,
+    qkv_s,
+    o_s,
+    lse_s,
+    cos_s,
+    sin_s,
+    meta_s,
+    mixed_s,
+    middle_s,
+    n2_s,
+    w_s,
+    local_sem,
+    x_send,
+    x_recv,
+    n_send,
+    n_recv,
+    t_send,
+    t_recv,
+    q_send,
+    q_recv,
+    c_send,
+    c_recv,
+    r_send,
+    r_recv,
+    e_send,
+    e_recv,
+    d_send,
+    d_recv,
+    s_send,
+    s_recv,
+    h_send,
+    h_recv,
+):
+    r, c = place()
+    heads = 3
+    local = x_ref.shape[0]
+    rows = local * cols
+    width = heads * HEAD_DIM
+    depth = D // ranks
+    odd, high = c % 2, c // 2
+    again = again_ref[...].astype(F32).reshape(1, D)
+    fgain = fgain_ref[...].astype(F32).reshape(1, D)
+    greet(col_peers(cols) + [(flip(r, m), c) for m in (1, 2, 4, 6)])
+
+    for s in range(3):
+        q_parts[s] = wq_ref[:, s * width : (s + 1) * width]
+    q_copies = [
+        send_to(q_parts.at[1], q_land.at[(c + 1) // 2], q_send.at[0], q_recv.at[0], (r, flip(c, 1))),
+        send_to(q_parts.at[2 - 2 * odd], q_land.at[2 * high], q_send.at[1], q_recv.at[1], (r, flip(c, 2))),
+    ]
+    start_all(q_copies)
+    o_parts[...] = wo_ref[...].astype(F32).T.astype(BF)
+    prev_s[...] = jnp.concatenate([prev_ref[...].astype(F32), jnp.zeros((16 - ROUTES, local), F32)], axis=0).astype(BF)
+    o_copies = to_cols(lambda d: o_parts, o_land, c_send.at[0], c_recv.at[0], cols)
+    prev_copies = to_cols(lambda d: prev_s, prevw, c_send.at[1], c_recv.at[1], cols)
+    x_step, x_drain = gather_chain(x_ref, xw, x_send, x_recv, cols)
+    x_step(0)
+    start_all(o_copies + prev_copies)
+    q_land[(c + 1) // 2] = q_parts[2 * odd]
+    o_land[c] = o_parts[...]
+    prevw[c] = prev_s[...]
+    xw[c] = x_ref[...]
+
+    def rows_at(d):
+        return pl.ds(pl.multiple_of(d * depth, 16), depth)
+
+    def push(ref, at):
+        here = ref.at[rows_at(r)]
+        return [
+            send_to(here, here, r_send.at[at, k - 1], r_recv.at[at, k - 1], (flip(r, 2 * k), c))
+            for k in range(1, 4)
+        ]
+
+    def hand(ref, at):
+        copies = []
+        for k in range(4):
+            here = ref.at[rows_at(flip(r, 2 * k))]
+            copies.append(send_to(here, here, r_send.at[at, 3 + k], r_recv.at[at, 3 + k], (flip(r, 1), c)))
+        return copies
+
+    wait_all(q_copies)
+    wq[rows_at(r)] = jnp.concatenate([q_land[i] for i in range(3)], axis=1)
+    wq_push, wq_hand = push(wq, 0), hand(wq, 0)
+    start_all(wq_push)
+    wait_all(o_copies)
+    wo[rows_at(r)] = jnp.concatenate([o_land[i] for i in range(cols)], axis=1)
+    wo_push, wo_hand = push(wo, 1), hand(wo, 1)
+    start_all(wo_push)
+
+    weights = (gate_ref, up_ref, down_ref)
+    half = gate_ref.shape[0] // 2
+    held = moves([(ref, w_s.at[t]) for t, ref in enumerate(weights)], local_sem)
+    kept = moves([(w_s.at[t], wall_ref.at[t, :, rows_at(r)]) for t in range(3)], local_sem)
+
+    def to_near(t):
+        dst = wall_ref.at[t, :, rows_at(r)]
+        return [
+            send_to(weights[t], dst, e_send.at[t, k - 1], e_recv.at[t, k - 1], (flip(r, 2 * k), c))
+            for k in (1, 2)
+        ]
+
+    def to_far(t):
+        copies = []
+        for k in (1, 2):
+            here = wall_ref.at[t, pl.ds((k - 1) * half, half), rows_at(flip(r, 2 * k))]
+            copies.append(send_to(here, here, d_send.at[t, k - 1], d_recv.at[t, k - 1], (flip(r, 6 - 2 * k), c)))
+        return copies
+
+    def to_other_core(t):
+        copies = []
+        for k in range(4):
+            here = wall_ref.at[t, :, rows_at(flip(r, 2 * k))]
+            src = weights[t] if k == 0 else here
+            copies.append(send_to(src, here, s_send.at[t, k], s_recv.at[t, k], (flip(r, 1), c)))
+        return copies
+
+    def relay(t):
+        for near, far in zip(to_near(t), to_far(t)):
+            near.wait_recv()
+            far.start()
+
+    def hand_over(t):
+        for far in to_far(t):
+            far.wait_recv()
+        start_all(to_other_core(t))
+
+    for t in range(3):
+        start_all(to_near(t))
+    start_all(held)
+
+    small = [ref[...].astype(F32) for ref in (router_ref, const_ref.at[0], const_ref.at[1], vector_ref)]
+    small += [again, fgain, jnp.zeros((LANES - ROW_GAIN - 2, D), F32)]
+    rw_out[...] = jnp.concatenate(small, axis=0).astype(BF)
+    carry = jnp.concatenate([carry_ref[...].astype(F32), jnp.zeros((ROUTES, LANES - ROUTES), F32)], axis=1)
+    carry_out[...] = jnp.concatenate([carry, jnp.zeros((16 - ROUTES, LANES), F32)], axis=0).astype(BF)
+    slots, meta = tokens_meta(routes_ref, lengths_ref, rows, EXPERTS)
+    slots_ref[...] = slots
+    meta_s[...] = meta
+    sub = lax.broadcasted_iota(jnp.int32, (8, LANES), 0)
+    firsts, end, ends = jnp.zeros((8, LANES), F32), 0, []
+    for i in range(lengths_ref.shape[1]):
+        firsts = jnp.where(sub == i, jnp.asarray(end, jnp.int32).astype(F32), firsts)
+        end = end + lengths_ref[0, i]
+        ends.append(end)
+    angle = firsts * freq_ref[...]
+    cos_first, sin_first = jnp.cos(angle), jnp.sin(angle)
+    spot = lax.broadcasted_iota(jnp.int32, (rows, LANES), 0)
+    cb, sb = jnp.ones((rows, LANES), F32), jnp.zeros((rows, LANES), F32)
+    for i in range(1, len(ends)):
+        cb = jnp.where(spot >= ends[i - 1], cos_first[i : i + 1], cb)
+        sb = jnp.where(spot >= ends[i - 1], sin_first[i : i + 1], sb)
+    cb, sb = jnp.where(spot >= end, 1.0, cb), jnp.where(spot >= end, 0.0, sb)
+    sign = jnp.where(lane_iota((rows, LANES)) % 2 == 0, -1.0, 1.0)
+    cos_s[...] = cos_ref[...] * cb + sin_ref[...] * sb
+    sin_s[...] = (sin_ref[...] * cb - cos_ref[...] * sb) * sign
+    lse_s[...] = jnp.zeros_like(lse_s)
+
+    def project(d):
+        at = pl.ds(pl.multiple_of(d * local, LANES), local)
+        x = xw[d].astype(F32)
+        normed = (x * norm_rows(x) * again).astype(BF)
+        proj = mm(normed, wq[...])
+        cosine, sines = cos_s[at], sin_s[at]
+        for part in range(2 * width // LANES):
+            v = proj[:, part * LANES : (part + 1) * LANES]
+            t = v * cosine + swap_pairs(v) * sines
+            for side in range(2):
+                head = 2 * part + side
+                piece = t[:, side * HEAD_DIM : (side + 1) * HEAD_DIM].astype(BF)
+                if head < heads:
+                    piece = piece * jnp.asarray(1.0 / math.sqrt(HEAD_DIM), BF)
+                qkv_s[head, at] = piece
+        for head in range(2 * heads, 3 * heads):
+            qkv_s[head, at] = proj[:, head * HEAD_DIM : (head + 1) * HEAD_DIM].astype(BF)
+
+    def project_at(k):
+        def side(way, carry):
+            d = c + k * (2 * way - 1)
+
+            @pl.when((d >= 0) & (d < cols))
+            def _():
+                project(jnp.clip(d, 0, cols - 1))
+
+            return carry
+
+        lax.fori_loop(0, 2 if k else 1, side, 0)
+
+    early = local // EARLY
+    cot_step, cot_drain = gather_chain(cot_ref.at[pl.ds(0, early)], cota_ref, t_send, t_recv, cols)
+    cot_kept = moves([(cot_ref.at[pl.ds(0, early)], cota_ref.at[c])], local_sem.at[pl.ds(3, 1)])
+
+    wait_all(held)
+    start_all(kept)
+    x_step(1)
+    for copy in wq_push:
+        copy.wait_recv()
+    start_all(wq_hand)
+    x_step(2)
+    for copy in wo_push:
+        copy.wait_recv()
+    start_all(wo_hand)
+    wait_all(wq_hand)
+    project_at(0)
+    project_at(1)
+    project_at(2)
+    relay(0)
+    x_step(3)
+    cot_step(0)
+    start_all(cot_kept)
+    project_at(3)
+    cot_step(1)
+
+    blocks = rows // Q_ROWS
+
+    def head_copies(h):
+        copies = []
+        for k in range(1, cols):
+            there = (c + k) % cols
+            copies.append(
+                send_to(a_send.at[there, h], a_land.at[c, h], h_send.at[h, k - 1], h_recv.at[h, k - 1], (r, there))
+            )
+        return copies
+
+    def one_head(h, carry):
+        for i in range(blocks):
+            at = slice(i * Q_ROWS, (i + 1) * Q_ROWS)
+            length = (i + 1) * Q_ROWS
+            s = mm(qkv_s[h, at], qkv_s[heads + h, :length], NT)
+            begin = column(meta_s, at, META_BEGIN).astype(jnp.int32)
+            s = jnp.where(seen(begin, i * Q_ROWS, Q_ROWS, length), s, NEG)
+            top = jnp.max(s, axis=1, keepdims=True)
+            p = jnp.exp(s - top)
+            total = jnp.sum(p, axis=1, keepdims=True)
+            o = mm(p.astype(BF), qkv_s[2 * heads + h, :length]) * (column(meta_s, at, META_VALID) / total)
+            o_s[h, at] = o.astype(BF)
+            lse_s[at] = jnp.where(lane_iota((Q_ROWS, LANES)) == h, top + jnp.log(total), lse_s[at])
+        for d in range(cols):
+            a_send[d, h] = pack_head(o_s[h, d * local : (d + 1) * local])
+        start_all(head_copies(h))
+        return carry
+
+    lax.fori_loop(0, 1, one_head, 0)
+    cot_step(2)
+    relay(1)
+    lax.fori_loop(1, heads, one_head, 0)
+    a_land[c] = a_send[c]
+    stored = moves(
+        [
+            (xw, xw_out),
+            (wq, wq_out),
+            (qkv_s, qkv_out),
+            (o_s, o_out),
+            (lse_s, lse_out),
+            (cos_s, cos_out),
+            (sin_s, sin_out),
+            (meta_s, meta_out),
+        ],
+        local_sem.at[pl.ds(4, 8)],
+    )
+    start_all(stored)
+    cot_step(3)
+    wait_all(wo_hand)
+    hand_over(0)
+    for h in range(heads):
+        wait_all(head_copies(h))
+    mixed = jnp.concatenate([unpack_head(a_land[i, h]) for i in range(cols) for h in range(heads)], axis=1)
+    mixed_s[...] = mixed
+    middle = x_ref[...].astype(F32) + mm(mixed, wo[...], NT)
+    middle_s[...] = middle
+    n2_s[...] = (middle * norm_rows(middle) * fgain).astype(BF)
+    n_step, n_drain = gather_chain(n2_s, n2w_ref, n_send, n_recv, cols)
+    n_step(0)
+    wait_all(prev_copies)
+    stored_late = moves(
+        [(n2_s, n2w_ref.at[c]), (wo, wo_out), (mixed_s, mixed_out), (middle_s, middle_out), (prevw, prevw_out)],
+        local_sem.at[pl.ds(12, 5)],
+    )
+    start_all(stored_late)
+    relay(2)
+    n_step(1)
+    hand_over(1)
+    n_step(2)
+    hand_over(2)
+    n_step(3)
+    x_drain()
+    n_drain()
+    cot_drain()
+    for copy in wq_push + wo_push:
+        copy.wait_send()
+    for t in range(3):
+        for copy in to_near(t) + to_far(t):
+            copy.wait_send()
+        wait_all(to_other_core(t))
+    wait_all(kept + cot_kept + stored + stored_late)
+
+
+def first_step(cols, ranks, x, cot, router, const, vector, again, fgain, carry, wq, wo, prev, routes, lengths, gate, up, down):
+    local = x.shape[0]
+    rows = local * cols
+    heads, width = 3, 3 * HEAD_DIM
+    experts, depth, ff = gate.shape
+    spots = np.arange(rows, dtype=np.float64)[:, None]
+    pair = np.arange(LANES) % HEAD_DIM // 2
+    freq = np.exp(-(2.0 * pair / HEAD_DIM) * math.log(BASE))[None, :]
+    tables = [np.cos(spots * freq), np.sin(spots * freq), freq]
+    tables = [jnp.asarray(value.astype(np.float32)) for value in tables]
+    vm = pl.BlockSpec(memory_space=pltpu.VMEM)
+    dma = pltpu.SemaphoreType.DMA
+    return pl.pallas_call(
+        functools.partial(first_kernel, cols, ranks),
+        out_shape=(
+            jax.ShapeDtypeStruct((3, experts, D, ff), BF),
+            jax.ShapeDtypeStruct((3 * heads, rows, HEAD_DIM), BF),
+            jax.ShapeDtypeStruct((heads, rows, HEAD_DIM), BF),
+            jax.ShapeDtypeStruct((rows, LANES), F32),
+            jax.ShapeDtypeStruct((cols, local, D), BF),
+            jax.ShapeDtypeStruct((D, 3 * width), BF),
+            jax.ShapeDtypeStruct((D, D), BF),
+            jax.ShapeDtypeStruct((rows, LANES), F32),
+            jax.ShapeDtypeStruct((rows, LANES), F32),
+            jax.ShapeDtypeStruct((rows, LANES), F32),
+            jax.ShapeDtypeStruct((experts, rows), jnp.int32),
+            jax.ShapeDtypeStruct((local, D), BF),
+            jax.ShapeDtypeStruct((local, D), F32),
+            jax.ShapeDtypeStruct((cols, local, D), BF),
+            jax.ShapeDtypeStruct((cols, 16, local), BF),
+            jax.ShapeDtypeStruct((cols, local // EARLY, D), BF),
+            jax.ShapeDtypeStruct((LANES, D), BF),
+            jax.ShapeDtypeStruct((16, LANES), BF),
+        ),
+        in_specs=[vm] * 12 + [pl.BlockSpec(memory_space=pltpu.SMEM)] + [vm] * 3 + [ANY] * 3,
+        out_specs=(ANY,) * 10 + (vm,) + (ANY,) * 5 + (vm, vm),
+        scratch_shapes=[
+            pltpu.VMEM((cols, local, D), BF),
+            pltpu.VMEM((3, depth, width), BF),
+            pltpu.VMEM((3, depth, width), BF),
+            pltpu.VMEM((depth, width), BF),
+            pltpu.VMEM((cols, depth, width), BF),
+            pltpu.VMEM((D, 3 * width), BF),
+            pltpu.VMEM((D, D), BF),
+            pltpu.VMEM((cols, heads, local // 2, LANES), BF),
+            pltpu.VMEM((cols, heads, local // 2, LANES), BF),
+            pltpu.VMEM((16, local), BF),
+            pltpu.VMEM((cols, 16, local), BF),
+            pltpu.VMEM((3 * heads, rows, HEAD_DIM), BF),
+            pltpu.VMEM((heads, rows, HEAD_DIM), BF),
+            pltpu.VMEM((rows, LANES), F32),
+            pltpu.VMEM((rows, LANES), F32),
+            pltpu.VMEM((rows, LANES), F32),
+            pltpu.VMEM((rows, LANES), F32),
+            pltpu.VMEM((local, D), BF),
+            pltpu.VMEM((local, D), F32),
+            pltpu.VMEM((local, D), BF),
+            pltpu.VMEM((3, experts, depth, ff), BF),
+            dma((17,)),
+            dma((2, cols - 1)),
+            dma((2, cols - 1)),
+            dma((2, cols - 1)),
+            dma((2, cols - 1)),
+            dma((2, cols - 1)),
+            dma((2, cols - 1)),
+            dma((2,)),
+            dma((2,)),
+            dma((2, cols - 1)),
+            dma((2, cols - 1)),
+            dma((2, 7)),
+            dma((2, 7)),
+            dma((3, 2)),
+            dma((3, 2)),
+            dma((3, 2)),
+            dma((3, 2)),
+            dma((3, 4)),
+            dma((3, 4)),
+            dma((heads, cols - 1)),
+            dma((heads, cols - 1)),
+        ],
+        compiler_params=pltpu.CompilerParams(
+            vmem_limit_bytes=60 * MIB, collective_id=5, has_side_effects=True
+        ),
+        cost_estimate=pl.CostEstimate(
+            flops=8 * heads * rows * rows * HEAD_DIM, bytes_accessed=40 * MIB, transcendentals=heads * rows * rows
+        ),
+        name="first_step",
+    )(x, cot, router, const, vector, again, fgain, carry, wq, wo, prev, routes, lengths, *tables, gate, up, down)
+
+
+def experts_forward_kernel(
+    cols,
+    capacity,
+    n2_ref,
+    prev_ref,
+    cot_ref,
+    rw_ref,
+    carry_ref,
+    slots_ref,
+    meta_ref,
+    w_ref,
+    x_ref,
+    gu_ref,
+    y_ref,
+    gates_ref,
+    cotb_ref,
+    send,
+    recv,
+    local_sem,
+):
+    e = pl.program_id(0)
+    experts = pl.num_programs(0)
+    r, c = place()
+    early = cot_ref.shape[0] // EARLY
+    late = cot_ref.at[pl.ds(early, cot_ref.shape[0] - early)]
+    step, drain = gather_chain(late, cotb_ref, send, recv, cols)
+    own_copy = pltpu.make_async_copy(late, cotb_ref.at[c], local_sem.at[0])
+
+    @pl.when(e == 0)
+    def _():
+        greet(col_peers(cols))
+        own_copy.start()
+        step(0)
+        prev = jnp.concatenate([mm(prev_ref[i], carry_ref[...], TN) for i in range(cols)], axis=0)
+        g = gate_lanes(mm(n2_ref[...], rw_ref[...], NT) + prev, meta_ref[...])
+        high = g.astype(BF)
+        gates_ref[:, :LANES] = high
+        gates_ref[:, LANES:] = (g - high.astype(F32)).astype(BF)
+
+    @pl.when(e == 3)
+    def _():
+        step(1)
+
+    @pl.when(e == 6)
+    def _():
+        step(2)
+
+    one = slot_rows(slots_ref, e, capacity)
+    x = mm(one, n2_ref[...]).astype(BF)
+    x_ref[0] = x
+    sg = slot_gates(one, gates_ref, e)
+    g = mm(x, w_ref[0, 0])
+    u = mm(x, w_ref[1, 0])
+    gu_ref[0, 0] = g.astype(BF)
+    gu_ref[0, 1] = u.astype(BF)
+    gh = (g * jax.nn.sigmoid(g) * u * sg).astype(BF)
+    y_ref[0] = mm(gh, w_ref[2, 0], NT).astype(BF)
+
+    @pl.when(e == experts - 1)
+    def _():
+        for k in range(3, cols):
+            step(k)
+        drain()
+        own_copy.wait()
+
+
+def experts_forward(cols, n2, prev, cot, rw, carry, meta, slots, w_all):
+    rows = n2.shape[0]
+    capacity = rows // 4
+    three, experts, deep, ff = w_all.shape
+    local = rows // cols
+    rest = local - local // EARLY
+    return pl.pallas_call(
+        functools.partial(experts_forward_kernel, cols, capacity),
+        grid=(experts,),
+        out_shape=(
+            jax.ShapeDtypeStruct((experts, capacity, D), BF),
+            jax.ShapeDtypeStruct((experts, 2, capacity, ff), BF),
+            jax.ShapeDtypeStruct((experts, capacity, D), BF),
+            jax.ShapeDtypeStruct((rows, 2 * LANES), BF),
+            jax.ShapeDtypeStruct((cols, rest, D), BF),
+        ),
+        in_specs=[
+            whole((rows, D)),
+            whole((cols, 16, local)),
+            whole((local, D)),
+            whole((LANES, D)),
+            whole((16, LANES)),
+            whole((experts, rows)),
+            whole((rows, LANES)),
+            pl.BlockSpec((three, 1, deep, ff), lambda e: (0, e, 0, 0)),
+        ],
+        out_specs=(
+            pl.BlockSpec((1, capacity, D), lambda e: (e, 0, 0)),
+            pl.BlockSpec((1, 2, capacity, ff), lambda e: (e, 0, 0, 0)),
+            pl.BlockSpec((1, capacity, D), lambda e: (e, 0, 0)),
+            whole((rows, 2 * LANES)),
+            ANY,
+        ),
+        scratch_shapes=[
+            pltpu.SemaphoreType.DMA((2, cols - 1)),
+            pltpu.SemaphoreType.DMA((2, cols - 1)),
+            pltpu.SemaphoreType.DMA((1,)),
+        ],
+        compiler_params=pltpu.CompilerParams(
+            vmem_limit_bytes=60 * MIB, collective_id=1, has_side_effects=True
+        ),
+        cost_estimate=pl.CostEstimate(
+            flops=experts * capacity * 2 * D * (3 * ff + rows),
+            bytes_accessed=40 * MIB,
+            transcendentals=experts * capacity * ff,
+        ),
+        name="experts_forward",
+    )(n2, prev, cot, rw, carry, slots, meta, w_all)
+
+
+def experts_backward_kernel(
+    cols,
+    capacity,
+    cota_ref,
+    cotb_ref,
+    y_ref,
+    gates_ref,
+    slots_ref,
+    meta_ref,
+    w_ref,
+    x_ref,
+    gu_ref,
+    dx_ref,
+    dots_ref,
+    mixsum_ref,
+    gown_ref,
+    sib_ref,
+    hin_ref,
+    cot_s,
+    mix_s,
+    gbuf,
+    out,
+    arrived,
+    send,
+    recv,
+    own_sem,
+    sib_send,
+    sib_recv,
+    cot_sem,
+    lbuf,
+    hbuf,
+    l_sem,
+    hsend,
+    hrecv,
+):
+    e = pl.program_id(0)
+    experts = pl.num_programs(0)
+    r, c = place()
+    core = r % 2
+    local = mix_s.shape[1]
+    early = cota_ref.shape[1]
+    place_now = lax.rem(e, 2)
+    slot, total, drain = reduce_chain(lambda d: mix_s[d], out, arrived, send, recv, cols)
+
+    def own_copy(expert, at):
+        return pltpu.make_async_copy(gbuf.at[at, :, :, core], gown_ref.at[expert], own_sem.at[at])
+
+    def sib_copy(expert, at):
+        return send_to(
+            gbuf.at[at, :, :, 1 - core],
+            sib_ref.at[expert],
+            sib_send.at[at],
+            sib_recv.at[expert],
+            (flip(r, 1), c),
+        )
+
+    cot_loads = moves(
+        [(cota_ref.at[d], cot_s.at[pl.ds(d * local, early)]) for d in range(cols)]
+        + [(cotb_ref.at[d], cot_s.at[pl.ds(d * local + early, local - early)]) for d in range(cols)],
+        cot_sem,
+    )
+    before = jnp.maximum(e - 1, 0)
+    sib_load = pltpu.make_async_copy(sib_ref.at[before], lbuf, l_sem.at[0])
+    sends_now = (e >= 1) & (e <= SENT_SOON)
+
+    def h_sends(i):
+        return to_chips(lambda there: hbuf.at[i, :, there], hin_ref.at[i], hsend.at[i], hrecv.at[i])
+
+    @pl.when(e == 0)
+    def _():
+        start_all(cot_loads)
+        greet(col_peers(cols) + [(flip(r, m), c) for m in (1, 2, 4, 6)])
+        for n, d in enumerate((3, 0, 2, 1)):
+            mix_s[d] = combine(meta_ref, y_ref, d, local)
+            if n == 1:
+                slot(0)
+        wait_all(cot_loads)
+
+    @pl.when(e == 2)
+    def _():
+        slot(1)
+
+    @pl.when(e == 5)
+    def _():
+        slot(2)
+
+    one = slot_rows(slots_ref, e, capacity)
+    ct = mm(one, cot_s[...]).astype(BF)
+    sg = slot_gates(one, gates_ref, e)
+    x = x_ref[0]
+
+    @pl.when(sends_now)
+    def _():
+        sib_copy(before, 1 - place_now).wait_recv()
+        sib_load.start()
+
+    g, u = gu_ref[0, 0].astype(F32), gu_ref[0, 1].astype(F32)
+    v = mm(ct, w_ref[2, 0])
+    sig = jax.nn.sigmoid(g)
+    act = g * sig
+    h = act * u
+    dot = jnp.sum(h * v, axis=1, keepdims=True)
+    dots_ref[pl.ds(e, 1)] = jnp.sum(one.astype(F32) * dot, axis=0, keepdims=True)
+    gh = (h * sg).astype(BF)
+    gv = v * sg
+    dg = (gv * u * (sig * (1.0 + g * (1.0 - sig)))).astype(BF)
+    du = (gv * act).astype(BF)
+    dx_ref[0] = (mm(dg, w_ref[0, 0], NT) + mm(du, w_ref[1, 0], NT)).astype(BF)
+
+    @pl.when(e >= 2)
+    def _():
+        own_copy(e - 2, place_now).wait()
+        sib_copy(e - 2, place_now).wait_send()
+
+    shape = gbuf.shape[2:]
+    gbuf[place_now, 0] = mm(x, dg, TN).astype(BF).reshape(shape)
+    gbuf[place_now, 1] = mm(x, du, TN).astype(BF).reshape(shape)
+    gbuf[place_now, 2] = mm(ct, gh, TN).astype(BF).reshape(shape)
+    own_copy(e, place_now).start()
+    sib_copy(e, place_now).start()
+
+    @pl.when(sends_now)
+    def _():
+        sib_load.wait()
+        hbuf[before] = (gbuf[1 - place_now, :, :, core].astype(F32) + lbuf[...].astype(F32)).astype(BF)
+        start_all(h_sends(before))
+
+    @pl.when(e == experts - 1)
+    def _():
+        for s in range(3, cols):
+            slot(s)
+        total(mixsum_ref)
+        drain()
+        for back in (1, 0):
+            own_copy(e - back, lax.rem(e - back, 2)).wait()
+            sib_copy(e - back, lax.rem(e - back, 2)).wait_send()
+        for i in range(SENT_SOON, EXPERTS):
+            sib_copy(i, i % 2).wait_recv()
+        for i in range(SENT_SOON):
+            wait_all(h_sends(i))
+
+
+def experts_backward(cols, ranks, cota, cotb, y, gates, meta, slots, w_all, x, gu):
+    experts, capacity, _ = y.shape
+    rows = slots.shape[1]
+    three, _, deep, ff = w_all.shape
+    local = rows // cols
+    chips = ranks // 2
+    depth = deep // ranks
+    half = jax.ShapeDtypeStruct((experts, three, chips, depth, ff), BF)
+    return pl.pallas_call(
+        functools.partial(experts_backward_kernel, cols, capacity),
+        grid=(experts,),
+        out_shape=(
+            jax.ShapeDtypeStruct((experts, capacity, D), BF),
+            jax.ShapeDtypeStruct((experts, rows), F32),
+            jax.ShapeDtypeStruct((local, D), F32),
+            half,
+            half,
+            jax.ShapeDtypeStruct((SENT_SOON, 3, three, depth, ff), BF),
+        ),
+        in_specs=[
+            ANY,
+            ANY,
+            whole((experts, capacity, D)),
+            whole((rows, 2 * LANES)),
+            whole((experts, rows)),
+            whole((rows, LANES)),
+            pl.BlockSpec((three, 1, deep, ff), lambda e: (0, e, 0, 0)),
+            pl.BlockSpec((1, capacity, D), lambda e: (e, 0, 0)),
+            pl.BlockSpec((1, 2, capacity, ff), lambda e: (e, 0, 0, 0)),
+        ],
+        out_specs=(
+            pl.BlockSpec((1, capacity, D), lambda e: (e, 0, 0)),
+            whole((experts, rows)),
+            whole((local, D)),
+            ANY,
+            ANY,
+            ANY,
+        ),
+        scratch_shapes=[
+            pltpu.VMEM((rows, D), BF),
+            pltpu.VMEM((cols, local, D), BF),
+            pltpu.VMEM((2, three, chips, 2, depth, ff), BF),
+            *chain_scratch(cols, local),
+            pltpu.SemaphoreType.DMA((2,)),
+            pltpu.SemaphoreType.DMA((2,)),
+            pltpu.SemaphoreType.DMA((experts,)),
+            pltpu.SemaphoreType.DMA((2 * cols,)),
+            pltpu.VMEM((three, chips, depth, ff), BF),
+            pltpu.VMEM((SENT_SOON, three, chips, depth, ff), BF),
+            pltpu.SemaphoreType.DMA((1,)),
+            pltpu.SemaphoreType.DMA((SENT_SOON, 3)),
+            pltpu.SemaphoreType.DMA((SENT_SOON, 3)),
+        ],
+        compiler_params=pltpu.CompilerParams(
+            vmem_limit_bytes=60 * MIB, collective_id=2, has_side_effects=True
+        ),
+        cost_estimate=pl.CostEstimate(
+            flops=experts * capacity * 4 * D * (3 * ff + rows),
+            bytes_accessed=60 * MIB,
+            transcendentals=experts * capacity * ff,
+        ),
+        name="experts_backward",
+    )(cota, cotb, y, gates, slots, meta, w_all, x, gu)
+
+
+def resid_kernel(
+    cols,
+    count,
+    dx_ref,
+    meta_ref,
+    dots_ref,
+    rw_ref,
+    prev_ref,
+    carry_ref,
+    cot_ref,
+    mixsum_in,
+    n2w_in,
+    middle_in,
+    out_t_in,
+    mixed_in,
+    gown_ref,
+    sib_ref,
+    layer_ref,
+    resid_ref,
+    gm_ref,
+    og_ref,
+    small_ref,
+    pg_ref,
+    hin_ref,
+    hrest_ref,
+    mixsum,
+    n2_s,
+    middle_s,
+    out_t,
+    mixed_s,
+    resid_s,
+    load_sem,
+    gt_s,
+    out,
+    arrived,
+    send,
+    recv,
+    dots_in,
+    dsend,
+    drecv,
+    grad,
+    gm_out,
+    gsend,
+    grecv,
+    gm_sem,
+    lbuf,
+    hbuf,
+    hload,
+    hsend,
+    hrecv,
+    hkeep,
+):
+    r, c = place()
+    chip = r // 2
+    local = cot_ref.shape[0]
+    held = hbuf.shape[0]
+    loads = moves(
+        [
+            (n2w_in.at[c], n2_s),
+            (middle_in, middle_s),
+            (mixsum_in, mixsum),
+            (out_t_in, out_t),
+            (mixed_in, mixed_s),
+        ],
+        load_sem,
+    )
+    greet(col_peers(cols) + [(flip(r, 2 * k), c) for k in range(1, 4)])
+    slot, total, drain = reduce_chain(lambda d: gt_s[d], out, arrived, send, recv, cols)
+
+    def dots_of(d):
+        return dots_ref.at[:, pl.ds(pl.multiple_of(d * local, LANES), local)]
+
+    dot_copies = to_cols(dots_of, dots_in, dsend, drecv, cols)
+    start_all(dot_copies)
+    dots_in[c] = dots_of(c)[...]
+    for n, d in enumerate((3, 0, 2, 1)):
+        gt_s[d] = combine(meta_ref, dx_ref, d, local)
+        if n == 1:
+            slot(0)
+
+    def h_loads(i):
+        at = lax.rem(i, 2)
+        return [
+            pltpu.make_async_copy(ref.at[SENT_SOON + i], lbuf.at[at, j], hload.at[at, j])
+            for j, ref in enumerate((gown_ref, sib_ref))
+        ]
+
+    def h_sends(i):
+        return to_chips(lambda there: hbuf.at[i, :, there], hin_ref.at[i], hsend.at[i], hrecv.at[i])
+
+    def h_keeps(i):
+        return moves(
+            [(hbuf.at[i, :, flip(chip, k)], hrest_ref.at[i - count, k - 1]) for k in range(1, 4)],
+            hkeep.at[i - count],
+        )
+
+    start_all(h_loads(0))
+
+    def add_cores(i, carry):
+        @pl.when(i + 1 < held)
+        def _():
+            start_all(h_loads(i + 1))
+
+        wait_all(h_loads(i))
+        at = lax.rem(i, 2)
+        hbuf[i] = (lbuf[at, 0].astype(F32) + lbuf[at, 1].astype(F32)).astype(BF)
+
+        @pl.when(i < count)
+        def _():
+            start_all(h_sends(i))
+
+        @pl.when(i >= count)
+        def _():
+            start_all(h_keeps(jnp.maximum(i, count)))
+
+        return carry
+
+    lax.fori_loop(0, held, add_cores, 0)
+    start_all(loads)
+    slot(1)
+    wait_all(loads)
+
+    meta = meta_ref[pl.ds(pl.multiple_of(c * local, LANES), local)]
+    n2, cot = n2_s[...], cot_ref[...]
+    n2f, cotf = n2.astype(F32), cot.astype(F32)
+    middle = middle_s[...]
+    rw = rw_ref[...]
+    lin = mm(n2, rw, NT)
+    prev = prev_ref[c]
+    gates = gate_lanes(lin + mm(prev, carry_ref[...], TN), meta)
+    lane = lane_iota((local, LANES))
+    cot_lin = mm(cot, rw, NT)
+    dot_keep = jnp.sum(cotf * n2f, axis=1, keepdims=True)
+    wait_all(dot_copies)
+    d = jnp.concatenate([all_sum(dots_in, cols), jnp.zeros((LANES - EXPERTS, local), F32)], axis=0).T
+    g_gates = jnp.where(lane == EXPERTS + 1, dot_keep, d)
+    keep = gates[:, EXPERTS + 1 : EXPERTS + 2]
+    mixes, packs = [], jnp.zeros((local, LANES), F32)
+    for j in range(2):
+        l0 = lin[:, ROW_CONST + 2 * j : ROW_CONST + 2 * j + 1]
+        l1 = lin[:, ROW_CONST + 2 * j + 1 : ROW_CONST + 2 * j + 2]
+        top = jnp.maximum(l0, l1)
+        e0, e1 = jnp.exp(l0 - top), jnp.exp(l1 - top)
+        a0, a1 = e0 / (e0 + e1), e1 / (e0 + e1)
+        share = gates[:, EXPERTS + 2 + j : EXPERTS + 3 + j]
+        dot_vec = cot_lin[:, ROW_VEC + j : ROW_VEC + j + 1]
+        keep = keep + share * a0
+        mixes.append(share * a1)
+        g_gates = jnp.where(lane == EXPERTS + 2 + j, a0 * dot_keep + a1 * dot_vec, g_gates)
+        gk, gv = share * dot_keep, share * dot_vec
+        mean = a0 * gk + a1 * gv
+        packs = packs + jnp.where(lane == ROW_CONST + 2 * j, a0 * (gk - mean), 0.0)
+        packs = packs + jnp.where(lane == ROW_CONST + 2 * j + 1, a1 * (gv - mean), 0.0)
+        packs = packs + jnp.where(lane == ROW_VEC + j, share * a1, 0.0)
+    packs = packs + gates * (g_gates - jnp.sum(gates * g_gates, axis=1, keepdims=True))
+    vec = rw[ROW_VEC : ROW_VEC + 2].astype(F32)
+    layer = middle + mixsum[...] + keep * n2f + mixes[0] * vec[0:1] + mixes[1] * vec[1:2]
+    layer_ref[...] = layer.astype(BF)
+
+    high = packs.astype(BF)
+    low = (packs - high.astype(F32)).astype(BF)
+    back = lane < ROW_VEC
+    high_b = jnp.where(back, packs, 0.0).astype(BF)
+    low_b = jnp.where(back, packs - high.astype(F32), 0.0).astype(BF)
+    grad_local = keep * cotf + mm(high_b, rw) + mm(low_b, rw)
+    by_n2 = mm(high, n2, TN) + mm(low, n2, TN)
+    by_cot = mm(high, cot, TN) + mm(low, cot, TN)
+    by_prev = mm(prev, high) + mm(prev, low)
+    pg = mm(carry_ref[...], high_b, NT) + mm(carry_ref[...], low_b, NT)
+    pg_ref[...] = pg[:ROUTES]
+    sub = lax.broadcasted_iota(jnp.int32, (SMALL_ROWS, D), 0)
+    small_ref[:, :D] = jnp.where(sub < ROW_VEC, by_n2[:SMALL_ROWS], by_cot[:SMALL_ROWS])
+    small_ref[:16, D : D + LANES] = by_prev
+    small_ref[16:, D : D + LANES] = jnp.zeros((SMALL_ROWS - 16, LANES), F32)
+    small_ref[:, D + LANES :] = jnp.zeros((SMALL_ROWS, LANES), F32)
+    fgain = rw[ROW_GAIN + 1 : ROW_GAIN + 2].astype(F32)
+    scale = norm_rows(middle)
+
+    for s in range(2, cols):
+        slot(s)
+    total(grad)
+    grad_normed = grad[...] + grad_local
+    gained = grad_normed * fgain
+    mid_dot = jnp.sum(gained * middle, axis=1, keepdims=True)
+    resid = cotf + scale * gained - middle * (scale * scale * scale * (mid_dot * (1.0 / D)))
+    cut = resid.astype(BF)
+    gm = (mm(cut, out_t[...]) * meta[:, META_VALID : META_VALID + 1]).astype(BF)
+    width = D // cols
+    for i in range(cols):
+        for h in range(width // HEAD_DIM):
+            at = i * width + h * HEAD_DIM
+            gm_out[i, h] = pack_head(gm[:, at : at + HEAD_DIM])
+    gm_copies = to_cols(lambda i: gm_out.at[i], gm_ref, gsend, grecv, cols)
+    start_all(gm_copies)
+    resid_s[...] = resid
+    stored = moves([(gm_out.at[c], gm_ref.at[c]), (resid_s, resid_ref)], gm_sem)
+    start_all(stored)
+    small_ref[ROW_GAIN : ROW_GAIN + 1, :D] = jnp.sum(grad_normed * middle * scale, axis=0, keepdims=True)
+    og_ref[...] = mm(cut, mixed_s[...], TN).astype(BF)
+    wait_all(stored + gm_copies)
+    drain()
+
+    def end(i, carry):
+        @pl.when(i < count)
+        def _():
+            wait_all(h_sends(i))
+
+        @pl.when(i >= count)
+        def _():
+            wait_all(h_keeps(jnp.maximum(i, count)))
+
+        return carry
+
+    lax.fori_loop(0, held, end, 0)
+
+
+def resid_step(cols, dx, meta, dots, rw, prev, carry, cot, mixsum, n2w, middle, out_t, mixed, gown, sib):
+    local = cot.shape[0]
+    experts, three, chips, depth, ff = gown.shape
+    count, held = SENT_NEXT, experts - SENT_SOON
+    vm = pl.BlockSpec(memory_space=pltpu.VMEM)
+    dma = pltpu.SemaphoreType.DMA
+    return pl.pallas_call(
+        functools.partial(resid_kernel, cols, count),
+        out_shape=(
+            jax.ShapeDtypeStruct((local, D), BF),
+            jax.ShapeDtypeStruct((local, D), F32),
+            jax.ShapeDtypeStruct((cols, 3, local // 2, LANES), BF),
+            jax.ShapeDtypeStruct((D, D), BF),
+            jax.ShapeDtypeStruct((SMALL_ROWS, D + 2 * LANES), F32),
+            jax.ShapeDtypeStruct((ROUTES, local), F32),
+            jax.ShapeDtypeStruct((count, 3, three, depth, ff), BF),
+            jax.ShapeDtypeStruct((held - count, 3, three, depth, ff), BF),
+        ),
+        in_specs=[vm] * 7 + [ANY] * 7,
+        out_specs=(vm, ANY, ANY, vm, vm, vm, ANY, ANY),
+        scratch_shapes=[
+            pltpu.VMEM((local, D), F32),
+            pltpu.VMEM((local, D), BF),
+            pltpu.VMEM((local, D), F32),
+            pltpu.VMEM((D, D), BF),
+            pltpu.VMEM((local, D), BF),
+            pltpu.VMEM((local, D), F32),
+            dma((5,)),
+            pltpu.VMEM((cols, local, D), BF),
+            *chain_scratch(cols, local),
+            pltpu.VMEM((cols, EXPERTS, local), F32),
+            dma((cols - 1,)),
+            dma((cols - 1,)),
+            pltpu.VMEM((local, D), F32),
+            pltpu.VMEM((cols, 3, local // 2, LANES), BF),
+            dma((cols - 1,)),
+            dma((cols - 1,)),
+            dma((2,)),
+            pltpu.VMEM((2, 2, three, chips, depth, ff), BF),
+            pltpu.VMEM((held, three, chips, depth, ff), BF),
+            dma((2, 2)),
+            dma((count, 3)),
+            dma((count, 3)),
+            dma((held - count, 3)),
+        ],
+        compiler_params=pltpu.CompilerParams(
+            vmem_limit_bytes=60 * MIB, collective_id=3, has_side_effects=True
+        ),
+        cost_estimate=pl.CostEstimate(flops=6 * local * D * D, bytes_accessed=40 * MIB, transcendentals=0),
+        name="resid_step",
+    )(dx, meta, dots, rw, prev, carry, cot, mixsum, n2w, middle, out_t, mixed, gown, sib)
+
+
+def finish_kernel(
+    cols,
+    ranks,
+    gm_ref,
+    meta_ref,
+    lse_ref,
+    small_ref,
+    og_ref,
+    xown_ref,
+    rw_ref,
+    qkv_in,
+    o_in,
+    x_in,
+    w_in,
+    cos_in,
+    sin_in,
+    resid_in,
+    gown_ref,
+    sib_ref,
+    hsoon_ref,
+    hin0_ref,
+    hrest_ref,
+    ig_ref,
+    small_out,
+    qg_out,
+    og_out,
+    gg_ref,
+    ug_ref,
+    dg_ref,
+    hin_ref,
+    qkv_s,
+    o_s,
+    x_s,
+    w_s,
+    cos_s,
+    sin_s,
+    resid_s,
+    head_sem,
+    load_sem,
+    do_s,
+    dq_s,
+    dk_s,
+    dv_s,
+    gn_s,
+    qg_acc,
+    qg_cut,
+    out,
+    arrived,
+    send,
+    recv,
+    small_s,
+    small_rows,
+    small_cols,
+    small_all,
+    og_sib,
+    og_half,
+    og_chips,
+    og_parts,
+    og_cols,
+    qg_sib,
+    qg_half,
+    qg_chips,
+    q_parts,
+    q_land,
+    total_s,
+    fbuf,
+    fsem,
+    row_send,
+    row_recv,
+    chip_send,
+    chip_recv,
+    sib_send,
+    sib_recv,
+    col_send,
+    col_recv,
+    hsend,
+    hrecv,
+):
+    r, c = place()
+    chip, core = r // 2, r % 2
+    heads = 3
+    rows = meta_ref.shape[0]
+    local = rows // cols
+    width = heads * HEAD_DIM
+    rest = hrest_ref.shape[0]
+    first = gown_ref.shape[0] - rest
+    score_scale = 1.0 / math.sqrt(HEAD_DIM)
+
+    def head_loads(h):
+        pairs = [(qkv_in.at[i * heads + h], qkv_s.at[i * heads + h]) for i in range(3)]
+        return moves(pairs + [(o_in.at[h], o_s.at[h])], head_sem.at[h])
+
+    loads = moves(
+        [(x_in, x_s), (w_in, w_s), (cos_in, cos_s), (sin_in, sin_s), (resid_in, resid_s)], load_sem
+    )
+    start_all(head_loads(0))
+    greet(col_peers(cols) + [(flip(r, m), c) for m in range(1, ranks)])
+    for h in range(1, heads):
+        start_all(head_loads(h))
+    start_all(loads)
+
+    def to_sibling(src, dst, at):
+        return send_to(src.at[:, 1 - core], dst, sib_send.at[at], sib_recv.at[at], (flip(r, 1), c))
+
+    og_across = to_sibling(og_ref, og_sib, 0)
+    og_across.start()
+
+    for d in range(cols):
+        at = slice(d * local, (d + 1) * local)
+        for h in range(heads):
+            do_s[h, at] = unpack_head(gm_ref[d, h])
+
+    def halves(ref, sib, half):
+        for k in range(ranks // 2):
+            half[k] = (ref[k, core].astype(F32) + sib[k].astype(F32)).astype(BF)
+
+    og_across.wait()
+    halves(og_ref, og_sib, og_half)
+    og_to_chips = to_chips(lambda there: og_half.at[there], og_chips, chip_send.at[0], chip_recv.at[0])
+    start_all(og_to_chips)
+
+    def h_sends(i):
+        r_, c_ = place()
+        return [
+            send_to(
+                hrest_ref.at[i, k - 1],
+                hin_ref.at[i, k - 1],
+                hsend.at[i, k - 1],
+                hrecv.at[i, k - 1],
+                (flip(r_, 2 * k), c_),
+            )
+            for k in range(1, 4)
+        ]
+
+    def start_sends(i, carry):
+        start_all(h_sends(i))
+        return carry
+
+    lax.fori_loop(0, rest, start_sends, 0)
+
+    blocks = rows // Q_ROWS
+
+    def one_head(h, carry):
+        wait_all(head_loads(h))
+        for i in reversed(range(blocks)):
+            at = slice(i * Q_ROWS, (i + 1) * Q_ROWS)
+            length = (i + 1) * Q_ROWS
+            q, do = qkv_s[h, at], do_s[h, at]
+            k, v = qkv_s[heads + h, :length], qkv_s[2 * heads + h, :length]
+            delta = jnp.sum(do.astype(F32) * o_s[h, at].astype(F32), axis=1, keepdims=True)
+            lse = jnp.sum(jnp.where(lane_iota((Q_ROWS, LANES)) == h, lse_ref[at], 0.0), axis=1, keepdims=True)
+            s = mm(q, k, NT)
+            ok = seen(column(meta_ref, at, META_BEGIN).astype(jnp.int32), i * Q_ROWS, Q_ROWS, length)
+            p = jnp.where(ok, jnp.exp(s - lse), 0.0)
+            ds = (p * (mm(do, v, NT) - delta)).astype(BF)
+            dq_s[h, at] = mm(ds, k) * score_scale
+            dk, dv = mm(ds, q, TN), mm(p.astype(BF), do, TN)
+            if i == blocks - 1:
+                dk_s[h], dv_s[h] = dk, dv
+            else:
+                dk_s[h, :length] += dk
+                dv_s[h, :length] += dv
+        return carry
+
+    lax.fori_loop(0, heads, one_head, 0)
+
+    slot, total, drain = reduce_chain(lambda d: gn_s[d], out, arrived, send, recv, cols)
+    wait_all(loads)
+    gain_total = jnp.zeros((1, D), F32)
+    weight = w_s[...]
+    again = rw_ref[ROW_GAIN : ROW_GAIN + 1].astype(F32)
+    for n, d in enumerate((3, 0, 2, 1)):
+        at = slice(d * local, (d + 1) * local)
+        cosine, sines = cos_s[at], sin_s[at]
+        turned = [dq_s[h, at] for h in range(heads)] + [dk_s[h, at] for h in range(heads)]
+        parts = []
+        for part in range(heads):
+            v = jnp.concatenate(turned[2 * part : 2 * part + 2], axis=1)
+            parts.append((v * cosine - swap_pairs(v) * sines).astype(BF))
+        parts += [dv_s[h, at].astype(BF) for h in range(heads)]
+        gp = jnp.concatenate(parts, axis=1)
+        x = x_s[d].astype(F32)
+        xs = x * norm_rows(x)
+        gn = mm(gp, weight, NT)
+        gn_s[d] = gn.astype(BF)
+        if n == 1:
+            slot(0)
+        gain_total = gain_total + jnp.sum(gn * xs, axis=0, keepdims=True)
+        grad = mm((xs * again).astype(BF), gp, TN)
+        if n == 0:
+            qg_acc[...] = grad
+        else:
+            qg_acc[...] += grad
+    qg_cut[...] = qg_acc[...].astype(BF).reshape(qg_cut.shape)
+    qg_across = to_sibling(qg_cut, qg_sib, 1)
+    qg_across.start()
+
+    sub = lax.broadcasted_iota(jnp.int32, (SMALL_ROWS, D), 0)
+    for i in range(ranks):
+        block = small_ref[:, i * LANES : (i + 1) * LANES]
+        if i < D // LANES:
+            own = sub[:, :LANES] == ROW_GAIN + 1
+            block = jnp.where(own, gain_total[:, i * LANES : (i + 1) * LANES], block)
+        small_s[i] = block
+    small_to_rows = to_rows(lambda d: small_s.at[d], small_rows, row_send.at[0], row_recv.at[0], ranks)
+    start_all(small_to_rows)
+    small_rows[r] = small_s[r]
+    slot(1)
+
+    def sum_grads(low, high, hin, base):
+        def f_loads(i):
+            at = lax.rem(i, 2)
+            return moves(
+                [
+                    (gown_ref.at[i, :, chip], fbuf.at[at, 0]),
+                    (sib_ref.at[i, :, chip], fbuf.at[at, 1]),
+                    (hin.at[i - base], fbuf.at[at, pl.ds(2, 3)]),
+                ],
+                fsem.at[at],
+            )
+
+        start_all(f_loads(low))
+
+        def body(i, carry):
+            @pl.when(i + 1 < high)
+            def _():
+                start_all(f_loads(jnp.minimum(i + 1, high - 1)))
+
+            wait_all(f_loads(i))
+            at = lax.rem(i, 2)
+            total_grad = fbuf[at, 0].astype(F32)
+            for j in range(1, 5):
+                total_grad = total_grad + fbuf[at, j].astype(F32)
+            gg_ref[i] = total_grad[0]
+            ug_ref[i] = total_grad[1]
+            dg_ref[i] = total_grad[2]
+            return carry
+
+        lax.fori_loop(low, high, body, 0)
+
+    qg_across.wait()
+    halves(qg_cut, qg_sib, qg_half)
+    qg_to_chips = to_chips(lambda there: qg_half.at[there], qg_chips, chip_send.at[1], chip_recv.at[1])
+    start_all(qg_to_chips)
+    wait_all(small_to_rows)
+    small_cols[c] = all_sum(small_rows, ranks)
+    small_to_cols = to_cols(lambda d: small_cols.at[c], small_cols, col_send.at[0], col_recv.at[0], cols)
+    start_all(small_to_cols)
+    wait_all(og_to_chips)
+    og_sum = og_ref[chip, core].astype(F32) + og_sib[chip].astype(F32) + all_sum(og_chips, 3)
+    for i in range(cols):
+        og_parts[i] = og_sum[:, i * width : (i + 1) * width]
+    og_to_cols = to_cols(lambda d: og_parts.at[d], og_cols, col_send.at[1], col_recv.at[1], cols)
+    start_all(og_to_cols)
+    og_cols[c] = og_parts[c]
+    sum_grads(0, SENT_SOON, hsoon_ref, 0)
+    sum_grads(SENT_SOON, first, hin0_ref, SENT_SOON)
+    slot(2)
+    wait_all(qg_to_chips)
+    q_sum = qg_cut[chip, core].astype(F32) + qg_sib[chip].astype(F32) + all_sum(qg_chips, 3)
+    for i in range(3):
+        q_parts[i] = q_sum[:, i * width : (i + 1) * width]
+    odd, high = c % 2, c // 2
+    q_copies = [
+        send_to(
+            q_parts.at[1 - odd + high],
+            q_land.at[1],
+            col_send.at[2, 0],
+            col_recv.at[2, 0],
+            (r, flip(c, 1)),
+        ),
+        send_to(
+            q_parts.at[2 - 2 * high],
+            q_land.at[2 - 2 * odd],
+            col_send.at[2, 1],
+            col_recv.at[2, 1],
+            (r, flip(c, 2)),
+        ),
+    ]
+    start_all(q_copies)
+    q_land[2 * odd] = q_parts[(c + 1) // 2]
+    wait_all(small_to_cols)
+    small_all[r] = all_sum(small_cols, cols)
+    small_back = to_rows(lambda d: small_all.at[r], small_all, row_send.at[1], row_recv.at[1], ranks)
+    start_all(small_back)
+
+    def end_sends(i, carry):
+        wait_all(h_sends(i))
+        return carry
+
+    lax.fori_loop(0, rest, end_sends, 0)
+    sum_grads(first, first + rest, hin_ref, first)
+    wait_all(og_to_cols + q_copies + small_back)
+    og_out[...] = all_sum(og_cols, cols)
+    for i in range(3):
+        qg_out[:, i * width : (i + 1) * width] = q_land[i]
+    for i in range(ranks):
+        small_out[:, i * LANES : (i + 1) * LANES] = small_all[i]
+    slot(3)
+    total(total_s)
+    gn = total_s[...]
+    x = xown_ref[...].astype(F32)
+    scale = norm_rows(x)
+    gained = gn * again
+    x_dot = jnp.sum(gained * x, axis=1, keepdims=True)
+    ig_ref[...] = resid_s[...] + scale * gained - x * (scale * scale * scale * (x_dot * (1.0 / D)))
+    drain()
+
+
+def finish_step(cols, ranks, gm, meta, lse, small, og, xown, rw, qkv, o, x, w, cosine, sines, resid, gown, sib, hsoon, hin0, hrest):
+    rows = meta.shape[0]
+    local = rows // cols
+    experts, three, chips, depth, ff = gown.shape
+    rest = hrest.shape[0]
+    heads, width = 3, 3 * HEAD_DIM
+    vm = pl.BlockSpec(memory_space=pltpu.VMEM)
+    dma = pltpu.SemaphoreType.DMA
+    wide = D + 2 * LANES
+    weight_grad = jax.ShapeDtypeStruct((experts, depth, ff), F32)
+    return pl.pallas_call(
+        functools.partial(finish_kernel, cols, ranks),
+        out_shape=(
+            jax.ShapeDtypeStruct((local, D), F32),
+            jax.ShapeDtypeStruct((SMALL_ROWS, wide), F32),
+            jax.ShapeDtypeStruct((depth, 3 * width), F32),
+            jax.ShapeDtypeStruct((depth, width), F32),
+            weight_grad,
+            weight_grad,
+            weight_grad,
+            jax.ShapeDtypeStruct((rest, 3, three, depth, ff), BF),
+        ),
+        in_specs=[vm] * 7 + [ANY] * 12,
+        out_specs=(vm,) * 7 + (ANY,),
+        scratch_shapes=[
+            pltpu.VMEM((3 * heads, rows, HEAD_DIM), BF),
+            pltpu.VMEM((heads, rows, HEAD_DIM), BF),
+            pltpu.VMEM((cols, local, D), BF),
+            pltpu.VMEM((D, 3 * width), BF),
+            pltpu.VMEM((rows, LANES), F32),
+            pltpu.VMEM((rows, LANES), F32),
+            pltpu.VMEM((local, D), F32),
+            dma((heads, 4)),
+            dma((5,)),
+            pltpu.VMEM((heads, rows, HEAD_DIM), BF),
+            pltpu.VMEM((heads, rows, HEAD_DIM), F32),
+            pltpu.VMEM((heads, rows, HEAD_DIM), F32),
+            pltpu.VMEM((heads, rows, HEAD_DIM), F32),
+            pltpu.VMEM((cols, local, D), BF),
+            pltpu.VMEM((D, 3 * width), F32),
+            pltpu.VMEM((chips, 2, depth, 3 * width), BF),
+            *chain_scratch(cols, local),
+            pltpu.VMEM((ranks, SMALL_ROWS, LANES), F32),
+            pltpu.VMEM((ranks, SMALL_ROWS, LANES), F32),
+            pltpu.VMEM((cols, SMALL_ROWS, LANES), F32),
+            pltpu.VMEM((ranks, SMALL_ROWS, LANES), F32),
+            pltpu.VMEM((chips, depth, D), BF),
+            pltpu.VMEM((chips, depth, D), BF),
+            pltpu.VMEM((3, depth, D), BF),
+            pltpu.VMEM((cols, depth, width), F32),
+            pltpu.VMEM((cols, depth, width), F32),
+            pltpu.VMEM((chips, depth, 3 * width), BF),
+            pltpu.VMEM((chips, depth, 3 * width), BF),
+            pltpu.VMEM((3, depth, 3 * width), BF),
+            pltpu.VMEM((3, depth, width), F32),
+            pltpu.VMEM((3, depth, width), F32),
+            pltpu.VMEM((local, D), F32),
+            pltpu.VMEM((2, 5, three, depth, ff), BF),
+            dma((2, 3)),
+            dma((2, ranks - 1)),
+            dma((2, ranks - 1)),
+            dma((2, 3)),
+            dma((2, 3)),
+            dma((2,)),
+            dma((2,)),
+            dma((3, cols - 1)),
+            dma((3, cols - 1)),
+            dma((rest, 3)),
+            dma((rest, 3)),
+        ],
+        compiler_params=pltpu.CompilerParams(
+            vmem_limit_bytes=62 * MIB, collective_id=4, has_side_effects=True
+        ),
+        cost_estimate=pl.CostEstimate(
+            flops=20 * heads * rows * rows * HEAD_DIM, bytes_accessed=40 * MIB, transcendentals=heads * rows * rows
+        ),
+        name="finish_step",
+    )(gm, meta, lse, small, og, xown, rw, qkv, o, x, w, cosine, sines, resid, gown, sib, hsoon, hin0, hrest)
+
+
+def place_kernel(
+    small_ref,
+    qg_ref,
+    og_ref,
+    pg_ref,
+    layer_in,
+    ig_in,
+    gg_in,
+    ug_in,
+    dg_in,
+    layer_ref,
+    ig_ref,
+    gg_ref,
+    ug_ref,
+    dg_ref,
+    again_ref,
+    qkv_ref,
+    out_ref,
+    fgain_ref,
+    router_ref,
+    carry_ref,
+    const_ref,
+    vector_ref,
+    prev_ref,
+):
+    for src, dst in ((gg_in, gg_ref), (ug_in, ug_ref), (dg_in, dg_ref), (ig_in, ig_ref), (layer_in, layer_ref)):
+        dst[...] = src[...]
+    again_ref[...] = small_ref[ROW_GAIN + 1 : ROW_GAIN + 2, :D].reshape(D)
+    fgain_ref[...] = small_ref[ROW_GAIN : ROW_GAIN + 1, :D].reshape(D)
+    qkv_ref[...] = qg_ref[...]
+    out_ref[...] = og_ref[...].T
+    router_ref[...] = small_ref[:ROUTES, :D]
+    carry_ref[...] = small_ref[:ROUTES, D : D + ROUTES]
+    for j in range(2):
+        const_ref[j] = small_ref[ROW_CONST + 2 * j : ROW_CONST + 2 * j + 2, :D]
+    vector_ref[...] = small_ref[ROW_VEC : ROW_VEC + 2, :D]
+    prev_ref[...] = pg_ref[...]
+
+
+def place_outputs(small, qg, og, pg, layer, ig, gg, ug, dg):
+    vm = pl.BlockSpec(memory_space=pltpu.VMEM)
+    shapes = [layer.shape, ig.shape, gg.shape, ug.shape, dg.shape]
+    shapes += [(D,), qg.shape, og.shape[::-1], (D,), (ROUTES, D), (ROUTES, ROUTES), (2, 2, D), (2, D), pg.shape]
+    return pl.pallas_call(
+        place_kernel,
+        out_shape=[jax.ShapeDtypeStruct(shape, F32 if i else BF) for i, shape in enumerate(shapes)],
+        in_specs=[vm] * 9,
+        out_specs=[vm] * 14,
+        compiler_params=pltpu.CompilerParams(vmem_limit_bytes=48 * MIB),
+        cost_estimate=pl.CostEstimate(flops=0, bytes_accessed=16 * MIB, transcendentals=0),
+        name="place_outputs",
+    )(small, qg, og, pg, layer, ig, gg, ug, dg)
+
+
+def on_device_heads(
+    sizes,
+    inputs,
+    attn_gain,
+    qkv_weight,
+    out_weight,
+    ffn_gain,
+    router_weight,
+    carry_weight,
+    const_weight,
+    const_vector,
+    gate_weight,
+    up_weight,
+    down_weight,
+    prev_logits,
+    seq_lengths,
+    expert_routes,
+    cotangent,
+):
+    ranks, cols = sizes
+    row_total = expert_routes.shape[0]
+    depth = qkv_weight.shape[0]
+
+    (
+        w_all,
+        qkv,
+        mixed_heads,
+        lse,
+        whole_in,
+        qkv_own,
+        out_t,
+        cosine,
+        sines,
+        meta,
+        slots,
+        mixed,
+        middle,
+        n2_whole,
+        prev_whole,
+        cot_early,
+        rw,
+        carry,
+    ) = first_step(
+        cols,
+        ranks,
+        inputs,
+        cotangent,
+        router_weight.T,
+        const_weight.transpose(0, 2, 1),
+        const_vector,
+        attn_gain,
+        ffn_gain,
+        carry_weight,
+        qkv_weight,
+        out_weight,
+        prev_logits,
+        expert_routes.T,
+        seq_lengths,
+        gate_weight,
+        up_weight,
+        down_weight.transpose(0, 2, 1),
+    )
+    x, gu, y, gates, cot_late = experts_forward(
+        cols, n2_whole.reshape(row_total, D), prev_whole, cotangent, rw, carry, meta, slots, w_all
+    )
+    dx, dots, mixsum, gown, sib, hsoon = experts_backward(
+        cols, ranks, cot_early, cot_late, y, gates, meta, slots, w_all, x, gu
+    )
+    layer_out, resid, gm, og, small, prev_grad, hin0, hrest = resid_step(
+        cols, dx, meta, dots, rw, prev_whole, carry, cotangent, mixsum, n2_whole, middle, out_t, mixed, gown, sib
+    )
+    input_grad, small_all, qkv_grad, og_own, gate_grad, up_grad, down_grad, _ = finish_step(
+        cols,
+        ranks,
+        gm,
+        meta,
+        lse,
+        small,
+        og.reshape(ranks // 2, 2, depth, D),
+        inputs,
+        rw,
+        qkv,
+        mixed_heads,
+        whole_in,
+        qkv_own,
+        cosine,
+        sines,
+        resid,
+        gown,
+        sib,
+        hsoon,
+        hin0,
+        hrest,
+    )
+    layer_out, input_grad, gate_grad, up_grad, down_grad, again, qkv_grad, out_grad, fgain, router, carry, const, vector, prev = (
+        place_outputs(small_all, qkv_grad, og_own, prev_grad, layer_out, input_grad, gate_grad, up_grad, down_grad)
+    )
+    return (
+        layer_out,
+        input_grad,
+        again,
+        qkv_grad,
+        out_grad,
+        fgain,
+        router.T,
+        carry,
+        const.transpose(0, 2, 1),
+        vector,
+        gate_grad,
+        up_grad,
+        down_grad.transpose(0, 2, 1),
+        prev,
+    )
+
+
 def solution(mesh):
+    sizes = (mesh.shape["row"], mesh.shape["col"])
+    body = functools.partial(on_device_heads, sizes) if sizes == (8, 4) else on_device
     placed = (
         P(("row", "col"), None),
         P(),
@@ -500,7 +2418,7 @@
         P(("row", "col"), None),
     )
     return jax.shard_map(
-        on_device,
+        body,
         mesh=mesh,
         in_specs=placed,
         out_specs=(

time: 1520 us -> 397 us (0.26)
  waiting for transfers between devices: 690 us -> 0 us
  Pallas kernels: 0 us -> 386 us
  local copies, waits for them, and re-layouts: 269 us -> 6.81 us
  matrix products: 201 us -> 0 us
  blocking collectives: 186 us -> 0 us
  other arithmetic: 132 us -> 0 us
    pallas_call x0 -> x6, Pallas kernels: none -> 386 us  [the longest x1 133 us: first_step(): pl.pallas_call(functools.partial(first_kernel, cols, ranks), out_shape=(j...]
    all_gather x8 -> x0, waiting for transfers between devices: 310 us -> none  [the longest x1 88.3 us: on_device(): key_values = lax.all_gather(token_qkv[:, D:], 'col', axis=0, tiled=True)]
    reduce_scatter x8 -> x0, waiting for transfers between devices: 306 us -> none  [the longest x4 94.8 us: partial_sums(): lax.psum_scatter(term_value.astype(jnp.bfloat16), 'col', scatter_dimensio...]
    dot_general x47 -> x0, matrix products: 201 us -> none  [the longest x6 20.1 us: key_scores(): jnp.einsum('qhd,khd->hqk', query_heads, key_block, preferred_element_type...]
    all_to_all x2 -> x0, blocking collectives: 89.3 us -> none  [the longest x1 45.2 us: to_features(): lax.all_to_all(block_value, 'col', split_axis=1, concat_axis=0, tiled=True)]
    reduce_sum x17 -> x0, other arithmetic: 78.7 us -> none  [the longest x1 27.5 us: on_device(): grad_tokens = jnp.sum(grad_slots[target].reshape(row_total, 2, D), axis=1)]
    gather x4 -> x0, local copies, waits for them, and re-layouts: 65.6 us -> none  [the longest x1 19.2 us: on_device(): chosen_out = out_rows[target].reshape(row_total, 2, D)]
    psum x2 -> x0, blocking collectives: 60.8 us -> none  [the longest x1 41.6 us: on_device(): lax.psum((attn_gain_grad, ffn_gain_grad, router_grad, carry_grad, const_g...]
  transfers between devices with their start and end apart: 20 -> 0, of which waited for: 17 -> 0; matrix products, arithmetic and copies ran while one was open for 18% -> 0% of each run, Pallas kernels for 0% -> 0%
where the time goes in v4:
time: 397 us; the launch traced here: 394 us
  Pallas kernels  386 us (97%)
  local copies, waits for them, and re-layouts  6.81 us (2%)
    pallas_call x1, Pallas kernels, first_step(): pl.pallas_call(functools.partial(first_kernel, cols, ranks), out_shape=(j...  133 us
    pallas_call x1, Pallas kernels, finish_step(): pl.pallas_call(functools.partial(finish_kernel, cols, ranks), out_shape=(...  89.9 us
    pallas_call x1, Pallas kernels, resid_step(): pl.pallas_call(functools.partial(resid_kernel, cols, count), out_shape=(j...  64.4 us
    pallas_call x1, Pallas kernels, experts_backward(): pl.pallas_call(functools.partial(experts_backward_kernel, cols, capacity)...  62.4 us
    pallas_call x1, Pallas kernels, experts_forward(): pl.pallas_call(functools.partial(experts_forward_kernel, cols, capacity),...  31.4 us

profile of v4, /device:TPU:0, one launch (start us, length us, event | category | flops | bytes accessed | tf_op | source)
XLA Modules:
  0.0 393.7 jit_solution(8354989493979267623)
XLA Ops:
  0.7 133.5 %first_step.1 = (bf16[3,8,768,512]{3,2,1,0:T(8,128)(2,1)}, bf16[9,1536,64]{2,1,0:T(8,128)(2,1)}, bf16[3,1536,64]{2,1,0:T(8,128)(2,1)}, f32[1536,128]{1,0:T(8,128...) custom-call(bf16[384,768]{1,0:T(8,128)(2,1)} %xown_ref.1, ...), custom_call_target="tpu_custom_call" | custom-call | flops 3623878656 | bytes 41943040 | tf_op jit(solution)/shard_map/first_step/pallas_call | solution.py:1171
  134.2 31.4 %experts_forward.1 = (bf16[8,384,768]{2,1,0:T(8,128)(2,1)}, bf16[8,2,384,512]{3,2,1,0:T(8,128)(2,1)}, bf16[8,384,768]{2,1,0:T(8,128)(2,1)}, bf16[1536,256]{1,0:T(8,128)(2,1)}, bf16[4,256,768]{2,1,0:T(8,128)(2,1)}) custom-call(bf16[1536,768]{1,0:T(8,128)(2,1)} %bitcast.9, bf16[4,16,384]{2,1,0:T(8,128)(2,1)} %get-tuple-element.74.prev_ref, ...), custom_call_target="tpu_custom_call" | custom-call | flops 14495514624 | bytes 41943040 | tf_op jit(solution)/shard_map/experts_forward/pallas_call | solution.py:1321
  165.5 62.4 %experts_backward.1 = (bf16[8,384,768]{2,1,0:T(8,128)(2,1)}, f32[8,1536]{1,0:T(8,128)}, f32[384,768]{1,0:T(8,128)}, bf16[8,3,4,96,512]{4,3,2,1,0:T(8,128)(2,1)},...) custom-call(bf16[4,128,768]{2,1,0:T(8,128)(2,1)} %get-tuple-element.72.cota_ref, ...), custom_call_target="tpu_custom_call" | custom-call | flops 28991029248 | bytes 62914560 | tf_op jit(solution)/shard_map/experts_backward/pallas_call | solution.py:1515
  227.9 64.4 %resid_step.1 = (bf16[384,768]{1,0:T(8,128)(2,1)}, f32[384,768]{1,0:T(8,128)}, bf16[4,3,192,128]{3,2,1,0:T(8,128)(2,1)}, bf16[768,768]{1,0:T(8,128)(2,1)}, f32[2...) custom-call(bf16[8,384,768]{2,1,0:T(8,128)(2,1)} %get-tuple-element., ...), custom_call_target="tpu_custom_call" | custom-call | flops 1358954496 | bytes 41943040 | tf_op jit(solution)/shard_map/resid_step/pallas_call | solution.py:1794
  292.3 0.0 copy-start.3
  292.3 0.0 copy-start.7
  292.3 89.9 %finish_step.1 = (f32[384,768]{1,0:T(8,128)}, f32[24,1024]{1,0:T(8,128)}, f32[96,576]{1,0:T(8,128)}, f32[96,192]{1,0:T(8,128)}, f32[8,96,512]{2,1,0:T(8,128)}, /...) custom-call(bf16[4,3,192,128]{3,2,1,0:T(8,128)(2,1)} %get-tuple-element.93.gm_ref, ...), custom_call_target="tpu_custom_call" | custom-call | flops 9059696640 | bytes 41943040 | tf_op jit(solution)/shard_map/finish_step/pallas_call | solution.py:2160
  382.2 0.0 copy-done.3
  382.2 0.0 copy-done.7
  382.2 0.0 copy-start
  382.2 1.4 copy-done
  383.6 0.0 copy-start.1
  383.6 1.4 copy-done.1
  385.1 0.0 copy-start.2
  385.1 1.3 copy-done.2
  386.3 0.0 copy-start.4
  386.3 0.9 copy-done.4
  387.3 0.0 copy-start.5
  387.3 0.9 copy-done.5
  388.2 0.0 copy-start.6
  388.2 0.9 copy-done.6
  389.1 4.3 %place_outputs.1 = (bf16[384,768]{1,0:T(8,128)(2,1)}, f32[384,768]{1,0:T(8,128)}, f32[8,96,512]{2,1,0:T(8,128)}, f32[8,96,512]{2,1,0:T(8,128)}, f32[8,96,512]{2,...) custom-call(f32[24,1024]{1,0:T(8,128)S(1)} %copy-done.5, ...), custom_call_target="tpu_custom_call" | custom-call | bytes 16777216 | tf_op jit(solution)/shard_map/place_outputs/pallas_call | solution.py:2273
Async XLA Ops:
  292.3 89.9 %copy-start.3 = (bf16[384,768]{1,0:T(8,128)(2,1)S(1)}, bf16[384,768]{1,0:T(8,128)(2,1)}, u32[]{:S(2)}) copy-start(bf16[384,768]{1,0:T(8,128)(2,1)} %get-tuple-element.111.layer_in) | copy-start | bytes 1769476
  292.3 89.9 %copy-start.7 = (f32[12,384]{1,0:T(8,128)S(1)}, f32[12,384]{1,0:T(8,128)}, u32[]{:S(2)}) copy-start(f32[12,384]{1,0:T(8,128)} %get-tuple-element.110.pg_ref) | copy-start | bytes 55300
  382.2 1.4 copy-start
  383.6 1.4 copy-start.1
  385.1 1.3 copy-start.2
  386.3 0.9 copy-start.4
  387.3 0.9 copy-start.5
  388.2 0.9 copy-start.6

commit v5 on v4

--- a/solution.py
+++ b/solution.py
@@ -711,9 +711,13 @@
     return jnp.sum(jnp.where(lane_iota(sg.shape) % LANES == e, sg, 0.0), axis=1, keepdims=True)
 
 
+def chain_order(c):
+    return [d + (3 - 2 * d) * (c // 2) for d in (3, 2, 0, 1)]
+
+
 def combine(meta_ref, y_ref, d, local):
     experts, capacity, width = y_ref.shape
-    at = slice(d * local, (d + 1) * local)
+    at = pl.ds(pl.multiple_of(d * local, LANES), local)
     lane = lane_iota((local, capacity)).astype(F32)
     ones = [jnp.where(lane == column(meta_ref, at, e), 1.0, 0.0).astype(BF) for e in range(experts)]
     return mm(jnp.concatenate(ones, axis=1), y_ref[...].reshape(experts * capacity, width)).astype(BF)
@@ -977,17 +981,19 @@
         return copies
 
     def relay(t):
-        for near, far in zip(to_near(t), to_far(t)):
+        for near, far, across in zip(to_near(t), to_far(t), to_other_core(t)[1:3]):
             near.wait_recv()
             far.start()
+            across.start()
 
     def hand_over(t):
         for far in to_far(t):
             far.wait_recv()
-        start_all(to_other_core(t))
+        to_other_core(t)[3].start()
 
     for t in range(3):
         start_all(to_near(t))
+        to_other_core(t)[0].start()
     start_all(held)
 
     small = [ref[...].astype(F32) for ref in (router_ref, const_ref.at[0], const_ref.at[1], vector_ref)]
@@ -1103,7 +1109,6 @@
 
     lax.fori_loop(0, 1, one_head, 0)
     cot_step(2)
-    relay(1)
     lax.fori_loop(1, heads, one_head, 0)
     a_land[c] = a_send[c]
     stored = moves(
@@ -1120,9 +1125,8 @@
         local_sem.at[pl.ds(4, 8)],
     )
     start_all(stored)
-    cot_step(3)
+    relay(1)
     wait_all(wo_hand)
-    hand_over(0)
     for h in range(heads):
         wait_all(head_copies(h))
     mixed = jnp.concatenate([unpack_head(a_land[i, h]) for i in range(cols) for h in range(heads)], axis=1)
@@ -1140,10 +1144,12 @@
     start_all(stored_late)
     relay(2)
     n_step(1)
+    hand_over(0)
+    n_step(2)
     hand_over(1)
-    n_step(2)
     hand_over(2)
     n_step(3)
+    cot_step(3)
     x_drain()
     n_drain()
     cot_drain()
@@ -1380,6 +1386,7 @@
     gown_ref,
     sib_ref,
     hin_ref,
+    glast_ref,
     cot_s,
     mix_s,
     gbuf,
@@ -1409,6 +1416,9 @@
     def own_copy(expert, at):
         return pltpu.make_async_copy(gbuf.at[at, :, :, core], gown_ref.at[expert], own_sem.at[at])
 
+    def last_copy(at):
+        return pltpu.make_async_copy(gbuf.at[at, :, :, 1 - core], glast_ref, sib_send.at[at])
+
     def sib_copy(expert, at):
         return send_to(
             gbuf.at[at, :, :, 1 - core],
@@ -1434,9 +1444,9 @@
     def _():
         start_all(cot_loads)
         greet(col_peers(cols) + [(flip(r, m), c) for m in (1, 2, 4, 6)])
-        for n, d in enumerate((3, 0, 2, 1)):
+        for n, d in enumerate(chain_order(c)):
             mix_s[d] = combine(meta_ref, y_ref, d, local)
-            if n == 1:
+            if n == 0:
                 slot(0)
         wait_all(cot_loads)
 
@@ -1481,7 +1491,14 @@
     gbuf[place_now, 1] = mm(x, du, TN).astype(BF).reshape(shape)
     gbuf[place_now, 2] = mm(ct, gh, TN).astype(BF).reshape(shape)
     own_copy(e, place_now).start()
-    sib_copy(e, place_now).start()
+
+    @pl.when(e < experts - 1)
+    def _():
+        sib_copy(e, place_now).start()
+
+    @pl.when(e == experts - 1)
+    def _():
+        last_copy(place_now).start()
 
     @pl.when(sends_now)
     def _():
@@ -1497,8 +1514,9 @@
         drain()
         for back in (1, 0):
             own_copy(e - back, lax.rem(e - back, 2)).wait()
-            sib_copy(e - back, lax.rem(e - back, 2)).wait_send()
-        for i in range(SENT_SOON, EXPERTS):
+        sib_copy(e - 1, 1 - place_now).wait_send()
+        last_copy(place_now).wait()
+        for i in range(SENT_SOON, EXPERTS - 1):
             sib_copy(i, i % 2).wait_recv()
         for i in range(SENT_SOON):
             wait_all(h_sends(i))
@@ -1522,6 +1540,7 @@
             half,
             half,
             jax.ShapeDtypeStruct((SENT_SOON, 3, three, depth, ff), BF),
+            jax.ShapeDtypeStruct((three, chips, depth, ff), BF),
         ),
         in_specs=[
             ANY,
@@ -1538,6 +1557,7 @@
             pl.BlockSpec((1, capacity, D), lambda e: (e, 0, 0)),
             whole((experts, rows)),
             whole((local, D)),
+            ANY,
             ANY,
             ANY,
             ANY,
@@ -1585,7 +1605,8 @@
     out_t_in,
     mixed_in,
     gown_ref,
-    sib_ref,
+    glast_ref,
+    sib_in,
     layer_ref,
     resid_ref,
     gm_ref,
@@ -1594,6 +1615,7 @@
     pg_ref,
     hin_ref,
     hrest_ref,
+    sib_ref,
     mixsum,
     n2_s,
     middle_s,
@@ -1620,6 +1642,9 @@
     hsend,
     hrecv,
     hkeep,
+    last_sem,
+    og_s,
+    og_sib,
 ):
     r, c = place()
     chip = r // 2
@@ -1635,7 +1660,10 @@
         ],
         load_sem,
     )
-    greet(col_peers(cols) + [(flip(r, 2 * k), c) for k in range(1, 4)])
+    greet(col_peers(cols) + [(flip(r, m), c) for m in (1, 2, 4, 6)])
+    last = gown_ref.shape[0] - 1
+    across = send_to(glast_ref, sib_ref.at[last], last_sem.at[0], last_sem.at[1], (flip(r, 1), c))
+    across.start()
     slot, total, drain = reduce_chain(lambda d: gt_s[d], out, arrived, send, recv, cols)
 
     def dots_of(d):
@@ -1644,9 +1672,9 @@
     dot_copies = to_cols(dots_of, dots_in, dsend, drecv, cols)
     start_all(dot_copies)
     dots_in[c] = dots_of(c)[...]
-    for n, d in enumerate((3, 0, 2, 1)):
+    for n, d in enumerate(chain_order(c)):
         gt_s[d] = combine(meta_ref, dx_ref, d, local)
-        if n == 1:
+        if n == 0:
             slot(0)
 
     def h_loads(i):
@@ -1668,6 +1696,10 @@
     start_all(h_loads(0))
 
     def add_cores(i, carry):
+        @pl.when(i + 2 == held)
+        def _():
+            across.wait()
+
         @pl.when(i + 1 < held)
         def _():
             start_all(h_loads(i + 1))
@@ -1767,7 +1799,13 @@
     stored = moves([(gm_out.at[c], gm_ref.at[c]), (resid_s, resid_ref)], gm_sem)
     start_all(stored)
     small_ref[ROW_GAIN : ROW_GAIN + 1, :D] = jnp.sum(grad_normed * middle * scale, axis=0, keepdims=True)
-    og_ref[...] = mm(cut, mixed_s[...], TN).astype(BF)
+    core = r % 2
+    og_s[...] = mm(cut, mixed_s[...], TN).astype(BF).reshape(og_s.shape)
+    og_across = send_to(og_s.at[:, 1 - core], og_sib, last_sem.at[2], last_sem.at[3], (flip(r, 1), c))
+    og_across.start()
+    og_across.wait()
+    for k in range(og_s.shape[0]):
+        og_ref[k] = (og_s[k, core].astype(F32) + og_sib[k].astype(F32)).astype(BF)
     wait_all(stored + gm_copies)
     drain()
 
@@ -1785,7 +1823,7 @@
     lax.fori_loop(0, held, end, 0)
 
 
-def resid_step(cols, dx, meta, dots, rw, prev, carry, cot, mixsum, n2w, middle, out_t, mixed, gown, sib):
+def resid_step(cols, dx, meta, dots, rw, prev, carry, cot, mixsum, n2w, middle, out_t, mixed, gown, glast, sib):
     local = cot.shape[0]
     experts, three, chips, depth, ff = gown.shape
     count, held = SENT_NEXT, experts - SENT_SOON
@@ -1797,14 +1835,16 @@
             jax.ShapeDtypeStruct((local, D), BF),
             jax.ShapeDtypeStruct((local, D), F32),
             jax.ShapeDtypeStruct((cols, 3, local // 2, LANES), BF),
-            jax.ShapeDtypeStruct((D, D), BF),
+            jax.ShapeDtypeStruct((chips, depth, D), BF),
             jax.ShapeDtypeStruct((SMALL_ROWS, D + 2 * LANES), F32),
             jax.ShapeDtypeStruct((ROUTES, local), F32),
             jax.ShapeDtypeStruct((count, 3, three, depth, ff), BF),
             jax.ShapeDtypeStruct((held - count, 3, three, depth, ff), BF),
+            jax.ShapeDtypeStruct(sib.shape, BF),
         ),
-        in_specs=[vm] * 7 + [ANY] * 7,
-        out_specs=(vm, ANY, ANY, vm, vm, vm, ANY, ANY),
+        in_specs=[vm] * 7 + [ANY] * 8,
+        out_specs=(vm, ANY, ANY, vm, vm, vm, ANY, ANY, ANY),
+        input_output_aliases={14: 8},
         scratch_shapes=[
             pltpu.VMEM((local, D), F32),
             pltpu.VMEM((local, D), BF),
@@ -1829,13 +1869,16 @@
             dma((count, 3)),
             dma((count, 3)),
             dma((held - count, 3)),
+            dma((4,)),
+            pltpu.VMEM((chips, 2, depth, D), BF),
+            pltpu.VMEM((chips, depth, D), BF),
         ],
         compiler_params=pltpu.CompilerParams(
             vmem_limit_bytes=60 * MIB, collective_id=3, has_side_effects=True
         ),
         cost_estimate=pl.CostEstimate(flops=6 * local * D * D, bytes_accessed=40 * MIB, transcendentals=0),
         name="resid_step",
-    )(dx, meta, dots, rw, prev, carry, cot, mixsum, n2w, middle, out_t, mixed, gown, sib)
+    )(dx, meta, dots, rw, prev, carry, cot, mixsum, n2w, middle, out_t, mixed, gown, glast, sib)
 
 
 def finish_kernel(
@@ -1892,8 +1935,6 @@
     small_rows,
     small_cols,
     small_all,
-    og_sib,
-    og_half,
     og_chips,
     og_parts,
     og_cols,
@@ -1942,8 +1983,8 @@
     def to_sibling(src, dst, at):
         return send_to(src.at[:, 1 - core], dst, sib_send.at[at], sib_recv.at[at], (flip(r, 1), c))
 
-    og_across = to_sibling(og_ref, og_sib, 0)
-    og_across.start()
+    og_to_chips = to_chips(lambda there: og_ref.at[there], og_chips, chip_send.at[0], chip_recv.at[0])
+    start_all(og_to_chips)
 
     for d in range(cols):
         at = slice(d * local, (d + 1) * local)
@@ -1953,11 +1994,6 @@
     def halves(ref, sib, half):
         for k in range(ranks // 2):
             half[k] = (ref[k, core].astype(F32) + sib[k].astype(F32)).astype(BF)
-
-    og_across.wait()
-    halves(og_ref, og_sib, og_half)
-    og_to_chips = to_chips(lambda there: og_half.at[there], og_chips, chip_send.at[0], chip_recv.at[0])
-    start_all(og_to_chips)
 
     def h_sends(i):
         r_, c_ = place()
@@ -2009,8 +2045,8 @@
     gain_total = jnp.zeros((1, D), F32)
     weight = w_s[...]
     again = rw_ref[ROW_GAIN : ROW_GAIN + 1].astype(F32)
-    for n, d in enumerate((3, 0, 2, 1)):
-        at = slice(d * local, (d + 1) * local)
+    for n, d in enumerate(chain_order(c)):
+        at = pl.ds(pl.multiple_of(d * local, LANES), local)
         cosine, sines = cos_s[at], sin_s[at]
         turned = [dq_s[h, at] for h in range(heads)] + [dk_s[h, at] for h in range(heads)]
         parts = []
@@ -2023,7 +2059,7 @@
         xs = x * norm_rows(x)
         gn = mm(gp, weight, NT)
         gn_s[d] = gn.astype(BF)
-        if n == 1:
+        if n == 0:
             slot(0)
         gain_total = gain_total + jnp.sum(gn * xs, axis=0, keepdims=True)
         grad = mm((xs * again).astype(BF), gp, TN)
@@ -2032,7 +2068,7 @@
         else:
             qg_acc[...] += grad
     qg_cut[...] = qg_acc[...].astype(BF).reshape(qg_cut.shape)
-    qg_across = to_sibling(qg_cut, qg_sib, 1)
+    qg_across = to_sibling(qg_cut, qg_sib, 0)
     qg_across.start()
 
     sub = lax.broadcasted_iota(jnp.int32, (SMALL_ROWS, D), 0)
@@ -2045,7 +2081,6 @@
     small_to_rows = to_rows(lambda d: small_s.at[d], small_rows, row_send.at[0], row_recv.at[0], ranks)
     start_all(small_to_rows)
     small_rows[r] = small_s[r]
-    slot(1)
 
     def sum_grads(low, high, hin, base):
         def f_loads(i):
@@ -2071,13 +2106,15 @@
             total_grad = fbuf[at, 0].astype(F32)
             for j in range(1, 5):
                 total_grad = total_grad + fbuf[at, j].astype(F32)
-            gg_ref[i] = total_grad[0]
-            ug_ref[i] = total_grad[1]
-            dg_ref[i] = total_grad[2]
+            gg_ref[i] = total_grad[0].astype(BF)
+            ug_ref[i] = total_grad[1].astype(BF)
+            dg_ref[i] = total_grad[2].astype(BF)
             return carry
 
         lax.fori_loop(low, high, body, 0)
 
+    sum_grads(0, SENT_SOON, hsoon_ref, 0)
+    slot(1)
     qg_across.wait()
     halves(qg_cut, qg_sib, qg_half)
     qg_to_chips = to_chips(lambda there: qg_half.at[there], qg_chips, chip_send.at[1], chip_recv.at[1])
@@ -2086,16 +2123,14 @@
     small_cols[c] = all_sum(small_rows, ranks)
     small_to_cols = to_cols(lambda d: small_cols.at[c], small_cols, col_send.at[0], col_recv.at[0], cols)
     start_all(small_to_cols)
+    slot(2)
     wait_all(og_to_chips)
-    og_sum = og_ref[chip, core].astype(F32) + og_sib[chip].astype(F32) + all_sum(og_chips, 3)
+    og_sum = og_ref[chip].astype(F32) + all_sum(og_chips, 3)
     for i in range(cols):
         og_parts[i] = og_sum[:, i * width : (i + 1) * width]
     og_to_cols = to_cols(lambda d: og_parts.at[d], og_cols, col_send.at[1], col_recv.at[1], cols)
     start_all(og_to_cols)
     og_cols[c] = og_parts[c]
-    sum_grads(0, SENT_SOON, hsoon_ref, 0)
-    sum_grads(SENT_SOON, first, hin0_ref, SENT_SOON)
-    slot(2)
     wait_all(qg_to_chips)
     q_sum = qg_cut[chip, core].astype(F32) + qg_sib[chip].astype(F32) + all_sum(qg_chips, 3)
     for i in range(3):
@@ -2123,6 +2158,7 @@
     small_all[r] = all_sum(small_cols, cols)
     small_back = to_rows(lambda d: small_all.at[r], small_all, row_send.at[1], row_recv.at[1], ranks)
     start_all(small_back)
+    sum_grads(SENT_SOON, first, hin0_ref, SENT_SOON)
 
     def end_sends(i, carry):
         wait_all(h_sends(i))
@@ -2156,7 +2192,7 @@
     vm = pl.BlockSpec(memory_space=pltpu.VMEM)
     dma = pltpu.SemaphoreType.DMA
     wide = D + 2 * LANES
-    weight_grad = jax.ShapeDtypeStruct((experts, depth, ff), F32)
+    weight_grad = jax.ShapeDtypeStruct((experts, depth, ff), BF)
     return pl.pallas_call(
         functools.partial(finish_kernel, cols, ranks),
         out_shape=(
@@ -2193,8 +2229,6 @@
             pltpu.VMEM((ranks, SMALL_ROWS, LANES), F32),
             pltpu.VMEM((cols, SMALL_ROWS, LANES), F32),
             pltpu.VMEM((ranks, SMALL_ROWS, LANES), F32),
-            pltpu.VMEM((chips, depth, D), BF),
-            pltpu.VMEM((chips, depth, D), BF),
             pltpu.VMEM((3, depth, D), BF),
             pltpu.VMEM((cols, depth, width), F32),
             pltpu.VMEM((cols, depth, width), F32),
@@ -2210,8 +2244,8 @@
             dma((2, ranks - 1)),
             dma((2, 3)),
             dma((2, 3)),
-            dma((2,)),
-            dma((2,)),
+            dma((1,)),
+            dma((1,)),
             dma((3, cols - 1)),
             dma((3, cols - 1)),
             dma((rest, 3)),
@@ -2251,9 +2285,28 @@
     const_ref,
     vector_ref,
     prev_ref,
+    g_low,
+    g_full,
+    ig_s,
+    layer_s,
+    load_sem,
+    store_sem,
 ):
-    for src, dst in ((gg_in, gg_ref), (ug_in, ug_ref), (dg_in, dg_ref), (ig_in, ig_ref), (layer_in, layer_ref)):
-        dst[...] = src[...]
+    loads = moves(
+        [(gg_in, g_low.at[0]), (ug_in, g_low.at[1]), (dg_in, g_low.at[2]), (ig_in, ig_s), (layer_in, layer_s)], load_sem
+    )
+    stores = moves(
+        [(g_full.at[0], gg_ref), (g_full.at[1], ug_ref), (g_full.at[2], dg_ref), (ig_s, ig_ref), (layer_s, layer_ref)],
+        store_sem,
+    )
+    start_all(loads)
+    for i in (3, 4):
+        loads[i].wait()
+        stores[i].start()
+    for i in range(3):
+        loads[i].wait()
+        g_full[i] = g_low[i].astype(F32)
+        stores[i].start()
     again_ref[...] = small_ref[ROW_GAIN + 1 : ROW_GAIN + 2, :D].reshape(D)
     fgain_ref[...] = small_ref[ROW_GAIN : ROW_GAIN + 1, :D].reshape(D)
     qkv_ref[...] = qg_ref[...]
@@ -2264,6 +2317,7 @@
         const_ref[j] = small_ref[ROW_CONST + 2 * j : ROW_CONST + 2 * j + 2, :D]
     vector_ref[...] = small_ref[ROW_VEC : ROW_VEC + 2, :D]
     prev_ref[...] = pg_ref[...]
+    wait_all(stores)
 
 
 def place_outputs(small, qg, og, pg, layer, ig, gg, ug, dg):
@@ -2273,9 +2327,17 @@
     return pl.pallas_call(
         place_kernel,
         out_shape=[jax.ShapeDtypeStruct(shape, F32 if i else BF) for i, shape in enumerate(shapes)],
-        in_specs=[vm] * 9,
-        out_specs=[vm] * 14,
-        compiler_params=pltpu.CompilerParams(vmem_limit_bytes=48 * MIB),
+        in_specs=[vm] * 4 + [ANY] * 5,
+        out_specs=[ANY] * 5 + [vm] * 9,
+        scratch_shapes=[
+            pltpu.VMEM((3, *gg.shape), BF),
+            pltpu.VMEM((3, *gg.shape), F32),
+            pltpu.VMEM(ig.shape, F32),
+            pltpu.VMEM(layer.shape, BF),
+            pltpu.SemaphoreType.DMA((5,)),
+            pltpu.SemaphoreType.DMA((5,)),
+        ],
+        compiler_params=pltpu.CompilerParams(vmem_limit_bytes=60 * MIB),
         cost_estimate=pl.CostEstimate(flops=0, bytes_accessed=16 * MIB, transcendentals=0),
         name="place_outputs",
     )(small, qg, og, pg, layer, ig, gg, ug, dg)
@@ -2346,11 +2408,11 @@
     x, gu, y, gates, cot_late = experts_forward(
         cols, n2_whole.reshape(row_total, D), prev_whole, cotangent, rw, carry, meta, slots, w_all
     )
-    dx, dots, mixsum, gown, sib, hsoon = experts_backward(
+    dx, dots, mixsum, gown, sib, hsoon, glast = experts_backward(
         cols, ranks, cot_early, cot_late, y, gates, meta, slots, w_all, x, gu
     )
-    layer_out, resid, gm, og, small, prev_grad, hin0, hrest = resid_step(
-        cols, dx, meta, dots, rw, prev_whole, carry, cotangent, mixsum, n2_whole, middle, out_t, mixed, gown, sib
+    layer_out, resid, gm, og, small, prev_grad, hin0, hrest, sib = resid_step(
+        cols, dx, meta, dots, rw, prev_whole, carry, cotangent, mixsum, n2_whole, middle, out_t, mixed, gown, glast, sib
     )
     input_grad, small_all, qkv_grad, og_own, gate_grad, up_grad, down_grad, _ = finish_step(
         cols,
@@ -2359,7 +2421,7 @@
         meta,
         lse,
         small,
-        og.reshape(ranks // 2, 2, depth, D),
+        og,
         inputs,
         rw,
         qkv,

time: 397 us -> 375 us (0.945)
  Pallas kernels: 386 us -> 371 us
  local copies, waits for them, and re-layouts: 6.81 us -> 0 us
    pallas_call x1, Pallas kernels: 133 us -> 120 us  [first_step(): pl.pallas_call(functools.partial(first_kernel, cols, ranks), out_shape=(j...]
    unnamed x16 -> x0, local copies, waits for them, and re-layouts: 6.81 us -> none
where the time goes in v5:
time: 375 us; the launch traced here: 372 us
  Pallas kernels  371 us (99%)
    pallas_call x1, Pallas kernels, first_step(): pl.pallas_call(functools.partial(first_kernel, cols, ranks), out_shape=(j...  120 us
    pallas_call x1, Pallas kernels, finish_step(): pl.pallas_call(functools.partial(finish_kernel, cols, ranks), out_shape=(...  87.2 us
    pallas_call x1, Pallas kernels, experts_backward(): pl.pallas_call(functools.partial(experts_backward_kernel, cols, capacity)...  62.9 us
    pallas_call x1, Pallas kernels, resid_step(): pl.pallas_call(functools.partial(resid_kernel, cols, count), out_shape=(j...  61 us
    pallas_call x1, Pallas kernels, experts_forward(): pl.pallas_call(functools.partial(experts_forward_kernel, cols, capacity),...  33.1 us

profile of v5, /device:TPU:0, one launch (start us, length us, event | category | flops | bytes accessed | tf_op | source)
XLA Modules:
  0.0 371.6 jit_solution(4162411504021952904)
XLA Ops:
  0.7 119.8 %first_step.1 = (bf16[3,8,768,512]{3,2,1,0:T(8,128)(2,1)}, bf16[9,1536,64]{2,1,0:T(8,128)(2,1)}, bf16[3,1536,64]{2,1,0:T(8,128)(2,1)}, f32[1536,128]{1,0:T(8,128...) custom-call(bf16[384,768]{1,0:T(8,128)(2,1)} %xown_ref.1, ...), custom_call_target="tpu_custom_call" | custom-call | flops 3623878656 | bytes 41943040 | tf_op jit(solution)/shard_map/first_step/pallas_call | solution.py:1177
  120.5 33.1 %experts_forward.1 = (bf16[8,384,768]{2,1,0:T(8,128)(2,1)}, bf16[8,2,384,512]{3,2,1,0:T(8,128)(2,1)}, bf16[8,384,768]{2,1,0:T(8,128)(2,1)}, bf16[1536,256]{1,0:T(8,128)(2,1)}, bf16[4,256,768]{2,1,0:T(8,128)(2,1)}) custom-call(bf16[1536,768]{1,0:T(8,128)(2,1)} %bitcast.8, bf16[4,16,384]{2,1,0:T(8,128)(2,1)} %get-tuple-element.76.prev_ref, ...), custom_call_target="tpu_custom_call" | custom-call | flops 14495514624 | bytes 41943040 | tf_op jit(solution)/shard_map/experts_forward/pallas_call | solution.py:1327
  153.5 62.9 %experts_backward.1 = (bf16[8,384,768]{2,1,0:T(8,128)(2,1)}, f32[8,1536]{1,0:T(8,128)}, f32[384,768]{1,0:T(8,128)}, bf16[8,3,4,96,512]{4,3,2,1,0:T(8,128)(2,1)},...) custom-call(bf16[4,128,768]{2,1,0:T(8,128)(2,1)} %get-tuple-element.74.cot, ...), custom_call_target="tpu_custom_call" | custom-call | flops 28991029248 | bytes 62914560 | tf_op jit(solution)/shard_map/experts_backward/pallas_call | solution.py:1533
  216.5 61.0 %resid_step.1 = (bf16[384,768]{1,0:T(8,128)(2,1)}, f32[384,768]{1,0:T(8,128)}, bf16[4,3,192,128]{3,2,1,0:T(8,128)(2,1)}, bf16[4,96,768]{2,1,0:T(8,128)(2,1)}, f3...) custom-call(bf16[8,384,768]{2,1,0:T(8,128)(2,1)} %get-tuple-element., ...), custom_call_target="tpu_custom_call", output_to_operand_aliasing={{8}: (14, {})} | custom-call | flops 1358954496 | bytes 41943040 | tf_op jit(solution)/shard_map/resid_step/pallas_call | solution.py:1832
  277.4 87.2 %finish_step.1 = (f32[384,768]{1,0:T(8,128)}, f32[24,1024]{1,0:T(8,128)}, f32[96,576]{1,0:T(8,128)}, f32[96,192]{1,0:T(8,128)}, bf16[8,96,512]{2,1,0:T(8,128)(2,...) custom-call(bf16[4,3,192,128]{3,2,1,0:T(8,128)(2,1)} %get-tuple-element.96.gm_ref,, ...), custom_call_target="tpu_custom_call" | custom-call | flops 9059696640 | bytes 41943040 | tf_op jit(solution)/shard_map/finish_step/pallas_call | solution.py:2196
  364.6 6.7 %place_outputs.1 = (bf16[384,768]{1,0:T(8,128)(2,1)}, f32[384,768]{1,0:T(8,128)}, f32[8,96,512]{2,1,0:T(8,128)}, f32[8,96,512]{2,1,0:T(8,128)}, f32[8,96,512]{2,...) custom-call(f32[24,1024]{1,0:T(8,128)} %get-tuple-element.111.small_, ...), custom_call_target="tpu_custom_call" | custom-call | bytes 16777216 | tf_op jit(solution)/shard_map/place_outputs/pallas_call | solution.py:2327

commit v6 on v5

--- a/solution.py
+++ b/solution.py
@@ -1462,12 +1462,6 @@
     ct = mm(one, cot_s[...]).astype(BF)
     sg = slot_gates(one, gates_ref, e)
     x = x_ref[0]
-
-    @pl.when(sends_now)
-    def _():
-        sib_copy(before, 1 - place_now).wait_recv()
-        sib_load.start()
-
     g, u = gu_ref[0, 0].astype(F32), gu_ref[0, 1].astype(F32)
     v = mm(ct, w_ref[2, 0])
     sig = jax.nn.sigmoid(g)
@@ -1485,6 +1479,11 @@
     def _():
         own_copy(e - 2, place_now).wait()
         sib_copy(e - 2, place_now).wait_send()
+
+    @pl.when(sends_now)
+    def _():
+        sib_copy(before, 1 - place_now).wait_recv()
+        sib_load.start()
 
     shape = gbuf.shape[2:]
     gbuf[place_now, 0] = mm(x, dg, TN).astype(BF).reshape(shape)
@@ -1956,6 +1955,8 @@
     col_recv,
     hsend,
     hrecv,
+    g_s,
+    store_sem,
 ):
     r, c = place()
     chip, core = r // 2, r % 2
@@ -2012,7 +2013,7 @@
         start_all(h_sends(i))
         return carry
 
-    lax.fori_loop(0, rest, start_sends, 0)
+    lax.fori_loop(0, rest - 1, start_sends, 0)
 
     blocks = rows // Q_ROWS
 
@@ -2106,23 +2107,24 @@
             total_grad = fbuf[at, 0].astype(F32)
             for j in range(1, 5):
                 total_grad = total_grad + fbuf[at, j].astype(F32)
-            gg_ref[i] = total_grad[0].astype(BF)
-            ug_ref[i] = total_grad[1].astype(BF)
-            dg_ref[i] = total_grad[2].astype(BF)
+            for t in range(3):
+                g_s[t, i] = total_grad[t].astype(BF)
             return carry
 
         lax.fori_loop(low, high, body, 0)
 
-    sum_grads(0, SENT_SOON, hsoon_ref, 0)
-    slot(1)
     qg_across.wait()
     halves(qg_cut, qg_sib, qg_half)
     qg_to_chips = to_chips(lambda there: qg_half.at[there], qg_chips, chip_send.at[1], chip_recv.at[1])
     start_all(qg_to_chips)
+    start_sends(rest - 1, 0)
+    slot(1)
+    sum_grads(0, SENT_SOON, hsoon_ref, 0)
     wait_all(small_to_rows)
     small_cols[c] = all_sum(small_rows, ranks)
     small_to_cols = to_cols(lambda d: small_cols.at[c], small_cols, col_send.at[0], col_recv.at[0], cols)
     start_all(small_to_cols)
+    sum_grads(SENT_SOON, first, hin0_ref, SENT_SOON)
     slot(2)
     wait_all(og_to_chips)
     og_sum = og_ref[chip].astype(F32) + all_sum(og_chips, 3)
@@ -2158,7 +2160,6 @@
     small_all[r] = all_sum(small_cols, cols)
     small_back = to_rows(lambda d: small_all.at[r], small_all, row_send.at[1], row_recv.at[1], ranks)
     start_all(small_back)
-    sum_grads(SENT_SOON, first, hin0_ref, SENT_SOON)
 
     def end_sends(i, carry):
         wait_all(h_sends(i))
@@ -2170,6 +2171,8 @@
     og_out[...] = all_sum(og_cols, cols)
     for i in range(3):
         qg_out[:, i * width : (i + 1) * width] = q_land[i]
+    stored = moves([(g_s.at[i], ref) for i, ref in enumerate((gg_ref, ug_ref, dg_ref))], store_sem)
+    start_all(stored)
     for i in range(ranks):
         small_out[:, i * LANES : (i + 1) * LANES] = small_all[i]
     slot(3)
@@ -2180,6 +2183,7 @@
     gained = gn * again
     x_dot = jnp.sum(gained * x, axis=1, keepdims=True)
     ig_ref[...] = resid_s[...] + scale * gained - x * (scale * scale * scale * (x_dot * (1.0 / D)))
+    wait_all(stored)
     drain()
 
 
@@ -2206,7 +2210,7 @@
             jax.ShapeDtypeStruct((rest, 3, three, depth, ff), BF),
         ),
         in_specs=[vm] * 7 + [ANY] * 12,
-        out_specs=(vm,) * 7 + (ANY,),
+        out_specs=(vm,) * 4 + (ANY,) * 4,
         scratch_shapes=[
             pltpu.VMEM((3 * heads, rows, HEAD_DIM), BF),
             pltpu.VMEM((heads, rows, HEAD_DIM), BF),
@@ -2250,6 +2254,8 @@
             dma((3, cols - 1)),
             dma((rest, 3)),
             dma((rest, 3)),
+            pltpu.VMEM((three, experts, depth, ff), BF),
+            dma((3,)),
         ],
         compiler_params=pltpu.CompilerParams(
             vmem_limit_bytes=62 * MIB, collective_id=4, has_side_effects=True
@@ -2261,86 +2267,57 @@
     )(gm, meta, lse, small, og, xown, rw, qkv, o, x, w, cosine, sines, resid, gown, sib, hsoon, hin0, hrest)
 
 
-def place_kernel(
-    small_ref,
-    qg_ref,
-    og_ref,
-    pg_ref,
-    layer_in,
-    ig_in,
-    gg_in,
-    ug_in,
-    dg_in,
-    layer_ref,
-    ig_ref,
-    gg_ref,
-    ug_ref,
-    dg_ref,
-    again_ref,
-    qkv_ref,
-    out_ref,
-    fgain_ref,
-    router_ref,
-    carry_ref,
-    const_ref,
-    vector_ref,
-    prev_ref,
-    g_low,
-    g_full,
-    ig_s,
-    layer_s,
-    load_sem,
-    store_sem,
-):
-    loads = moves(
-        [(gg_in, g_low.at[0]), (ug_in, g_low.at[1]), (dg_in, g_low.at[2]), (ig_in, ig_s), (layer_in, layer_s)], load_sem
-    )
-    stores = moves(
-        [(g_full.at[0], gg_ref), (g_full.at[1], ug_ref), (g_full.at[2], dg_ref), (ig_s, ig_ref), (layer_s, layer_ref)],
-        store_sem,
-    )
+def place_kernel(*refs):
+    ins, refs = refs[:9], refs[9:]
+    outs, refs = refs[:14], refs[14:]
+    held, refs = refs[:9], refs[9:]
+    made, (load_sem, store_sem) = refs[:8], refs[8:]
+    loads = moves(list(zip(ins, held)), load_sem)
     start_all(loads)
-    for i in (3, 4):
-        loads[i].wait()
+    small, qg, og, pg, layer, ig, *low = held
+    full, again, out, fgain, router, carry, const, vector = made
+    sources = [layer, ig, full.at[0], full.at[1], full.at[2], again, qg, out, fgain, router, carry, const, vector, pg]
+    stores = moves(list(zip(sources, outs)), store_sem)
+    for load, store in ((4, 0), (5, 1), (1, 6), (3, 13)):
+        loads[load].wait()
+        stores[store].start()
+    for i in range(3):
+        loads[6 + i].wait()
+        full[i] = low[i][...].astype(F32)
+        stores[2 + i].start()
+    loads[2].wait()
+    out[...] = og[...].T
+    loads[0].wait()
+    again[...] = small[ROW_GAIN + 1 : ROW_GAIN + 2, :D].reshape(D)
+    fgain[...] = small[ROW_GAIN : ROW_GAIN + 1, :D].reshape(D)
+    router[...] = small[:ROUTES, :D]
+    carry[...] = small[:ROUTES, D : D + ROUTES]
+    for j in range(2):
+        const[j] = small[ROW_CONST + 2 * j : ROW_CONST + 2 * j + 2, :D]
+    vector[...] = small[ROW_VEC : ROW_VEC + 2, :D]
+    for i in (5, 7, 8, 9, 10, 11, 12):
         stores[i].start()
-    for i in range(3):
-        loads[i].wait()
-        g_full[i] = g_low[i].astype(F32)
-        stores[i].start()
-    again_ref[...] = small_ref[ROW_GAIN + 1 : ROW_GAIN + 2, :D].reshape(D)
-    fgain_ref[...] = small_ref[ROW_GAIN : ROW_GAIN + 1, :D].reshape(D)
-    qkv_ref[...] = qg_ref[...]
-    out_ref[...] = og_ref[...].T
-    router_ref[...] = small_ref[:ROUTES, :D]
-    carry_ref[...] = small_ref[:ROUTES, D : D + ROUTES]
-    for j in range(2):
-        const_ref[j] = small_ref[ROW_CONST + 2 * j : ROW_CONST + 2 * j + 2, :D]
-    vector_ref[...] = small_ref[ROW_VEC : ROW_VEC + 2, :D]
-    prev_ref[...] = pg_ref[...]
     wait_all(stores)
 
 
-def place_outputs(small, qg, og, pg, layer, ig, gg, ug, dg):
-    vm = pl.BlockSpec(memory_space=pltpu.VMEM)
+def place_outputs(*values):
+    small, qg, og, pg, layer, ig, gg, ug, dg = values
+    made = [(D,), og.shape[::-1], (D,), (ROUTES, D), (ROUTES, ROUTES), (2, 2, D), (2, D)]
     shapes = [layer.shape, ig.shape, gg.shape, ug.shape, dg.shape]
-    shapes += [(D,), qg.shape, og.shape[::-1], (D,), (ROUTES, D), (ROUTES, ROUTES), (2, 2, D), (2, D), pg.shape]
+    shapes += [made[0], qg.shape, *made[1:], pg.shape]
     return pl.pallas_call(
         place_kernel,
         out_shape=[jax.ShapeDtypeStruct(shape, F32 if i else BF) for i, shape in enumerate(shapes)],
-        in_specs=[vm] * 4 + [ANY] * 5,
-        out_specs=[ANY] * 5 + [vm] * 9,
-        scratch_shapes=[
-            pltpu.VMEM((3, *gg.shape), BF),
-            pltpu.VMEM((3, *gg.shape), F32),
-            pltpu.VMEM(ig.shape, F32),
-            pltpu.VMEM(layer.shape, BF),
-            pltpu.SemaphoreType.DMA((5,)),
-            pltpu.SemaphoreType.DMA((5,)),
-        ],
+        in_specs=[ANY] * 9,
+        out_specs=[ANY] * 14,
+        scratch_shapes=[pltpu.VMEM(value.shape, value.dtype) for value in values]
+        + [pltpu.VMEM((3, *gg.shape), F32)]
+        + [pltpu.VMEM(shape, F32) for shape in made]
+        + [pltpu.SemaphoreType.DMA((9,)), pltpu.SemaphoreType.DMA((14,))],
         compiler_params=pltpu.CompilerParams(vmem_limit_bytes=60 * MIB),
         cost_estimate=pl.CostEstimate(flops=0, bytes_accessed=16 * MIB, transcendentals=0),
         name="place_outputs",
-    )(small, qg, og, pg, layer, ig, gg, ug, dg)
+    )(*values)
 
 
 def on_device_heads(

time: 375 us -> 364 us (0.971)
  Pallas kernels: 371 us -> 360 us
    pallas_call x1, Pallas kernels: 87.2 us -> 80.3 us  [finish_step(): pl.pallas_call(functools.partial(finish_kernel, cols, ranks), out_shape=(...]
where the time goes in v6:
time: 364 us; the launch traced here: 361 us
  Pallas kernels  360 us (99%)
    pallas_call x1, Pallas kernels, first_step(): pl.pallas_call(functools.partial(first_kernel, cols, ranks), out_shape=(j...  120 us
    pallas_call x1, Pallas kernels, finish_step(): pl.pallas_call(functools.partial(finish_kernel, cols, ranks), out_shape=(...  80.3 us
    pallas_call x1, Pallas kernels, resid_step(): pl.pallas_call(functools.partial(resid_kernel, cols, count), out_shape=(j...  62.7 us
    pallas_call x1, Pallas kernels, experts_backward(): pl.pallas_call(functools.partial(experts_backward_kernel, cols, capacity)...  59.6 us
    pallas_call x1, Pallas kernels, experts_forward(): pl.pallas_call(functools.partial(experts_forward_kernel, cols, capacity),...  33.1 us

profile of v6, /device:TPU:0, one launch (start us, length us, event | category | flops | bytes accessed | tf_op | source)
XLA Modules:
  0.0 361.0 jit_solution(18107288891532227877)
XLA Ops:
  0.7 119.8 %first_step.1 = (bf16[3,8,768,512]{3,2,1,0:T(8,128)(2,1)}, bf16[9,1536,64]{2,1,0:T(8,128)(2,1)}, bf16[3,1536,64]{2,1,0:T(8,128)(2,1)}, f32[1536,128]{1,0:T(8,128...) custom-call(bf16[384,768]{1,0:T(8,128)(2,1)} %xown_ref.1, ...), custom_call_target="tpu_custom_call" | custom-call | flops 3623878656 | bytes 41943040 | tf_op jit(solution)/shard_map/first_step/pallas_call | solution.py:1177
  120.5 33.1 %experts_forward.1 = (bf16[8,384,768]{2,1,0:T(8,128)(2,1)}, bf16[8,2,384,512]{3,2,1,0:T(8,128)(2,1)}, bf16[8,384,768]{2,1,0:T(8,128)(2,1)}, bf16[1536,256]{1,0:T(8,128)(2,1)}, bf16[4,256,768]{2,1,0:T(8,128)(2,1)}) custom-call(bf16[1536,768]{1,0:T(8,128)(2,1)} %bitcast.8, bf16[4,16,384]{2,1,0:T(8,128)(2,1)} %get-tuple-element.76.prev_ref, ...), custom_call_target="tpu_custom_call" | custom-call | flops 14495514624 | bytes 41943040 | tf_op jit(solution)/shard_map/experts_forward/pallas_call | solution.py:1327
  153.5 59.6 %experts_backward.1 = (bf16[8,384,768]{2,1,0:T(8,128)(2,1)}, f32[8,1536]{1,0:T(8,128)}, f32[384,768]{1,0:T(8,128)}, bf16[8,3,4,96,512]{4,3,2,1,0:T(8,128)(2,1)},...) custom-call(bf16[4,128,768]{2,1,0:T(8,128)(2,1)} %get-tuple-element.74.cot, ...), custom_call_target="tpu_custom_call" | custom-call | flops 28991029248 | bytes 62914560 | tf_op jit(solution)/shard_map/experts_backward/pallas_call | solution.py:1532
  213.2 62.7 %resid_step.1 = (bf16[384,768]{1,0:T(8,128)(2,1)}, f32[384,768]{1,0:T(8,128)}, bf16[4,3,192,128]{3,2,1,0:T(8,128)(2,1)}, bf16[4,96,768]{2,1,0:T(8,128)(2,1)}, f3...) custom-call(bf16[8,384,768]{2,1,0:T(8,128)(2,1)} %get-tuple-element., ...), custom_call_target="tpu_custom_call", output_to_operand_aliasing={{8}: (14, {})} | custom-call | flops 1358954496 | bytes 41943040 | tf_op jit(solution)/shard_map/resid_step/pallas_call | solution.py:1831
  275.8 80.3 %finish_step.1 = (f32[384,768]{1,0:T(8,128)}, f32[24,1024]{1,0:T(8,128)}, f32[96,576]{1,0:T(8,128)}, f32[96,192]{1,0:T(8,128)}, bf16[8,96,512]{2,1,0:T(8,128)(2,...) custom-call(bf16[4,3,192,128]{3,2,1,0:T(8,128)(2,1)} %get-tuple-element.96.gm_ref,, ...), custom_call_target="tpu_custom_call" | custom-call | flops 9059696640 | bytes 41943040 | tf_op jit(solution)/shard_map/finish_step/pallas_call | solution.py:2200
  356.1 4.6 %place_outputs.1 = (bf16[384,768]{1,0:T(8,128)(2,1)}, f32[384,768]{1,0:T(8,128)}, f32[8,96,512]{2,1,0:T(8,128)}, f32[8,96,512]{2,1,0:T(8,128)}, f32[8,96,512]{2,...) custom-call(f32[24,1024]{1,0:T(8,128)} %get-tuple-element.111.refs_0, ...), custom_call_target="tpu_custom_call" | custom-call | bytes 16777216 | tf_op jit(solution)/shard_map/place_outputs/pallas_call | solution.py:2308

commit v7 on v6

--- a/solution.py
+++ b/solution.py
@@ -724,7 +724,7 @@
 
 
 META_HIT, META_BEGIN, META_VALID = 8, 20, 21
-EARLY = 3
+EARLY = 6
 SENT_SOON, SENT_NEXT = 2, 3
 
 
@@ -830,8 +830,8 @@
     prev_ref,
     routes_ref,
     lengths_ref,
-    cos_ref,
-    sin_ref,
+    cos_in,
+    sin_in,
     freq_ref,
     gate_ref,
     up_ref,
@@ -896,6 +896,9 @@
     s_recv,
     h_send,
     h_recv,
+    cos_ref,
+    sin_ref,
+    soon_sem,
 ):
     r, c = place()
     heads = 3
@@ -906,6 +909,8 @@
     odd, high = c % 2, c // 2
     again = again_ref[...].astype(F32).reshape(1, D)
     fgain = fgain_ref[...].astype(F32).reshape(1, D)
+    soon = moves([(cos_in, cos_ref), (sin_in, sin_ref)], soon_sem)
+    start_all(soon)
     greet(col_peers(cols) + [(flip(r, m), c) for m in (1, 2, 4, 6)])
 
     for s in range(3):
@@ -915,12 +920,12 @@
         send_to(q_parts.at[2 - 2 * odd], q_land.at[2 * high], q_send.at[1], q_recv.at[1], (r, flip(c, 2))),
     ]
     start_all(q_copies)
+    x_step, x_drain = gather_chain(x_ref, xw, x_send, x_recv, cols)
+    x_step(0)
     o_parts[...] = wo_ref[...].astype(F32).T.astype(BF)
     prev_s[...] = jnp.concatenate([prev_ref[...].astype(F32), jnp.zeros((16 - ROUTES, local), F32)], axis=0).astype(BF)
     o_copies = to_cols(lambda d: o_parts, o_land, c_send.at[0], c_recv.at[0], cols)
     prev_copies = to_cols(lambda d: prev_s, prevw, c_send.at[1], c_recv.at[1], cols)
-    x_step, x_drain = gather_chain(x_ref, xw, x_send, x_recv, cols)
-    x_step(0)
     start_all(o_copies + prev_copies)
     q_land[(c + 1) // 2] = q_parts[2 * odd]
     o_land[c] = o_parts[...]
@@ -1019,6 +1024,7 @@
         sb = jnp.where(spot >= ends[i - 1], sin_first[i : i + 1], sb)
     cb, sb = jnp.where(spot >= end, 1.0, cb), jnp.where(spot >= end, 0.0, sb)
     sign = jnp.where(lane_iota((rows, LANES)) % 2 == 0, -1.0, 1.0)
+    wait_all(soon)
     cos_s[...] = cos_ref[...] * cb + sin_ref[...] * sb
     sin_s[...] = (sin_ref[...] * cb - cos_ref[...] * sb) * sign
     lse_s[...] = jnp.zeros_like(lse_s)
@@ -1196,7 +1202,7 @@
             jax.ShapeDtypeStruct((LANES, D), BF),
             jax.ShapeDtypeStruct((16, LANES), BF),
         ),
-        in_specs=[vm] * 12 + [pl.BlockSpec(memory_space=pltpu.SMEM)] + [vm] * 3 + [ANY] * 3,
+        in_specs=[vm] * 12 + [pl.BlockSpec(memory_space=pltpu.SMEM)] + [ANY, ANY, vm] + [ANY] * 3,
         out_specs=(ANY,) * 10 + (vm,) + (ANY,) * 5 + (vm, vm),
         scratch_shapes=[
             pltpu.VMEM((cols, local, D), BF),
@@ -1241,6 +1247,9 @@
             dma((3, 4)),
             dma((heads, cols - 1)),
             dma((heads, cols - 1)),
+            pltpu.VMEM((rows, LANES), F32),
+            pltpu.VMEM((rows, LANES), F32),
+            dma((2,)),
         ],
         compiler_params=pltpu.CompilerParams(
             vmem_limit_bytes=60 * MIB, collective_id=5, has_side_effects=True
@@ -1486,8 +1495,9 @@
         sib_load.start()
 
     shape = gbuf.shape[2:]
-    gbuf[place_now, 0] = mm(x, dg, TN).astype(BF).reshape(shape)
-    gbuf[place_now, 1] = mm(x, du, TN).astype(BF).reshape(shape)
+    pair = mm(x, jnp.concatenate([dg, du], axis=1), TN).astype(BF)
+    gbuf[place_now, 0] = pair[:, : dg.shape[1]].reshape(shape)
+    gbuf[place_now, 1] = pair[:, dg.shape[1] :].reshape(shape)
     gbuf[place_now, 2] = mm(ct, gh, TN).astype(BF).reshape(shape)
     own_copy(e, place_now).start()
 
@@ -1591,8 +1601,8 @@
 def resid_kernel(
     cols,
     count,
-    dx_ref,
-    meta_ref,
+    dx_in,
+    meta_in,
     dots_ref,
     rw_ref,
     prev_ref,
@@ -1644,6 +1654,9 @@
     last_sem,
     og_s,
     og_sib,
+    dx_ref,
+    meta_ref,
+    soon_sem,
 ):
     r, c = place()
     chip = r // 2
@@ -1659,6 +1672,8 @@
         ],
         load_sem,
     )
+    soon = moves([(meta_in, meta_ref), (dx_in, dx_ref)], soon_sem)
+    start_all(soon)
     greet(col_peers(cols) + [(flip(r, m), c) for m in (1, 2, 4, 6)])
     last = gown_ref.shape[0] - 1
     across = send_to(glast_ref, sib_ref.at[last], last_sem.at[0], last_sem.at[1], (flip(r, 1), c))
@@ -1671,6 +1686,7 @@
     dot_copies = to_cols(dots_of, dots_in, dsend, drecv, cols)
     start_all(dot_copies)
     dots_in[c] = dots_of(c)[...]
+    wait_all(soon)
     for n, d in enumerate(chain_order(c)):
         gt_s[d] = combine(meta_ref, dx_ref, d, local)
         if n == 0:
@@ -1841,7 +1857,7 @@
             jax.ShapeDtypeStruct((held - count, 3, three, depth, ff), BF),
             jax.ShapeDtypeStruct(sib.shape, BF),
         ),
-        in_specs=[vm] * 7 + [ANY] * 8,
+        in_specs=[ANY] * 2 + [vm] * 5 + [ANY] * 8,
         out_specs=(vm, ANY, ANY, vm, vm, vm, ANY, ANY, ANY),
         input_output_aliases={14: 8},
         scratch_shapes=[
@@ -1871,6 +1887,9 @@
             dma((4,)),
             pltpu.VMEM((chips, 2, depth, D), BF),
             pltpu.VMEM((chips, depth, D), BF),
+            pltpu.VMEM(dx.shape, BF),
+            pltpu.VMEM(meta.shape, F32),
+            dma((2,)),
         ],
         compiler_params=pltpu.CompilerParams(
             vmem_limit_bytes=60 * MIB, collective_id=3, has_side_effects=True
@@ -1883,9 +1902,9 @@
 def finish_kernel(
     cols,
     ranks,
-    gm_ref,
-    meta_ref,
-    lse_ref,
+    gm_in,
+    meta_in,
+    lse_in,
     small_ref,
     og_ref,
     xown_ref,
@@ -1957,6 +1976,10 @@
     hrecv,
     g_s,
     store_sem,
+    gm_ref,
+    meta_ref,
+    lse_ref,
+    soon_sem,
 ):
     r, c = place()
     chip, core = r // 2, r % 2
@@ -1975,6 +1998,8 @@
     loads = moves(
         [(x_in, x_s), (w_in, w_s), (cos_in, cos_s), (sin_in, sin_s), (resid_in, resid_s)], load_sem
     )
+    soon = moves([(gm_in, gm_ref), (meta_in, meta_ref), (lse_in, lse_ref)], soon_sem)
+    start_all(soon)
     start_all(head_loads(0))
     greet(col_peers(cols) + [(flip(r, m), c) for m in range(1, ranks)])
     for h in range(1, heads):
@@ -1987,6 +2012,7 @@
     og_to_chips = to_chips(lambda there: og_ref.at[there], og_chips, chip_send.at[0], chip_recv.at[0])
     start_all(og_to_chips)
 
+    wait_all(soon)
     for d in range(cols):
         at = slice(d * local, (d + 1) * local)
         for h in range(heads):
@@ -2209,7 +2235,7 @@
             weight_grad,
             jax.ShapeDtypeStruct((rest, 3, three, depth, ff), BF),
         ),
-        in_specs=[vm] * 7 + [ANY] * 12,
+        in_specs=[ANY] * 3 + [vm] * 4 + [ANY] * 12,
         out_specs=(vm,) * 4 + (ANY,) * 4,
         scratch_shapes=[
             pltpu.VMEM((3 * heads, rows, HEAD_DIM), BF),
@@ -2256,6 +2282,10 @@
             dma((rest, 3)),
             pltpu.VMEM((three, experts, depth, ff), BF),
             dma((3,)),
+            pltpu.VMEM(gm.shape, BF),
+            pltpu.VMEM(meta.shape, F32),
+            pltpu.VMEM(lse.shape, F32),
+            dma((3,)),
         ],
         compiler_params=pltpu.CompilerParams(
             vmem_limit_bytes=62 * MIB, collective_id=4, has_side_effects=True

time: 364 us -> 363 us (level)
    pallas_call x1, Pallas kernels: 33.1 us -> 38.2 us  [experts_forward(): pl.pallas_call(functools.partial(experts_forward_kernel, cols, capacity),...]
where the time goes in v7:
time: 363 us; the launch traced here: 360 us
  Pallas kernels  359 us (99%)
    pallas_call x1, Pallas kernels, first_step(): pl.pallas_call(functools.partial(first_kernel, cols, ranks), out_shape=(j...  117 us
    pallas_call x1, Pallas kernels, finish_step(): pl.pallas_call(functools.partial(finish_kernel, cols, ranks), out_shape=(...  79.6 us
    pallas_call x1, Pallas kernels, resid_step(): pl.pallas_call(functools.partial(resid_kernel, cols, count), out_shape=(j...  62.7 us
    pallas_call x1, Pallas kernels, experts_backward(): pl.pallas_call(functools.partial(experts_backward_kernel, cols, capacity)...  56.5 us
    pallas_call x1, Pallas kernels, experts_forward(): pl.pallas_call(functools.partial(experts_forward_kernel, cols, capacity),...  38.2 us

profile of v7, /device:TPU:0, one launch (start us, length us, event | category | flops | bytes accessed | tf_op | source)
XLA Modules:
  0.0 359.7 jit_solution(9780346433558413158)
XLA Ops:
  0.7 117.1 %first_step.1 = (bf16[3,8,768,512]{3,2,1,0:T(8,128)(2,1)}, bf16[9,1536,64]{2,1,0:T(8,128)(2,1)}, bf16[3,1536,64]{2,1,0:T(8,128)(2,1)}, f32[1536,128]{1,0:T(8,128...) custom-call(bf16[384,768]{1,0:T(8,128)(2,1)} %xown_ref.1, ...), custom_call_target="tpu_custom_call" | custom-call | flops 3623878656 | bytes 41943040 | tf_op jit(solution)/shard_map/first_step/pallas_call | solution.py:1183
  117.8 38.2 %experts_forward.1 = (bf16[8,384,768]{2,1,0:T(8,128)(2,1)}, bf16[8,2,384,512]{3,2,1,0:T(8,128)(2,1)}, bf16[8,384,768]{2,1,0:T(8,128)(2,1)}, bf16[1536,256]{1,0:T(8,128)(2,1)}, bf16[4,320,768]{2,1,0:T(8,128)(2,1)}) custom-call(bf16[1536,768]{1,0:T(8,128)(2,1)} %bitcast.8, bf16[4,16,384]{2,1,0:T(8,128)(2,1)} %get-tuple-element.76.prev_ref, ...), custom_call_target="tpu_custom_call" | custom-call | flops 14495514624 | bytes 41943040 | tf_op jit(solution)/shard_map/experts_forward/pallas_call | solution.py:1336
  156.0 56.5 %experts_backward.1 = (bf16[8,384,768]{2,1,0:T(8,128)(2,1)}, f32[8,1536]{1,0:T(8,128)}, f32[384,768]{1,0:T(8,128)}, bf16[8,3,4,96,512]{4,3,2,1,0:T(8,128)(2,1)},...) custom-call(bf16[4,64,768]{2,1,0:T(8,128)(2,1)} %get-tuple-element.74.cota, ...), custom_call_target="tpu_custom_call" | custom-call | flops 28991029248 | bytes 62914560 | tf_op jit(solution)/shard_map/experts_backward/pallas_call | solution.py:1542
  212.5 62.7 %resid_step.1 = (bf16[384,768]{1,0:T(8,128)(2,1)}, f32[384,768]{1,0:T(8,128)}, bf16[4,3,192,128]{3,2,1,0:T(8,128)(2,1)}, bf16[4,96,768]{2,1,0:T(8,128)(2,1)}, f3...) custom-call(bf16[8,384,768]{2,1,0:T(8,128)(2,1)} %get-tuple-element., ...), custom_call_target="tpu_custom_call", output_to_operand_aliasing={{8}: (14, {})} | custom-call | flops 1358954496 | bytes 41943040 | tf_op jit(solution)/shard_map/resid_step/pallas_call | solution.py:1847
  275.2 79.6 %finish_step.1 = (f32[384,768]{1,0:T(8,128)}, f32[24,1024]{1,0:T(8,128)}, f32[96,576]{1,0:T(8,128)}, f32[96,192]{1,0:T(8,128)}, bf16[8,96,512]{2,1,0:T(8,128)(2,...) custom-call(bf16[4,3,192,128]{3,2,1,0:T(8,128)(2,1)} %get-tuple-element.96.gm_in, ...), custom_call_target="tpu_custom_call" | custom-call | flops 9059696640 | bytes 41943040 | tf_op jit(solution)/shard_map/finish_step/pallas_call | solution.py:2226
  354.8 4.6 %place_outputs.1 = (bf16[384,768]{1,0:T(8,128)(2,1)}, f32[384,768]{1,0:T(8,128)}, f32[8,96,512]{2,1,0:T(8,128)}, f32[8,96,512]{2,1,0:T(8,128)}, f32[8,96,512]{2,...) custom-call(f32[24,1024]{1,0:T(8,128)} %get-tuple-element.111.refs_0, ...), custom_call_target="tpu_custom_call" | custom-call | bytes 16777216 | tf_op jit(solution)/shard_map/place_outputs/pallas_call | solution.py:2338

commit v8 on v7

--- a/solution.py
+++ b/solution.py
@@ -1274,9 +1274,10 @@
     w_ref,
     x_ref,
     gu_ref,
-    y_ref,
+    mix_ref,
     gates_ref,
     cotb_ref,
+    y_s,
     send,
     recv,
     local_sem,
@@ -1317,10 +1318,12 @@
     gu_ref[0, 0] = g.astype(BF)
     gu_ref[0, 1] = u.astype(BF)
     gh = (g * jax.nn.sigmoid(g) * u * sg).astype(BF)
-    y_ref[0] = mm(gh, w_ref[2, 0], NT).astype(BF)
+    y_s[e] = mm(gh, w_ref[2, 0], NT).astype(BF)
 
     @pl.when(e == experts - 1)
     def _():
+        for d in range(cols):
+            mix_ref[d] = combine(meta_ref, y_s, d, mix_ref.shape[1])
         for k in range(3, cols):
             step(k)
         drain()
@@ -1339,7 +1342,7 @@
         out_shape=(
             jax.ShapeDtypeStruct((experts, capacity, D), BF),
             jax.ShapeDtypeStruct((experts, 2, capacity, ff), BF),
-            jax.ShapeDtypeStruct((experts, capacity, D), BF),
+            jax.ShapeDtypeStruct((cols, local, D), BF),
             jax.ShapeDtypeStruct((rows, 2 * LANES), BF),
             jax.ShapeDtypeStruct((cols, rest, D), BF),
         ),
@@ -1356,11 +1359,12 @@
         out_specs=(
             pl.BlockSpec((1, capacity, D), lambda e: (e, 0, 0)),
             pl.BlockSpec((1, 2, capacity, ff), lambda e: (e, 0, 0, 0)),
-            pl.BlockSpec((1, capacity, D), lambda e: (e, 0, 0)),
+            whole((cols, local, D)),
             whole((rows, 2 * LANES)),
             ANY,
         ),
         scratch_shapes=[
+            pltpu.VMEM((experts, capacity, D), BF),
             pltpu.SemaphoreType.DMA((2, cols - 1)),
             pltpu.SemaphoreType.DMA((2, cols - 1)),
             pltpu.SemaphoreType.DMA((1,)),
@@ -1382,7 +1386,7 @@
     capacity,
     cota_ref,
     cotb_ref,
-    y_ref,
+    mix_s,
     gates_ref,
     slots_ref,
     meta_ref,
@@ -1397,7 +1401,6 @@
     hin_ref,
     glast_ref,
     cot_s,
-    mix_s,
     gbuf,
     out,
     arrived,
@@ -1453,10 +1456,7 @@
     def _():
         start_all(cot_loads)
         greet(col_peers(cols) + [(flip(r, m), c) for m in (1, 2, 4, 6)])
-        for n, d in enumerate(chain_order(c)):
-            mix_s[d] = combine(meta_ref, y_ref, d, local)
-            if n == 0:
-                slot(0)
+        slot(0)
         wait_all(cot_loads)
 
     @pl.when(e == 2)
@@ -1531,8 +1531,8 @@
             wait_all(h_sends(i))
 
 
-def experts_backward(cols, ranks, cota, cotb, y, gates, meta, slots, w_all, x, gu):
-    experts, capacity, _ = y.shape
+def experts_backward(cols, ranks, cota, cotb, mix, gates, meta, slots, w_all, x, gu):
+    experts, capacity, _ = x.shape
     rows = slots.shape[1]
     three, _, deep, ff = w_all.shape
     local = rows // cols
@@ -1554,7 +1554,7 @@
         in_specs=[
             ANY,
             ANY,
-            whole((experts, capacity, D)),
+            whole((cols, local, D)),
             whole((rows, 2 * LANES)),
             whole((experts, rows)),
             whole((rows, LANES)),
@@ -1573,7 +1573,6 @@
         ),
         scratch_shapes=[
             pltpu.VMEM((rows, D), BF),
-            pltpu.VMEM((cols, local, D), BF),
             pltpu.VMEM((2, three, chips, 2, depth, ff), BF),
             *chain_scratch(cols, local),
             pltpu.SemaphoreType.DMA((2,)),
@@ -1595,7 +1594,7 @@
             transcendentals=experts * capacity * ff,
         ),
         name="experts_backward",
-    )(cota, cotb, y, gates, slots, meta, w_all, x, gu)
+    )(cota, cotb, mix, gates, slots, meta, w_all, x, gu)
 
 
 def resid_kernel(
@@ -2412,11 +2411,11 @@
         up_weight,
         down_weight.transpose(0, 2, 1),
     )
-    x, gu, y, gates, cot_late = experts_forward(
+    x, gu, mix, gates, cot_late = experts_forward(
         cols, n2_whole.reshape(row_total, D), prev_whole, cotangent, rw, carry, meta, slots, w_all
     )
     dx, dots, mixsum, gown, sib, hsoon, glast = experts_backward(
-        cols, ranks, cot_early, cot_late, y, gates, meta, slots, w_all, x, gu
+        cols, ranks, cot_early, cot_late, mix, gates, meta, slots, w_all, x, gu
     )
     layer_out, resid, gm, og, small, prev_grad, hin0, hrest, sib = resid_step(
         cols, dx, meta, dots, rw, prev_whole, carry, cotangent, mixsum, n2_whole, middle, out_t, mixed, gown, glast, sib

time: 363 us -> 362 us (level)
    pallas_call x1, Pallas kernels: 56.5 us -> 48.9 us  [experts_backward(): pl.pallas_call(functools.partial(experts_backward_kernel, cols, capacity)...]
    pallas_call x1, Pallas kernels: 38.2 us -> 42.9 us  [experts_forward(): pl.pallas_call(functools.partial(experts_forward_kernel, cols, capacity),...]
where the time goes in v8:
time: 362 us; the launch traced here: 359 us
  Pallas kernels  358 us (99%)
    pallas_call x1, Pallas kernels, first_step(): pl.pallas_call(functools.partial(first_kernel, cols, ranks), out_shape=(j...  117 us
    pallas_call x1, Pallas kernels, finish_step(): pl.pallas_call(functools.partial(finish_kernel, cols, ranks), out_shape=(...  78.9 us
    pallas_call x1, Pallas kernels, resid_step(): pl.pallas_call(functools.partial(resid_kernel, cols, count), out_shape=(j...  65.1 us
    pallas_call x1, Pallas kernels, experts_backward(): pl.pallas_call(functools.partial(experts_backward_kernel, cols, capacity)...  48.9 us
    pallas_call x1, Pallas kernels, experts_forward(): pl.pallas_call(functools.partial(experts_forward_kernel, cols, capacity),...  42.9 us

profile of v8, /device:TPU:0, one launch (start us, length us, event | category | flops | bytes accessed | tf_op | source)
XLA Modules:
  0.0 358.6 jit_solution(5175338243342685894)
XLA Ops:
  0.7 117.1 %first_step.1 = (bf16[3,8,768,512]{3,2,1,0:T(8,128)(2,1)}, bf16[9,1536,64]{2,1,0:T(8,128)(2,1)}, bf16[3,1536,64]{2,1,0:T(8,128)(2,1)}, f32[1536,128]{1,0:T(8,128...) custom-call(bf16[384,768]{1,0:T(8,128)(2,1)} %xown_ref.1, ...), custom_call_target="tpu_custom_call" | custom-call | flops 3623878656 | bytes 41943040 | tf_op jit(solution)/shard_map/first_step/pallas_call | solution.py:1183
  117.8 42.9 %experts_forward.1 = (bf16[8,384,768]{2,1,0:T(8,128)(2,1)}, bf16[8,2,384,512]{3,2,1,0:T(8,128)(2,1)}, bf16[4,384,768]{2,1,0:T(8,128)(2,1)}, bf16[1536,256]{1,0:T(8,128)(2,1)}, bf16[4,320,768]{2,1,0:T(8,128)(2,1)}) custom-call(bf16[1536,768]{1,0:T(8,128)(2,1)} %bitcast.8, bf16[4,16,384]{2,1,0:T(8,128)(2,1)} %get-tuple-element.76.prev_ref, ...), custom_call_target="tpu_custom_call" | custom-call | flops 14495514624 | bytes 41943040 | tf_op jit(solution)/shard_map/experts_forward/pallas_call | solution.py:1339
  160.7 48.9 %experts_backward.1 = (bf16[8,384,768]{2,1,0:T(8,128)(2,1)}, f32[8,1536]{1,0:T(8,128)}, f32[384,768]{1,0:T(8,128)}, bf16[8,3,4,96,512]{4,3,2,1,0:T(8,128)(2,1)},...) custom-call(bf16[4,64,768]{2,1,0:T(8,128)(2,1)} %get-tuple-element.74.cota, ...), custom_call_target="tpu_custom_call" | custom-call | flops 28991029248 | bytes 62914560 | tf_op jit(solution)/shard_map/experts_backward/pallas_call | solution.py:1542
  209.7 65.1 %resid_step.1 = (bf16[384,768]{1,0:T(8,128)(2,1)}, f32[384,768]{1,0:T(8,128)}, bf16[4,3,192,128]{3,2,1,0:T(8,128)(2,1)}, bf16[4,96,768]{2,1,0:T(8,128)(2,1)}, f3...) custom-call(bf16[8,384,768]{2,1,0:T(8,128)(2,1)} %get-tuple-element., ...), custom_call_target="tpu_custom_call", output_to_operand_aliasing={{8}: (14, {})} | custom-call | flops 1358954496 | bytes 41943040 | tf_op jit(solution)/shard_map/resid_step/pallas_call | solution.py:1846
  274.7 78.9 %finish_step.1 = (f32[384,768]{1,0:T(8,128)}, f32[24,1024]{1,0:T(8,128)}, f32[96,576]{1,0:T(8,128)}, f32[96,192]{1,0:T(8,128)}, bf16[8,96,512]{2,1,0:T(8,128)(2,...) custom-call(bf16[4,3,192,128]{3,2,1,0:T(8,128)(2,1)} %get-tuple-element.96.gm_in, ...), custom_call_target="tpu_custom_call" | custom-call | flops 9059696640 | bytes 41943040 | tf_op jit(solution)/shard_map/finish_step/pallas_call | solution.py:2225
  353.7 4.6 %place_outputs.1 = (bf16[384,768]{1,0:T(8,128)(2,1)}, f32[384,768]{1,0:T(8,128)}, f32[8,96,512]{2,1,0:T(8,128)}, f32[8,96,512]{2,1,0:T(8,128)}, f32[8,96,512]{2,...) custom-call(f32[24,1024]{1,0:T(8,128)} %get-tuple-element.111.refs_0, ...), custom_call_target="tpu_custom_call" | custom-call | bytes 16777216 | tf_op jit(solution)/shard_map/place_outputs/pallas_call | solution.py:2337
